TPU v7x, 32 devices: a whole 2x2x4 slice. The times are simulated.
32 devices in a mesh: freq: 4 (over z), px: 4 (over y, x), py: 2 (over core).
Axes of the slice: x: 2, y: 2, z: 4, core: 2. Of those that a mesh axis runs over, the one named last changes fastest.
Arguments:
- observed: float32 [4, 32, 2, 128], P('freq', ('px', 'py')), may hold values from -6 to 6
- noise_scale: float32 [4, 32], P('freq', ('px', 'py')), may hold values from 0.5 to 2
- forward_kernel: bfloat16 [4, 32, 128, 2, 32], P('freq', 'px', 'py'), may hold values from -0.125 to 0.125
- model_field: float32 [32, 128, 128], P('px', 'py'), may hold values from -6 to 6
- classes: int32 [32, 128], P('px', 'py'), may hold values from 0 to 15
- kappa_table: float32 [16], replicated, may hold values from 0.1 to 0.6
- coupling_table: float32 [4, 16], replicated, may hold values from 0.15 to 0.35
Outputs:
- weighted_residual: float32 [4, 32, 2, 128], P('freq', ('px', 'py'))
- gradient: float32 [32, 128, 128], P('px', 'py')
All inputs are finite; a program needn't handle non-finite values.
Results may differ from a plain program's by a relative error of at most 0.003.
Values may be sent and summed in bfloat16 or wider, within the bound.
No kernel may reach another device: no remote copies, remote signals or barrier semaphores. Data moves between devices by JAX's collectives and lax.ppermute only.
A program may use at most 64 MiB of HBM per device.

v0:
```python
import jax
import jax.numpy as jnp
from jax import lax
from jax.sharding import PartitionSpec as P

SWEEPS = 4


FREEDOM = 4.0
PRIOR_WEIGHT = 0.04


def with_halo(shard, sides, width):
    for axis, dim in sides:
        peers, length = (lax.axis_size(axis), shard.shape[dim])
        up = [(i, (i + 1) % peers) for i in range(peers - 1)]
        down = [(j, i) for i, j in up]
        last = lax.slice_in_dim(shard, length - width, length, axis=dim)
        initial = lax.slice_in_dim(shard, 0, width, axis=dim)
        before = lax.ppermute(last, axis, up)
        after = lax.ppermute(initial, axis, down)
        shard = jnp.concatenate([before, shard, after], axis=dim)
    return shard


def student_weights(misfit, noise):
    inverse = 1.0 / (noise * noise)
    spread = (misfit[:, 0] * misfit[:, 0] + misfit[:, 1] * misfit[:, 1]) * inverse[:, None]
    factor = (FREEDOM + 2.0) / (FREEDOM + spread) * inverse[:, None]
    return misfit * factor[:, None, :]


def coefficients(classes, kappa_table, coupling_table):
    levels = jnp.arange(kappa_table.shape[0], dtype=jnp.int32)
    onehot = (classes[..., None] == levels).astype(jnp.float32)
    diagonal = kappa_table + jnp.sum(coupling_table, axis=0)
    class_table = jnp.concatenate([diagonal[None, :], coupling_table], axis=0)
    return jnp.einsum("xyk,ck->xyc", onehot, class_table, precision=lax.Precision.HIGHEST)


def operate(padded, coefficient):
    center = padded[1:-1, 1:-1]
    beside = coefficient[..., 1:2] * padded[:-2, 1:-1] + coefficient[..., 2:3] * padded[2:, 1:-1]
    beside = (
        beside
        + coefficient[..., 3:4] * padded[1:-1, :-2]
        + coefficient[..., 4:5] * padded[1:-1, 2:]
    )
    return coefficient[..., 0:1] * center - beside


def prior_sweeps(state_field, coefficient):
    state_field, coef_rim = (
        with_halo(state_field, (("px", 0), ("py", 1)), SWEEPS),
        with_halo(coefficient, (("px", 0), ("py", 1)), SWEEPS),
    )
    for sweep_index in range(SWEEPS):
        cropped = coef_rim[
            sweep_index + 1 : coef_rim.shape[0] - sweep_index - 1,
            sweep_index + 1 : coef_rim.shape[1] - sweep_index - 1,
        ]
        state_field = operate(state_field, cropped)
    return state_field


def local(observed, noise_scale, forward_kernel, model_field, classes, kappa_table, coupling_table):
    kernel_flat = forward_kernel.reshape(-1, forward_kernel.shape[3], forward_kernel.shape[4])
    realizations = model_field.shape[2]
    cells = kernel_flat.shape[0]
    model_low = model_field.astype(jnp.bfloat16).reshape(cells, realizations)
    kernel_part = kernel_flat
    predicted = lax.psum_scatter(
        jnp.einsum("pcs,pr->scr", kernel_part, model_low, preferred_element_type=jnp.float32),
        ("px", "py"),
        scatter_dimension=0,
        tiled=True,
    )
    weighted = student_weights(predicted - observed[0], noise_scale[0])
    weighted_low = weighted.astype(jnp.bfloat16)
    kernel_part = kernel_flat
    data_grad = jnp.einsum(
        "pcs,scr->pr",
        kernel_part,
        lax.all_gather(weighted_low, ("px", "py"), axis=0, tiled=True),
        preferred_element_type=jnp.float32,
    )
    data_grad = data_grad.reshape(model_field.shape)
    coefficient = coefficients(classes, kappa_table, coupling_table)
    data_total = lax.psum(data_grad, "freq")
    prior_term = prior_sweeps(model_field, coefficient)
    gradient = data_total + PRIOR_WEIGHT * prior_term
    return (weighted[None], gradient)


def solution(mesh):
    in_specs = (
        P("freq", ("px", "py"), None, None),
        P("freq", ("px", "py")),
        P("freq", "px", "py", None, None),
        P("px", "py", None),
        P("px", "py"),
        P(),
        P(),
    )
    out_specs = (P("freq", ("px", "py"), None, None), P("px", "py", None))
    return jax.shard_map(local, mesh=mesh, in_specs=in_specs, out_specs=out_specs, check_vma=False)
```

profile of v0, /device:TPU:0, one launch (start us, length us, event | category | flops | bytes accessed | tf_op | source)
XLA Modules:
  0.0 114.3 jit_solution(12405483103650886351)
XLA Ops:
  7.2 0.7 reduce_sum.9
  8.0 0.8 fusion.18
  8.8 4.8 %collective-permute-start = (f32[4,64,5]{1,2,0:T(8,128)S(1)}, f32[4,64,5]{1,2,0:T(8,128)S(1)}, u32[]{:S(2)}, u32[]{:S(2)}) collective-permute-start(f32[4,64,5]{1,2,0:T(8,128)S(1)} %get-tuple-element.36), channel_id=1, source_target_pairs={{0,2},{2,4},{4,6},{1,3},{3,5},{5,7},{8,10},{10,12},{12,14},{9,11},... | collective-permute-start | bytes 15368 | tf_op jit(solution)/shard_map/ppermute | solution.py:20
  13.7 1.3 %collective-permute-start.1 = (f32[4,64,5]{1,2,0:T(8,128)S(1)}, f32[4,64,5]{1,2,0:T(8,128)S(1)}, u32[]{:S(2)}, u32[]{:S(2)}) collective-permute-start(f32[4,64,5]{1,2,0:T(8,128)S(1)} %get-tuple-element.37), channel_id=1, source_target_pairs={{2,0},{4,2},{6,4},{3,1},{5,3},{7,5},{10,8},{12,10},{14,12},{11,9},... | collective-permute-start | bytes 15368 | tf_op jit(solution)/shard_map/ppermute | solution.py:21
  15.0 1.0 fusion.29
  15.9 4.6 %collective-permute-start.4 = (f32[4,64,128]{2,1,0:T(8,128)S(1)}, f32[4,64,128]{2,1,0:T(8,128)S(1)}, u32[]{:S(2)}, u32[]{:S(2)}) collective-permute-start(f32[4,64,128]{2,1,0:T(8,128)S(1)} %get-tuple-element.11), channel_id=1, source_target_pairs={{0,2},{2,4},{4,6},{1,3},{3,5},{5,7},{8,10},{10,12},{12,14},{9,11},... | collective-permute-start | bytes 393224 | tf_op jit(solution)/shard_map/ppermute | solution.py:20
  20.5 1.3 %collective-permute-start.5 = (f32[4,64,128]{2,1,0:T(8,128)S(1)}, f32[4,64,128]{2,1,0:T(8,128)S(1)}, u32[]{:S(2)}, u32[]{:S(2)}) collective-permute-start(f32[4,64,128]{2,1,0:T(8,128)S(1)} %get-tuple-element.10), channel_id=1, source_target_pairs={{2,0},{4,2},{6,4},{3,1},{5,3},{7,5},{10,8},{12,10},{14,12},{11,9},... | collective-permute-start | bytes 393224 | tf_op jit(solution)/shard_map/ppermute | solution.py:21
  22.0 1.4 %collective-permute-start.2 = (f32[16,4,5]{1,2,0:T(8,128)S(1)}, f32[16,4,5]{1,2,0:T(8,128)S(1)}, u32[]{:S(2)}, u32[]{:S(2)}) collective-permute-start(f32[16,4,5]{1,2,0:T(8,128)S(1)} %get-tuple-element.29), channel_id=1, source_target_pairs={{0,1},{2,3},{4,5},{6,7},{8,9},{10,11},{12,13},{14,15},{16,17},{18,... | collective-permute-start | bytes 3848 | tf_op jit(solution)/shard_map/ppermute | solution.py:20
  23.4 1.3 %collective-permute-start.3 = (f32[16,4,5]{1,2,0:T(8,128)S(1)}, f32[16,4,5]{1,2,0:T(8,128)S(1)}, u32[]{:S(2)}, u32[]{:S(2)}) collective-permute-start(f32[16,4,5]{1,2,0:T(8,128)S(1)} %get-tuple-element.30), channel_id=1, source_target_pairs={{1,0},{3,2},{5,4},{7,6},{9,8},{11,10},{13,12},{15,14},{17,16},{19,... | collective-permute-start | bytes 3848 | tf_op jit(solution)/shard_map/ppermute | solution.py:21
  24.7 0.1 copy.16
  24.8 0.1 reshape.38
  25.0 0.1 reshape.36
  25.1 0.6 copy-done.6
  25.8 0.6 dynamic-slice
  27.0 0.1 pad_maximum_fusion.2
  27.2 0.1 fusion.32
  27.3 0.1 fusion.31
  27.4 0.1 fusion.30
  27.7 0.8 copy-done
  28.7 3.0 %collective-permute-start.6 = (f32[16,4,128]{2,1,0:T(4,128)S(1)}, f32[16,4,128]{2,1,0:T(4,128)S(1)}, u32[]{:S(2)}, u32[]{:S(2)}) collective-permute-start(f32[16,4,128]{2,1,0:T(4,128)S(1)} %get-tuple-element.8), channel_id=1, source_target_pairs={{0,1},{2,3},{4,5},{6,7},{8,9},{10,11},{12,13},{14,15},{16,17},{18,... | collective-permute-start | bytes 98312 | tf_op jit(solution)/shard_map/ppermute | solution.py:20
  31.6 1.3 %collective-permute-start.7 = (f32[16,4,128]{2,1,0:T(4,128)S(1)}, f32[16,4,128]{2,1,0:T(4,128)S(1)}, u32[]{:S(2)}, u32[]{:S(2)}) collective-permute-start(f32[16,4,128]{2,1,0:T(4,128)S(1)} %get-tuple-element.9), channel_id=1, source_target_pairs={{1,0},{3,2},{5,4},{7,6},{9,8},{11,10},{13,12},{15,14},{17,16},{19,... | collective-permute-start | bytes 98312 | tf_op jit(solution)/shard_map/ppermute | solution.py:21
  32.9 0.2 fusion.36
  33.1 26.6 %all-reduce = f32[32,2,128]{2,0,1:T(8,128)S(1)} all-reduce(f32[32,2,128]{2,0,1:T(8,128)S(1)} %bitcast.74), channel_id=2, replica_groups=mesh['freq'=4,'px'=4,'py'=2] {'px','py'}, use_global_device_ids=true, to_apply=%region_0.0.clone | all-reduce | flops 8192 | bytes 65536
  59.9 8.7 %all_gather.3 = bf16[32,2,128]{2,1,0:T(2,128)(2,1)S(1)} all-gather(bf16[4,2,128]{2,1,0:T(2,128)(2,1)S(1)} %copy.18), channel_id=1, replica_groups=mesh['freq'=4,'px'=4,'py'=2] {'px','py'}, dimensions={0}, use_global_device_ids=true | all-gather | bytes 18432 | tf_op jit(solution)/shard_map/all_gather | solution.py:84
  68.5 0.2 convolution_bitcast_fusion
  68.7 0.8 copy.20
  69.6 0.6 copy.21
  70.3 0.9 fusion.1
  71.1 0.8 fusion.5
  71.9 0.5 fusion.9
  72.5 32.9 %all-reduce.3.cloned.1.call-done = f32[8,64,128]{2,1,0:T(8,128)} async-done(((f32[8,64,128]{2,1,0:T(8,128)}), f32[8,64,128]{2,1,0:T(8,128)}) %all-reduce.3.cloned.1.call-update) | async-done | bytes 262160 | tf_op jit(solution)/shard_map/psum | solution.py:89
  105.4 2.1 %fusion.15 = f32[8,64,128]{2,1,0:T(8,128)} fusion(f32[8,64,128]{2,1,0:T(8,128)} %all-reduce.3.cloned.1.call-done, f32[10,66,128]{2,1,0:T(8,128)S(1)} %fusion.9, f32[8,64]{1,0:T(8,128)S(1)} %bitcast.79, f32[8,64]{1,0:T(8,128)S(1)} %bitcast.80, f32[8,64]{1,0:T(8,128)S(1)} %bitcast.81, f32[8,64]{1,0:T(8,128)S(1)} %bitcast.82, f32[8,64]{1,0:T(8,128)S(1)} %bitcast.78), kind=kLoop, calls=%fused_computation.33 | loop fusion | flops 720896 | bytes 1845248 | tf_op jit(solution)/shard_map/add | solution.py:91
  (46 shorter events, 0.6 us)
Async XLA Ops:
  7.2 0.8 copy-start.2
  7.2 0.8 copy-start.4
  7.2 98.2 %all-reduce.3.cloned.1.call-start = ((), (), s32[]{:S(2)}) async-start(), calls=%async_computation | async-start | bytes 524288 | tf_op jit(solution)/shard_map/psum | solution.py:89
  8.8 13.0 %collective-permute-start = (f32[4,64,5]{1,2,0:T(8,128)S(1)}, f32[4,64,5]{1,2,0:T(8,128)S(1)}, u32[]{:S(2)}, u32[]{:S(2)}) collective-permute-start(f32[4,64,5]{1,2,0:T(8,128)S(1)} %get-tuple-element.36), channel_id=1, source_target_pairs={{0,2},{2,4},{4,6},{1,3},{3,5},{5,7},{8,10},{10,12},{12,14},{9,11},... | collective-permute-start | bytes 15368 | tf_op jit(solution)/shard_map/ppermute | solution.py:20
  13.7 8.2 %collective-permute-start.1 = (f32[4,64,5]{1,2,0:T(8,128)S(1)}, f32[4,64,5]{1,2,0:T(8,128)S(1)}, u32[]{:S(2)}, u32[]{:S(2)}) collective-permute-start(f32[4,64,5]{1,2,0:T(8,128)S(1)} %get-tuple-element.37), channel_id=1, source_target_pairs={{2,0},{4,2},{6,4},{3,1},{5,3},{7,5},{10,8},{12,10},{14,12},{11,9},... | collective-permute-start | bytes 15368 | tf_op jit(solution)/shard_map/ppermute | solution.py:21
  15.9 11.7 %collective-permute-start.4 = (f32[4,64,128]{2,1,0:T(8,128)S(1)}, f32[4,64,128]{2,1,0:T(8,128)S(1)}, u32[]{:S(2)}, u32[]{:S(2)}) collective-permute-start(f32[4,64,128]{2,1,0:T(8,128)S(1)} %get-tuple-element.11), channel_id=1, source_target_pairs={{0,2},{2,4},{4,6},{1,3},{3,5},{5,7},{8,10},{10,12},{12,14},{9,11},... | collective-permute-start | bytes 393224 | tf_op jit(solution)/shard_map/ppermute | solution.py:20
  20.5 8.1 %collective-permute-start.5 = (f32[4,64,128]{2,1,0:T(8,128)S(1)}, f32[4,64,128]{2,1,0:T(8,128)S(1)}, u32[]{:S(2)}, u32[]{:S(2)}) collective-permute-start(f32[4,64,128]{2,1,0:T(8,128)S(1)} %get-tuple-element.10), channel_id=1, source_target_pairs={{2,0},{4,2},{6,4},{3,1},{5,3},{7,5},{10,8},{12,10},{14,12},{11,9},... | collective-permute-start | bytes 393224 | tf_op jit(solution)/shard_map/ppermute | solution.py:21
  21.9 2.9 %copy-start.1 = (bf16[1,8,64,2,32]{2,4,3,1,0:T(8,128)(2,1)S(1)}, bf16[1,8,64,2,32]{2,4,3,1,0:T(8,128)(2,1)}, u32[]{:S(2)}) copy-start(bf16[1,8,64,2,32]{2,4,3,1,0:T(8,128)(2,1)} %param.9) | copy-start | bytes 196612
  22.0 2.7 %copy-start.5 = (f32[1,4]{1,0:T(1,128)S(1)}, f32[1,4]{1,0:T(1,128)}, u32[]{:S(2)}) copy-start(f32[1,4]{1,0:T(1,128)} %param.8) | copy-start | bytes 52
  22.0 5.1 %collective-permute-start.2 = (f32[16,4,5]{1,2,0:T(8,128)S(1)}, f32[16,4,5]{1,2,0:T(8,128)S(1)}, u32[]{:S(2)}, u32[]{:S(2)}) collective-permute-start(f32[16,4,5]{1,2,0:T(8,128)S(1)} %get-tuple-element.29), channel_id=1, source_target_pairs={{0,1},{2,3},{4,5},{6,7},{8,9},{10,11},{12,13},{14,15},{16,17},{18,... | collective-permute-start | bytes 3848 | tf_op jit(solution)/shard_map/ppermute | solution.py:20
  23.4 3.6 %collective-permute-start.3 = (f32[16,4,5]{1,2,0:T(8,128)S(1)}, f32[16,4,5]{1,2,0:T(8,128)S(1)}, u32[]{:S(2)}, u32[]{:S(2)}) collective-permute-start(f32[16,4,5]{1,2,0:T(8,128)S(1)} %get-tuple-element.30), channel_id=1, source_target_pairs={{1,0},{3,2},{5,4},{7,6},{9,8},{11,10},{13,12},{15,14},{17,16},{19,... | collective-permute-start | bytes 3848 | tf_op jit(solution)/shard_map/ppermute | solution.py:21
  25.1 0.7 copy-start.6
  27.5 1.0 copy-start
  28.7 41.5 %collective-permute-start.6 = (f32[16,4,128]{2,1,0:T(4,128)S(1)}, f32[16,4,128]{2,1,0:T(4,128)S(1)}, u32[]{:S(2)}, u32[]{:S(2)}) collective-permute-start(f32[16,4,128]{2,1,0:T(4,128)S(1)} %get-tuple-element.8), channel_id=1, source_target_pairs={{0,1},{2,3},{4,5},{6,7},{8,9},{10,11},{12,13},{14,15},{16,17},{18,... | collective-permute-start | bytes 98312 | tf_op jit(solution)/shard_map/ppermute | solution.py:20
  31.6 38.6 %collective-permute-start.7 = (f32[16,4,128]{2,1,0:T(4,128)S(1)}, f32[16,4,128]{2,1,0:T(4,128)S(1)}, u32[]{:S(2)}, u32[]{:S(2)}) collective-permute-start(f32[16,4,128]{2,1,0:T(4,128)S(1)} %get-tuple-element.9), channel_id=1, source_target_pairs={{1,0},{3,2},{5,4},{7,6},{9,8},{11,10},{13,12},{15,14},{17,16},{19,... | collective-permute-start | bytes 98312 | tf_op jit(solution)/shard_map/ppermute | solution.py:21
  33.1 26.7 %copy-start.3 = (f32[1,4,2,128]{3,2,1,0:T(2,128)S(1)}, f32[1,4,2,128]{3,2,1,0:T(2,128)}, u32[]{:S(2)}) copy-start(f32[1,4,2,128]{3,2,1,0:T(2,128)} %param.7) | copy-start | bytes 12292
Sparse Core Ops, SparseCore 0:
  69.7 35.5 all-reduce.2
where the time goes:
time: 115 us; the launch traced here: 114 us
  blocking collectives  35.3 us (31%)
  waiting for transfers between devices  33 us (29%)
  starting transfers between devices  19 us (17%)
  between operations  15.1 us (13%)
  local copies, waits for them, and re-layouts  5.42 us (5%)
  other arithmetic  5.27 us (5%)
  matrix products  1.19 us (1%)
    psum x1, waiting for transfers between devices, local(): data_total = lax.psum(data_grad, 'freq')  32.9 us
    unnamed x1, blocking collectives  26.6 us
    ppermute x4, starting transfers between devices, with_halo(): before = lax.ppermute(last, axis, up)  13.8 us
    all_gather x1, blocking collectives, local(): lax.all_gather(weighted_low, ('px', 'py'), axis=0, tiled=True)  8.66 us
    ppermute x4, starting transfers between devices, with_halo(): after = lax.ppermute(initial, axis, down)  5.17 us
    unnamed x28, local copies, waits for them, and re-layouts  2.94 us
  transfers between devices with their start and end apart: 9, of which 2 were waited for; matrix products, arithmetic and copies ran while one was open for 6% of the time, Pallas kernels for 0%

commit v1 on v0

v1 whole, which is shorter than its diff:
```python
import jax
import jax.numpy as jnp
from jax import lax
from jax.sharding import PartitionSpec as P

SWEEPS = 4
FREEDOM = 4.0
PRIOR_WEIGHT = 0.04
GATHER_LIMIT = 4 << 20


def rim(shard, axis, dim, width):
    peers, length = lax.axis_size(axis), shard.shape[dim]
    last = lax.slice_in_dim(shard, length - width, length, axis=dim)
    first = lax.slice_in_dim(shard, 0, width, axis=dim)
    even = lax.axis_index(axis) % 2 == 0

    def swap(start, own):
        pairs = [(i, i + 1) for i in range(start, peers - 1, 2)]
        if not pairs:
            return jnp.zeros_like(own)
        return lax.ppermute(own, axis, pairs + [(j, i) for i, j in pairs])

    one = swap(0, jnp.where(even, last, first))
    two = swap(1, jnp.where(even, first, last))
    before = jnp.where(even, two, one)
    after = jnp.where(even, one, two)
    return jnp.concatenate([before, shard, after], axis=dim)


def coefficients(classes, kappa_table, coupling_table):
    levels = jnp.arange(kappa_table.shape[0], dtype=jnp.int32)
    onehot = (classes[..., None] == levels).astype(jnp.float32)
    diagonal = kappa_table + jnp.sum(coupling_table, axis=0)
    class_table = jnp.concatenate([diagonal[None, :], coupling_table], axis=0)
    return jnp.einsum("xyk,ck->xyc", onehot, class_table, precision=lax.Precision.HIGHEST)


def operate(padded, coefficient):
    center = padded[1:-1, 1:-1]
    beside = coefficient[..., 1:2] * padded[:-2, 1:-1] + coefficient[..., 2:3] * padded[2:, 1:-1]
    beside = (
        beside
        + coefficient[..., 3:4] * padded[1:-1, :-2]
        + coefficient[..., 4:5] * padded[1:-1, 2:]
    )
    return coefficient[..., 0:1] * center - beside


def local(observed, noise_scale, forward_kernel, model_field, classes, kappa_table, coupling_table):
    space = ("px", "py")
    peers = lax.axis_size("px") * lax.axis_size("py")
    rows, cols, real = model_field.shape
    comps, sensors = forward_kernel.shape[3:]
    own = observed.shape[1]
    place = lax.axis_index(space)
    kernel_own = forward_kernel[0].transpose(0, 2, 3, 1)
    kernel_all = lax.all_gather(kernel_own, "freq", axis=0)
    model_low = model_field.astype(jnp.bfloat16)
    partial = jnp.einsum("xcsy,xyr->csr", kernel_own, model_low, preferred_element_type=jnp.float32)
    minus = lax.dynamic_update_slice(
        jnp.zeros_like(partial), observed[0].transpose(1, 0, 2), (0, place * own, 0)
    )
    partial = (partial - minus).reshape(comps * sensors, real)
    noise_row = lax.dynamic_update_slice(
        jnp.zeros((sensors,), jnp.float32), noise_scale[0], (place * own,)
    )
    noise_rows = jnp.broadcast_to(noise_row[:, None], (sensors, real))
    payload = jnp.concatenate([partial, noise_rows], axis=0)
    if peers * payload.size * 4 <= GATHER_LIMIT:
        total = jnp.sum(lax.all_gather(payload, space, axis=0), axis=0)
    else:
        total = lax.psum(payload, space)
    misfit = total[: comps * sensors].reshape(comps, sensors, real)
    noise = total[comps * sensors :]
    inverse = 1.0 / (noise * noise)
    spread = (misfit[0] * misfit[0] + misfit[1] * misfit[1]) * inverse
    factor = (FREEDOM + 2.0) / (FREEDOM + spread) * inverse
    weighted = misfit * factor
    weighted_low = lax.all_gather(weighted.astype(jnp.bfloat16), "freq", axis=0)
    weighted_own = lax.dynamic_slice_in_dim(weighted, place * own, own, axis=1).transpose(1, 0, 2)
    data_grad = jnp.einsum(
        "fxcsy,fcsr->xyr", kernel_all, weighted_low, preferred_element_type=jnp.float32
    )
    grid = lax.all_gather(classes, "py", axis=1, tiled=True)
    grid = lax.all_gather(grid, "px", axis=0, tiled=True)
    grid = jnp.pad(grid, SWEEPS, constant_values=-1)
    wide = lax.dynamic_slice(
        grid,
        (lax.axis_index("px") * rows, lax.axis_index("py") * cols),
        (rows + 2 * SWEEPS, cols + 2 * SWEEPS),
    )
    coefficient = coefficients(wide, kappa_table, coupling_table)
    state = rim(rim(model_field, "px", 0, SWEEPS), "py", 1, SWEEPS)
    for step in range(SWEEPS):
        lo = step + 1
        state = operate(
            state, coefficient[lo : coefficient.shape[0] - lo, lo : coefficient.shape[1] - lo]
        )
    return weighted_own[None], data_grad + PRIOR_WEIGHT * state


def solution(mesh):
    in_specs = (
        P("freq", ("px", "py"), None, None),
        P("freq", ("px", "py")),
        P("freq", "px", "py", None, None),
        P("px", "py", None),
        P("px", "py"),
        P(),
        P(),
    )
    out_specs = (P("freq", ("px", "py"), None, None), P("px", "py", None))
    return jax.shard_map(local, mesh=mesh, in_specs=in_specs, out_specs=out_specs, check_vma=False)
```

time: 115 us -> 63.9 us (0.56)
  waiting for transfers between devices: 33 us -> 0.01 us
  between operations: 15.1 us -> 0.97 us
  blocking collectives: 35.3 us -> 47.8 us
  starting transfers between devices: 19 us -> 6.95 us
  local copies, waits for them, and re-layouts: 5.42 us -> 2.8 us
  other arithmetic: 5.27 us -> 3.47 us
    all_gather x1 -> x5, blocking collectives: 8.66 us -> 47.8 us  [the longest x1 16.2 us: local(): kernel_all = lax.all_gather(kernel_own, 'freq', axis=0)]
    psum x1 -> x0, waiting for transfers between devices: 32.9 us -> none  [local(): data_total = lax.psum(data_grad, 'freq')]
    unnamed x1 -> x0, blocking collectives: 26.6 us -> none
    ppermute x8 -> x3, starting transfers between devices: 19 us -> 6.95 us  [swap(): return lax.ppermute(own, axis, pairs + [(j, i) for i, j in pairs])]
    add x1 -> x0, other arithmetic: 2.06 us -> none  [local(): gradient = data_total + PRIOR_WEIGHT * prior_term]
    dot_general x1 -> x2, matrix products: 0.2 us -> 1.49 us  [the longest x1 1.28 us: local(): jnp.einsum('fxcsy,fcsr->xyr', kernel_all, weighted_low, preferred_element...]
    unnamed x28 -> x25, local copies, waits for them, and re-layouts: 2.94 us -> 2.04 us
  transfers between devices with their start and end apart: 9 -> 3, of which waited for: 2 -> 0; matrix products, arithmetic and copies ran while one was open for 6% -> 3% of each run, Pallas kernels for 0% -> 0%
where the time goes in v1:
time: 63.9 us; the launch traced here: 63.7 us
  blocking collectives  47.8 us (75%)
  starting transfers between devices  6.95 us (11%)
  other arithmetic  3.47 us (5%)
  local copies, waits for them, and re-layouts  2.8 us (4%)
  matrix products  1.65 us (3%)
  between operations  0.97 us (2%)
    all_gather x1, blocking collectives, local(): kernel_all = lax.all_gather(kernel_own, 'freq', axis=0)  16.2 us
    all_gather x1, blocking collectives, local(): weighted_low = lax.all_gather(weighted.astype(jnp.bfloat16), 'freq', axis=0)  13.1 us
    all_gather x1, blocking collectives, local(): total = jnp.sum(lax.all_gather(payload, space, axis=0), axis=0)  10.1 us
    ppermute x3, starting transfers between devices, swap(): return lax.ppermute(own, axis, pairs + [(j, i) for i, j in pairs])  6.95 us
    all_gather x1, blocking collectives, local(): grid = lax.all_gather(grid, 'px', axis=0, tiled=True)  6.67 us
    sub x3, other arithmetic, operate(): return coefficient[..., 0:1] * center - beside  2.2 us
    unnamed x25, local copies, waits for them, and re-layouts  2.04 us
    all_gather x1, blocking collectives, local(): grid = lax.all_gather(classes, 'py', axis=1, tiled=True)  1.78 us
  transfers between devices with their start and end apart: 3, of which 0 were waited for; matrix products, arithmetic and copies ran while one was open for 3% of the time, Pallas kernels for 0%

profile of v1, /device:TPU:0, one launch (start us, length us, event | category | flops | bytes accessed | tf_op | source)
XLA Modules:
  0.0 63.7 jit_solution(5651129639815986834)
XLA Ops:
  0.7 1.0 %slice_select_fusion.1 = (f32[4,64,128]{2,1,0:T(8,128)S(1)}, f32[4,64,128]{2,1,0:T(8,128)S(1)}) fusion(f32[8,64,128]{2,1,0:T(8,128)} %param.10, pred[]{:T(512)S(6)} %eq.26), kind=kLoop, calls=%fused_computation.48 | loop fusion | flops 65536 | bytes 524289 | tf_op jit(solution)/shard_map/jit(_where)/select_n | solution.py:25
  1.7 0.0 copy-start
  1.7 0.8 %collective-permute-start = (f32[4,64,128]{2,1,0:T(8,128)S(1)}, f32[4,64,128]{2,1,0:T(8,128)S(1)}, u32[]{:S(2)}, u32[]{:S(2)}) collective-permute-start(f32[4,64,128]{2,1,0:T(8,128)S(1)} %get-tuple-element.8), channel_id=1, source_target_pairs={{2,4},{4,2},{3,5},{5,3},{10,12},{12,10},{11,13},{13,11},{18,20},{2... | collective-permute-start | bytes 393224 | tf_op jit(solution)/shard_map/ppermute | solution.py:22
  2.5 5.7 %collective-permute-start.1 = (f32[4,64,128]{2,1,0:T(8,128)S(1)}, f32[4,64,128]{2,1,0:T(8,128)S(1)}, u32[]{:S(2)}, u32[]{:S(2)}) collective-permute-start(f32[4,64,128]{2,1,0:T(8,128)S(1)} %get-tuple-element.9), channel_id=1, source_target_pairs={{0,2},{4,6},{2,0},{6,4},{1,3},{5,7},{3,1},{7,5},{8,10},{12,14},{10... | collective-permute-start | bytes 393224 | tf_op jit(solution)/shard_map/ppermute | solution.py:22
  8.2 1.8 %all-gather.2 = s32[2,64,8]{1,2,0:T(8,128)S(1)} all-gather(s32[1,64,8]{1,2,0:T(8,128)S(1)} %bitcast.101), channel_id=1, replica_groups=mesh['freq'=4,'px'=4,'py'=2] {'py'}, dimensions={0}, use_global_device_ids=true | all-gather | bytes 6144 | tf_op jit(solution)/shard_map/all_gather | solution.py:85
  10.0 0.1 reshape.43
  10.1 6.7 %all_gather.28 = s32[32,128]{1,0:T(8,128)S(1)} all-gather(s32[8,128]{1,0:T(8,128)S(1)} %bitcast.100), channel_id=1, replica_groups=mesh['freq'=4,'px'=4,'py'=2] {'px'}, dimensions={0}, use_global_device_ids=true | all-gather | bytes 20480 | tf_op jit(solution)/shard_map/all_gather | solution.py:86
  16.8 0.1 pad_dynamic-slice_fusion
  16.9 0.2 fusion.22
  17.1 0.0 copy-start.1
  17.1 0.1 fusion.40
  17.2 0.1 fusion.39
  17.4 0.1 fusion.38
  17.5 0.0 copy-start.4
  17.5 0.7 %copy-done.4 = f32[1,4,2,128]{3,2,1,0:T(2,128)S(1)} copy-done((f32[1,4,2,128]{3,2,1,0:T(2,128)S(1)}, f32[1,4,2,128]{3,2,1,0:T(2,128)}, u32[]{:S(2)}) %copy-start.4) | copy-done | bytes 4120
  18.2 0.2 fusion.1
  18.4 0.0 copy-start.6
  18.4 0.6 copy-done.6
  19.1 0.1 bitcast_dynamic-update-slice_fusion.1
  19.2 0.1 pad.16.clone
  19.2 0.1 pad_maximum_fusion.1
  19.3 10.1 %all-gather = f32[768,128]{1,0:T(8,128)S(1)} all-gather(f32[96,128]{1,0:T(8,128)S(1)} %pad_maximum_fusion.1), channel_id=2, replica_groups=mesh['freq'=4,'px'=4,'py'=2] {'px','py'}, dimensions={0}, use_global_device_ids=true | all-gather | bytes 442368 | tf_op jit(solution)/shard_map/all_gather | solution.py:71
  29.4 0.1 fusion.37
  29.8 0.4 collective-permute-start.2
  30.2 16.2 %all-gather.1 = bf16[32,2,32,64]{3,2,1,0:T(8,128)(2,1)S(1)} all-gather(bf16[8,2,32,64]{3,2,1,0:T(8,128)(2,1)S(1)} %bitcast.92), channel_id=3, replica_groups=mesh['freq'=4,'px'=4,'py'=2] {'freq'}, dimensions={0}, use_global_device_ids=true | all-gather | bytes 327680 | tf_op jit(solution)/shard_map/all_gather | solution.py:58
  46.3 0.6 copy.19
  46.9 13.1 %all_gather.24 = bf16[4,2,32,128]{3,2,0,1:T(8,128)(2,1)S(1)} all-gather(bf16[1,2,32,128]{3,2,0,1:T(8,128)(2,1)S(1)} %multiply_convert_fusion), channel_id=1, replica_groups=mesh['freq'=4,'px'=4,'py'=2] {'freq'}, dimensions={0}, use_global_device_ids=true | all-gather | bytes 81920 | tf_op jit(solution)/shard_map/all_gather | solution.py:80
  60.1 0.1 pad_maximum_fusion
  60.1 0.9 %fusion.4 = f32[14,70,128]{2,1,0:T(8,128)S(1)} fusion(f32[16,72,128]{2,1,0:T(8,128)S(1)} %pad_maximum_fusion, f32[14,70]{1,0:T(8,128)S(1)} %get-tuple-element.32, f32[14,70]{1,0:T(8,128)S(1)} %get-tuple-element.33, f32[14,70]{1,0:T(8,128)S(1)} %get-tuple-element.34, f32[14,70]{1,0:T(8,128)S(1)} %get-tuple-element.35, f32[14,70]{1,0:T(8,128)S(1)} %bitcast.99), kind=kLoop, calls=%fused_computation.8 | loop fusion | flops 1128960 | bytes 3030160 | tf_op jit(solution)/shard_map/sub | solution.py:47
  61.0 0.8 %fusion.8 = f32[12,68,128]{2,1,0:T(8,128)S(1)} fusion(f32[14,70,128]{2,1,0:T(8,128)S(1)} %fusion.4, f32[12,68]{1,0:T(8,128)S(1)} %get-tuple-element.36, f32[12,68]{1,0:T(8,128)S(1)} %get-tuple-element.37, f32[12,68]{1,0:T(8,128)S(1)} %get-tuple-element.38, f32[12,68]{1,0:T(8,128)S(1)} %get-tuple-element.39, f32[12,68]{1,0:T(8,128)S(1)} %bitcast.97), kind=kLoop, calls=%fused_computation.17 | loop fusion | flops 940032 | bytes 2523072 | tf_op jit(solution)/shard_map/sub | solution.py:47
  61.8 0.5 fusion.12
  62.4 1.3 %fusion = f32[8,64,128]{2,1,0:T(8,128)} fusion(bf16[4,8,2,32,64]{4,3,2,1,0:T(8,128)(2,1)S(1)} %bitcast.93, f32[10,66,128]{2,1,0:T(8,128)S(1)} %fusion.12, f32[8,64]{1,0:T(8,128)S(1)} %bitcast.103, f32[8,64]{1,0:T(8,128)S(1)} %bitcast.104, f32[8,64]{1,0:T(8,128)S(1)} %bitcast.105, f32[8,64]{1,0:T(8,128)S(1)} %bitcast.106, f32[8,64]{1,0:T(8,128)S(1)} %bitcast.102, ...), kind=kOutput, calls=%fused_computation.1 | convolution fusion | flops 34275328 | bytes 1910784 | tf_op jit(solution)/shard_map/fxcsy,fcsr->xyr/dot_general | solution.py:82
  (35 shorter events, 0.2 us)
Async XLA Ops:
  0.6 7.6 %copy-start.3 = (s32[8,64]{1,0:T(8,128)S(1)}, s32[8,64]{1,0:T(8,128)}, u32[]{:S(2)}) copy-start(s32[8,64]{1,0:T(8,128)} %param.11) | copy-start | bytes 6148
  0.7 16.1 %copy-start.2 = (f32[4,16]{1,0:T(4,128)S(1)}, f32[4,16]{1,0:T(4,128)}, u32[]{:S(2)}) copy-start(f32[4,16]{1,0:T(4,128)} %param.13) | copy-start | bytes 772
  0.7 16.1 %copy-start.5 = (f32[16]{0:T(128)S(1)}, f32[16]{0:T(128)}, u32[]{:S(2)}) copy-start(f32[16]{0:T(128)} %param.12) | copy-start | bytes 196
  1.7 16.5 %copy-start = (f32[8,64,128]{2,1,0:T(8,128)S(1)}, f32[8,64,128]{2,1,0:T(8,128)}, u32[]{:S(2)}) copy-start(f32[8,64,128]{2,1,0:T(8,128)} %param.10) | copy-start | bytes 786436
  1.7 28.0 %collective-permute-start = (f32[4,64,128]{2,1,0:T(8,128)S(1)}, f32[4,64,128]{2,1,0:T(8,128)S(1)}, u32[]{:S(2)}, u32[]{:S(2)}) collective-permute-start(f32[4,64,128]{2,1,0:T(8,128)S(1)} %get-tuple-element.8), channel_id=1, source_target_pairs={{2,4},{4,2},{3,5},{5,3},{10,12},{12,10},{11,13},{13,11},{18,20},{2... | collective-permute-start | bytes 393224 | tf_op jit(solution)/shard_map/ppermute | solution.py:22
  2.5 27.2 %collective-permute-start.1 = (f32[4,64,128]{2,1,0:T(8,128)S(1)}, f32[4,64,128]{2,1,0:T(8,128)S(1)}, u32[]{:S(2)}, u32[]{:S(2)}) collective-permute-start(f32[4,64,128]{2,1,0:T(8,128)S(1)} %get-tuple-element.9), channel_id=1, source_target_pairs={{0,2},{4,6},{2,0},{6,4},{1,3},{5,7},{3,1},{7,5},{8,10},{12,14},{10... | collective-permute-start | bytes 393224 | tf_op jit(solution)/shard_map/ppermute | solution.py:22
  17.1 1.1 %copy-start.1 = (bf16[1,8,64,2,32]{2,4,3,1,0:T(8,128)(2,1)S(1)}, bf16[1,8,64,2,32]{2,4,3,1,0:T(8,128)(2,1)}, u32[]{:S(2)}) copy-start(bf16[1,8,64,2,32]{2,4,3,1,0:T(8,128)(2,1)} %param.9) | copy-start | bytes 196612
  17.5 0.7 %copy-start.4 = (f32[1,4,2,128]{3,2,1,0:T(2,128)S(1)}, f32[1,4,2,128]{3,2,1,0:T(2,128)}, u32[]{:S(2)}) copy-start(f32[1,4,2,128]{3,2,1,0:T(2,128)} %param.7) | copy-start | bytes 12292
  18.4 0.7 %copy-start.6 = (f32[1,4]{1,0:T(1,128)S(1)}, f32[1,4]{1,0:T(1,128)}, u32[]{:S(2)}) copy-start(f32[1,4]{1,0:T(1,128)} %param.8) | copy-start | bytes 52
  29.8 30.3 %collective-permute-start.2 = (f32[16,4,128]{2,1,0:T(4,128)S(1)}, f32[16,4,128]{2,1,0:T(4,128)S(1)}, u32[]{:S(2)}, u32[]{:S(2)}) collective-permute-start(f32[16,4,128]{2,1,0:T(4,128)S(1)} %fusion.25), channel_id=1, source_target_pairs={{0,1},{1,0},{2,3},{3,2},{4,5},{5,4},{6,7},{7,6},{8,9},{9,8},{10,11... | collective-permute-start | bytes 98312 | tf_op jit(solution)/shard_map/ppermute | solution.py:22

commit v2 on v1

v2 whole, which is shorter than its diff:
```python
import jax
import jax.numpy as jnp
from jax import lax
from jax.sharding import PartitionSpec as P

SWEEPS = 4
FREEDOM = 4.0
PRIOR_WEIGHT = 0.04
LANES = 128


def swap(own, axis, partner):
    return lax.ppermute(own, axis, [(i, partner(i)) for i in range(lax.axis_size(axis))])


def bits(axis):
    size = lax.axis_size(axis)
    assert size & (size - 1) == 0
    return [1 << k for k in range(size.bit_length() - 1)]


def summed(own, axes):
    for axis in axes:
        for bit in bits(axis):
            own = own + swap(own, axis, lambda i: i ^ bit)
    return own


def gathered(own, axis):
    blocks = own[None]
    for bit in bits(axis):
        blocks = jnp.concatenate([blocks, swap(blocks, axis, lambda i: i ^ bit)], axis=0)
    return blocks


def rims(shard, axis, width):
    peers, length = lax.axis_size(axis), shard.shape[0]
    me = lax.axis_index(axis)
    even = me % 2 == 0
    last, first = shard[length - width :], shard[:width]
    one = swap(jnp.where(even, last, first), axis, lambda i: i ^ 1)
    if peers > 2:
        two = swap(
            jnp.where(even, first, last), axis, lambda i: (((i + 1) ^ 1) - 1) % peers
        )
        before = jnp.where(even, two, one)
        after = jnp.where(even, one, two)
    else:
        before, after = one, one
    before = jnp.where(me == 0, 0.0, before)
    after = jnp.where(me == peers - 1, 0.0, after)
    return before, after


def coefficients(classes, kappa_table, coupling_table):
    levels = jnp.arange(kappa_table.shape[0], dtype=jnp.float32)
    onehot = (classes[..., None] == levels).astype(jnp.float32)
    diagonal = kappa_table + jnp.sum(coupling_table, axis=0)
    class_table = jnp.concatenate([diagonal[None, :], coupling_table], axis=0)
    return jnp.einsum("xyk,ck->xyc", onehot, class_table, precision=lax.Precision.HIGHEST)


def operate(padded, coefficient):
    center = padded[1:-1, 1:-1]
    beside = coefficient[..., 1:2] * padded[:-2, 1:-1] + coefficient[..., 2:3] * padded[2:, 1:-1]
    beside = (
        beside
        + coefficient[..., 3:4] * padded[1:-1, :-2]
        + coefficient[..., 4:5] * padded[1:-1, 2:]
    )
    return coefficient[..., 0:1] * center - beside


def local(observed, noise_scale, forward_kernel, model_field, classes, kappa_table, coupling_table):
    space = ("py", "px")
    rows, cols, real = model_field.shape
    comps, sensors = forward_kernel.shape[3:]
    own = observed.shape[1]
    place = lax.axis_index(("px", "py"))
    kernel_own = forward_kernel[0].transpose(0, 2, 3, 1)
    model_low = model_field.astype(jnp.bfloat16)
    partial = jnp.einsum("xcsy,xyr->csr", kernel_own, model_low, preferred_element_type=jnp.float32)
    minus = lax.dynamic_update_slice(
        jnp.zeros_like(partial), observed[0].transpose(1, 0, 2), (0, place * own, 0)
    )
    partial = (partial - minus).reshape(comps * sensors, real)
    noise_rows = -(-sensors // real)
    noise_row = lax.dynamic_update_slice(
        jnp.zeros((noise_rows * real,), jnp.float32), noise_scale[0], (place * own,)
    ).reshape(noise_rows, real)
    total = summed(jnp.concatenate([partial, noise_row], axis=0), space)
    misfit = total[: comps * sensors].reshape(comps, sensors, real)
    noise = total[comps * sensors :].reshape(-1)[:sensors, None]
    inverse = 1.0 / (noise * noise)
    spread = (misfit[0] * misfit[0] + misfit[1] * misfit[1]) * inverse
    factor = (FREEDOM + 2.0) / (FREEDOM + spread) * inverse
    weighted = misfit * factor
    weighted_low = gathered(weighted.astype(jnp.bfloat16), "freq")
    weighted_own = lax.dynamic_slice_in_dim(weighted, place * own, own, axis=1).transpose(1, 0, 2)
    kernel_all = gathered(kernel_own, "freq")
    data_grad = jnp.einsum(
        "fxcsy,fcsr->xyr", kernel_all, weighted_low, preferred_element_type=jnp.float32
    )
    marks = (classes + 1).astype(jnp.float32)
    field_t = model_field.transpose(1, 0, 2)
    before, after = rims(
        jnp.concatenate(
            [field_t, jnp.pad(marks.T, ((0, 0), (0, real - rows)))[:, None, :]], axis=1
        ),
        "py",
        SWEEPS,
    )
    state = jnp.concatenate([before[:, :rows], field_t, after[:, :rows]], axis=0).transpose(1, 0, 2)
    marks = jnp.concatenate([before[:, rows, :rows], marks.T, after[:, rows, :rows]], axis=0).T
    wide = cols + 2 * SWEEPS
    mark_rows = -(-wide // real)
    before, after = rims(
        jnp.concatenate(
            [
                state,
                jnp.pad(marks, ((0, 0), (0, mark_rows * real - wide))).reshape(rows, mark_rows, real),
            ],
            axis=1,
        ),
        "px",
        SWEEPS,
    )
    state = jnp.concatenate([before[:, :wide], state, after[:, :wide]], axis=0)
    marks = jnp.concatenate(
        [
            before[:, wide:].reshape(SWEEPS, -1)[:, :wide],
            marks,
            after[:, wide:].reshape(SWEEPS, -1)[:, :wide],
        ],
        axis=0,
    )
    coefficient = coefficients(marks - 1.0, kappa_table, coupling_table)
    for step in range(SWEEPS):
        lo = step + 1
        state = operate(
            state, coefficient[lo : coefficient.shape[0] - lo, lo : coefficient.shape[1] - lo]
        )
    return weighted_own[None], data_grad + PRIOR_WEIGHT * state


def solution(mesh):
    in_specs = (
        P("freq", ("px", "py"), None, None),
        P("freq", ("px", "py")),
        P("freq", "px", "py", None, None),
        P("px", "py", None),
        P("px", "py"),
        P(),
        P(),
    )
    out_specs = (P("freq", ("px", "py"), None, None), P("px", "py", None))
    return jax.shard_map(local, mesh=mesh, in_specs=in_specs, out_specs=out_specs, check_vma=False)
```

time: 63.9 us -> 30 us (0.47)
  blocking collectives: 47.8 us -> 0 us
  starting transfers between devices: 6.95 us -> 15.3 us
  waiting for transfers between devices: 0.01 us -> 4.77 us
  local copies, waits for them, and re-layouts: 2.8 us -> 3.51 us
    all_gather x5 -> x0, blocking collectives: 47.8 us -> none  [the longest x1 16.2 us: local(): kernel_all = lax.all_gather(kernel_own, 'freq', axis=0)]
    ppermute x3 -> x10, starting transfers between devices: 6.95 us -> 15.3 us  [swap(): lax.ppermute(own, axis, [(i, partner(i)) for i in range(lax.axis_size(axi...]
    ppermute x3 -> x10, waiting for transfers between devices: 0.01 us -> 4.77 us  [swap(): lax.ppermute(own, axis, [(i, partner(i)) for i in range(lax.axis_size(axi...]
    unnamed x25 -> x30, local copies, waits for them, and re-layouts: 2.04 us -> 2.66 us
  transfers between devices with their start and end apart: 3 -> 10, of which waited for: 0 -> 3; matrix products, arithmetic and copies ran while one was open for 3% -> 15% of each run, Pallas kernels for 0% -> 0%
where the time goes in v2:
time: 30 us; the launch traced here: 29.8 us
  starting transfers between devices  15.3 us (51%)
  waiting for transfers between devices  4.77 us (16%)
  local copies, waits for them, and re-layouts  3.51 us (12%)
  other arithmetic  3.46 us (12%)
  matrix products  1.65 us (6%)
  between operations  1.07 us (4%)
    ppermute x10, starting transfers between devices, swap(): lax.ppermute(own, axis, [(i, partner(i)) for i in range(lax.axis_size(axi...  15.3 us
    ppermute x10, waiting for transfers between devices, swap(): lax.ppermute(own, axis, [(i, partner(i)) for i in range(lax.axis_size(axi...  4.77 us
    unnamed x30, local copies, waits for them, and re-layouts  2.66 us
    sub x3, other arithmetic, operate(): return coefficient[..., 0:1] * center - beside  2.2 us
    dot_general x1, matrix products, local(): jnp.einsum('fxcsy,fcsr->xyr', kernel_all, weighted_low, preferred_element...  1.27 us
    select_n x1, other arithmetic, rims(): one = swap(jnp.where(even, last, first), axis, lambda i: i ^ 1)  0.82 us
  transfers between devices with their start and end apart: 10, of which 3 were waited for; matrix products, arithmetic and copies ran while one was open for 15% of the time, Pallas kernels for 0%

profile of v2, /device:TPU:0, one launch (start us, length us, event | category | flops | bytes accessed | tf_op | source)
XLA Modules:
  0.0 29.8 jit_solution(13164464396131990690)
XLA Ops:
  0.7 0.7 %copy-done.3 = s32[8,64]{1,0:T(8,128)S(1)} copy-done((s32[8,64]{1,0:T(8,128)S(1)}, s32[8,64]{1,0:T(8,128)}, u32[]{:S(2)}) %copy-start.3) | copy-done | bytes 2072
  1.4 0.8 %fusion.36 = f32[4,9,128]{2,0,1:T(4,128)S(1)} fusion(f32[64,1,128]{2,0,1:T(8,128)S(1)} %copy.16, f32[64,8,128]{2,0,1:T(8,128)} %bitcast.117, pred[]{:T(512)S(6)} %eq.37), kind=kLoop, calls=%fused_computation.74 | loop fusion | flops 13824 | bytes 313345 | tf_op jit(solution)/shard_map/jit(_where)/select_n | solution.py:41
  2.2 0.5 %collective-permute-start.7 = (f32[4,9,128]{2,0,1:T(4,128)S(1)}, f32[4,9,128]{2,0,1:T(4,128)S(1)}, u32[]{:S(2)}, u32[]{:S(2)}) collective-permute-start(f32[4,9,128]{2,0,1:T(4,128)S(1)} %fusion.36), channel_id=1, source_target_pairs={{0,1},{1,0},{2,3},{3,2},{4,5},{5,4},{6,7},{7,6},{8,9},{9,8},{10,11... | collective-permute-start | bytes 55304 | tf_op jit(solution)/shard_map/ppermute | solution.py:13
  2.7 0.7 %copy-done.4 = f32[1,4,2,128]{3,2,1,0:T(2,128)S(1)} copy-done((f32[1,4,2,128]{3,2,1,0:T(2,128)S(1)}, f32[1,4,2,128]{3,2,1,0:T(2,128)}, u32[]{:S(2)}) %copy-start.4) | copy-done | bytes 4120
  3.4 0.2 fusion.1
  3.6 0.6 %copy-done.5 = f32[1,4]{1,0:T(1,128)S(1)} copy-done((f32[1,4]{1,0:T(1,128)S(1)}, f32[1,4]{1,0:T(1,128)}, u32[]{:S(2)}) %copy-start.5) | copy-done | bytes 40
  4.4 0.2 collective-permute-start
  4.6 3.0 %collective-permute-start.3 = (bf16[1,8,2,32,64]{4,3,0,2,1:T(8,128)(2,1)S(1)}, bf16[1,8,2,32,64]{4,3,0,2,1:T(8,128)(2,1)S(1)}, u32[]{:S(2)}, u32[]{:S(2)}) collective-permute-start(bf16[1,8,2,32,64]{4,3,0,2,1:T(8,128)(2,1)S(1)} %bitcast.119), channel_id=1, source_target_pairs={{0,8},{8,0},{16,24},{24,16},{1,9},{9,1},{17,25},{25,17},{2,10},{10... | collective-permute-start | bytes 196616 | tf_op jit(solution)/shard_map/ppermute | solution.py:13
  7.7 0.1 copy.17
  7.8 0.1 copy.18
  7.9 0.1 maximum_bitcast_fusion.1
  8.0 1.6 %collective-permute-start.1 = (f32[65,128]{1,0:T(8,128)S(1)}, f32[65,128]{1,0:T(8,128)S(1)}, u32[]{:S(2)}, u32[]{:S(2)}) collective-permute-start(f32[65,128]{1,0:T(8,128)S(1)} %fusion.49), channel_id=1, source_target_pairs={{0,2},{2,0},{4,6},{6,4},{1,3},{3,1},{5,7},{7,5},{8,10},{10,8},{12,... | collective-permute-start | bytes 99848 | tf_op jit(solution)/shard_map/ppermute | solution.py:13
  9.6 1.6 %collective-permute-start.8 = (f32[4,73,128]{2,1,0:T(8,128)S(1)}, f32[4,73,128]{2,1,0:T(8,128)S(1)}, u32[]{:S(2)}, u32[]{:S(2)}) collective-permute-start(f32[4,73,128]{2,1,0:T(8,128)S(1)} %get-tuple-element.6), channel_id=1, source_target_pairs={{0,6},{2,4},{4,2},{6,0},{1,7},{3,5},{5,3},{7,1},{8,14},{10,12},{12... | collective-permute-start | bytes 448520 | tf_op jit(solution)/shard_map/ppermute | solution.py:13
  11.2 1.5 %collective-permute-start.9 = (f32[4,73,128]{2,1,0:T(8,128)S(1)}, f32[4,73,128]{2,1,0:T(8,128)S(1)}, u32[]{:S(2)}, u32[]{:S(2)}) collective-permute-start(f32[4,73,128]{2,1,0:T(8,128)S(1)} %get-tuple-element.7), channel_id=1, source_target_pairs={{0,2},{2,0},{4,6},{6,4},{1,3},{3,1},{5,7},{7,5},{8,10},{10,8},{12,... | collective-permute-start | bytes 448520 | tf_op jit(solution)/shard_map/ppermute | solution.py:13
  12.7 1.2 %collective-permute-start.2 = (f32[65,128]{1,0:T(8,128)S(1)}, f32[65,128]{1,0:T(8,128)S(1)}, u32[]{:S(2)}, u32[]{:S(2)}) collective-permute-start(f32[65,128]{1,0:T(8,128)S(1)} %add.100), channel_id=1, source_target_pairs={{0,4},{2,6},{4,0},{6,2},{1,5},{3,7},{5,1},{7,3},{8,12},{10,14},{12... | collective-permute-start | bytes 99848 | tf_op jit(solution)/shard_map/ppermute | solution.py:13
  14.0 2.6 %collective-permute-start.4 = (bf16[2,8,2,32,64]{4,3,0,2,1:T(8,128)(2,1)S(1)}, bf16[2,8,2,32,64]{4,3,0,2,1:T(8,128)(2,1)S(1)}, u32[]{:S(2)}, u32[]{:S(2)}) collective-permute-start(bf16[2,8,2,32,64]{4,3,0,2,1:T(8,128)(2,1)S(1)} %pad_maximum_fusion.1), channel_id=1, source_target_pairs={{0,16},{8,24},{16,0},{24,8},{1,17},{9,25},{17,1},{25,9},{2,18},{10... | collective-permute-start | bytes 393224 | tf_op jit(solution)/shard_map/ppermute | solution.py:13
  16.6 0.5 %collective-permute-done.2 = f32[65,128]{1,0:T(8,128)S(1)} collective-permute-done((f32[65,128]{1,0:T(8,128)S(1)}, f32[65,128]{1,0:T(8,128)S(1)}, u32[]{:S(2)}, u32[]{:S(2)}) %collective-permute-start.2) | collective-permute-done | bytes 33312 | tf_op jit(solution)/shard_map/ppermute | solution.py:13
  17.1 0.1 fusion.41
  17.3 0.6 %collective-permute-start.5 = (bf16[1,2,32,128]{3,2,0,1:T(8,128)(2,1)S(1)}, bf16[1,2,32,128]{3,2,0,1:T(8,128)(2,1)S(1)}, u32[]{:S(2)}, u32[]{:S(2)}) collective-permute-start(bf16[1,2,32,128]{3,2,0,1:T(8,128)(2,1)S(1)} %multiply_convert_fusion), channel_id=1, source_target_pairs={{0,8},{8,0},{16,24},{24,16},{1,9},{9,1},{17,25},{25,17},{2,10},{10... | collective-permute-start | bytes 49160 | tf_op jit(solution)/shard_map/ppermute | solution.py:13
  17.9 0.6 %copy.19 = f32[1,4,2,128]{3,2,1,0:T(2,128)} copy(f32[1,4,2,128]{3,1,2,0:T(4,128)S(1)} %fusion.42) | data formatting | bytes 8192
  18.5 2.6 %collective-permute-done.5 = bf16[1,2,32,128]{3,2,0,1:T(8,128)(2,1)S(1)} collective-permute-done((bf16[1,2,32,128]{3,2,0,1:T(8,128)(2,1)S(1)}, bf16[1,2,32,128]{3,2,0,1:T(8,128)(2,1)S(1)}, u32[]{:S(2)}, u32[]{:S(2)}) %collective-permute-start.5) | collective-permute-done | bytes 16416 | tf_op jit(solution)/shard_map/ppermute | solution.py:13
  21.1 2.5 %collective-permute-start.6 = (bf16[2,2,32,128]{3,2,0,1:T(8,128)(2,1)S(1)}, bf16[2,2,32,128]{3,2,0,1:T(8,128)(2,1)S(1)}, u32[]{:S(2)}, u32[]{:S(2)}) collective-permute-start(bf16[2,2,32,128]{3,2,0,1:T(8,128)(2,1)S(1)} %pad_maximum_fusion.4), channel_id=1, source_target_pairs={{0,16},{8,24},{16,0},{24,8},{1,17},{9,25},{17,1},{25,9},{2,18},{10... | collective-permute-start | bytes 98312 | tf_op jit(solution)/shard_map/ppermute | solution.py:13
  23.8 0.2 fusion.28
  23.9 0.1 fusion.53
  24.1 0.1 fusion.52
  24.2 0.1 fusion.51
  24.5 0.9 %fusion.8 = f32[14,70,128]{2,1,0:T(8,128)S(1)} fusion(f32[16,72,128]{2,1,0:T(8,128)S(1)} %pad_maximum_fusion, f32[14,70]{1,0:T(8,128)S(1)} %bitcast.131, f32[14,70]{1,0:T(8,128)S(1)} %bitcast.132, f32[14,70]{1,0:T(8,128)S(1)} %bitcast.133, f32[14,70]{1,0:T(8,128)S(1)} %bitcast.134, f32[14,70]{1,0:T(8,128)S(1)} %bitcast.135), kind=kLoop, calls=%fused_computation.12 | loop fusion | flops 1128960 | bytes 3030160 | tf_op jit(solution)/shard_map/sub | solution.py:71
  25.4 0.8 %fusion.12 = f32[12,68,128]{2,1,0:T(8,128)S(1)} fusion(f32[14,70,128]{2,1,0:T(8,128)S(1)} %fusion.8, f32[12,68]{1,0:T(8,128)S(1)} %bitcast.126, f32[12,68]{1,0:T(8,128)S(1)} %bitcast.127, f32[12,68]{1,0:T(8,128)S(1)} %bitcast.128, f32[12,68]{1,0:T(8,128)S(1)} %bitcast.129, f32[12,68]{1,0:T(8,128)S(1)} %bitcast.130), kind=kLoop, calls=%fused_computation.21 | loop fusion | flops 940032 | bytes 2523072 | tf_op jit(solution)/shard_map/sub | solution.py:71
  26.2 0.5 %fusion.16 = f32[10,66,128]{2,1,0:T(8,128)S(1)} fusion(f32[12,68,128]{2,1,0:T(8,128)S(1)} %fusion.12, f32[10,66]{1,0:T(8,128)S(1)} %bitcast.136, f32[10,66]{1,0:T(8,128)S(1)} %bitcast.137, f32[10,66]{1,0:T(8,128)S(1)} %bitcast.138, f32[10,66]{1,0:T(8,128)S(1)} %bitcast.139, f32[10,66]{1,0:T(8,128)S(1)} %bitcast.140), kind=kLoop, calls=%fused_computation.30 | loop fusion | flops 760320 | bytes 2040720 | tf_op jit(solution)/shard_map/sub | solution.py:71
  26.8 0.1 fusion.50
  26.9 1.7 %collective-permute-done.6 = bf16[2,2,32,128]{3,2,0,1:T(8,128)(2,1)S(1)} collective-permute-done((bf16[2,2,32,128]{3,2,0,1:T(8,128)(2,1)S(1)}, bf16[2,2,32,128]{3,2,0,1:T(8,128)(2,1)S(1)}, u32[]{:S(2)}, u32[]{:S(2)}) %collective-permute-start.6) | collective-permute-done | bytes 32800 | tf_op jit(solution)/shard_map/ppermute | solution.py:13
  28.5 1.3 %fusion = f32[8,64,128]{2,1,0:T(8,128)} fusion(bf16[2,8,2,32,64]{4,3,0,2,1:T(8,128)(2,1)S(1)} %collective-permute-done.4, bf16[1,8,2,32,64]{4,3,0,2,1:T(8,128)(2,1)S(1)} %collective-permute-done.3, bf16[1,8,2,32,64]{4,3,0,2,1:T(8,128)(2,1)S(1)} %bitcast.121, f32[10,66,128]{2,1,0:T(8,128)S(1)} %fusion.16, f32[8,64]{1,0:T(8,128)S(1)} %bitcast.145, ...), kind=kOutput, calls=%fused_computation.1 | convolution fusion | flops 34603008 | bytes 1910784 | tf_op jit(solution)/shard_map/fxcsy,fcsr->xyr/dot_general | solution.py:101
  (67 shorter events, 0.6 us)
Async XLA Ops:
  0.6 0.7 %copy-start.3 = (s32[8,64]{1,0:T(8,128)S(1)}, s32[8,64]{1,0:T(8,128)}, u32[]{:S(2)}) copy-start(s32[8,64]{1,0:T(8,128)} %param.11) | copy-start | bytes 6148
  1.3 2.1 %copy-start = (f32[8,64,128]{2,1,0:T(8,128)S(1)}, f32[8,64,128]{2,1,0:T(8,128)}, u32[]{:S(2)}) copy-start(f32[8,64,128]{2,1,0:T(8,128)} %param.10) | copy-start | bytes 786436
  1.4 2.0 %copy-start.1 = (bf16[1,8,64,2,32]{2,4,3,1,0:T(8,128)(2,1)S(1)}, bf16[1,8,64,2,32]{2,4,3,1,0:T(8,128)(2,1)}, u32[]{:S(2)}) copy-start(bf16[1,8,64,2,32]{2,4,3,1,0:T(8,128)(2,1)} %param.9) | copy-start | bytes 196612
  2.2 5.4 %collective-permute-start.7 = (f32[4,9,128]{2,0,1:T(4,128)S(1)}, f32[4,9,128]{2,0,1:T(4,128)S(1)}, u32[]{:S(2)}, u32[]{:S(2)}) collective-permute-start(f32[4,9,128]{2,0,1:T(4,128)S(1)} %fusion.36), channel_id=1, source_target_pairs={{0,1},{1,0},{2,3},{3,2},{4,5},{5,4},{6,7},{7,6},{8,9},{9,8},{10,11... | collective-permute-start | bytes 55304 | tf_op jit(solution)/shard_map/ppermute | solution.py:13
  2.7 0.7 %copy-start.4 = (f32[1,4,2,128]{3,2,1,0:T(2,128)S(1)}, f32[1,4,2,128]{3,2,1,0:T(2,128)}, u32[]{:S(2)}) copy-start(f32[1,4,2,128]{3,2,1,0:T(2,128)} %param.7) | copy-start | bytes 12292
  3.6 0.7 %copy-start.5 = (f32[1,4]{1,0:T(1,128)S(1)}, f32[1,4]{1,0:T(1,128)}, u32[]{:S(2)}) copy-start(f32[1,4]{1,0:T(1,128)} %param.8) | copy-start | bytes 52
  4.3 3.3 %copy-start.2 = (f32[4,16]{1,0:T(4,128)S(1)}, f32[4,16]{1,0:T(4,128)}, u32[]{:S(2)}) copy-start(f32[4,16]{1,0:T(4,128)} %param.13) | copy-start | bytes 772
  4.4 3.7 %collective-permute-start = (f32[65,128]{1,0:T(8,128)S(1)}, f32[65,128]{1,0:T(8,128)S(1)}, u32[]{:S(2)}, u32[]{:S(2)}) collective-permute-start(f32[65,128]{1,0:T(8,128)S(1)} %pad_maximum_fusion.3), channel_id=1, source_target_pairs={{0,1},{1,0},{2,3},{3,2},{4,5},{5,4},{6,7},{7,6},{8,9},{9,8},{10,11... | collective-permute-start | bytes 99848 | tf_op jit(solution)/shard_map/ppermute | solution.py:13
  4.6 3.1 %copy-start.6 = (f32[16]{0:T(128)S(1)}, f32[16]{0:T(128)}, u32[]{:S(2)}) copy-start(f32[16]{0:T(128)} %param.12) | copy-start | bytes 196
  4.6 9.3 %collective-permute-start.3 = (bf16[1,8,2,32,64]{4,3,0,2,1:T(8,128)(2,1)S(1)}, bf16[1,8,2,32,64]{4,3,0,2,1:T(8,128)(2,1)S(1)}, u32[]{:S(2)}, u32[]{:S(2)}) collective-permute-start(bf16[1,8,2,32,64]{4,3,0,2,1:T(8,128)(2,1)S(1)} %bitcast.119), channel_id=1, source_target_pairs={{0,8},{8,0},{16,24},{24,16},{1,9},{9,1},{17,25},{25,17},{2,10},{10... | collective-permute-start | bytes 196616 | tf_op jit(solution)/shard_map/ppermute | solution.py:13
  8.0 4.6 %collective-permute-start.1 = (f32[65,128]{1,0:T(8,128)S(1)}, f32[65,128]{1,0:T(8,128)S(1)}, u32[]{:S(2)}, u32[]{:S(2)}) collective-permute-start(f32[65,128]{1,0:T(8,128)S(1)} %fusion.49), channel_id=1, source_target_pairs={{0,2},{2,0},{4,6},{6,4},{1,3},{3,1},{5,7},{7,5},{8,10},{10,8},{12,... | collective-permute-start | bytes 99848 | tf_op jit(solution)/shard_map/ppermute | solution.py:13
  9.6 14.0 %collective-permute-start.8 = (f32[4,73,128]{2,1,0:T(8,128)S(1)}, f32[4,73,128]{2,1,0:T(8,128)S(1)}, u32[]{:S(2)}, u32[]{:S(2)}) collective-permute-start(f32[4,73,128]{2,1,0:T(8,128)S(1)} %get-tuple-element.6), channel_id=1, source_target_pairs={{0,6},{2,4},{4,2},{6,0},{1,7},{3,5},{5,3},{7,1},{8,14},{10,12},{12... | collective-permute-start | bytes 448520 | tf_op jit(solution)/shard_map/ppermute | solution.py:13
  11.2 12.5 %collective-permute-start.9 = (f32[4,73,128]{2,1,0:T(8,128)S(1)}, f32[4,73,128]{2,1,0:T(8,128)S(1)}, u32[]{:S(2)}, u32[]{:S(2)}) collective-permute-start(f32[4,73,128]{2,1,0:T(8,128)S(1)} %get-tuple-element.7), channel_id=1, source_target_pairs={{0,2},{2,0},{4,6},{6,4},{1,3},{3,1},{5,7},{7,5},{8,10},{10,8},{12,... | collective-permute-start | bytes 448520 | tf_op jit(solution)/shard_map/ppermute | solution.py:13
  12.7 4.4 %collective-permute-start.2 = (f32[65,128]{1,0:T(8,128)S(1)}, f32[65,128]{1,0:T(8,128)S(1)}, u32[]{:S(2)}, u32[]{:S(2)}) collective-permute-start(f32[65,128]{1,0:T(8,128)S(1)} %add.100), channel_id=1, source_target_pairs={{0,4},{2,6},{4,0},{6,2},{1,5},{3,7},{5,1},{7,3},{8,12},{10,14},{12... | collective-permute-start | bytes 99848 | tf_op jit(solution)/shard_map/ppermute | solution.py:13
  14.0 14.6 %collective-permute-start.4 = (bf16[2,8,2,32,64]{4,3,0,2,1:T(8,128)(2,1)S(1)}, bf16[2,8,2,32,64]{4,3,0,2,1:T(8,128)(2,1)S(1)}, u32[]{:S(2)}, u32[]{:S(2)}) collective-permute-start(bf16[2,8,2,32,64]{4,3,0,2,1:T(8,128)(2,1)S(1)} %pad_maximum_fusion.1), channel_id=1, source_target_pairs={{0,16},{8,24},{16,0},{24,8},{1,17},{9,25},{17,1},{25,9},{2,18},{10... | collective-permute-start | bytes 393224 | tf_op jit(solution)/shard_map/ppermute | solution.py:13
  17.3 3.9 %collective-permute-start.5 = (bf16[1,2,32,128]{3,2,0,1:T(8,128)(2,1)S(1)}, bf16[1,2,32,128]{3,2,0,1:T(8,128)(2,1)S(1)}, u32[]{:S(2)}, u32[]{:S(2)}) collective-permute-start(bf16[1,2,32,128]{3,2,0,1:T(8,128)(2,1)S(1)} %multiply_convert_fusion), channel_id=1, source_target_pairs={{0,8},{8,0},{16,24},{24,16},{1,9},{9,1},{17,25},{25,17},{2,10},{10... | collective-permute-start | bytes 49160 | tf_op jit(solution)/shard_map/ppermute | solution.py:13
  21.1 7.4 %collective-permute-start.6 = (bf16[2,2,32,128]{3,2,0,1:T(8,128)(2,1)S(1)}, bf16[2,2,32,128]{3,2,0,1:T(8,128)(2,1)S(1)}, u32[]{:S(2)}, u32[]{:S(2)}) collective-permute-start(bf16[2,2,32,128]{3,2,0,1:T(8,128)(2,1)S(1)} %pad_maximum_fusion.4), channel_id=1, source_target_pairs={{0,16},{8,24},{16,0},{24,8},{1,17},{9,25},{17,1},{25,9},{2,18},{10... | collective-permute-start | bytes 98312 | tf_op jit(solution)/shard_map/ppermute | solution.py:13

commit v3 on v2

v3 whole, which is shorter than its diff:
```python
import jax
import jax.numpy as jnp
from jax import lax
from jax.experimental import pallas as pl
from jax.experimental.pallas import tpu as pltpu
from jax.sharding import PartitionSpec as P

SWEEPS = 4
FREEDOM = 4.0
PRIOR_WEIGHT = 0.04
LANES = 128
TILE = 8
VMEM_BYTES = 40 << 20
ALL_VMEM_BYTES = 63 << 20


def swap(own, axis, partner):
    return lax.ppermute(own, axis, [(i, partner(i)) for i in range(lax.axis_size(axis))])


def bits(axis):
    size = lax.axis_size(axis)
    assert size & (size - 1) == 0
    return [1 << k for k in range(size.bit_length() - 1)]


def near(i):
    return i ^ 1


def far(axis):
    return lambda i: (((i + 1) ^ 1) - 1) % lax.axis_size(axis)


def both_sides(one, two, axis):
    peers, me = lax.axis_size(axis), lax.axis_index(axis)
    even = me % 2 == 0
    zero = jnp.zeros_like(one)
    before, after = jnp.where(even, two, one), jnp.where(even, one, two)
    return jnp.where(me == 0, zero, before), jnp.where(me == peers - 1, zero, after)


def call(body, *out_shapes, fetch=False):
    def run(*operands):
        count = len(operands)

        def fetched(*refs):
            outs, held, sems = (
                refs[count : count + len(out_shapes)],
                refs[count + len(out_shapes) : -1],
                refs[-1],
            )
            copies = [
                pltpu.make_async_copy(src, dst, sems.at[k])
                for k, (src, dst) in enumerate(zip(refs[:count], held))
            ]
            for copy in copies:
                copy.start()
            for copy in copies:
                copy.wait()
            body(*held, *outs)

        return pl.pallas_call(
            fetched if fetch else body,
            out_shape=[jax.ShapeDtypeStruct(shape, dtype) for shape, dtype in out_shapes],
            in_specs=[pl.BlockSpec(memory_space=pltpu.HBM if fetch else pltpu.VMEM)] * count,
            out_specs=[pl.BlockSpec(memory_space=pltpu.VMEM)] * len(out_shapes),
            scratch_shapes=[pltpu.VMEM(x.shape, x.dtype) for x in operands] * fetch
            + [pltpu.SemaphoreType.DMA((count,))] * fetch,
            compiler_params=pltpu.CompilerParams(vmem_limit_bytes=ALL_VMEM_BYTES if fetch else VMEM_BYTES),
        )(*operands)

    return run


def prepare(noise_ref, observed_ref, kernel_ref, field_ref, classes_ref, pay_ref, packed_ref, *far_ref):
    beside, points, width = packed_ref.shape
    rows, cols, real = field_ref.shape
    own, comps = observed_ref.shape[:2]
    sensors = points // comps
    place = lax.axis_index("px") * lax.axis_size("py") + lax.axis_index("py")
    even = lax.axis_index("py") % 2 == 0
    total = jnp.zeros((points, real), jnp.float32)
    for x in range(beside):
        picks = range(x, rows, beside)
        packed = jnp.concatenate([kernel_ref[k] for k in picks], axis=1)
        packed_ref[x] = packed
        field = jnp.concatenate([field_ref[k].astype(jnp.bfloat16) for k in picks], axis=0)
        total = total + jnp.dot(packed, field, preferred_element_type=jnp.float32)
    spot = lax.broadcasted_iota(jnp.int32, (points, real), 0)
    for c in range(comps):
        for k in range(own):
            row = c * sensors + place * own + k
            total = total - jnp.where(spot == row, observed_ref[k, c : c + 1, :], 0.0)
    pay_ref[:points] = total
    spot = lax.broadcasted_iota(jnp.int32, (TILE, real), 0) * real + lax.broadcasted_iota(
        jnp.int32, (TILE, real), 1
    )
    noise = jnp.zeros((TILE, real), jnp.float32)
    for k in range(own):
        noise = noise + jnp.where(spot == place * own + k, noise_ref[0:1, k : k + 1], 0.0)
    pay_ref[points : points + TILE] = noise
    marks = (classes_ref[...] + 1).astype(jnp.float32)
    edges = [
        (field_ref[:, cols - SWEEPS :, :], marks[:, cols - SWEEPS :]),
        (field_ref[:, :SWEEPS, :], marks[:, :SWEEPS]),
    ]

    def put(ref, start, chosen):
        for x in range(rows):
            ref[start + x * SWEEPS : start + (x + 1) * SWEEPS] = jnp.where(
                chosen, edges[0][0][x], edges[1][0][x]
            )
        start = start + rows * SWEEPS
        ref[start : start + rows] = jnp.zeros((rows, real), jnp.float32)
        ref[start : start + rows, :SWEEPS] = jnp.where(chosen, edges[0][1], edges[1][1])

    put(pay_ref, points + TILE, even)
    for ref in far_ref:
        put(ref, 0, jnp.logical_not(even))


def add_first(mine_ref, got_ref, out_ref):
    size = out_ref.shape[0]
    out_ref[...] = mine_ref[:size] + got_ref[:size]


def add_and_join(mine_ref, got_ref, one_ref, two_ref, out_ref, joined_ref):
    out_ref[...] = mine_ref[...] + got_ref[...]
    half = one_ref.shape[0]
    joined_ref[:half] = one_ref[...]
    joined_ref[half:] = two_ref[...]


def weigh(mine_ref, got_ref, held_ref, low_ref, weighted_ref, passed_ref):
    comps, sensors, real = weighted_ref.shape
    points = comps * sensors
    total = mine_ref[...] + got_ref[...]
    chunk = min(sensors, real)
    eye = lax.broadcasted_iota(jnp.int32, (chunk, real), 0) == lax.broadcasted_iota(
        jnp.int32, (chunk, real), 1
    )
    for k in range(sensors // chunk):
        row = total[points + k : points + k + 1]
        noise = jnp.sum(jnp.where(eye, row, 0.0), axis=1, keepdims=True)
        inverse = 1.0 / (noise * noise)
        misfit = [total[c * sensors + k * chunk : c * sensors + (k + 1) * chunk] for c in range(comps)]
        spread = sum(part * part for part in misfit) * inverse
        factor = (FREEDOM + 2.0) / (FREEDOM + spread) * inverse
        for c in range(comps):
            weighted = misfit[c] * factor
            weighted_ref[c, k * chunk : (k + 1) * chunk] = weighted
            low_ref[c * sensors + k * chunk : c * sensors + (k + 1) * chunk] = weighted.astype(
                jnp.bfloat16
            )
    passed_ref[...] = held_ref[...]


def coefficients(classes, kappa_table, coupling_table):
    levels = jnp.arange(kappa_table.shape[0], dtype=jnp.float32)
    onehot = (classes[..., None] == levels).astype(jnp.float32)
    diagonal = kappa_table + jnp.sum(coupling_table, axis=0)
    class_table = jnp.concatenate([diagonal[None, :], coupling_table], axis=0)
    return jnp.einsum("xyk,ck->xyc", onehot, class_table, precision=lax.Precision.HIGHEST)


def operate(padded, coefficient):
    center = padded[1:-1, 1:-1]
    beside = coefficient[..., 1:2] * padded[:-2, 1:-1] + coefficient[..., 2:3] * padded[2:, 1:-1]
    beside = (
        beside
        + coefficient[..., 3:4] * padded[1:-1, :-2]
        + coefficient[..., 4:5] * padded[1:-1, 2:]
    )
    return coefficient[..., 0:1] * center - beside


def local(observed, noise_scale, forward_kernel, model_field, classes, kappa_table, coupling_table):
    rows, cols, real = model_field.shape
    comps, sensors = forward_kernel.shape[3:]
    own = observed.shape[1]
    points = comps * sensors
    place = lax.axis_index(("px", "py"))
    kernel_own = forward_kernel[0].transpose(0, 2, 3, 1).reshape(rows, points, cols)
    beside = rows // max(1, min(rows, LANES // cols))
    side = rows // beside
    assert sensors <= TILE * real
    rim_rows = rows * (SWEEPS + 1)
    wide_py, wide_px = lax.axis_size("py") > 2, lax.axis_size("px") > 2
    payload, kernel_own, *far_rim = call(
        prepare,
        ((points + TILE + rim_rows, real), jnp.float32),
        ((beside, points, side * cols), jnp.bfloat16),
        *[((rim_rows, real), jnp.float32)] * wide_py,
        fetch=True,
    )(noise_scale, observed[0], kernel_own, model_field, classes)
    got = swap(payload, "py", near)
    kernel_next = swap(kernel_own, "freq", near)
    (total,) = call(add_first, ((points + TILE, real), jnp.float32))(payload, got)
    for bit in bits("py")[1:]:
        total = total + swap(total, "py", lambda i: i ^ bit)

    one = got[points + TILE :]
    two = swap(far_rim[0], "py", far("py")) if wide_py else one
    before, after = both_sides(one, two, "py")
    marks = (classes + 1).astype(jnp.float32)

    def fields(rim):
        return rim[: rows * SWEEPS].reshape(rows, SWEEPS, real)

    wide_field = jnp.concatenate([fields(before), model_field, fields(after)], axis=1)
    marks = jnp.concatenate(
        [before[rows * SWEEPS :, :SWEEPS], marks, after[rows * SWEEPS :, :SWEEPS]], axis=1
    )
    wide = cols + 2 * SWEEPS
    even = lax.axis_index("px") % 2 == 0
    mark_rows = -(-wide // real)

    def sent(chosen):
        return jnp.concatenate(
            [
                jnp.where(chosen, wide_field[rows - SWEEPS :], wide_field[:SWEEPS]),
                jnp.pad(
                    jnp.where(chosen, marks[rows - SWEEPS :], marks[:SWEEPS]),
                    ((0, 0), (0, mark_rows * real - wide)),
                ).reshape(SWEEPS, mark_rows, real),
            ],
            axis=1,
        ).astype(jnp.bfloat16)

    one = swap(sent(even), "px", near)
    held = sent(jnp.logical_not(even))

    steps = bits("px")
    for bit in steps[:-1]:
        got = swap(total, "px", lambda i: i ^ bit)
        if bit == steps[-2]:
            total, kernel_pair = call(
                add_and_join,
                ((points + TILE, real), jnp.float32),
                ((2 * beside, points, side * cols), jnp.bfloat16),
            )(total, got, kernel_own, kernel_next)
        else:
            total = total + got
    kernel_far = swap(kernel_pair, "freq", lambda i: i ^ 2)
    got = swap(total, "px", lambda i: i ^ steps[-1])
    weighted_low, weighted, held = call(
        weigh,
        ((points, real), jnp.bfloat16),
        ((comps, sensors, real), jnp.float32),
        (held.shape, held.dtype),
    )(total, got, held)
    low_next = swap(weighted_low, "freq", near)
    low_pair = jnp.concatenate([weighted_low[None], low_next[None]], axis=0)
    low_far = swap(low_pair, "freq", lambda i: i ^ 2)
    weighted_own = lax.dynamic_slice_in_dim(weighted, place * own, own, axis=1).transpose(1, 0, 2)

    two = swap(held, "px", far("px")) if wide_px else one
    before, after = both_sides(one, two, "px")
    state = jnp.concatenate(
        [
            before[:, :wide].astype(jnp.float32),
            wide_field,
            after[:, :wide].astype(jnp.float32),
        ],
        axis=0,
    )
    marks = jnp.concatenate(
        [
            before[:, wide:].reshape(SWEEPS, -1)[:, :wide].astype(jnp.float32),
            marks,
            after[:, wide:].reshape(SWEEPS, -1)[:, :wide].astype(jnp.float32),
        ],
        axis=0,
    )
    coefficient = coefficients(marks - 1.0, kappa_table, coupling_table)
    for step in range(SWEEPS):
        lo = step + 1
        state = operate(
            state, coefficient[lo : coefficient.shape[0] - lo, lo : coefficient.shape[1] - lo]
        )

    data_grad = jnp.einsum(
        "fxqy,fqr->xyr",
        jnp.concatenate([kernel_pair, kernel_far]).reshape(4, beside, points, side * cols),
        jnp.concatenate([low_pair, low_far]),
        preferred_element_type=jnp.float32,
    )
    data_grad = jnp.concatenate(
        [data_grad[:, k * cols : (k + 1) * cols] for k in range(side)], axis=0
    )
    return weighted_own[None], data_grad + PRIOR_WEIGHT * state


def solution(mesh):
    in_specs = (
        P("freq", ("px", "py"), None, None),
        P("freq", ("px", "py")),
        P("freq", "px", "py", None, None),
        P("px", "py", None),
        P("px", "py"),
        P(),
        P(),
    )
    out_specs = (P("freq", ("px", "py"), None, None), P("px", "py", None))
    return jax.shard_map(local, mesh=mesh, in_specs=in_specs, out_specs=out_specs, check_vma=False)
```

time: 30 us -> 27.8 us (0.927)
  Pallas kernels: 0 us -> 2.1 us
  starting transfers between devices: 15.3 us -> 13.8 us
  matrix products: 1.65 us -> 0.43 us
  local copies, waits for them, and re-layouts: 3.51 us -> 2.6 us
  waiting for transfers between devices: 4.77 us -> 3.86 us
    pallas_call x0 -> x4, Pallas kernels: none -> 2.1 us  [run(): pl.pallas_call(fetched if fetch else body, out_shape=[jax.ShapeDtypeStruc...]
    ppermute x10 -> x9, starting transfers between devices: 15.3 us -> 13.8 us  [swap(): lax.ppermute(own, axis, [(i, partner(i)) for i in range(lax.axis_size(axi...]
    dot_general x2 -> x1, matrix products: 1.48 us -> 0.27 us  [local(): jnp.einsum('fxqy,fqr->xyr', jnp.concatenate([kernel_pair, kernel_far]).re...]
    add x3 -> x1, other arithmetic: 0.02 us -> 1.12 us  [local(): return (weighted_own[None], data_grad + PRIOR_WEIGHT * state)]
    ppermute x10 -> x9, waiting for transfers between devices: 4.77 us -> 3.86 us  [swap(): lax.ppermute(own, axis, [(i, partner(i)) for i in range(lax.axis_size(axi...]
    select_n x4 -> x2, other arithmetic: 0.88 us -> 0.02 us  [both_sides(): jnp.where(me == 0, zero, before)]
    unnamed x30, local copies, waits for them, and re-layouts: 2.66 us -> 2.06 us
  transfers between devices with their start and end apart: 10 -> 9, of which waited for: 3 -> 4; matrix products, arithmetic and copies ran while one was open for 15% -> 14% of each run, Pallas kernels for 0% -> 0%
where the time goes in v3:
time: 27.8 us; the launch traced here: 27.6 us
  starting transfers between devices  13.8 us (50%)
  waiting for transfers between devices  3.86 us (14%)
  other arithmetic  3.73 us (13%)
  local copies, waits for them, and re-layouts  2.6 us (9%)
  Pallas kernels  2.1 us (8%)
  between operations  1.06 us (4%)
  matrix products  0.43 us (2%)
    ppermute x9, starting transfers between devices, swap(): lax.ppermute(own, axis, [(i, partner(i)) for i in range(lax.axis_size(axi...  13.8 us
    ppermute x9, waiting for transfers between devices, swap(): lax.ppermute(own, axis, [(i, partner(i)) for i in range(lax.axis_size(axi...  3.86 us
    sub x3, other arithmetic, operate(): return coefficient[..., 0:1] * center - beside  2.2 us
    pallas_call x4, Pallas kernels, run(): pl.pallas_call(fetched if fetch else body, out_shape=[jax.ShapeDtypeStruc...  2.1 us
    unnamed x30, local copies, waits for them, and re-layouts  2.06 us
    add x1, other arithmetic, local(): return (weighted_own[None], data_grad + PRIOR_WEIGHT * state)  1.12 us
  transfers between devices with their start and end apart: 9, of which 4 were waited for; matrix products, arithmetic and copies ran while one was open for 14% of the time, Pallas kernels for 0%

profile of v3, /device:TPU:0, one launch (start us, length us, event | category | flops | bytes accessed | tf_op | source)
XLA Modules:
  0.0 27.6 jit_solution(11735250163883649792)
XLA Ops:
  0.7 2.0 %shard_map.86 = (f32[112,128]{1,0:T(8,128)}, bf16[4,64,128]{2,1,0:T(8,128)(2,1)}) custom-call(f32[1,4]{1,0:T(1,128)} %refs_0_.1, f32[4,2,128]{2,1,0:T(2,128)} %bitcast.118, bf16[8,64,64]{2,1,0:T(8,128)(2,1)} %bitcast.95, f32[8,64,128]{2,1,0:T(8,128)} %refs_3_.1, s32[8,64]{1,0:T(8,128)} %refs_4_.1), custom_call_target="tpu_custom_call" | custom-call | tf_op jit(solution)/shard_map/pallas_call | solution.py:63
  2.6 0.5 %collective-permute-start = (f32[112,128]{1,0:T(8,128)}, f32[112,128]{1,0:T(8,128)S(1)}, u32[]{:S(2)}, u32[]{:S(2)}) collective-permute-start(f32[112,128]{1,0:T(8,128)} %get-tuple-element.9.mine_ref), channel_id=1, source_target_pairs={{0,1},{1,0},{2,3},{3,2},{4,5},{5,4},{6,7},{7,6},{8,9},{9,8},{10,11... | collective-permute-start | bytes 172040 | tf_op jit(solution)/shard_map/ppermute | solution.py:18
  3.2 2.7 %collective-permute-start.2 = (bf16[4,64,128]{2,1,0:T(8,128)(2,1)}, bf16[4,64,128]{2,1,0:T(8,128)(2,1)S(1)}, u32[]{:S(2)}, u32[]{:S(2)}) collective-permute-start(bf16[4,64,128]{2,1,0:T(8,128)(2,1)} %get-tuple-element.10.one_ref), channel_id=1, source_target_pairs={{0,8},{8,0},{16,24},{24,16},{1,9},{9,1},{17,25},{25,17},{2,10},{10... | collective-permute-start | bytes 196616 | tf_op jit(solution)/shard_map/ppermute | solution.py:18
  5.8 0.0 copy-start.5
  5.9 0.6 %copy-done.5 = f32[16]{0:T(128)S(1)} copy-done((f32[16]{0:T(128)S(1)}, f32[16]{0:T(128)}, u32[]{:S(2)}) %copy-start.5) | copy-done | bytes 88
  6.6 0.8 %copy-done.1 = f32[112,128]{1,0:T(8,128)S(1)} copy-done((f32[112,128]{1,0:T(8,128)S(1)}, f32[112,128]{1,0:T(8,128)}, u32[]{:S(2)}) %copy-start.1) | copy-done | bytes 57368
  7.3 1.5 %collective-permute-start.1 = (f32[72,128]{1,0:T(8,128)S(1)}, f32[72,128]{1,0:T(8,128)S(1)}, u32[]{:S(2)}, u32[]{:S(2)}) collective-permute-start(f32[72,128]{1,0:T(8,128)S(1)} %shard_map.87.mine_ref), channel_id=1, source_target_pairs={{0,2},{2,0},{4,6},{6,4},{1,3},{3,1},{5,7},{7,5},{8,10},{10,8},{12,... | collective-permute-start | bytes 110600 | tf_op jit(solution)/shard_map/ppermute | solution.py:18
  8.8 0.1 pad_maximum_fusion.6
  9.1 0.6 %collective-permute-start.8 = (bf16[4,73,128]{2,1,0:T(8,128)(2,1)S(1)}, bf16[4,73,128]{2,1,0:T(8,128)(2,1)S(1)}, u32[]{:S(2)}, u32[]{:S(2)}) collective-permute-start(bf16[4,73,128]{2,1,0:T(8,128)(2,1)S(1)} %pad_maximum_fusion.4), channel_id=1, source_target_pairs={{0,2},{2,0},{4,6},{6,4},{1,3},{3,1},{5,7},{7,5},{8,10},{10,8},{12,... | collective-permute-start | bytes 224264 | tf_op jit(solution)/shard_map/ppermute | solution.py:18
  9.7 1.6 %collective-permute-done.1.got_ref = f32[72,128]{1,0:T(8,128)S(1)} collective-permute-done((f32[72,128]{1,0:T(8,128)S(1)}, f32[72,128]{1,0:T(8,128)S(1)}, u32[]{:S(2)}, u32[]{:S(2)}) %collective-permute-start.1) | collective-permute-done | bytes 36896 | tf_op jit(solution)/shard_map/ppermute | solution.py:18
  11.3 1.6 %collective-permute-start.3 = (f32[72,128]{1,0:T(8,128)S(1)}, f32[72,128]{1,0:T(8,128)S(1)}, u32[]{:S(2)}, u32[]{:S(2)}) collective-permute-start(f32[72,128]{1,0:T(8,128)S(1)} %get-tuple-element.11.mine_ref), channel_id=1, source_target_pairs={{0,4},{2,6},{4,0},{6,2},{1,5},{3,7},{5,1},{7,3},{8,12},{10,14},{12... | collective-permute-start | bytes 110600 | tf_op jit(solution)/shard_map/ppermute | solution.py:18
  12.9 2.7 %collective-permute-start.4 = (bf16[8,64,128]{2,1,0:T(8,128)(2,1)S(1)}, bf16[8,64,128]{2,1,0:T(8,128)(2,1)S(1)}, u32[]{:S(2)}, u32[]{:S(2)}) collective-permute-start(bf16[8,64,128]{2,1,0:T(8,128)(2,1)S(1)} %get-tuple-element.13), channel_id=1, source_target_pairs={{0,16},{8,24},{16,0},{24,8},{1,17},{9,25},{17,1},{25,9},{2,18},{10... | collective-permute-start | bytes 393224 | tf_op jit(solution)/shard_map/ppermute | solution.py:18
  15.6 0.1 shard_map.89
  15.7 0.7 %collective-permute-start.5 = (bf16[64,128]{1,0:T(8,128)(2,1)S(1)}, bf16[64,128]{1,0:T(8,128)(2,1)S(1)}, u32[]{:S(2)}, u32[]{:S(2)}) collective-permute-start(bf16[64,128]{1,0:T(8,128)(2,1)S(1)} %get-tuple-element.14), channel_id=1, source_target_pairs={{0,8},{8,0},{16,24},{24,16},{1,9},{9,1},{17,25},{25,17},{2,10},{10... | collective-permute-start | bytes 49160 | tf_op jit(solution)/shard_map/ppermute | solution.py:18
  16.4 0.6 %copy.42 = f32[1,4,2,128]{3,2,1,0:T(2,128)} copy(f32[1,4,2,128]{3,1,2,0:T(4,128)S(1)} %dynamic-slice_bitcast_fusion) | data formatting | bytes 8192
  17.0 2.6 %collective-permute-start.7 = (bf16[4,73,128]{2,1,0:T(8,128)(2,1)S(1)}, bf16[4,73,128]{2,1,0:T(8,128)(2,1)S(1)}, u32[]{:S(2)}, u32[]{:S(2)}) collective-permute-start(bf16[4,73,128]{2,1,0:T(8,128)(2,1)S(1)} %get-tuple-element.15), channel_id=1, source_target_pairs={{0,6},{2,4},{4,2},{6,0},{1,7},{3,5},{5,3},{7,1},{8,14},{10,12},{12... | collective-permute-start | bytes 224264 | tf_op jit(solution)/shard_map/ppermute | solution.py:18
  19.6 1.7 %collective-permute-done.5 = bf16[64,128]{1,0:T(8,128)(2,1)S(1)} collective-permute-done((bf16[64,128]{1,0:T(8,128)(2,1)S(1)}, bf16[64,128]{1,0:T(8,128)(2,1)S(1)}, u32[]{:S(2)}, u32[]{:S(2)}) %collective-permute-start.5) | collective-permute-done | bytes 16416 | tf_op jit(solution)/shard_map/ppermute | solution.py:18
  21.3 0.9 %collective-permute-start.6 = (bf16[2,64,128]{2,1,0:T(8,128)(2,1)S(1)}, bf16[2,64,128]{2,1,0:T(8,128)(2,1)S(1)}, u32[]{:S(2)}, u32[]{:S(2)}) collective-permute-start(bf16[2,64,128]{2,1,0:T(8,128)(2,1)S(1)} %pad_maximum_fusion.5), channel_id=1, source_target_pairs={{0,16},{8,24},{16,0},{24,8},{1,17},{9,25},{17,1},{25,9},{2,18},{10... | collective-permute-start | bytes 98312 | tf_op jit(solution)/shard_map/ppermute | solution.py:18
  22.3 0.1 collective-permute-done.7
  22.5 0.1 maximum_add_fusion
  22.6 0.2 fusion.18
  22.8 0.1 fusion.32
  22.9 0.1 fusion.31
  23.0 0.1 fusion.30
  23.3 0.1 pad_maximum_fusion
  23.4 0.9 %fusion.1 = f32[14,70,128]{2,1,0:T(8,128)S(1)} fusion(f32[16,72,128]{2,1,0:T(8,128)S(1)} %pad_maximum_fusion, f32[14,70]{1,0:T(8,128)S(1)} %bitcast.103, f32[14,70]{1,0:T(8,128)S(1)} %bitcast.104, f32[14,70]{1,0:T(8,128)S(1)} %bitcast.105, f32[14,70]{1,0:T(8,128)S(1)} %bitcast.106, f32[14,70]{1,0:T(8,128)S(1)} %bitcast.107), kind=kLoop, calls=%fused_computation.4 | loop fusion | flops 1128960 | bytes 3030160 | tf_op jit(solution)/shard_map/sub | solution.py:175
  24.2 0.8 %fusion.5 = f32[12,68,128]{2,1,0:T(8,128)S(1)} fusion(f32[14,70,128]{2,1,0:T(8,128)S(1)} %fusion.1, f32[12,68]{1,0:T(8,128)S(1)} %bitcast.98, f32[12,68]{1,0:T(8,128)S(1)} %bitcast.99, f32[12,68]{1,0:T(8,128)S(1)} %bitcast.100, f32[12,68]{1,0:T(8,128)S(1)} %bitcast.101, f32[12,68]{1,0:T(8,128)S(1)} %bitcast.102), kind=kLoop, calls=%fused_computation.13 | loop fusion | flops 940032 | bytes 2523072 | tf_op jit(solution)/shard_map/sub | solution.py:175
  25.0 0.5 %fusion.9 = f32[10,66,128]{2,1,0:T(8,128)S(1)} fusion(f32[12,68,128]{2,1,0:T(8,128)S(1)} %fusion.5, f32[10,66]{1,0:T(8,128)S(1)} %bitcast.108, f32[10,66]{1,0:T(8,128)S(1)} %bitcast.109, f32[10,66]{1,0:T(8,128)S(1)} %bitcast.110, f32[10,66]{1,0:T(8,128)S(1)} %bitcast.111, f32[10,66]{1,0:T(8,128)S(1)} %bitcast.112), kind=kLoop, calls=%fused_computation.22 | loop fusion | flops 760320 | bytes 2040720 | tf_op jit(solution)/shard_map/sub | solution.py:175
  25.6 0.1 fusion.29
  25.7 0.4 %collective-permute-done.6 = bf16[2,64,128]{2,1,0:T(8,128)(2,1)S(1)} collective-permute-done((bf16[2,64,128]{2,1,0:T(8,128)(2,1)S(1)}, bf16[2,64,128]{2,1,0:T(8,128)(2,1)S(1)}, u32[]{:S(2)}, u32[]{:S(2)}) %collective-permute-start.6) | collective-permute-done | bytes 32800 | tf_op jit(solution)/shard_map/ppermute | solution.py:18
  26.2 0.3 convolution_bitcast_fusion
  26.5 1.1 %fusion.15 = f32[8,64,128]{2,1,0:T(8,128)} fusion(f32[10,66,128]{2,1,0:T(8,128)S(1)} %fusion.9, f32[4,64,128]{2,1,0:T(8,128)S(1)} %get-tuple-element.23, f32[4,64,128]{2,1,0:T(8,128)S(1)} %get-tuple-element.22, f32[8,64]{1,0:T(8,128)S(1)} %bitcast.114, f32[8,64]{1,0:T(8,128)S(1)} %bitcast.115, f32[8,64]{1,0:T(8,128)S(1)} %bitcast.116, ...), kind=kLoop, calls=%fused_computation.34 | loop fusion | flops 786432 | bytes 1845248 | tf_op jit(solution)/shard_map/add | solution.py:292
  (60 shorter events, 0.4 us)
Async XLA Ops:
  0.6 5.2 %copy-start.3 = (s32[8,64]{1,0:T(8,128)S(1)}, s32[8,64]{1,0:T(8,128)}, u32[]{:S(2)}) copy-start(s32[8,64]{1,0:T(8,128)} %refs_4_.1) | copy-start | bytes 6148
  0.6 8.3 %copy-start.2 = (f32[8,64,128]{2,1,0:T(8,128)S(1)}, f32[8,64,128]{2,1,0:T(8,128)}, u32[]{:S(2)}) copy-start(f32[8,64,128]{2,1,0:T(8,128)} %refs_3_.1) | copy-start | bytes 786436
  2.6 3.9 %collective-permute-start = (f32[112,128]{1,0:T(8,128)}, f32[112,128]{1,0:T(8,128)S(1)}, u32[]{:S(2)}, u32[]{:S(2)}) collective-permute-start(f32[112,128]{1,0:T(8,128)} %get-tuple-element.9.mine_ref), channel_id=1, source_target_pairs={{0,1},{1,0},{2,3},{3,2},{4,5},{5,4},{6,7},{7,6},{8,9},{9,8},{10,11... | collective-permute-start | bytes 172040 | tf_op jit(solution)/shard_map/ppermute | solution.py:18
  3.2 2.7 %copy-start.4 = (f32[4,16]{1,0:T(4,128)S(1)}, f32[4,16]{1,0:T(4,128)}, u32[]{:S(2)}) copy-start(f32[4,16]{1,0:T(4,128)} %param.13) | copy-start | bytes 772
  3.2 6.5 %collective-permute-start.2 = (bf16[4,64,128]{2,1,0:T(8,128)(2,1)}, bf16[4,64,128]{2,1,0:T(8,128)(2,1)S(1)}, u32[]{:S(2)}, u32[]{:S(2)}) collective-permute-start(bf16[4,64,128]{2,1,0:T(8,128)(2,1)} %get-tuple-element.10.one_ref), channel_id=1, source_target_pairs={{0,8},{8,0},{16,24},{24,16},{1,9},{9,1},{17,25},{25,17},{2,10},{10... | collective-permute-start | bytes 196616 | tf_op jit(solution)/shard_map/ppermute | solution.py:18
  5.8 0.7 %copy-start.5 = (f32[16]{0:T(128)S(1)}, f32[16]{0:T(128)}, u32[]{:S(2)}) copy-start(f32[16]{0:T(128)} %param.12) | copy-start | bytes 196
  6.5 0.8 %copy-start.1 = (f32[112,128]{1,0:T(8,128)S(1)}, f32[112,128]{1,0:T(8,128)}, u32[]{:S(2)}) copy-start(f32[112,128]{1,0:T(8,128)} %get-tuple-element.9.mine_ref) | copy-start | bytes 172036
  7.3 4.0 %collective-permute-start.1 = (f32[72,128]{1,0:T(8,128)S(1)}, f32[72,128]{1,0:T(8,128)S(1)}, u32[]{:S(2)}, u32[]{:S(2)}) collective-permute-start(f32[72,128]{1,0:T(8,128)S(1)} %shard_map.87.mine_ref), channel_id=1, source_target_pairs={{0,2},{2,0},{4,6},{6,4},{1,3},{3,1},{5,7},{7,5},{8,10},{10,8},{12,... | collective-permute-start | bytes 110600 | tf_op jit(solution)/shard_map/ppermute | solution.py:18
  9.0 2.3 %copy-start = (bf16[4,64,128]{2,1,0:T(8,128)(2,1)S(1)}, bf16[4,64,128]{2,1,0:T(8,128)(2,1)}, u32[]{:S(2)}) copy-start(bf16[4,64,128]{2,1,0:T(8,128)(2,1)} %get-tuple-element.10.one_ref) | copy-start | bytes 196612
  9.1 13.2 %collective-permute-start.8 = (bf16[4,73,128]{2,1,0:T(8,128)(2,1)S(1)}, bf16[4,73,128]{2,1,0:T(8,128)(2,1)S(1)}, u32[]{:S(2)}, u32[]{:S(2)}) collective-permute-start(bf16[4,73,128]{2,1,0:T(8,128)(2,1)S(1)} %pad_maximum_fusion.4), channel_id=1, source_target_pairs={{0,2},{2,0},{4,6},{6,4},{1,3},{3,1},{5,7},{7,5},{8,10},{10,8},{12,... | collective-permute-start | bytes 224264 | tf_op jit(solution)/shard_map/ppermute | solution.py:18
  11.3 4.3 %collective-permute-start.3 = (f32[72,128]{1,0:T(8,128)S(1)}, f32[72,128]{1,0:T(8,128)S(1)}, u32[]{:S(2)}, u32[]{:S(2)}) collective-permute-start(f32[72,128]{1,0:T(8,128)S(1)} %get-tuple-element.11.mine_ref), channel_id=1, source_target_pairs={{0,4},{2,6},{4,0},{6,2},{1,5},{3,7},{5,1},{7,3},{8,12},{10,14},{12... | collective-permute-start | bytes 110600 | tf_op jit(solution)/shard_map/ppermute | solution.py:18
  12.9 12.8 %collective-permute-start.4 = (bf16[8,64,128]{2,1,0:T(8,128)(2,1)S(1)}, bf16[8,64,128]{2,1,0:T(8,128)(2,1)S(1)}, u32[]{:S(2)}, u32[]{:S(2)}) collective-permute-start(bf16[8,64,128]{2,1,0:T(8,128)(2,1)S(1)} %get-tuple-element.13), channel_id=1, source_target_pairs={{0,16},{8,24},{16,0},{24,8},{1,17},{9,25},{17,1},{25,9},{2,18},{10... | collective-permute-start | bytes 393224 | tf_op jit(solution)/shard_map/ppermute | solution.py:18
  15.7 5.7 %collective-permute-start.5 = (bf16[64,128]{1,0:T(8,128)(2,1)S(1)}, bf16[64,128]{1,0:T(8,128)(2,1)S(1)}, u32[]{:S(2)}, u32[]{:S(2)}) collective-permute-start(bf16[64,128]{1,0:T(8,128)(2,1)S(1)} %get-tuple-element.14), channel_id=1, source_target_pairs={{0,8},{8,0},{16,24},{24,16},{1,9},{9,1},{17,25},{25,17},{2,10},{10... | collective-permute-start | bytes 49160 | tf_op jit(solution)/shard_map/ppermute | solution.py:18
  17.0 5.3 %collective-permute-start.7 = (bf16[4,73,128]{2,1,0:T(8,128)(2,1)S(1)}, bf16[4,73,128]{2,1,0:T(8,128)(2,1)S(1)}, u32[]{:S(2)}, u32[]{:S(2)}) collective-permute-start(bf16[4,73,128]{2,1,0:T(8,128)(2,1)S(1)} %get-tuple-element.15), channel_id=1, source_target_pairs={{0,6},{2,4},{4,2},{6,0},{1,7},{3,5},{5,3},{7,1},{8,14},{10,12},{12... | collective-permute-start | bytes 224264 | tf_op jit(solution)/shard_map/ppermute | solution.py:18
  21.3 4.8 %collective-permute-start.6 = (bf16[2,64,128]{2,1,0:T(8,128)(2,1)S(1)}, bf16[2,64,128]{2,1,0:T(8,128)(2,1)S(1)}, u32[]{:S(2)}, u32[]{:S(2)}) collective-permute-start(bf16[2,64,128]{2,1,0:T(8,128)(2,1)S(1)} %pad_maximum_fusion.5), channel_id=1, source_target_pairs={{0,16},{8,24},{16,0},{24,8},{1,17},{9,25},{17,1},{25,9},{2,18},{10... | collective-permute-start | bytes 98312 | tf_op jit(solution)/shard_map/ppermute | solution.py:18

commit v4 on v3

--- a/solution.py
+++ b/solution.py
@@ -73,12 +73,12 @@
     return run
 
 
-def prepare(noise_ref, observed_ref, kernel_ref, field_ref, classes_ref, pay_ref, packed_ref, *far_ref):
+def prepare(kernel_ref, field_ref, classes_ref, pay_ref, packed_ref, rim_ref, *far_ref):
     beside, points, width = packed_ref.shape
     rows, cols, real = field_ref.shape
-    own, comps = observed_ref.shape[:2]
-    sensors = points // comps
-    place = lax.axis_index("px") * lax.axis_size("py") + lax.axis_index("py")
+    owners, block = pay_ref.shape[:2]
+    comps = 2
+    own = block // comps
     even = lax.axis_index("py") % 2 == 0
     total = jnp.zeros((points, real), jnp.float32)
     for x in range(beside):
@@ -87,19 +87,10 @@
         packed_ref[x] = packed
         field = jnp.concatenate([field_ref[k].astype(jnp.bfloat16) for k in picks], axis=0)
         total = total + jnp.dot(packed, field, preferred_element_type=jnp.float32)
-    spot = lax.broadcasted_iota(jnp.int32, (points, real), 0)
-    for c in range(comps):
-        for k in range(own):
-            row = c * sensors + place * own + k
-            total = total - jnp.where(spot == row, observed_ref[k, c : c + 1, :], 0.0)
-    pay_ref[:points] = total
-    spot = lax.broadcasted_iota(jnp.int32, (TILE, real), 0) * real + lax.broadcasted_iota(
-        jnp.int32, (TILE, real), 1
-    )
-    noise = jnp.zeros((TILE, real), jnp.float32)
-    for k in range(own):
-        noise = noise + jnp.where(spot == place * own + k, noise_ref[0:1, k : k + 1], 0.0)
-    pay_ref[points : points + TILE] = noise
+    for p in range(owners):
+        for c in range(comps):
+            start = (c * owners + p) * own
+            pay_ref[p, c * own : (c + 1) * own] = total[start : start + own]
     marks = (classes_ref[...] + 1).astype(jnp.float32)
     edges = [
         (field_ref[:, cols - SWEEPS :, :], marks[:, cols - SWEEPS :]),
@@ -115,45 +106,25 @@
         ref[start : start + rows] = jnp.zeros((rows, real), jnp.float32)
         ref[start : start + rows, :SWEEPS] = jnp.where(chosen, edges[0][1], edges[1][1])
 
-    put(pay_ref, points + TILE, even)
+    put(rim_ref, 0, even)
     for ref in far_ref:
         put(ref, 0, jnp.logical_not(even))
 
 
-def add_first(mine_ref, got_ref, out_ref):
-    size = out_ref.shape[0]
-    out_ref[...] = mine_ref[:size] + got_ref[:size]
-
-
-def add_and_join(mine_ref, got_ref, one_ref, two_ref, out_ref, joined_ref):
-    out_ref[...] = mine_ref[...] + got_ref[...]
-    half = one_ref.shape[0]
-    joined_ref[:half] = one_ref[...]
-    joined_ref[half:] = two_ref[...]
-
-
-def weigh(mine_ref, got_ref, held_ref, low_ref, weighted_ref, passed_ref):
-    comps, sensors, real = weighted_ref.shape
-    points = comps * sensors
-    total = mine_ref[...] + got_ref[...]
-    chunk = min(sensors, real)
-    eye = lax.broadcasted_iota(jnp.int32, (chunk, real), 0) == lax.broadcasted_iota(
-        jnp.int32, (chunk, real), 1
-    )
-    for k in range(sensors // chunk):
-        row = total[points + k : points + k + 1]
-        noise = jnp.sum(jnp.where(eye, row, 0.0), axis=1, keepdims=True)
-        inverse = 1.0 / (noise * noise)
-        misfit = [total[c * sensors + k * chunk : c * sensors + (k + 1) * chunk] for c in range(comps)]
-        spread = sum(part * part for part in misfit) * inverse
-        factor = (FREEDOM + 2.0) / (FREEDOM + spread) * inverse
-        for c in range(comps):
-            weighted = misfit[c] * factor
-            weighted_ref[c, k * chunk : (k + 1) * chunk] = weighted
-            low_ref[c * sensors + k * chunk : c * sensors + (k + 1) * chunk] = weighted.astype(
-                jnp.bfloat16
-            )
-    passed_ref[...] = held_ref[...]
+def weigh(got_ref, observed_ref, noise_ref, low_ref, weighted_ref):
+    own, comps, real = weighted_ref.shape
+    total = got_ref[0]
+    for p in range(1, got_ref.shape[0]):
+        total = total + got_ref[p]
+    misfit = [total[c * own : (c + 1) * own] - observed_ref[:, c, :] for c in range(comps)]
+    noise = noise_ref[...]
+    inverse = 1.0 / (noise * noise)
+    spread = sum(part * part for part in misfit) * inverse
+    factor = (FREEDOM + 2.0) / (FREEDOM + spread) * inverse
+    weighted = [part * factor for part in misfit]
+    for c in range(comps):
+        weighted_ref[:, c, :] = weighted[c]
+    low_ref[...] = jnp.concatenate(weighted, axis=0).astype(jnp.bfloat16)
 
 
 def coefficients(classes, kappa_table, coupling_table):
@@ -180,28 +151,46 @@
     comps, sensors = forward_kernel.shape[3:]
     own = observed.shape[1]
     points = comps * sensors
-    place = lax.axis_index(("px", "py"))
     kernel_own = forward_kernel[0].transpose(0, 2, 3, 1).reshape(rows, points, cols)
     beside = rows // max(1, min(rows, LANES // cols))
     side = rows // beside
-    assert sensors <= TILE * real
     rim_rows = rows * (SWEEPS + 1)
+    space = ("px", "py")
+    everyone = ("freq", "px", "py")
+    owners = lax.axis_size(space)
+    peers = lax.axis_size(everyone)
     wide_py, wide_px = lax.axis_size("py") > 2, lax.axis_size("px") > 2
-    payload, kernel_own, *far_rim = call(
+    payload, kernel_own, *rim = call(
         prepare,
-        ((points + TILE + rim_rows, real), jnp.float32),
+        ((owners, comps * own, real), jnp.float32),
         ((beside, points, side * cols), jnp.bfloat16),
-        *[((rim_rows, real), jnp.float32)] * wide_py,
+        *[((rim_rows, real), jnp.float32)] * (1 + wide_py),
         fetch=True,
-    )(noise_scale, observed[0], kernel_own, model_field, classes)
-    got = swap(payload, "py", near)
+    )(kernel_own, model_field, classes)
+    got = lax.all_to_all(payload, space, split_axis=0, concat_axis=0, tiled=True)
     kernel_next = swap(kernel_own, "freq", near)
-    (total,) = call(add_first, ((points + TILE, real), jnp.float32))(payload, got)
-    for bit in bits("py")[1:]:
-        total = total + swap(total, "py", lambda i: i ^ bit)
-
-    one = got[points + TILE :]
-    two = swap(far_rim[0], "py", far("py")) if wide_py else one
+    kernel_pair = jnp.concatenate([kernel_own, kernel_next])
+    kernel_far = swap(kernel_pair, "freq", lambda i: i ^ 2)
+    weighted_low, weighted_own = call(
+        weigh,
+        ((comps * own, real), jnp.bfloat16),
+        ((own, comps, real), jnp.float32),
+    )(got, observed[0], noise_scale.reshape(own, 1))
+    low_all = lax.all_to_all(
+        jnp.broadcast_to(weighted_low[None], (peers, comps * own, real)),
+        everyone,
+        split_axis=0,
+        concat_axis=0,
+        tiled=True,
+    )
+    low_all = low_all.reshape(-1, owners, comps, own, real).transpose(0, 2, 1, 3, 4).reshape(-1, points, real)
+    me = lax.axis_index("freq")
+    low_all = jnp.stack(
+        [lax.dynamic_index_in_dim(low_all, me ^ k, 0, keepdims=False) for k in range(4)]
+    )
+
+    one = swap(rim[0], "py", near)
+    two = swap(rim[1], "py", far("py")) if wide_py else one
     before, after = both_sides(one, two, "py")
     marks = (classes + 1).astype(jnp.float32)
 
@@ -230,31 +219,6 @@
 
     one = swap(sent(even), "px", near)
     held = sent(jnp.logical_not(even))
-
-    steps = bits("px")
-    for bit in steps[:-1]:
-        got = swap(total, "px", lambda i: i ^ bit)
-        if bit == steps[-2]:
-            total, kernel_pair = call(
-                add_and_join,
-                ((points + TILE, real), jnp.float32),
-                ((2 * beside, points, side * cols), jnp.bfloat16),
-            )(total, got, kernel_own, kernel_next)
-        else:
-            total = total + got
-    kernel_far = swap(kernel_pair, "freq", lambda i: i ^ 2)
-    got = swap(total, "px", lambda i: i ^ steps[-1])
-    weighted_low, weighted, held = call(
-        weigh,
-        ((points, real), jnp.bfloat16),
-        ((comps, sensors, real), jnp.float32),
-        (held.shape, held.dtype),
-    )(total, got, held)
-    low_next = swap(weighted_low, "freq", near)
-    low_pair = jnp.concatenate([weighted_low[None], low_next[None]], axis=0)
-    low_far = swap(low_pair, "freq", lambda i: i ^ 2)
-    weighted_own = lax.dynamic_slice_in_dim(weighted, place * own, own, axis=1).transpose(1, 0, 2)
-
     two = swap(held, "px", far("px")) if wide_px else one
     before, after = both_sides(one, two, "px")
     state = jnp.concatenate(
@@ -283,7 +247,7 @@
     data_grad = jnp.einsum(
         "fxqy,fqr->xyr",
         jnp.concatenate([kernel_pair, kernel_far]).reshape(4, beside, points, side * cols),
-        jnp.concatenate([low_pair, low_far]),
+        low_all,
         preferred_element_type=jnp.float32,
     )
     data_grad = jnp.concatenate(

time: 27.8 us -> 32 us (1.15)
  starting transfers between devices: 13.8 us -> 17.7 us
  local copies, waits for them, and re-layouts: 2.6 us -> 1.44 us
  waiting for transfers between devices: 3.86 us -> 4.61 us
  Pallas kernels: 2.1 us -> 2.58 us
    all_to_all x0 -> x2, starting transfers between devices: none -> 9.61 us  [the longest x1 5.31 us: local(): lax.all_to_all(payload, space, split_axis=0, concat_axis=0, tiled=True)]
    ppermute x9 -> x5, starting transfers between devices: 13.8 us -> 8.09 us  [swap(): lax.ppermute(own, axis, [(i, partner(i)) for i in range(lax.axis_size(axi...]
    unnamed x30 -> x31, local copies, waits for them, and re-layouts: 2.06 us -> 0.12 us
    all_to_all x0 -> x2, waiting for transfers between devices: none -> 1.54 us  [the longest x1 1.54 us: local(): lax.all_to_all(jnp.broadcast_to(weighted_low[None], (peers, comps * own,...]
    ppermute x9 -> x5, waiting for transfers between devices: 3.86 us -> 3.06 us  [swap(): lax.ppermute(own, axis, [(i, partner(i)) for i in range(lax.axis_size(axi...]
    broadcast_in_dim x1, local copies, waits for them, and re-layouts: 0.01 us -> 0.64 us  [local(): jnp.broadcast_to(weighted_low[None], (peers, comps * own, real))]
    pallas_call x4 -> x2, Pallas kernels: 2.1 us -> 2.58 us  [run(): pl.pallas_call(fetched if fetch else body, out_shape=[jax.ShapeDtypeStruc...]
  transfers between devices with their start and end apart: 9 -> 7, of which waited for: 4 -> 2; matrix products, arithmetic and copies ran while one was open for 14% -> 13% of each run, Pallas kernels for 0% -> 2%
where the time goes in v4:
time: 32 us; the launch traced here: 31.6 us
  starting transfers between devices  17.7 us (55%)
  waiting for transfers between devices  4.61 us (14%)
  other arithmetic  3.75 us (12%)
  Pallas kernels  2.58 us (8%)
  local copies, waits for them, and re-layouts  1.44 us (4%)
  between operations  1.13 us (4%)
  matrix products  0.43 us (1%)
    ppermute x5, starting transfers between devices, swap(): lax.ppermute(own, axis, [(i, partner(i)) for i in range(lax.axis_size(axi...  8.09 us
    all_to_all x1, starting transfers between devices, local(): lax.all_to_all(payload, space, split_axis=0, concat_axis=0, tiled=True)  5.31 us
    all_to_all x1, starting transfers between devices, local(): lax.all_to_all(jnp.broadcast_to(weighted_low[None], (peers, comps * own,...  4.29 us
    ppermute x5, waiting for transfers between devices, swap(): lax.ppermute(own, axis, [(i, partner(i)) for i in range(lax.axis_size(axi...  3.06 us
    pallas_call x2, Pallas kernels, run(): pl.pallas_call(fetched if fetch else body, out_shape=[jax.ShapeDtypeStruc...  2.58 us
    sub x3, other arithmetic, operate(): return coefficient[..., 0:1] * center - beside  2.2 us
    all_to_all x1, waiting for transfers between devices, local(): lax.all_to_all(jnp.broadcast_to(weighted_low[None], (peers, comps * own,...  1.54 us
    add x1, other arithmetic, local(): return (weighted_own[None], data_grad + PRIOR_WEIGHT * state)  1.12 us
  transfers between devices with their start and end apart: 7, of which 2 were waited for; matrix products, arithmetic and copies ran while one was open for 13% of the time, Pallas kernels for 2%

profile of v4, /device:TPU:0, one launch (start us, length us, event | category | flops | bytes accessed | tf_op | source)
XLA Modules:
  0.0 31.6 jit_solution(8119752959174799582)
XLA Ops:
  0.7 1.9 %shard_map.86 = (f32[8,8,128]{2,1,0:T(8,128)}, bf16[4,64,128]{2,1,0:T(8,128)(2,1)}, f32[40,128]{1,0:T(8,128)}) custom-call(bf16[8,64,64]{2,1,0:T(8,128)(2,1)} %bitcast.96, f32[8,64,128]{2,1,0:T(8,128)} %refs_1_.1, s32[8,64]{1,0:T(8,128)} %refs_2_.1), custom_call_target="tpu_custom_call" | custom-call | tf_op jit(solution)/shard_map/pallas_call | solution.py:63
  2.6 0.0 copy-start.1
  2.6 5.3 %all-to-all-start = ((f32[8,8,128]{2,1,0:T(8,128)}), f32[8,8,128]{2,1,0:T(8,128)S(1)}, u32[]{:S(2)}, u32[]{:S(2)}) async-start(f32[8,8,128]{2,1,0:T(8,128)} %get-tuple-element.7), calls=%async_computation | async-start | bytes 65536 | tf_op jit(solution)/shard_map/all_to_all | solution.py:170
  7.9 0.5 %collective-permute-start.2 = (f32[40,128]{1,0:T(8,128)}, f32[40,128]{1,0:T(8,128)S(1)}, u32[]{:S(2)}, u32[]{:S(2)}) collective-permute-start(f32[40,128]{1,0:T(8,128)} %get-tuple-element.11), channel_id=1, source_target_pairs={{0,1},{1,0},{2,3},{3,2},{4,5},{5,4},{6,7},{7,6},{8,9},{9,8},{10,11... | collective-permute-start | bytes 61448 | tf_op jit(solution)/shard_map/ppermute | solution.py:18
  8.4 1.6 %collective-permute-start = (bf16[4,64,128]{2,1,0:T(8,128)(2,1)}, bf16[4,64,128]{2,1,0:T(8,128)(2,1)S(1)}, u32[]{:S(2)}, u32[]{:S(2)}) collective-permute-start(bf16[4,64,128]{2,1,0:T(8,128)(2,1)} %get-tuple-element.9), channel_id=1, source_target_pairs={{0,8},{8,0},{16,24},{24,16},{1,9},{9,1},{17,25},{25,17},{2,10},{10... | collective-permute-start | bytes 196616 | tf_op jit(solution)/shard_map/ppermute | solution.py:18
  10.1 0.1 copy.20.noise_ref
  10.2 0.0 collective-permute-done.2
  10.2 0.1 pad_maximum_fusion.6
  10.4 2.6 %collective-permute-start.3 = (bf16[4,73,128]{2,1,0:T(8,128)(2,1)S(1)}, bf16[4,73,128]{2,1,0:T(8,128)(2,1)S(1)}, u32[]{:S(2)}, u32[]{:S(2)}) collective-permute-start(bf16[4,73,128]{2,1,0:T(8,128)(2,1)S(1)} %pad_maximum_fusion.4), channel_id=1, source_target_pairs={{0,6},{2,4},{4,2},{6,0},{1,7},{3,5},{5,3},{7,1},{8,14},{10,12},{12... | collective-permute-start | bytes 224264 | tf_op jit(solution)/shard_map/ppermute | solution.py:18
  13.1 0.6 %collective-permute-start.4 = (bf16[4,73,128]{2,1,0:T(8,128)(2,1)S(1)}, bf16[4,73,128]{2,1,0:T(8,128)(2,1)S(1)}, u32[]{:S(2)}, u32[]{:S(2)}) collective-permute-start(bf16[4,73,128]{2,1,0:T(8,128)(2,1)S(1)} %pad_maximum_fusion.5), channel_id=1, source_target_pairs={{0,2},{2,0},{4,6},{6,4},{1,3},{3,1},{5,7},{7,5},{8,10},{10,8},{12,... | collective-permute-start | bytes 224264 | tf_op jit(solution)/shard_map/ppermute | solution.py:18
  13.7 0.0 all-to-all-done.got_ref
  13.7 0.0 copy-done
  13.8 0.7 %shard_map.87 = (bf16[8,128]{1,0:T(8,128)(2,1)S(1)}, f32[4,2,128]{2,1,0:T(2,128)}) custom-call(f32[8,8,128]{2,1,0:T(8,128)S(1)} %all-to-all-done.got_ref, f32[4,2,128]{2,1,0:T(2,128)S(1)} %bitcast.88, f32[4,1]{1,0:T(4,128)S(1)} %copy.20.noise_ref), custom_call_target="tpu_custom_call" | custom-call | tf_op jit(solution)/shard_map/pallas_call | solution.py:63
  14.5 0.6 %broadcast_in_dim.21 = bf16[32,8,128]{2,1,0:T(8,128)(2,1)} broadcast(bf16[8,128]{1,0:T(8,128)(2,1)S(1)} %get-tuple-element.10), dimensions={1,2} | broadcast | bytes 67584 | tf_op jit(solution)/shard_map/broadcast_in_dim | solution.py:180
  15.1 4.3 %all-to-all-start.1 = ((bf16[32,8,128]{2,1,0:T(8,128)(2,1)}), bf16[32,8,128]{2,1,0:T(8,128)(2,1)S(1)}, u32[]{:S(2)}, u32[]{:S(2)}) async-start(bf16[32,8,128]{2,1,0:T(8,128)(2,1)} %broadcast_in_dim.21), calls=%async_computation.1 | async-start | bytes 131072 | tf_op jit(solution)/shard_map/all_to_all | solution.py:179
  19.4 0.0 collective-permute-done
  19.4 2.7 %collective-permute-start.1 = (bf16[8,64,128]{2,1,0:T(8,128)(2,1)S(1)}, bf16[8,64,128]{2,1,0:T(8,128)(2,1)S(1)}, u32[]{:S(2)}, u32[]{:S(2)}) collective-permute-start(bf16[8,64,128]{2,1,0:T(8,128)(2,1)S(1)} %pad_maximum_fusion.3), channel_id=1, source_target_pairs={{0,16},{8,24},{16,0},{24,8},{1,17},{9,25},{17,1},{25,9},{2,18},{10... | collective-permute-start | bytes 393224 | tf_op jit(solution)/shard_map/ppermute | solution.py:18
  22.2 0.0 collective-permute-done.3
  22.3 0.1 maximum_add_fusion
  22.4 0.2 fusion.18
  22.6 0.1 fusion.34
  22.7 0.1 fusion.33
  22.8 0.1 fusion.32
  23.1 0.1 pad_maximum_fusion
  23.2 0.9 %fusion.1 = f32[14,70,128]{2,1,0:T(8,128)S(1)} fusion(f32[16,72,128]{2,1,0:T(8,128)S(1)} %pad_maximum_fusion, f32[14,70]{1,0:T(8,128)S(1)} %bitcast.102, f32[14,70]{1,0:T(8,128)S(1)} %bitcast.103, f32[14,70]{1,0:T(8,128)S(1)} %bitcast.104, f32[14,70]{1,0:T(8,128)S(1)} %bitcast.105, f32[14,70]{1,0:T(8,128)S(1)} %bitcast.106), kind=kLoop, calls=%fused_computation.4 | loop fusion | flops 1128960 | bytes 3030160 | tf_op jit(solution)/shard_map/sub | solution.py:146
  24.1 0.8 %fusion.5 = f32[12,68,128]{2,1,0:T(8,128)S(1)} fusion(f32[14,70,128]{2,1,0:T(8,128)S(1)} %fusion.1, f32[12,68]{1,0:T(8,128)S(1)} %bitcast.97, f32[12,68]{1,0:T(8,128)S(1)} %bitcast.98, f32[12,68]{1,0:T(8,128)S(1)} %bitcast.99, f32[12,68]{1,0:T(8,128)S(1)} %bitcast.100, f32[12,68]{1,0:T(8,128)S(1)} %bitcast.101), kind=kLoop, calls=%fused_computation.13 | loop fusion | flops 940032 | bytes 2523072 | tf_op jit(solution)/shard_map/sub | solution.py:146
  24.9 0.5 %fusion.9 = f32[10,66,128]{2,1,0:T(8,128)S(1)} fusion(f32[12,68,128]{2,1,0:T(8,128)S(1)} %fusion.5, f32[10,66]{1,0:T(8,128)S(1)} %bitcast.107, f32[10,66]{1,0:T(8,128)S(1)} %bitcast.108, f32[10,66]{1,0:T(8,128)S(1)} %bitcast.109, f32[10,66]{1,0:T(8,128)S(1)} %bitcast.110, f32[10,66]{1,0:T(8,128)S(1)} %bitcast.111), kind=kLoop, calls=%fused_computation.22 | loop fusion | flops 760320 | bytes 2040720 | tf_op jit(solution)/shard_map/sub | solution.py:146
  25.4 0.1 fusion.31
  25.5 1.5 %all-to-all-done.1 = bf16[32,8,128]{2,1,0:T(8,128)(2,1)S(1)} async-done(((bf16[32,8,128]{2,1,0:T(8,128)(2,1)}), bf16[32,8,128]{2,1,0:T(8,128)(2,1)S(1)}, u32[]{:S(2)}, u32[]{:S(2)}) %all-to-all-start.1) | async-done | bytes 65568 | tf_op jit(solution)/shard_map/all_to_all | solution.py:179
  27.1 3.1 %collective-permute-done.1 = bf16[8,64,128]{2,1,0:T(8,128)(2,1)S(1)} collective-permute-done((bf16[8,64,128]{2,1,0:T(8,128)(2,1)S(1)}, bf16[8,64,128]{2,1,0:T(8,128)(2,1)S(1)}, u32[]{:S(2)}, u32[]{:S(2)}) %collective-permute-start.1) | collective-permute-done | bytes 131104 | tf_op jit(solution)/shard_map/ppermute | solution.py:18
  30.2 0.3 convolution_bitcast_fusion
  30.5 1.1 %fusion.15 = f32[8,64,128]{2,1,0:T(8,128)} fusion(f32[10,66,128]{2,1,0:T(8,128)S(1)} %fusion.9, f32[4,64,128]{2,1,0:T(8,128)S(1)} %get-tuple-element.13, f32[4,64,128]{2,1,0:T(8,128)S(1)} %get-tuple-element.12, f32[8,64]{1,0:T(8,128)S(1)} %bitcast.113, f32[8,64]{1,0:T(8,128)S(1)} %bitcast.114, f32[8,64]{1,0:T(8,128)S(1)} %bitcast.115, ...), kind=kLoop, calls=%fused_computation.34 | loop fusion | flops 786432 | bytes 1845248 | tf_op jit(solution)/shard_map/add | solution.py:256
  (59 shorter events, 0.4 us)
Async XLA Ops:
  0.6 9.4 %copy-start.3 = (s32[8,64]{1,0:T(8,128)S(1)}, s32[8,64]{1,0:T(8,128)}, u32[]{:S(2)}) copy-start(s32[8,64]{1,0:T(8,128)} %refs_2_.1) | copy-start | bytes 6148
  0.6 9.4 %copy-start.4 = (f32[4,16]{1,0:T(4,128)S(1)}, f32[4,16]{1,0:T(4,128)}, u32[]{:S(2)}) copy-start(f32[4,16]{1,0:T(4,128)} %param.13) | copy-start | bytes 772
  0.7 9.4 %copy-start.6 = (f32[16]{0:T(128)S(1)}, f32[16]{0:T(128)}, u32[]{:S(2)}) copy-start(f32[16]{0:T(128)} %param.12) | copy-start | bytes 196
  0.7 9.4 %copy-start.5 = (f32[1,4]{1,0:T(1,128)S(1)}, f32[1,4]{1,0:T(1,128)}, u32[]{:S(2)}) copy-start(f32[1,4]{1,0:T(1,128)} %param.8) | copy-start | bytes 52
  2.6 7.8 %copy-start.1 = (f32[8,64,128]{2,1,0:T(8,128)S(1)}, f32[8,64,128]{2,1,0:T(8,128)}, u32[]{:S(2)}) copy-start(f32[8,64,128]{2,1,0:T(8,128)} %refs_1_.1) | copy-start | bytes 786436
  2.6 11.1 %all-to-all-start = ((f32[8,8,128]{2,1,0:T(8,128)}), f32[8,8,128]{2,1,0:T(8,128)S(1)}, u32[]{:S(2)}, u32[]{:S(2)}) async-start(f32[8,8,128]{2,1,0:T(8,128)} %get-tuple-element.7), calls=%async_computation | async-start | bytes 65536 | tf_op jit(solution)/shard_map/all_to_all | solution.py:170
  7.9 2.3 %collective-permute-start.2 = (f32[40,128]{1,0:T(8,128)}, f32[40,128]{1,0:T(8,128)S(1)}, u32[]{:S(2)}, u32[]{:S(2)}) collective-permute-start(f32[40,128]{1,0:T(8,128)} %get-tuple-element.11), channel_id=1, source_target_pairs={{0,1},{1,0},{2,3},{3,2},{4,5},{5,4},{6,7},{7,6},{8,9},{9,8},{10,11... | collective-permute-start | bytes 61448 | tf_op jit(solution)/shard_map/ppermute | solution.py:18
  8.4 11.0 %collective-permute-start = (bf16[4,64,128]{2,1,0:T(8,128)(2,1)}, bf16[4,64,128]{2,1,0:T(8,128)(2,1)S(1)}, u32[]{:S(2)}, u32[]{:S(2)}) collective-permute-start(bf16[4,64,128]{2,1,0:T(8,128)(2,1)} %get-tuple-element.9), channel_id=1, source_target_pairs={{0,8},{8,0},{16,24},{24,16},{1,9},{9,1},{17,25},{25,17},{2,10},{10... | collective-permute-start | bytes 196616 | tf_op jit(solution)/shard_map/ppermute | solution.py:18
  10.4 11.8 %collective-permute-start.3 = (bf16[4,73,128]{2,1,0:T(8,128)(2,1)S(1)}, bf16[4,73,128]{2,1,0:T(8,128)(2,1)S(1)}, u32[]{:S(2)}, u32[]{:S(2)}) collective-permute-start(bf16[4,73,128]{2,1,0:T(8,128)(2,1)S(1)} %pad_maximum_fusion.4), channel_id=1, source_target_pairs={{0,6},{2,4},{4,2},{6,0},{1,7},{3,5},{5,3},{7,1},{8,14},{10,12},{12... | collective-permute-start | bytes 224264 | tf_op jit(solution)/shard_map/ppermute | solution.py:18
  13.1 0.7 %copy-start = (f32[1,4,2,128]{3,2,1,0:T(2,128)S(1)}, f32[1,4,2,128]{3,2,1,0:T(2,128)}, u32[]{:S(2)}) copy-start(f32[1,4,2,128]{3,2,1,0:T(2,128)} %param.7) | copy-start | bytes 12292
  13.1 9.1 %collective-permute-start.4 = (bf16[4,73,128]{2,1,0:T(8,128)(2,1)S(1)}, bf16[4,73,128]{2,1,0:T(8,128)(2,1)S(1)}, u32[]{:S(2)}, u32[]{:S(2)}) collective-permute-start(bf16[4,73,128]{2,1,0:T(8,128)(2,1)S(1)} %pad_maximum_fusion.5), channel_id=1, source_target_pairs={{0,2},{2,0},{4,6},{6,4},{1,3},{3,1},{5,7},{7,5},{8,10},{10,8},{12,... | collective-permute-start | bytes 224264 | tf_op jit(solution)/shard_map/ppermute | solution.py:18
  15.1 4.3 %copy-start.2 = (bf16[4,64,128]{2,1,0:T(8,128)(2,1)S(1)}, bf16[4,64,128]{2,1,0:T(8,128)(2,1)}, u32[]{:S(2)}) copy-start(bf16[4,64,128]{2,1,0:T(8,128)(2,1)} %get-tuple-element.9) | copy-start | bytes 196612
  15.1 12.0 %all-to-all-start.1 = ((bf16[32,8,128]{2,1,0:T(8,128)(2,1)}), bf16[32,8,128]{2,1,0:T(8,128)(2,1)S(1)}, u32[]{:S(2)}, u32[]{:S(2)}) async-start(bf16[32,8,128]{2,1,0:T(8,128)(2,1)} %broadcast_in_dim.21), calls=%async_computation.1 | async-start | bytes 131072 | tf_op jit(solution)/shard_map/all_to_all | solution.py:179
  19.4 10.7 %collective-permute-start.1 = (bf16[8,64,128]{2,1,0:T(8,128)(2,1)S(1)}, bf16[8,64,128]{2,1,0:T(8,128)(2,1)S(1)}, u32[]{:S(2)}, u32[]{:S(2)}) collective-permute-start(bf16[8,64,128]{2,1,0:T(8,128)(2,1)S(1)} %pad_maximum_fusion.3), channel_id=1, source_target_pairs={{0,16},{8,24},{16,0},{24,8},{1,17},{9,25},{17,1},{25,9},{2,18},{10... | collective-permute-start | bytes 393224 | tf_op jit(solution)/shard_map/ppermute | solution.py:18

commit v5 on v3

--- a/solution.py
+++ b/solution.py
@@ -11,7 +11,6 @@
 LANES = 128
 TILE = 8
 VMEM_BYTES = 40 << 20
-ALL_VMEM_BYTES = 63 << 20
 
 
 def swap(own, axis, partner):
@@ -43,6 +42,8 @@
 def call(body, *out_shapes, fetch=False):
     def run(*operands):
         count = len(operands)
+        if fetch:
+            operands = [pltpu.with_memory_space_constraint(x, pltpu.HBM) for x in operands]
 
         def fetched(*refs):
             outs, held, sems = (
@@ -67,13 +68,27 @@
             out_specs=[pl.BlockSpec(memory_space=pltpu.VMEM)] * len(out_shapes),
             scratch_shapes=[pltpu.VMEM(x.shape, x.dtype) for x in operands] * fetch
             + [pltpu.SemaphoreType.DMA((count,))] * fetch,
-            compiler_params=pltpu.CompilerParams(vmem_limit_bytes=ALL_VMEM_BYTES if fetch else VMEM_BYTES),
+            compiler_params=pltpu.CompilerParams(vmem_limit_bytes=VMEM_BYTES),
         )(*operands)
 
     return run
 
 
-def prepare(noise_ref, observed_ref, kernel_ref, field_ref, classes_ref, pay_ref, packed_ref, *far_ref):
+def prepare(
+    noise_ref,
+    observed_ref,
+    kernel_ref,
+    field_ref,
+    classes_ref,
+    kappa_ref,
+    coupling_ref,
+    pay_ref,
+    packed_ref,
+    held_ref,
+    marks_ref,
+    table_ref,
+    *far_ref,
+):
     beside, points, width = packed_ref.shape
     rows, cols, real = field_ref.shape
     own, comps = observed_ref.shape[:2]
@@ -100,7 +115,12 @@
     for k in range(own):
         noise = noise + jnp.where(spot == place * own + k, noise_ref[0:1, k : k + 1], 0.0)
     pay_ref[points : points + TILE] = noise
+    held_ref[...] = field_ref[...]
+    coupling = coupling_ref[...]
+    table_ref[0:1] = kappa_ref[...] + jnp.sum(coupling, axis=0, keepdims=True)
+    table_ref[1:] = coupling
     marks = (classes_ref[...] + 1).astype(jnp.float32)
+    marks_ref[...] = marks
     edges = [
         (field_ref[:, cols - SWEEPS :, :], marks[:, cols - SWEEPS :]),
         (field_ref[:, :SWEEPS, :], marks[:, :SWEEPS]),
@@ -132,7 +152,7 @@
     joined_ref[half:] = two_ref[...]
 
 
-def weigh(mine_ref, got_ref, held_ref, low_ref, weighted_ref, passed_ref):
+def weigh(mine_ref, got_ref, low_ref, weighted_ref):
     comps, sensors, real = weighted_ref.shape
     points = comps * sensors
     total = mine_ref[...] + got_ref[...]
@@ -153,15 +173,12 @@
             low_ref[c * sensors + k * chunk : c * sensors + (k + 1) * chunk] = weighted.astype(
                 jnp.bfloat16
             )
-    passed_ref[...] = held_ref[...]
-
-
-def coefficients(classes, kappa_table, coupling_table):
-    levels = jnp.arange(kappa_table.shape[0], dtype=jnp.float32)
+
+
+def coefficients(classes, table):
+    levels = jnp.arange(table.shape[1], dtype=jnp.float32)
     onehot = (classes[..., None] == levels).astype(jnp.float32)
-    diagonal = kappa_table + jnp.sum(coupling_table, axis=0)
-    class_table = jnp.concatenate([diagonal[None, :], coupling_table], axis=0)
-    return jnp.einsum("xyk,ck->xyc", onehot, class_table, precision=lax.Precision.HIGHEST)
+    return jnp.einsum("xyk,ck->xyc", onehot, table, precision=lax.Precision.HIGHEST)
 
 
 def operate(padded, coefficient):
@@ -187,13 +204,24 @@
     assert sensors <= TILE * real
     rim_rows = rows * (SWEEPS + 1)
     wide_py, wide_px = lax.axis_size("py") > 2, lax.axis_size("px") > 2
-    payload, kernel_own, *far_rim = call(
+    payload, kernel_own, model_field, marks, table, *far_rim = call(
         prepare,
         ((points + TILE + rim_rows, real), jnp.float32),
         ((beside, points, side * cols), jnp.bfloat16),
+        (model_field.shape, jnp.float32),
+        (classes.shape, jnp.float32),
+        ((1 + coupling_table.shape[0], coupling_table.shape[1]), jnp.float32),
         *[((rim_rows, real), jnp.float32)] * wide_py,
         fetch=True,
-    )(noise_scale, observed[0], kernel_own, model_field, classes)
+    )(
+        noise_scale,
+        observed[0],
+        kernel_own,
+        model_field,
+        classes,
+        kappa_table[None],
+        coupling_table,
+    )
     got = swap(payload, "py", near)
     kernel_next = swap(kernel_own, "freq", near)
     (total,) = call(add_first, ((points + TILE, real), jnp.float32))(payload, got)
@@ -203,7 +231,6 @@
     one = got[points + TILE :]
     two = swap(far_rim[0], "py", far("py")) if wide_py else one
     before, after = both_sides(one, two, "py")
-    marks = (classes + 1).astype(jnp.float32)
 
     def fields(rim):
         return rim[: rows * SWEEPS].reshape(rows, SWEEPS, real)
@@ -229,7 +256,7 @@
         ).astype(jnp.bfloat16)
 
     one = swap(sent(even), "px", near)
-    held = sent(jnp.logical_not(even))
+    two = swap(sent(jnp.logical_not(even)), "px", far("px")) if wide_px else one
 
     steps = bits("px")
     for bit in steps[:-1]:
@@ -244,18 +271,25 @@
             total = total + got
     kernel_far = swap(kernel_pair, "freq", lambda i: i ^ 2)
     got = swap(total, "px", lambda i: i ^ steps[-1])
-    weighted_low, weighted, held = call(
+    weighted_low, weighted = call(
         weigh,
         ((points, real), jnp.bfloat16),
         ((comps, sensors, real), jnp.float32),
-        (held.shape, held.dtype),
-    )(total, got, held)
-    low_next = swap(weighted_low, "freq", near)
-    low_pair = jnp.concatenate([weighted_low[None], low_next[None]], axis=0)
-    low_far = swap(low_pair, "freq", lambda i: i ^ 2)
+    )(total, got)
+    freqs = lax.axis_size("freq")
+    low_all = lax.all_to_all(
+        jnp.broadcast_to(weighted_low[None], (freqs, points, real)),
+        "freq",
+        split_axis=0,
+        concat_axis=0,
+        tiled=True,
+    )
+    me = lax.axis_index("freq")
+    low_all = jnp.stack(
+        [lax.dynamic_index_in_dim(low_all, me ^ k, 0, keepdims=False) for k in range(freqs)]
+    )
     weighted_own = lax.dynamic_slice_in_dim(weighted, place * own, own, axis=1).transpose(1, 0, 2)
 
-    two = swap(held, "px", far("px")) if wide_px else one
     before, after = both_sides(one, two, "px")
     state = jnp.concatenate(
         [
@@ -273,7 +307,7 @@
         ],
         axis=0,
     )
-    coefficient = coefficients(marks - 1.0, kappa_table, coupling_table)
+    coefficient = coefficients(marks - 1.0, table)
     for step in range(SWEEPS):
         lo = step + 1
         state = operate(
@@ -283,7 +317,7 @@
     data_grad = jnp.einsum(
         "fxqy,fqr->xyr",
         jnp.concatenate([kernel_pair, kernel_far]).reshape(4, beside, points, side * cols),
-        jnp.concatenate([low_pair, low_far]),
+        low_all,
         preferred_element_type=jnp.float32,
     )
     data_grad = jnp.concatenate(

time: 27.8 us -> 28.2 us (1.014)
  waiting for transfers between devices: 3.86 us -> 0.5 us
  local copies, waits for them, and re-layouts: 2.6 us -> 4.9 us
  starting transfers between devices: 13.8 us -> 15.7 us
  Pallas kernels: 2.1 us -> 1.48 us
    ppermute x9 -> x7, waiting for transfers between devices: 3.86 us -> 0.5 us  [swap(): lax.ppermute(own, axis, [(i, partner(i)) for i in range(lax.axis_size(axi...]
    all_to_all x0 -> x1, starting transfers between devices: none -> 3.28 us  [local(): lax.all_to_all(jnp.broadcast_to(weighted_low[None], (freqs, points, real)...]
    mul x0 -> x20, local copies, waits for them, and re-layouts: none -> 2.02 us  [the longest x4 0.41 us: operate(): coefficient[..., 4:5] * padded[1:-1, 2:]]
    ppermute x9 -> x7, starting transfers between devices: 13.8 us -> 12.4 us  [swap(): lax.ppermute(own, axis, [(i, partner(i)) for i in range(lax.axis_size(axi...]
    sub x3, other arithmetic: 2.2 us -> 2.97 us  [operate(): return coefficient[..., 0:1] * center - beside]
    add x1, other arithmetic: 1.12 us -> 0.41 us  [local(): return (weighted_own[None], data_grad + PRIOR_WEIGHT * state)]
    broadcast_in_dim x0 -> x1, local copies, waits for them, and re-layouts: none -> 0.64 us  [local(): jnp.broadcast_to(weighted_low[None], (freqs, points, real))]
    pallas_call x4, Pallas kernels: 2.1 us -> 1.48 us  [run(): pl.pallas_call(fetched if fetch else body, out_shape=[jax.ShapeDtypeStruc...]
  transfers between devices with their start and end apart: 9 -> 8, of which waited for: 4 -> 1; matrix products, arithmetic and copies ran while one was open for 14% -> 27% of each run, Pallas kernels for 0% -> 0%
where the time goes in v5:
time: 28.2 us; the launch traced here: 27.9 us
  starting transfers between devices  15.7 us (56%)
  local copies, waits for them, and re-layouts  4.9 us (17%)
  other arithmetic  3.98 us (14%)
  Pallas kernels  1.48 us (5%)
  between operations  0.96 us (3%)
  waiting for transfers between devices  0.5 us (2%)
  matrix products  0.43 us (2%)
    ppermute x7, starting transfers between devices, swap(): lax.ppermute(own, axis, [(i, partner(i)) for i in range(lax.axis_size(axi...  12.4 us
    all_to_all x1, starting transfers between devices, local(): lax.all_to_all(jnp.broadcast_to(weighted_low[None], (freqs, points, real)...  3.28 us
    sub x3, other arithmetic, operate(): return coefficient[..., 0:1] * center - beside  2.97 us
    unnamed x6, local copies, waits for them, and re-layouts  1.68 us
    pallas_call x4, Pallas kernels, run(): pl.pallas_call(fetched if fetch else body, out_shape=[jax.ShapeDtypeStruc...  1.48 us
    broadcast_in_dim x1, local copies, waits for them, and re-layouts, local(): jnp.broadcast_to(weighted_low[None], (freqs, points, real))  0.64 us
  transfers between devices with their start and end apart: 8, of which 1 were waited for; matrix products, arithmetic and copies ran while one was open for 27% of the time, Pallas kernels for 0%

profile of v5, /device:TPU:0, one launch (start us, length us, event | category | flops | bytes accessed | tf_op | source)
XLA Modules:
  0.0 27.9 jit_solution(2570688325411912685)
XLA Ops:
  0.6 1.4 %shard_map.86 = (f32[112,128]{1,0:T(8,128)S(1)}, bf16[4,64,128]{2,1,0:T(8,128)(2,1)S(1)}, f32[8,64,128]{2,1,0:T(8,128)S(1)}, f32[8,64]{1,0:T(8,128)S(1)}, f32[5,16]{1,0:T(8,128)S(1)}) custom-call(f32[1,4]{1,0:T(1,128)} %refs_0_.1, f32[4,2,128]{2,1,0:T(2,128)} %bitcast.77, bf16[8,64,64]{2,1,0:T(8,128)(2,1)} %bitcast.69, f32[8,64,128]{2,1,0:T(8,128)} %refs_3_.1, ...), custom_call_target="tpu_custom_call" | custom-call | tf_op jit(solution)/shard_map/pallas_call | solution.py:64
  2.0 0.5 %collective-permute-start = (f32[112,128]{1,0:T(8,128)S(1)}, f32[112,128]{1,0:T(8,128)S(1)}, u32[]{:S(2)}, u32[]{:S(2)}) collective-permute-start(f32[112,128]{1,0:T(8,128)S(1)} %get-tuple-element.11.mine_ref), channel_id=1, source_target_pairs={{0,1},{1,0},{2,3},{3,2},{4,5},{5,4},{6,7},{7,6},{8,9},{9,8},{10,11... | collective-permute-start | bytes 172040 | tf_op jit(solution)/shard_map/ppermute | solution.py:17
  2.5 2.6 %collective-permute-start.2 = (bf16[4,64,128]{2,1,0:T(8,128)(2,1)S(1)}, bf16[4,64,128]{2,1,0:T(8,128)(2,1)S(1)}, u32[]{:S(2)}, u32[]{:S(2)}) collective-permute-start(bf16[4,64,128]{2,1,0:T(8,128)(2,1)S(1)} %get-tuple-element.12.one_ref), channel_id=1, source_target_pairs={{0,8},{8,0},{16,24},{24,16},{1,9},{9,1},{17,25},{25,17},{2,10},{10... | collective-permute-start | bytes 196616 | tf_op jit(solution)/shard_map/ppermute | solution.py:17
  5.2 1.6 %collective-permute-start.1 = (f32[72,128]{1,0:T(8,128)S(1)}, f32[72,128]{1,0:T(8,128)S(1)}, u32[]{:S(2)}, u32[]{:S(2)}) collective-permute-start(f32[72,128]{1,0:T(8,128)S(1)} %shard_map.87.mine_ref), channel_id=1, source_target_pairs={{0,2},{2,0},{4,6},{6,4},{1,3},{3,1},{5,7},{7,5},{8,10},{10,8},{12,... | collective-permute-start | bytes 110600 | tf_op jit(solution)/shard_map/ppermute | solution.py:17
  6.9 0.2 copy_dynamic-update-slice_fusion
  7.2 1.6 %collective-permute-start.5 = (bf16[4,73,128]{2,0,1:T(4,128)(2,1)S(1)}, bf16[4,73,128]{2,0,1:T(4,128)(2,1)S(1)}, u32[]{:S(2)}, u32[]{:S(2)}) collective-permute-start(bf16[4,73,128]{2,0,1:T(4,128)(2,1)S(1)} %pad_maximum_fusion.2), channel_id=1, source_target_pairs={{0,6},{2,4},{4,2},{6,0},{1,7},{3,5},{5,3},{7,1},{8,14},{10,12},{12... | collective-permute-start | bytes 224264 | tf_op jit(solution)/shard_map/ppermute | solution.py:17
  8.8 0.5 %collective-permute-done.1.got_ref = f32[72,128]{1,0:T(8,128)S(1)} collective-permute-done((f32[72,128]{1,0:T(8,128)S(1)}, f32[72,128]{1,0:T(8,128)S(1)}, u32[]{:S(2)}, u32[]{:S(2)}) %collective-permute-start.1) | collective-permute-done | bytes 36896 | tf_op jit(solution)/shard_map/ppermute | solution.py:17
  9.3 1.6 %collective-permute-start.3 = (f32[72,128]{1,0:T(8,128)S(1)}, f32[72,128]{1,0:T(8,128)S(1)}, u32[]{:S(2)}, u32[]{:S(2)}) collective-permute-start(f32[72,128]{1,0:T(8,128)S(1)} %get-tuple-element.13.mine_ref), channel_id=1, source_target_pairs={{0,4},{2,6},{4,0},{6,2},{1,5},{3,7},{5,1},{7,3},{8,12},{10,14},{12... | collective-permute-start | bytes 110600 | tf_op jit(solution)/shard_map/ppermute | solution.py:17
  10.9 1.9 %collective-permute-start.6 = (bf16[4,73,128]{2,0,1:T(4,128)(2,1)S(1)}, bf16[4,73,128]{2,0,1:T(4,128)(2,1)S(1)}, u32[]{:S(2)}, u32[]{:S(2)}) collective-permute-start(bf16[4,73,128]{2,0,1:T(4,128)(2,1)S(1)} %pad_maximum_fusion.3), channel_id=1, source_target_pairs={{0,2},{2,0},{4,6},{6,4},{1,3},{3,1},{5,7},{7,5},{8,10},{10,8},{12,... | collective-permute-start | bytes 224264 | tf_op jit(solution)/shard_map/ppermute | solution.py:17
  12.9 2.6 %collective-permute-start.4 = (bf16[8,64,128]{2,1,0:T(8,128)(2,1)S(1)}, bf16[8,64,128]{2,1,0:T(8,128)(2,1)S(1)}, u32[]{:S(2)}, u32[]{:S(2)}) collective-permute-start(bf16[8,64,128]{2,1,0:T(8,128)(2,1)S(1)} %get-tuple-element.15), channel_id=1, source_target_pairs={{0,16},{8,24},{16,0},{24,8},{1,17},{9,25},{17,1},{25,9},{2,18},{10... | collective-permute-start | bytes 393224 | tf_op jit(solution)/shard_map/ppermute | solution.py:17
  15.6 0.6 %copy.35 = f32[1,4,2,128]{3,2,1,0:T(2,128)} copy(f32[1,4,2,128]{3,1,2,0:T(4,128)S(1)} %dynamic-slice_bitcast_fusion) | data formatting | bytes 8192
  16.2 0.6 %broadcast_in_dim.22 = bf16[4,64,128]{2,1,0:T(8,128)(2,1)} broadcast(bf16[64,128]{1,0:T(8,128)(2,1)S(1)} %get-tuple-element.16), dimensions={1,2} | broadcast | bytes 81920 | tf_op jit(solution)/shard_map/broadcast_in_dim | solution.py:281
  16.8 3.3 %all-to-all-start = ((bf16[4,64,128]{2,1,0:T(8,128)(2,1)}), bf16[4,64,128]{2,1,0:T(8,128)(2,1)S(1)}, u32[]{:S(2)}, u32[]{:S(2)}) async-start(bf16[4,64,128]{2,1,0:T(8,128)(2,1)} %broadcast_in_dim.22), calls=%async_computation | async-start | bytes 131072 | tf_op jit(solution)/shard_map/all_to_all | solution.py:280
  20.4 0.2 fusion.18
  20.5 0.1 fusion.32
  20.7 0.1 fusion.31
  20.8 0.1 fusion.30
  21.0 0.1 copy.45
  21.1 0.1 copy.44
  21.3 0.1 copy.43
  21.4 0.1 copy.42
  21.5 0.1 copy.41
  21.6 0.1 copy.49
  21.7 0.1 copy.48
  22.0 0.1 copy.40
  23.1 0.1 pad_maximum_fusion
  23.2 1.0 %fusion.1 = f32[14,70,128]{2,0,1:T(8,128)S(1)} fusion(f32[16,72,128]{2,0,1:T(8,128)S(1)} %pad_maximum_fusion, f32[14,70]{0,1:T(8,128)S(1)} %bitcast.59, f32[14,70]{0,1:T(8,128)S(1)} %bitcast.60, f32[14,70]{0,1:T(8,128)S(1)} %bitcast.61, f32[14,70]{0,1:T(8,128)S(1)} %bitcast.62, f32[14,70]{0,1:T(8,128)S(1)} %bitcast.63), kind=kLoop, calls=%fused_computation.4 | loop fusion | flops 1128960 | bytes 3030160 | tf_op jit(solution)/shard_map/sub | solution.py:192
  24.2 1.0 %fusion.5 = f32[12,68,128]{2,0,1:T(8,128)S(1)} fusion(f32[14,70,128]{2,0,1:T(8,128)S(1)} %fusion.1, f32[12,68]{0,1:T(8,128)S(1)} %bitcast.54, f32[12,68]{0,1:T(8,128)S(1)} %bitcast.55, f32[12,68]{0,1:T(8,128)S(1)} %bitcast.56, f32[12,68]{0,1:T(8,128)S(1)} %bitcast.57, f32[12,68]{0,1:T(8,128)S(1)} %bitcast.58), kind=kLoop, calls=%fused_computation.13 | loop fusion | flops 940032 | bytes 2523072 | tf_op jit(solution)/shard_map/sub | solution.py:192
  25.2 1.0 %fusion.9 = f32[10,66,128]{2,0,1:T(8,128)S(1)} fusion(f32[12,68,128]{2,0,1:T(8,128)S(1)} %fusion.5, f32[10,66]{0,1:T(8,128)S(1)} %bitcast.64, f32[10,66]{0,1:T(8,128)S(1)} %bitcast.65, f32[10,66]{0,1:T(8,128)S(1)} %bitcast.66, f32[10,66]{0,1:T(8,128)S(1)} %bitcast.67, f32[10,66]{0,1:T(8,128)S(1)} %bitcast.68), kind=kLoop, calls=%fused_computation.22 | loop fusion | flops 760320 | bytes 2040720 | tf_op jit(solution)/shard_map/sub | solution.py:192
  26.3 0.3 convolution_bitcast_fusion
  26.8 0.4 %fusion.15 = f32[8,64,128]{2,0,1:T(8,128)S(1)} fusion(f32[10,66,128]{2,0,1:T(8,128)S(1)} %fusion.9, f32[4,64,128]{2,0,1:T(4,128)S(1)} %copy.55, f32[4,64,128]{2,0,1:T(4,128)S(1)} %copy.54, f32[8,64]{0,1:T(8,128)S(1)} %copy.34, f32[8,64]{0,1:T(8,128)S(1)} %copy.33, f32[8,64]{0,1:T(8,128)S(1)} %copy.32, f32[8,64]{0,1:T(8,128)S(1)} %copy.31, f32[8,64]{0,1:T(8,128)S(1)} %copy.15), kind=kLoop, calls=%fused_computation.33 | loop fusion | flops 786432 | bytes 1845248 | tf_op jit(solution)/shard_map/add | solution.py:326
  27.2 0.8 %copy.36 = f32[8,64,128]{2,1,0:T(8,128)} copy(f32[8,64,128]{2,0,1:T(8,128)S(1)} %fusion.15) | data formatting | bytes 524288
  (49 shorter events, 2.1 us)
Async XLA Ops:
  2.0 3.2 %collective-permute-start = (f32[112,128]{1,0:T(8,128)S(1)}, f32[112,128]{1,0:T(8,128)S(1)}, u32[]{:S(2)}, u32[]{:S(2)}) collective-permute-start(f32[112,128]{1,0:T(8,128)S(1)} %get-tuple-element.11.mine_ref), channel_id=1, source_target_pairs={{0,1},{1,0},{2,3},{3,2},{4,5},{5,4},{6,7},{7,6},{8,9},{9,8},{10,11... | collective-permute-start | bytes 172040 | tf_op jit(solution)/shard_map/ppermute | solution.py:17
  2.5 6.3 %collective-permute-start.2 = (bf16[4,64,128]{2,1,0:T(8,128)(2,1)S(1)}, bf16[4,64,128]{2,1,0:T(8,128)(2,1)S(1)}, u32[]{:S(2)}, u32[]{:S(2)}) collective-permute-start(bf16[4,64,128]{2,1,0:T(8,128)(2,1)S(1)} %get-tuple-element.12.one_ref), channel_id=1, source_target_pairs={{0,8},{8,0},{16,24},{24,16},{1,9},{9,1},{17,25},{25,17},{2,10},{10... | collective-permute-start | bytes 196616 | tf_op jit(solution)/shard_map/ppermute | solution.py:17
  5.2 4.0 %collective-permute-start.1 = (f32[72,128]{1,0:T(8,128)S(1)}, f32[72,128]{1,0:T(8,128)S(1)}, u32[]{:S(2)}, u32[]{:S(2)}) collective-permute-start(f32[72,128]{1,0:T(8,128)S(1)} %shard_map.87.mine_ref), channel_id=1, source_target_pairs={{0,2},{2,0},{4,6},{6,4},{1,3},{3,1},{5,7},{7,5},{8,10},{10,8},{12,... | collective-permute-start | bytes 110600 | tf_op jit(solution)/shard_map/ppermute | solution.py:17
  7.2 12.9 %collective-permute-start.5 = (bf16[4,73,128]{2,0,1:T(4,128)(2,1)S(1)}, bf16[4,73,128]{2,0,1:T(4,128)(2,1)S(1)}, u32[]{:S(2)}, u32[]{:S(2)}) collective-permute-start(bf16[4,73,128]{2,0,1:T(4,128)(2,1)S(1)} %pad_maximum_fusion.2), channel_id=1, source_target_pairs={{0,6},{2,4},{4,2},{6,0},{1,7},{3,5},{5,3},{7,1},{8,14},{10,12},{12... | collective-permute-start | bytes 224264 | tf_op jit(solution)/shard_map/ppermute | solution.py:17
  9.3 6.2 %collective-permute-start.3 = (f32[72,128]{1,0:T(8,128)S(1)}, f32[72,128]{1,0:T(8,128)S(1)}, u32[]{:S(2)}, u32[]{:S(2)}) collective-permute-start(f32[72,128]{1,0:T(8,128)S(1)} %get-tuple-element.13.mine_ref), channel_id=1, source_target_pairs={{0,4},{2,6},{4,0},{6,2},{1,5},{3,7},{5,1},{7,3},{8,12},{10,14},{12... | collective-permute-start | bytes 110600 | tf_op jit(solution)/shard_map/ppermute | solution.py:17
  10.9 9.2 %collective-permute-start.6 = (bf16[4,73,128]{2,0,1:T(4,128)(2,1)S(1)}, bf16[4,73,128]{2,0,1:T(4,128)(2,1)S(1)}, u32[]{:S(2)}, u32[]{:S(2)}) collective-permute-start(bf16[4,73,128]{2,0,1:T(4,128)(2,1)S(1)} %pad_maximum_fusion.3), channel_id=1, source_target_pairs={{0,2},{2,0},{4,6},{6,4},{1,3},{3,1},{5,7},{7,5},{8,10},{10,8},{12,... | collective-permute-start | bytes 224264 | tf_op jit(solution)/shard_map/ppermute | solution.py:17
  12.9 13.3 %collective-permute-start.4 = (bf16[8,64,128]{2,1,0:T(8,128)(2,1)S(1)}, bf16[8,64,128]{2,1,0:T(8,128)(2,1)S(1)}, u32[]{:S(2)}, u32[]{:S(2)}) collective-permute-start(bf16[8,64,128]{2,1,0:T(8,128)(2,1)S(1)} %get-tuple-element.15), channel_id=1, source_target_pairs={{0,16},{8,24},{16,0},{24,8},{1,17},{9,25},{17,1},{25,9},{2,18},{10... | collective-permute-start | bytes 393224 | tf_op jit(solution)/shard_map/ppermute | solution.py:17
  16.8 9.4 %all-to-all-start = ((bf16[4,64,128]{2,1,0:T(8,128)(2,1)}), bf16[4,64,128]{2,1,0:T(8,128)(2,1)S(1)}, u32[]{:S(2)}, u32[]{:S(2)}) async-start(bf16[4,64,128]{2,1,0:T(8,128)(2,1)} %broadcast_in_dim.22), calls=%async_computation | async-start | bytes 131072 | tf_op jit(solution)/shard_map/all_to_all | solution.py:280

commit v6 on v5

--- a/solution.py
+++ b/solution.py
@@ -11,6 +11,7 @@
 LANES = 128
 TILE = 8
 VMEM_BYTES = 40 << 20
+PRIOR_FLOPS = 1 << 30
 
 
 def swap(own, axis, partner):
@@ -31,15 +32,7 @@
     return lambda i: (((i + 1) ^ 1) - 1) % lax.axis_size(axis)
 
 
-def both_sides(one, two, axis):
-    peers, me = lax.axis_size(axis), lax.axis_index(axis)
-    even = me % 2 == 0
-    zero = jnp.zeros_like(one)
-    before, after = jnp.where(even, two, one), jnp.where(even, one, two)
-    return jnp.where(me == 0, zero, before), jnp.where(me == peers - 1, zero, after)
-
-
-def call(body, *out_shapes, fetch=False):
+def call(body, *out_shapes, fetch=False, scratch=(), stored=(), flops=0):
     def run(*operands):
         count = len(operands)
         if fetch:
@@ -65,10 +58,15 @@
             fetched if fetch else body,
             out_shape=[jax.ShapeDtypeStruct(shape, dtype) for shape, dtype in out_shapes],
             in_specs=[pl.BlockSpec(memory_space=pltpu.HBM if fetch else pltpu.VMEM)] * count,
-            out_specs=[pl.BlockSpec(memory_space=pltpu.VMEM)] * len(out_shapes),
-            scratch_shapes=[pltpu.VMEM(x.shape, x.dtype) for x in operands] * fetch
+            out_specs=[
+                pl.BlockSpec(memory_space=pltpu.HBM if k in stored else pltpu.VMEM)
+                for k in range(len(out_shapes))
+            ],
+            scratch_shapes=list(scratch)
+            + [pltpu.VMEM(x.shape, x.dtype) for x in operands] * fetch
             + [pltpu.SemaphoreType.DMA((count,))] * fetch,
             compiler_params=pltpu.CompilerParams(vmem_limit_bytes=VMEM_BYTES),
+            cost_estimate=pl.CostEstimate(flops=flops, bytes_accessed=0, transcendentals=0),
         )(*operands)
 
     return run
@@ -120,7 +118,8 @@
     table_ref[0:1] = kappa_ref[...] + jnp.sum(coupling, axis=0, keepdims=True)
     table_ref[1:] = coupling
     marks = (classes_ref[...] + 1).astype(jnp.float32)
-    marks_ref[...] = marks
+    marks_ref[...] = jnp.zeros_like(marks_ref)
+    marks_ref[:, :cols] = marks
     edges = [
         (field_ref[:, cols - SWEEPS :, :], marks[:, cols - SWEEPS :]),
         (field_ref[:, :SWEEPS, :], marks[:, :SWEEPS]),
@@ -140,9 +139,47 @@
         put(ref, 0, jnp.logical_not(even))
 
 
-def add_first(mine_ref, got_ref, out_ref):
+def sides_of(one, two, axis):
+    me = lax.axis_index(axis)
+    even = me % 2 == 0
+    before = jnp.where(me == 0, 0.0, jnp.where(even, two, one))
+    after = jnp.where(me == lax.axis_size(axis) - 1, 0.0, jnp.where(even, one, two))
+    return before, after
+
+
+def add_and_edge(
+    mine_ref, got_ref, field_ref, marks_ref, *refs
+):
+    *far_ref, out_ref, side_ref, wide_ref, near_ref, far_rows_ref = refs
     size = out_ref.shape[0]
+    rows, cols, real = field_ref.shape
     out_ref[...] = mine_ref[:size] + got_ref[:size]
+    one = got_ref[size:]
+    before, after = sides_of(one, far_ref[0][...] if far_ref else one, "py")
+    fields = rows * SWEEPS
+    wide_ref[...] = (
+        marks_ref[...]
+        + pltpu.roll(after[fields:], cols, 1)
+        + pltpu.roll(before[fields:], cols + SWEEPS, 1)
+    )
+    for x in range(rows):
+        pick = slice(x * SWEEPS, (x + 1) * SWEEPS)
+        side_ref[x] = jnp.concatenate([after[pick], before[pick]], axis=0)
+    even = lax.axis_index("px") % 2 == 0
+    top = lax.broadcasted_iota(jnp.int32, (TILE, real), 0) == 0
+    step = near_ref.shape[0] // SWEEPS
+    for ref, chosen in ((near_ref, even), (far_rows_ref, jnp.logical_not(even))):
+        for k in range(SWEEPS):
+            last = rows - SWEEPS + k
+            marks = jnp.where(chosen, wide_ref[last : last + 1], wide_ref[k : k + 1])
+            ref[k * step : (k + 1) * step] = jnp.concatenate(
+                [
+                    jnp.where(chosen, field_ref[last], field_ref[k]),
+                    jnp.where(chosen, side_ref[last], side_ref[k]),
+                    jnp.where(top, marks, 0.0),
+                ],
+                axis=0,
+            ).astype(jnp.bfloat16)
 
 
 def add_and_join(mine_ref, got_ref, one_ref, two_ref, out_ref, joined_ref):
@@ -170,26 +207,119 @@
         for c in range(comps):
             weighted = misfit[c] * factor
             weighted_ref[c, k * chunk : (k + 1) * chunk] = weighted
-            low_ref[c * sensors + k * chunk : c * sensors + (k + 1) * chunk] = weighted.astype(
-                jnp.bfloat16
+            for f in range(low_ref.shape[0]):
+                low_ref[f, c * sensors + k * chunk : c * sensors + (k + 1) * chunk] = (
+                    weighted.astype(jnp.bfloat16)
+                )
+
+
+def prior(
+    field_ref,
+    side_ref,
+    wide_ref,
+    near_ref,
+    far_ref,
+    table_ref,
+    weighted_ref,
+    prior_ref,
+    own_out,
+    state_ref,
+    coef_ref,
+    own_ref,
+    sem,
+):
+    own, comps, real = own_ref.shape
+    sensors = weighted_ref.shape[1]
+    place = lax.axis_index("px") * lax.axis_size("py") + lax.axis_index("py")
+    spot = lax.broadcasted_iota(jnp.int32, (sensors, real), 0)
+    for c in range(comps):
+        for k in range(own):
+            own_ref[k, c : c + 1] = jnp.sum(
+                jnp.where(spot == place * own + k, weighted_ref[c], 0.0), axis=0, keepdims=True
             )
-
-
-def coefficients(classes, table):
-    levels = jnp.arange(table.shape[1], dtype=jnp.float32)
-    onehot = (classes[..., None] == levels).astype(jnp.float32)
-    return jnp.einsum("xyk,ck->xyc", onehot, table, precision=lax.Precision.HIGHEST)
-
-
-def operate(padded, coefficient):
-    center = padded[1:-1, 1:-1]
-    beside = coefficient[..., 1:2] * padded[:-2, 1:-1] + coefficient[..., 2:3] * padded[2:, 1:-1]
-    beside = (
-        beside
-        + coefficient[..., 3:4] * padded[1:-1, :-2]
-        + coefficient[..., 4:5] * padded[1:-1, 2:]
-    )
-    return coefficient[..., 0:1] * center - beside
+    out = pltpu.make_async_copy(own_ref, own_out, sem)
+    out.start()
+    rows, cols, _ = field_ref.shape
+    wide = cols + 2 * SWEEPS
+    step = near_ref.shape[0] // SWEEPS
+    before, after = sides_of(
+        near_ref[...].astype(jnp.float32), far_ref[...].astype(jnp.float32), "px"
+    )
+    marks = []
+    for k in range(SWEEPS):
+        state_ref[0, k] = before[k * step : k * step + wide]
+        state_ref[0, SWEEPS + rows + k] = after[k * step : k * step + wide]
+    for x in range(rows):
+        state_ref[0, SWEEPS + x] = jnp.concatenate([field_ref[x], side_ref[x]], axis=0)
+    marks = (
+        [before[k * step + wide : k * step + wide + 1] for k in range(SWEEPS)]
+        + [wide_ref[x : x + 1] for x in range(rows)]
+        + [after[k * step + wide : k * step + wide + 1] for k in range(SWEEPS)]
+    )
+    count, levels = table_ref.shape
+    spread = (
+        lax.broadcasted_iota(jnp.int32, (count, count * real), 1) // real
+        == lax.broadcasted_iota(jnp.int32, (count, count * real), 0)
+    ).astype(jnp.float32)
+    turn = (((0,), (0,)), ((), ()))
+    table = lax.dot_general(
+        table_ref[...],
+        spread,
+        turn,
+        precision=lax.Precision.HIGHEST,
+        preferred_element_type=jnp.float32,
+    )
+    high = table.astype(jnp.bfloat16)
+    rest = table - high.astype(jnp.float32)
+    middle = rest.astype(jnp.bfloat16)
+    low = (rest - middle.astype(jnp.float32)).astype(jnp.bfloat16)
+    table = jnp.concatenate([high, middle, low], axis=0)
+    level = lax.broadcasted_iota(jnp.int32, (levels, real), 0).astype(jnp.float32) + 1.0
+    for x in range(1, 2 * SWEEPS + rows - 1):
+        onehot = (level == marks[x]).astype(jnp.float32).astype(jnp.bfloat16)
+        onehot = jnp.concatenate([onehot] * 3, axis=0)[:, :wide]
+        coef = lax.dot_general(onehot, table, turn, preferred_element_type=jnp.float32)
+        for c in range(count):
+            coef_ref[x, c] = coef[:, c * real : (c + 1) * real]
+    for sweep in range(SWEEPS):
+        now, later = sweep % 2, (sweep + 1) % 2
+        for x in range(sweep + 1, 2 * SWEEPS + rows - sweep - 1):
+            center = state_ref[now, x]
+            beside = (
+                coef_ref[x, 1] * state_ref[now, x - 1]
+                + coef_ref[x, 2] * state_ref[now, x + 1]
+                + coef_ref[x, 3] * pltpu.roll(center, 1, 0)
+                + coef_ref[x, 4] * pltpu.roll(center, wide - 1, 0)
+            )
+            new = coef_ref[x, 0] * center - beside
+            if sweep < SWEEPS - 1:
+                state_ref[later, x] = new
+            else:
+                prior_ref[x - SWEEPS] = PRIOR_WEIGHT * new[:cols]
+    out.wait()
+
+
+def finish(pair_ref, far_ref, low_ref, prior_ref, out, held_ref, sems):
+    rows, cols, real = held_ref.shape
+    beside = pair_ref.shape[0] // 2
+    side = rows // beside
+    me = lax.axis_index("freq")
+    low = jnp.concatenate([low_ref[me ^ k] for k in range(low_ref.shape[0])], axis=0)
+    copies = []
+    for x in range(beside):
+        kernel = jnp.concatenate(
+            [pair_ref[x], pair_ref[beside + x], far_ref[x], far_ref[beside + x]], axis=0
+        )
+        grad = lax.dot_general(
+            kernel, low, (((0,), (0,)), ((), ())), preferred_element_type=jnp.float32
+        )
+        for k in range(side):
+            row = k * beside + x
+            held_ref[row] = grad[k * cols : (k + 1) * cols] + prior_ref[row]
+            copies.append(pltpu.make_async_copy(held_ref.at[row], out.at[row], sems.at[row]))
+            copies[-1].start()
+    for copy in copies:
+        copy.wait()
 
 
 def local(observed, noise_scale, forward_kernel, model_field, classes, kappa_table, coupling_table):
@@ -197,11 +327,11 @@
     comps, sensors = forward_kernel.shape[3:]
     own = observed.shape[1]
     points = comps * sensors
-    place = lax.axis_index(("px", "py"))
     kernel_own = forward_kernel[0].transpose(0, 2, 3, 1).reshape(rows, points, cols)
     beside = rows // max(1, min(rows, LANES // cols))
     side = rows // beside
-    assert sensors <= TILE * real
+    assert sensors <= TILE * real and cols + 2 * SWEEPS <= LANES
+    assert rows >= SWEEPS and (cols + 2 * SWEEPS + TILE) % 16 == 0
     rim_rows = rows * (SWEEPS + 1)
     wide_py, wide_px = lax.axis_size("py") > 2, lax.axis_size("px") > 2
     payload, kernel_own, model_field, marks, table, *far_rim = call(
@@ -209,7 +339,7 @@
         ((points + TILE + rim_rows, real), jnp.float32),
         ((beside, points, side * cols), jnp.bfloat16),
         (model_field.shape, jnp.float32),
-        (classes.shape, jnp.float32),
+        ((rows, LANES), jnp.float32),
         ((1 + coupling_table.shape[0], coupling_table.shape[1]), jnp.float32),
         *[((rim_rows, real), jnp.float32)] * wide_py,
         fetch=True,
@@ -224,39 +354,20 @@
     )
     got = swap(payload, "py", near)
     kernel_next = swap(kernel_own, "freq", near)
-    (total,) = call(add_first, ((points + TILE, real), jnp.float32))(payload, got)
+    two = [swap(rim, "py", far("py")) for rim in far_rim]
+    step = cols + 2 * SWEEPS + TILE
+    total, side_rim, wide_marks, near_rows, far_rows = call(
+        add_and_edge,
+        ((points + TILE, real), jnp.float32),
+        ((rows, 2 * SWEEPS, real), jnp.float32),
+        ((rows, LANES), jnp.float32),
+        ((SWEEPS * step, real), jnp.bfloat16),
+        ((SWEEPS * step, real), jnp.bfloat16),
+    )(payload, got, model_field, marks, *two)
     for bit in bits("py")[1:]:
         total = total + swap(total, "py", lambda i: i ^ bit)
-
-    one = got[points + TILE :]
-    two = swap(far_rim[0], "py", far("py")) if wide_py else one
-    before, after = both_sides(one, two, "py")
-
-    def fields(rim):
-        return rim[: rows * SWEEPS].reshape(rows, SWEEPS, real)
-
-    wide_field = jnp.concatenate([fields(before), model_field, fields(after)], axis=1)
-    marks = jnp.concatenate(
-        [before[rows * SWEEPS :, :SWEEPS], marks, after[rows * SWEEPS :, :SWEEPS]], axis=1
-    )
-    wide = cols + 2 * SWEEPS
-    even = lax.axis_index("px") % 2 == 0
-    mark_rows = -(-wide // real)
-
-    def sent(chosen):
-        return jnp.concatenate(
-            [
-                jnp.where(chosen, wide_field[rows - SWEEPS :], wide_field[:SWEEPS]),
-                jnp.pad(
-                    jnp.where(chosen, marks[rows - SWEEPS :], marks[:SWEEPS]),
-                    ((0, 0), (0, mark_rows * real - wide)),
-                ).reshape(SWEEPS, mark_rows, real),
-            ],
-            axis=1,
-        ).astype(jnp.bfloat16)
-
-    one = swap(sent(even), "px", near)
-    two = swap(sent(jnp.logical_not(even)), "px", far("px")) if wide_px else one
+    near_rows = swap(near_rows, "px", near)
+    far_rows = swap(far_rows, "px", far("px")) if wide_px else near_rows
 
     steps = bits("px")
     for bit in steps[:-1]:
@@ -271,59 +382,38 @@
             total = total + got
     kernel_far = swap(kernel_pair, "freq", lambda i: i ^ 2)
     got = swap(total, "px", lambda i: i ^ steps[-1])
+    freqs = lax.axis_size("freq")
+    assert freqs == 4
     weighted_low, weighted = call(
         weigh,
-        ((points, real), jnp.bfloat16),
+        ((freqs, points, real), jnp.bfloat16),
         ((comps, sensors, real), jnp.float32),
     )(total, got)
-    freqs = lax.axis_size("freq")
-    low_all = lax.all_to_all(
-        jnp.broadcast_to(weighted_low[None], (freqs, points, real)),
-        "freq",
-        split_axis=0,
-        concat_axis=0,
-        tiled=True,
-    )
-    me = lax.axis_index("freq")
-    low_all = jnp.stack(
-        [lax.dynamic_index_in_dim(low_all, me ^ k, 0, keepdims=False) for k in range(freqs)]
-    )
-    weighted_own = lax.dynamic_slice_in_dim(weighted, place * own, own, axis=1).transpose(1, 0, 2)
-
-    before, after = both_sides(one, two, "px")
-    state = jnp.concatenate(
-        [
-            before[:, :wide].astype(jnp.float32),
-            wide_field,
-            after[:, :wide].astype(jnp.float32),
-        ],
-        axis=0,
-    )
-    marks = jnp.concatenate(
-        [
-            before[:, wide:].reshape(SWEEPS, -1)[:, :wide].astype(jnp.float32),
-            marks,
-            after[:, wide:].reshape(SWEEPS, -1)[:, :wide].astype(jnp.float32),
-        ],
-        axis=0,
-    )
-    coefficient = coefficients(marks - 1.0, table)
-    for step in range(SWEEPS):
-        lo = step + 1
-        state = operate(
-            state, coefficient[lo : coefficient.shape[0] - lo, lo : coefficient.shape[1] - lo]
-        )
-
-    data_grad = jnp.einsum(
-        "fxqy,fqr->xyr",
-        jnp.concatenate([kernel_pair, kernel_far]).reshape(4, beside, points, side * cols),
-        low_all,
-        preferred_element_type=jnp.float32,
-    )
-    data_grad = jnp.concatenate(
-        [data_grad[:, k * cols : (k + 1) * cols] for k in range(side)], axis=0
-    )
-    return weighted_own[None], data_grad + PRIOR_WEIGHT * state
+    low_all = lax.all_to_all(weighted_low, "freq", split_axis=0, concat_axis=0, tiled=True)
+    wide = cols + 2 * SWEEPS
+    prior_term, weighted_own = call(
+        prior,
+        (model_field.shape, jnp.float32),
+        ((own, comps, real), jnp.float32),
+        stored=(1,),
+        scratch=(
+            pltpu.VMEM((2, rows + 2 * SWEEPS, wide, real), jnp.float32),
+            pltpu.VMEM((rows + 2 * SWEEPS, table.shape[0], wide, real), jnp.float32),
+            pltpu.VMEM((own, comps, real), jnp.float32),
+            pltpu.SemaphoreType.DMA(()),
+        ),
+        flops=PRIOR_FLOPS,
+    )(model_field, side_rim, wide_marks, near_rows, far_rows, table, weighted)
+    (gradient,) = call(
+        finish,
+        (model_field.shape, jnp.float32),
+        stored=(0,),
+        scratch=(
+            pltpu.VMEM(model_field.shape, jnp.float32),
+            pltpu.SemaphoreType.DMA((rows,)),
+        ),
+    )(kernel_pair, kernel_far, low_all, prior_term)
+    return weighted_own[None], gradient
 
 
 def solution(mesh):

time: 28.2 us -> 29 us (1.028)
  waiting for transfers between devices: 0.5 us -> 7.12 us
  local copies, waits for them, and re-layouts: 4.9 us -> 0 us
  other arithmetic: 3.98 us -> 0 us
  Pallas kernels: 1.48 us -> 5.03 us
  matrix products: 0.43 us -> 0 us
    all_to_all x1, waiting for transfers between devices: 0.01 us -> 3.85 us  [local(): lax.all_to_all(weighted_low, 'freq', split_axis=0, concat_axis=0, tiled=T...]
    pallas_call x4 -> x6, Pallas kernels: 1.48 us -> 5.03 us  [run(): pl.pallas_call(fetched if fetch else body, out_shape=[jax.ShapeDtypeStruc...]
    sub x4 -> x0, other arithmetic: 3.06 us -> none  [the longest x3 2.97 us: operate(): return coefficient[..., 0:1] * center - beside]
    ppermute x7, waiting for transfers between devices: 0.5 us -> 3.27 us  [swap(): lax.ppermute(own, axis, [(i, partner(i)) for i in range(lax.axis_size(axi...]
    mul x20 -> x0, local copies, waits for them, and re-layouts: 2.02 us -> none  [the longest x4 0.41 us: operate(): coefficient[..., 4:5] * padded[1:-1, 2:]]
    unnamed x6 -> x0, local copies, waits for them, and re-layouts: 1.68 us -> none
    all_to_all x1, starting transfers between devices: 3.28 us -> 4.45 us  [local(): lax.all_to_all(weighted_low, 'freq', split_axis=0, concat_axis=0, tiled=T...]
    ppermute x7, starting transfers between devices: 12.4 us -> 11.5 us  [swap(): lax.ppermute(own, axis, [(i, partner(i)) for i in range(lax.axis_size(axi...]
  transfers between devices with their start and end apart: 8 -> 8, of which waited for: 1 -> 3; matrix products, arithmetic and copies ran while one was open for 27% -> 0% of each run, Pallas kernels for 0% -> 9%
where the time goes in v6:
time: 29 us; the launch traced here: 28.7 us
  starting transfers between devices  15.9 us (55%)
  waiting for transfers between devices  7.12 us (25%)
  Pallas kernels  5.03 us (17%)
  between operations  0.67 us (2%)
    ppermute x7, starting transfers between devices, swap(): lax.ppermute(own, axis, [(i, partner(i)) for i in range(lax.axis_size(axi...  11.5 us
    pallas_call x6, Pallas kernels, run(): pl.pallas_call(fetched if fetch else body, out_shape=[jax.ShapeDtypeStruc...  5.03 us
    all_to_all x1, starting transfers between devices, local(): lax.all_to_all(weighted_low, 'freq', split_axis=0, concat_axis=0, tiled=T...  4.45 us
    all_to_all x1, waiting for transfers between devices, local(): lax.all_to_all(weighted_low, 'freq', split_axis=0, concat_axis=0, tiled=T...  3.85 us
    ppermute x7, waiting for transfers between devices, swap(): lax.ppermute(own, axis, [(i, partner(i)) for i in range(lax.axis_size(axi...  3.27 us
  transfers between devices with their start and end apart: 8, of which 3 were waited for; matrix products, arithmetic and copies ran while one was open for 0% of the time, Pallas kernels for 9%

profile of v6, /device:TPU:0, one launch (start us, length us, event | category | flops | bytes accessed | tf_op | source)
XLA Modules:
  0.0 28.7 jit_solution(9713411608276858733)
XLA Ops:
  0.6 1.4 %shard_map.86 = (f32[112,128]{1,0:T(8,128)S(1)}, bf16[4,64,128]{2,1,0:T(8,128)(2,1)S(1)}, f32[8,64,128]{2,1,0:T(8,128)S(1)}, f32[8,128]{1,0:T(8,128)S(1)}, f32[5,16]{1,0:T(8,128)S(1)}) custom-call(f32[1,4]{1,0:T(1,128)} %refs_0_.1, f32[4,2,128]{2,1,0:T(2,128)} %bitcast.9, bf16[8,64,64]{2,1,0:T(8,128)(2,1)} %bitcast.8, f32[8,64,128]{2,1,0:T(8,128)} %refs_3_.1, ...), custom_call_target="tpu_custom_call" | custom-call | tf_op jit(solution)/shard_map/pallas_call | solution.py:57
  2.0 0.5 %collective-permute-start = (f32[112,128]{1,0:T(8,128)S(1)}, f32[112,128]{1,0:T(8,128)S(1)}, u32[]{:S(2)}, u32[]{:S(2)}) collective-permute-start(f32[112,128]{1,0:T(8,128)S(1)} %get-tuple-element.19.mine_ref), channel_id=1, source_target_pairs={{0,1},{1,0},{2,3},{3,2},{4,5},{5,4},{6,7},{7,6},{8,9},{9,8},{10,11... | collective-permute-start | bytes 172040 | tf_op jit(solution)/shard_map/ppermute | solution.py:18
  2.5 2.6 %collective-permute-start.4 = (bf16[4,64,128]{2,1,0:T(8,128)(2,1)S(1)}, bf16[4,64,128]{2,1,0:T(8,128)(2,1)S(1)}, u32[]{:S(2)}, u32[]{:S(2)}) collective-permute-start(bf16[4,64,128]{2,1,0:T(8,128)(2,1)S(1)} %get-tuple-element.27.one_ref), channel_id=1, source_target_pairs={{0,8},{8,0},{16,24},{24,16},{1,9},{9,1},{17,25},{25,17},{2,10},{10... | collective-permute-start | bytes 196616 | tf_op jit(solution)/shard_map/ppermute | solution.py:18
  5.2 0.0 collective-permute-done.got_ref
  5.2 0.1 shard_map.87
  5.3 1.6 %collective-permute-start.1 = (bf16[320,128]{1,0:T(8,128)(2,1)S(1)}, bf16[320,128]{1,0:T(8,128)(2,1)S(1)}, u32[]{:S(2)}, u32[]{:S(2)}) collective-permute-start(bf16[320,128]{1,0:T(8,128)(2,1)S(1)} %get-tuple-element.23), channel_id=1, source_target_pairs={{0,2},{2,0},{4,6},{6,4},{1,3},{3,1},{5,7},{7,5},{8,10},{10,8},{12,... | collective-permute-start | bytes 245768 | tf_op jit(solution)/shard_map/ppermute | solution.py:18
  6.8 1.5 %collective-permute-start.2 = (bf16[320,128]{1,0:T(8,128)(2,1)S(1)}, bf16[320,128]{1,0:T(8,128)(2,1)S(1)}, u32[]{:S(2)}, u32[]{:S(2)}) collective-permute-start(bf16[320,128]{1,0:T(8,128)(2,1)S(1)} %get-tuple-element.24), channel_id=1, source_target_pairs={{0,6},{2,4},{4,2},{6,0},{1,7},{3,5},{5,3},{7,1},{8,14},{10,12},{12... | collective-permute-start | bytes 245768 | tf_op jit(solution)/shard_map/ppermute | solution.py:18
  8.3 1.5 %collective-permute-start.3 = (f32[72,128]{1,0:T(8,128)S(1)}, f32[72,128]{1,0:T(8,128)S(1)}, u32[]{:S(2)}, u32[]{:S(2)}) collective-permute-start(f32[72,128]{1,0:T(8,128)S(1)} %get-tuple-element.26.mine_ref), channel_id=1, source_target_pairs={{0,2},{2,0},{4,6},{6,4},{1,3},{3,1},{5,7},{7,5},{8,10},{10,8},{12,... | collective-permute-start | bytes 110600 | tf_op jit(solution)/shard_map/ppermute | solution.py:18
  9.8 0.0 collective-permute-done.4.two_ref
  9.8 3.0 %collective-permute-done.3.got_ref = f32[72,128]{1,0:T(8,128)S(1)} collective-permute-done((f32[72,128]{1,0:T(8,128)S(1)}, f32[72,128]{1,0:T(8,128)S(1)}, u32[]{:S(2)}, u32[]{:S(2)}) %collective-permute-start.3) | collective-permute-done | bytes 36896 | tf_op jit(solution)/shard_map/ppermute | solution.py:18
  12.8 1.2 %collective-permute-start.5 = (f32[72,128]{1,0:T(8,128)S(1)}, f32[72,128]{1,0:T(8,128)S(1)}, u32[]{:S(2)}, u32[]{:S(2)}) collective-permute-start(f32[72,128]{1,0:T(8,128)S(1)} %get-tuple-element.28.mine_ref), channel_id=1, source_target_pairs={{0,4},{2,6},{4,0},{6,2},{1,5},{3,7},{5,1},{7,3},{8,12},{10,14},{12... | collective-permute-start | bytes 110600 | tf_op jit(solution)/shard_map/ppermute | solution.py:18
  14.0 2.6 %collective-permute-start.6 = (bf16[8,64,128]{2,1,0:T(8,128)(2,1)S(1)}, bf16[8,64,128]{2,1,0:T(8,128)(2,1)S(1)}, u32[]{:S(2)}, u32[]{:S(2)}) collective-permute-start(bf16[8,64,128]{2,1,0:T(8,128)(2,1)S(1)} %get-tuple-element.31.pair_ref), channel_id=1, source_target_pairs={{0,16},{8,24},{16,0},{24,8},{1,17},{9,25},{17,1},{25,9},{2,18},{10... | collective-permute-start | bytes 393224 | tf_op jit(solution)/shard_map/ppermute | solution.py:18
  16.6 0.3 collective-permute-done.5.got_ref
  16.8 0.7 %shard_map.89 = (bf16[4,64,128]{2,1,0:T(8,128)(2,1)}, f32[2,32,128]{2,1,0:T(8,128)S(1)}) custom-call(f32[72,128]{1,0:T(8,128)S(1)} %get-tuple-element.28.mine_ref, f32[72,128]{1,0:T(8,128)S(1)} %collective-permute-done.5.got_ref), custom_call_target="tpu_custom_call" | custom-call | tf_op jit(solution)/shard_map/pallas_call | solution.py:57
  17.6 4.4 %all-to-all-start = ((bf16[4,64,128]{2,1,0:T(8,128)(2,1)}), bf16[4,64,128]{2,1,0:T(8,128)(2,1)S(1)}, u32[]{:S(2)}, u32[]{:S(2)}) async-start(bf16[4,64,128]{2,1,0:T(8,128)(2,1)} %get-tuple-element.32), calls=%async_computation | async-start | bytes 131072 | tf_op jit(solution)/shard_map/all_to_all | solution.py:392
  22.0 0.0 collective-permute-done.1.near_ref
  22.0 0.0 collective-permute-done.2.far_ref
  22.0 1.9 %shard_map.90 = (f32[8,64,128]{2,1,0:T(8,128)S(1)}, f32[4,2,128]{2,1,0:T(2,128)}) custom-call(f32[8,64,128]{2,1,0:T(8,128)S(1)} %get-tuple-element.18.field_ref, f32[8,8,128]{2,1,0:T(8,128)S(1)} %get-tuple-element.21.side_ref, f32[8,128]{1,0:T(8,128)S(1)} %get-tuple-element.22.wide_ref, bf16[320,128]{1,0:T(8,128)(2,1)S(1)} %collective-permute-done.1.near_ref, ...), custom_call_target="tpu_custom_call" | custom-call | flops 1073741824 | tf_op jit(solution)/shard_map/pallas_call | solution.py:57
  23.9 0.0 collective-permute-done.6.far_ref
  23.9 3.9 %all-to-all-done.low_ref = bf16[4,64,128]{2,1,0:T(8,128)(2,1)S(1)} async-done(((bf16[4,64,128]{2,1,0:T(8,128)(2,1)}), bf16[4,64,128]{2,1,0:T(8,128)(2,1)S(1)}, u32[]{:S(2)}, u32[]{:S(2)}) %all-to-all-start) | async-done | bytes 65568 | tf_op jit(solution)/shard_map/all_to_all | solution.py:392
  27.8 1.0 %shard_map.91 = f32[8,64,128]{2,1,0:T(8,128)} custom-call(bf16[8,64,128]{2,1,0:T(8,128)(2,1)S(1)} %get-tuple-element.31.pair_ref, bf16[8,64,128]{2,1,0:T(8,128)(2,1)S(1)} %collective-permute-done.6.far_ref, bf16[4,64,128]{2,1,0:T(8,128)(2,1)S(1)} %all-to-all-done.low_ref, f32[8,64,128]{2,1,0:T(8,128)S(1)} %get-tuple-element.33.prior_ref), custom_call_target="tpu_custom_call" | custom-call | tf_op jit(solution)/shard_map/pallas_call | solution.py:57
  (1 shorter events, 0.0 us)
Async XLA Ops:
  2.0 3.2 %collective-permute-start = (f32[112,128]{1,0:T(8,128)S(1)}, f32[112,128]{1,0:T(8,128)S(1)}, u32[]{:S(2)}, u32[]{:S(2)}) collective-permute-start(f32[112,128]{1,0:T(8,128)S(1)} %get-tuple-element.19.mine_ref), channel_id=1, source_target_pairs={{0,1},{1,0},{2,3},{3,2},{4,5},{5,4},{6,7},{7,6},{8,9},{9,8},{10,11... | collective-permute-start | bytes 172040 | tf_op jit(solution)/shard_map/ppermute | solution.py:18
  2.5 7.3 %collective-permute-start.4 = (bf16[4,64,128]{2,1,0:T(8,128)(2,1)S(1)}, bf16[4,64,128]{2,1,0:T(8,128)(2,1)S(1)}, u32[]{:S(2)}, u32[]{:S(2)}) collective-permute-start(bf16[4,64,128]{2,1,0:T(8,128)(2,1)S(1)} %get-tuple-element.27.one_ref), channel_id=1, source_target_pairs={{0,8},{8,0},{16,24},{24,16},{1,9},{9,1},{17,25},{25,17},{2,10},{10... | collective-permute-start | bytes 196616 | tf_op jit(solution)/shard_map/ppermute | solution.py:18
  5.3 16.8 %collective-permute-start.1 = (bf16[320,128]{1,0:T(8,128)(2,1)S(1)}, bf16[320,128]{1,0:T(8,128)(2,1)S(1)}, u32[]{:S(2)}, u32[]{:S(2)}) collective-permute-start(bf16[320,128]{1,0:T(8,128)(2,1)S(1)} %get-tuple-element.23), channel_id=1, source_target_pairs={{0,2},{2,0},{4,6},{6,4},{1,3},{3,1},{5,7},{7,5},{8,10},{10,8},{12,... | collective-permute-start | bytes 245768 | tf_op jit(solution)/shard_map/ppermute | solution.py:18
  6.8 15.2 %collective-permute-start.2 = (bf16[320,128]{1,0:T(8,128)(2,1)S(1)}, bf16[320,128]{1,0:T(8,128)(2,1)S(1)}, u32[]{:S(2)}, u32[]{:S(2)}) collective-permute-start(bf16[320,128]{1,0:T(8,128)(2,1)S(1)} %get-tuple-element.24), channel_id=1, source_target_pairs={{0,6},{2,4},{4,2},{6,0},{1,7},{3,5},{5,3},{7,1},{8,14},{10,12},{12... | collective-permute-start | bytes 245768 | tf_op jit(solution)/shard_map/ppermute | solution.py:18
  8.3 4.5 %collective-permute-start.3 = (f32[72,128]{1,0:T(8,128)S(1)}, f32[72,128]{1,0:T(8,128)S(1)}, u32[]{:S(2)}, u32[]{:S(2)}) collective-permute-start(f32[72,128]{1,0:T(8,128)S(1)} %get-tuple-element.26.mine_ref), channel_id=1, source_target_pairs={{0,2},{2,0},{4,6},{6,4},{1,3},{3,1},{5,7},{7,5},{8,10},{10,8},{12,... | collective-permute-start | bytes 110600 | tf_op jit(solution)/shard_map/ppermute | solution.py:18
  12.8 4.0 %collective-permute-start.5 = (f32[72,128]{1,0:T(8,128)S(1)}, f32[72,128]{1,0:T(8,128)S(1)}, u32[]{:S(2)}, u32[]{:S(2)}) collective-permute-start(f32[72,128]{1,0:T(8,128)S(1)} %get-tuple-element.28.mine_ref), channel_id=1, source_target_pairs={{0,4},{2,6},{4,0},{6,2},{1,5},{3,7},{5,1},{7,3},{8,12},{10,14},{12... | collective-permute-start | bytes 110600 | tf_op jit(solution)/shard_map/ppermute | solution.py:18
  14.0 9.9 %collective-permute-start.6 = (bf16[8,64,128]{2,1,0:T(8,128)(2,1)S(1)}, bf16[8,64,128]{2,1,0:T(8,128)(2,1)S(1)}, u32[]{:S(2)}, u32[]{:S(2)}) collective-permute-start(bf16[8,64,128]{2,1,0:T(8,128)(2,1)S(1)} %get-tuple-element.31.pair_ref), channel_id=1, source_target_pairs={{0,16},{8,24},{16,0},{24,8},{1,17},{9,25},{17,1},{25,9},{2,18},{10... | collective-permute-start | bytes 393224 | tf_op jit(solution)/shard_map/ppermute | solution.py:18
  17.6 10.2 %all-to-all-start = ((bf16[4,64,128]{2,1,0:T(8,128)(2,1)}), bf16[4,64,128]{2,1,0:T(8,128)(2,1)S(1)}, u32[]{:S(2)}, u32[]{:S(2)}) async-start(bf16[4,64,128]{2,1,0:T(8,128)(2,1)} %get-tuple-element.32), calls=%async_computation | async-start | bytes 131072 | tf_op jit(solution)/shard_map/all_to_all | solution.py:392

commit v7 on v6

--- a/solution.py
+++ b/solution.py
@@ -12,6 +12,7 @@
 TILE = 8
 VMEM_BYTES = 40 << 20
 PRIOR_FLOPS = 1 << 30
+EDGE_FLOPS = 1 << 30
 
 
 def swap(own, axis, partner):
@@ -147,14 +148,22 @@
     return before, after
 
 
-def add_and_edge(
-    mine_ref, got_ref, field_ref, marks_ref, *refs
-):
-    *far_ref, out_ref, side_ref, wide_ref, near_ref, far_rows_ref = refs
+def add(mine_ref, got_ref, out_ref):
     size = out_ref.shape[0]
+    out_ref[...] = mine_ref[:size] + got_ref[:size]
+
+
+def add_and_join(mine_ref, got_ref, one_ref, two_ref, out_ref, joined_ref):
+    out_ref[...] = mine_ref[...] + got_ref[...]
+    half = one_ref.shape[0]
+    joined_ref[:half] = one_ref[...]
+    joined_ref[half:] = two_ref[...]
+
+
+def edge(after_ref, got_ref, field_ref, marks_ref, *refs):
+    *far_ref, side_ref, wide_ref, near_ref = refs
     rows, cols, real = field_ref.shape
-    out_ref[...] = mine_ref[:size] + got_ref[:size]
-    one = got_ref[size:]
+    one = got_ref[got_ref.shape[0] - rows * (SWEEPS + 1) :]
     before, after = sides_of(one, far_ref[0][...] if far_ref else one, "py")
     fields = rows * SWEEPS
     wide_ref[...] = (
@@ -165,28 +174,28 @@
     for x in range(rows):
         pick = slice(x * SWEEPS, (x + 1) * SWEEPS)
         side_ref[x] = jnp.concatenate([after[pick], before[pick]], axis=0)
-    even = lax.axis_index("px") % 2 == 0
+    lay_rows(near_ref, lax.axis_index("px") % 2 == 0, field_ref, side_ref, wide_ref)
+
+
+def lay_rows(ref, chosen, field_ref, side_ref, wide_ref):
+    rows, _, real = field_ref.shape
     top = lax.broadcasted_iota(jnp.int32, (TILE, real), 0) == 0
-    step = near_ref.shape[0] // SWEEPS
-    for ref, chosen in ((near_ref, even), (far_rows_ref, jnp.logical_not(even))):
-        for k in range(SWEEPS):
-            last = rows - SWEEPS + k
-            marks = jnp.where(chosen, wide_ref[last : last + 1], wide_ref[k : k + 1])
-            ref[k * step : (k + 1) * step] = jnp.concatenate(
-                [
-                    jnp.where(chosen, field_ref[last], field_ref[k]),
-                    jnp.where(chosen, side_ref[last], side_ref[k]),
-                    jnp.where(top, marks, 0.0),
-                ],
-                axis=0,
-            ).astype(jnp.bfloat16)
-
-
-def add_and_join(mine_ref, got_ref, one_ref, two_ref, out_ref, joined_ref):
-    out_ref[...] = mine_ref[...] + got_ref[...]
-    half = one_ref.shape[0]
-    joined_ref[:half] = one_ref[...]
-    joined_ref[half:] = two_ref[...]
+    step = ref.shape[0] // SWEEPS
+    for k in range(SWEEPS):
+        last = rows - SWEEPS + k
+        marks = jnp.where(chosen, wide_ref[last : last + 1], wide_ref[k : k + 1])
+        ref[k * step : (k + 1) * step] = jnp.concatenate(
+            [
+                jnp.where(chosen, field_ref[last], field_ref[k]),
+                jnp.where(chosen, side_ref[last], side_ref[k]),
+                jnp.where(top, marks, 0.0),
+            ],
+            axis=0,
+        ).astype(jnp.bfloat16)
+
+
+def far_edge(after_ref, field_ref, side_ref, wide_ref, out_ref):
+    lay_rows(out_ref, lax.axis_index("px") % 2 != 0, field_ref, side_ref, wide_ref)
 
 
 def weigh(mine_ref, got_ref, low_ref, weighted_ref):
@@ -207,10 +216,9 @@
         for c in range(comps):
             weighted = misfit[c] * factor
             weighted_ref[c, k * chunk : (k + 1) * chunk] = weighted
-            for f in range(low_ref.shape[0]):
-                low_ref[f, c * sensors + k * chunk : c * sensors + (k + 1) * chunk] = (
-                    weighted.astype(jnp.bfloat16)
-                )
+            low_ref[c * sensors + k * chunk : c * sensors + (k + 1) * chunk] = weighted.astype(
+                jnp.bfloat16
+            )
 
 
 def prior(
@@ -299,12 +307,11 @@
     out.wait()
 
 
-def finish(pair_ref, far_ref, low_ref, prior_ref, out, held_ref, sems):
+def finish(pair_ref, far_ref, low0_ref, low1_ref, low2_ref, low3_ref, prior_ref, out, held_ref, sems):
     rows, cols, real = held_ref.shape
     beside = pair_ref.shape[0] // 2
     side = rows // beside
-    me = lax.axis_index("freq")
-    low = jnp.concatenate([low_ref[me ^ k] for k in range(low_ref.shape[0])], axis=0)
+    low = jnp.concatenate([low0_ref[...], low1_ref[...], low2_ref[...], low3_ref[...]], axis=0)
     copies = []
     for x in range(beside):
         kernel = jnp.concatenate(
@@ -355,41 +362,37 @@
     got = swap(payload, "py", near)
     kernel_next = swap(kernel_own, "freq", near)
     two = [swap(rim, "py", far("py")) for rim in far_rim]
+    summed = ((points + TILE, real), jnp.float32)
+    (total,) = call(add, summed)(payload, got)
+    for bit in bits("py")[1:]:
+        (total,) = call(add, summed)(total, swap(total, "py", lambda i: i ^ bit))
     step = cols + 2 * SWEEPS + TILE
-    total, side_rim, wide_marks, near_rows, far_rows = call(
-        add_and_edge,
-        ((points + TILE, real), jnp.float32),
+    side_rim, wide_marks, near_rows = call(
+        edge,
         ((rows, 2 * SWEEPS, real), jnp.float32),
         ((rows, LANES), jnp.float32),
         ((SWEEPS * step, real), jnp.bfloat16),
-        ((SWEEPS * step, real), jnp.bfloat16),
-    )(payload, got, model_field, marks, *two)
-    for bit in bits("py")[1:]:
-        total = total + swap(total, "py", lambda i: i ^ bit)
+        flops=EDGE_FLOPS,
+    )(total, got, model_field, marks, *two)
     near_rows = swap(near_rows, "px", near)
+    *steps, last = bits("px")
+    for bit in steps[:-1]:
+        (total,) = call(add, summed)(total, swap(total, "px", lambda i: i ^ bit))
+    total, kernel_pair = call(
+        add_and_join, summed, ((2 * beside, points, side * cols), jnp.bfloat16)
+    )(total, swap(total, "px", lambda i: i ^ steps[-1]), kernel_own, kernel_next)
+    kernel_far = swap(kernel_pair, "freq", lambda i: i ^ 2)
+    (far_rows,) = call(far_edge, ((SWEEPS * step, real), jnp.bfloat16), flops=EDGE_FLOPS)(
+        total, model_field, side_rim, wide_marks
+    )
     far_rows = swap(far_rows, "px", far("px")) if wide_px else near_rows
-
-    steps = bits("px")
-    for bit in steps[:-1]:
-        got = swap(total, "px", lambda i: i ^ bit)
-        if bit == steps[-2]:
-            total, kernel_pair = call(
-                add_and_join,
-                ((points + TILE, real), jnp.float32),
-                ((2 * beside, points, side * cols), jnp.bfloat16),
-            )(total, got, kernel_own, kernel_next)
-        else:
-            total = total + got
-    kernel_far = swap(kernel_pair, "freq", lambda i: i ^ 2)
-    got = swap(total, "px", lambda i: i ^ steps[-1])
-    freqs = lax.axis_size("freq")
-    assert freqs == 4
+    assert lax.axis_size("freq") == 4
     weighted_low, weighted = call(
         weigh,
-        ((freqs, points, real), jnp.bfloat16),
+        ((points, real), jnp.bfloat16),
         ((comps, sensors, real), jnp.float32),
-    )(total, got)
-    low_all = lax.all_to_all(weighted_low, "freq", split_axis=0, concat_axis=0, tiled=True)
+    )(total, swap(total, "px", lambda i: i ^ last))
+    lows = [swap(weighted_low, "freq", lambda i: i ^ k) for k in (3, 2, 1)][::-1]
     wide = cols + 2 * SWEEPS
     prior_term, weighted_own = call(
         prior,
@@ -412,7 +415,7 @@
             pltpu.VMEM(model_field.shape, jnp.float32),
             pltpu.SemaphoreType.DMA((rows,)),
         ),
-    )(kernel_pair, kernel_far, low_all, prior_term)
+    )(kernel_pair, kernel_far, weighted_low, *lows, prior_term)
     return weighted_own[None], gradient
 
 

time: 29 us -> 26.6 us (0.917)
  waiting for transfers between devices: 7.12 us -> 5.64 us
  Pallas kernels: 5.03 us -> 4.43 us
    all_to_all x1 -> x0, starting transfers between devices: 4.45 us -> none  [local(): lax.all_to_all(weighted_low, 'freq', split_axis=0, concat_axis=0, tiled=T...]
    ppermute x7 -> x10, starting transfers between devices: 11.5 us -> 15.7 us  [swap(): lax.ppermute(own, axis, [(i, partner(i)) for i in range(lax.axis_size(axi...]
    all_to_all x1 -> x0, waiting for transfers between devices: 3.85 us -> none  [local(): lax.all_to_all(weighted_low, 'freq', split_axis=0, concat_axis=0, tiled=T...]
    ppermute x7 -> x10, waiting for transfers between devices: 3.27 us -> 5.64 us  [swap(): lax.ppermute(own, axis, [(i, partner(i)) for i in range(lax.axis_size(axi...]
    pallas_call x6 -> x8, Pallas kernels: 5.03 us -> 4.43 us  [run(): pl.pallas_call(fetched if fetch else body, out_shape=[jax.ShapeDtypeStruc...]
  transfers between devices with their start and end apart: 8 -> 10, of which waited for: 3 -> 4; matrix products, arithmetic and copies ran while one was open for 0% -> 0% of each run, Pallas kernels for 9% -> 8%
where the time goes in v7:
time: 26.6 us; the launch traced here: 26.5 us
  starting transfers between devices  15.7 us (59%)
  waiting for transfers between devices  5.64 us (21%)
  Pallas kernels  4.43 us (17%)
  between operations  0.69 us (3%)
    ppermute x10, starting transfers between devices, swap(): lax.ppermute(own, axis, [(i, partner(i)) for i in range(lax.axis_size(axi...  15.7 us
    ppermute x10, waiting for transfers between devices, swap(): lax.ppermute(own, axis, [(i, partner(i)) for i in range(lax.axis_size(axi...  5.64 us
    pallas_call x8, Pallas kernels, run(): pl.pallas_call(fetched if fetch else body, out_shape=[jax.ShapeDtypeStruc...  4.43 us
  transfers between devices with their start and end apart: 10, of which 4 were waited for; matrix products, arithmetic and copies ran while one was open for 0% of the time, Pallas kernels for 8%

profile of v7, /device:TPU:0, one launch (start us, length us, event | category | flops | bytes accessed | tf_op | source)
XLA Modules:
  0.0 26.5 jit_solution(3250346081948636198)
XLA Ops:
  0.6 1.4 %shard_map.86 = (f32[112,128]{1,0:T(8,128)S(1)}, bf16[4,64,128]{2,1,0:T(8,128)(2,1)S(1)}, f32[8,64,128]{2,1,0:T(8,128)S(1)}, f32[8,128]{1,0:T(8,128)S(1)}, f32[5,16]{1,0:T(8,128)S(1)}) custom-call(f32[1,4]{1,0:T(1,128)} %refs_0_.1, f32[4,2,128]{2,1,0:T(2,128)} %bitcast.9, bf16[8,64,64]{2,1,0:T(8,128)(2,1)} %bitcast.8, f32[8,64,128]{2,1,0:T(8,128)} %refs_3_.1, ...), custom_call_target="tpu_custom_call" | custom-call | tf_op jit(solution)/shard_map/pallas_call | solution.py:58
  2.0 0.5 %collective-permute-start = (f32[112,128]{1,0:T(8,128)S(1)}, f32[112,128]{1,0:T(8,128)S(1)}, u32[]{:S(2)}, u32[]{:S(2)}) collective-permute-start(f32[112,128]{1,0:T(8,128)S(1)} %get-tuple-element.17.mine_ref), channel_id=1, source_target_pairs={{0,1},{1,0},{2,3},{3,2},{4,5},{5,4},{6,7},{7,6},{8,9},{9,8},{10,11... | collective-permute-start | bytes 172040 | tf_op jit(solution)/shard_map/ppermute | solution.py:19
  2.5 2.6 %collective-permute-start.3 = (bf16[4,64,128]{2,1,0:T(8,128)(2,1)S(1)}, bf16[4,64,128]{2,1,0:T(8,128)(2,1)S(1)}, u32[]{:S(2)}, u32[]{:S(2)}) collective-permute-start(bf16[4,64,128]{2,1,0:T(8,128)(2,1)S(1)} %get-tuple-element.22.one_ref), channel_id=1, source_target_pairs={{0,8},{8,0},{16,24},{24,16},{1,9},{9,1},{17,25},{25,17},{2,10},{10... | collective-permute-start | bytes 196616 | tf_op jit(solution)/shard_map/ppermute | solution.py:19
  5.2 0.0 collective-permute-done.got_ref
  5.2 1.6 %collective-permute-start.2 = (f32[72,128]{1,0:T(8,128)S(1)}, f32[72,128]{1,0:T(8,128)S(1)}, u32[]{:S(2)}, u32[]{:S(2)}) collective-permute-start(f32[72,128]{1,0:T(8,128)S(1)} %shard_map.87.after_ref.mine_ref), channel_id=1, source_target_pairs={{0,2},{2,0},{4,6},{6,4},{1,3},{3,1},{5,7},{7,5},{8,10},{10,8},{12,... | collective-permute-start | bytes 110600 | tf_op jit(solution)/shard_map/ppermute | solution.py:19
  6.7 0.1 shard_map.88
  6.8 0.6 %collective-permute-start.1 = (bf16[320,128]{1,0:T(8,128)(2,1)S(1)}, bf16[320,128]{1,0:T(8,128)(2,1)S(1)}, u32[]{:S(2)}, u32[]{:S(2)}) collective-permute-start(bf16[320,128]{1,0:T(8,128)(2,1)S(1)} %get-tuple-element.21), channel_id=1, source_target_pairs={{0,2},{2,0},{4,6},{6,4},{1,3},{3,1},{5,7},{7,5},{8,10},{10,8},{12,... | collective-permute-start | bytes 245768 | tf_op jit(solution)/shard_map/ppermute | solution.py:19
  7.4 0.5 %collective-permute-done.3.two_ref = bf16[4,64,128]{2,1,0:T(8,128)(2,1)S(1)} collective-permute-done((bf16[4,64,128]{2,1,0:T(8,128)(2,1)S(1)}, bf16[4,64,128]{2,1,0:T(8,128)(2,1)S(1)}, u32[]{:S(2)}, u32[]{:S(2)}) %collective-permute-start.3) | collective-permute-done | bytes 65568 | tf_op jit(solution)/shard_map/ppermute | solution.py:19
  7.9 1.3 %collective-permute-done.2.got_ref = f32[72,128]{1,0:T(8,128)S(1)} collective-permute-done((f32[72,128]{1,0:T(8,128)S(1)}, f32[72,128]{1,0:T(8,128)S(1)}, u32[]{:S(2)}, u32[]{:S(2)}) %collective-permute-start.2) | collective-permute-done | bytes 36896 | tf_op jit(solution)/shard_map/ppermute | solution.py:19
  9.3 2.9 %collective-permute-start.4 = (bf16[320,128]{1,0:T(8,128)(2,1)S(1)}, bf16[320,128]{1,0:T(8,128)(2,1)S(1)}, u32[]{:S(2)}, u32[]{:S(2)}) collective-permute-start(bf16[320,128]{1,0:T(8,128)(2,1)S(1)} %shard_map.90), channel_id=1, source_target_pairs={{0,6},{2,4},{4,2},{6,0},{1,7},{3,5},{5,3},{7,1},{8,14},{10,12},{12... | collective-permute-start | bytes 245768 | tf_op jit(solution)/shard_map/ppermute | solution.py:19
  12.1 0.5 %collective-permute-start.5 = (f32[72,128]{1,0:T(8,128)S(1)}, f32[72,128]{1,0:T(8,128)S(1)}, u32[]{:S(2)}, u32[]{:S(2)}) collective-permute-start(f32[72,128]{1,0:T(8,128)S(1)} %get-tuple-element.23.after_ref.mine_ref), channel_id=1, source_target_pairs={{0,4},{2,6},{4,0},{6,2},{1,5},{3,7},{5,1},{7,3},{8,12},{10,14},{12... | collective-permute-start | bytes 110600 | tf_op jit(solution)/shard_map/ppermute | solution.py:19
  12.6 2.6 %collective-permute-start.6 = (bf16[8,64,128]{2,1,0:T(8,128)(2,1)S(1)}, bf16[8,64,128]{2,1,0:T(8,128)(2,1)S(1)}, u32[]{:S(2)}, u32[]{:S(2)}) collective-permute-start(bf16[8,64,128]{2,1,0:T(8,128)(2,1)S(1)} %get-tuple-element.27.pair_ref), channel_id=1, source_target_pairs={{0,16},{8,24},{16,0},{24,8},{1,17},{9,25},{17,1},{25,9},{2,18},{10... | collective-permute-start | bytes 393224 | tf_op jit(solution)/shard_map/ppermute | solution.py:19
  15.2 0.9 %collective-permute-done.5.got_ref = f32[72,128]{1,0:T(8,128)S(1)} collective-permute-done((f32[72,128]{1,0:T(8,128)S(1)}, f32[72,128]{1,0:T(8,128)S(1)}, u32[]{:S(2)}, u32[]{:S(2)}) %collective-permute-start.5) | collective-permute-done | bytes 36896 | tf_op jit(solution)/shard_map/ppermute | solution.py:19
  16.1 0.1 shard_map.91
  16.2 1.2 %collective-permute-start.7 = (bf16[64,128]{1,0:T(8,128)(2,1)S(1)}, bf16[64,128]{1,0:T(8,128)(2,1)S(1)}, u32[]{:S(2)}, u32[]{:S(2)}) collective-permute-start(bf16[64,128]{1,0:T(8,128)(2,1)S(1)} %get-tuple-element.28.low0_ref), channel_id=1, source_target_pairs={{0,8},{8,0},{16,24},{24,16},{1,9},{9,1},{17,25},{25,17},{2,10},{10... | collective-permute-start | bytes 49160 | tf_op jit(solution)/shard_map/ppermute | solution.py:19
  17.4 2.6 %collective-permute-start.8 = (bf16[64,128]{1,0:T(8,128)(2,1)S(1)}, bf16[64,128]{1,0:T(8,128)(2,1)S(1)}, u32[]{:S(2)}, u32[]{:S(2)}) collective-permute-start(bf16[64,128]{1,0:T(8,128)(2,1)S(1)} %get-tuple-element.28.low0_ref), channel_id=1, source_target_pairs={{0,16},{8,24},{16,0},{24,8},{1,17},{9,25},{17,1},{25,9},{2,18},{10... | collective-permute-start | bytes 49160 | tf_op jit(solution)/shard_map/ppermute | solution.py:19
  19.9 0.0 collective-permute-done.1.near_ref
  20.0 0.7 %collective-permute-start.9 = (bf16[64,128]{1,0:T(8,128)(2,1)S(1)}, bf16[64,128]{1,0:T(8,128)(2,1)S(1)}, u32[]{:S(2)}, u32[]{:S(2)}) collective-permute-start(bf16[64,128]{1,0:T(8,128)(2,1)S(1)} %get-tuple-element.28.low0_ref), channel_id=1, source_target_pairs={{0,24},{8,16},{16,8},{24,0},{1,25},{9,17},{17,9},{25,1},{2,26},{10... | collective-permute-start | bytes 49160 | tf_op jit(solution)/shard_map/ppermute | solution.py:19
  20.7 0.0 collective-permute-done.4.far_ref
  20.7 1.9 %shard_map.92 = (f32[8,64,128]{2,1,0:T(8,128)S(1)}, f32[4,2,128]{2,1,0:T(2,128)}) custom-call(f32[8,64,128]{2,1,0:T(8,128)S(1)} %get-tuple-element.16.field_ref, f32[8,8,128]{2,1,0:T(8,128)S(1)} %get-tuple-element.19.side_ref, f32[8,128]{1,0:T(8,128)S(1)} %get-tuple-element.20.wide_ref, bf16[320,128]{1,0:T(8,128)(2,1)S(1)} %collective-permute-done.1.near_ref, ...), custom_call_target="tpu_custom_call" | custom-call | flops 1073741824 | tf_op jit(solution)/shard_map/pallas_call | solution.py:58
  22.5 0.0 collective-permute-done.7.low1_ref
  22.5 0.0 collective-permute-done.8.low2_ref
  22.6 2.9 %collective-permute-done.9.low3_ref = bf16[64,128]{1,0:T(8,128)(2,1)S(1)} collective-permute-done((bf16[64,128]{1,0:T(8,128)(2,1)S(1)}, bf16[64,128]{1,0:T(8,128)(2,1)S(1)}, u32[]{:S(2)}, u32[]{:S(2)}) %collective-permute-start.9) | collective-permute-done | bytes 16416 | tf_op jit(solution)/shard_map/ppermute | solution.py:19
  25.5 0.0 collective-permute-done.6.far_ref
  25.5 1.0 %shard_map.93 = f32[8,64,128]{2,1,0:T(8,128)} custom-call(bf16[8,64,128]{2,1,0:T(8,128)(2,1)S(1)} %get-tuple-element.27.pair_ref, bf16[8,64,128]{2,1,0:T(8,128)(2,1)S(1)} %collective-permute-done.6.far_ref, bf16[64,128]{1,0:T(8,128)(2,1)S(1)} %get-tuple-element.28.low0_ref, bf16[64,128]{1,0:T(8,128)(2,1)S(1)} %collective-permute-done.7.low1_ref, ...), custom_call_target="tpu_custom_call" | custom-call | tf_op jit(solution)/shard_map/pallas_call | solution.py:58
  (3 shorter events, 0.1 us)
Async XLA Ops:
  2.0 3.2 %collective-permute-start = (f32[112,128]{1,0:T(8,128)S(1)}, f32[112,128]{1,0:T(8,128)S(1)}, u32[]{:S(2)}, u32[]{:S(2)}) collective-permute-start(f32[112,128]{1,0:T(8,128)S(1)} %get-tuple-element.17.mine_ref), channel_id=1, source_target_pairs={{0,1},{1,0},{2,3},{3,2},{4,5},{5,4},{6,7},{7,6},{8,9},{9,8},{10,11... | collective-permute-start | bytes 172040 | tf_op jit(solution)/shard_map/ppermute | solution.py:19
  2.5 5.3 %collective-permute-start.3 = (bf16[4,64,128]{2,1,0:T(8,128)(2,1)S(1)}, bf16[4,64,128]{2,1,0:T(8,128)(2,1)S(1)}, u32[]{:S(2)}, u32[]{:S(2)}) collective-permute-start(bf16[4,64,128]{2,1,0:T(8,128)(2,1)S(1)} %get-tuple-element.22.one_ref), channel_id=1, source_target_pairs={{0,8},{8,0},{16,24},{24,16},{1,9},{9,1},{17,25},{25,17},{2,10},{10... | collective-permute-start | bytes 196616 | tf_op jit(solution)/shard_map/ppermute | solution.py:19
  5.2 4.0 %collective-permute-start.2 = (f32[72,128]{1,0:T(8,128)S(1)}, f32[72,128]{1,0:T(8,128)S(1)}, u32[]{:S(2)}, u32[]{:S(2)}) collective-permute-start(f32[72,128]{1,0:T(8,128)S(1)} %shard_map.87.after_ref.mine_ref), channel_id=1, source_target_pairs={{0,2},{2,0},{4,6},{6,4},{1,3},{3,1},{5,7},{7,5},{8,10},{10,8},{12,... | collective-permute-start | bytes 110600 | tf_op jit(solution)/shard_map/ppermute | solution.py:19
  6.8 13.1 %collective-permute-start.1 = (bf16[320,128]{1,0:T(8,128)(2,1)S(1)}, bf16[320,128]{1,0:T(8,128)(2,1)S(1)}, u32[]{:S(2)}, u32[]{:S(2)}) collective-permute-start(bf16[320,128]{1,0:T(8,128)(2,1)S(1)} %get-tuple-element.21), channel_id=1, source_target_pairs={{0,2},{2,0},{4,6},{6,4},{1,3},{3,1},{5,7},{7,5},{8,10},{10,8},{12,... | collective-permute-start | bytes 245768 | tf_op jit(solution)/shard_map/ppermute | solution.py:19
  9.3 11.4 %collective-permute-start.4 = (bf16[320,128]{1,0:T(8,128)(2,1)S(1)}, bf16[320,128]{1,0:T(8,128)(2,1)S(1)}, u32[]{:S(2)}, u32[]{:S(2)}) collective-permute-start(bf16[320,128]{1,0:T(8,128)(2,1)S(1)} %shard_map.90), channel_id=1, source_target_pairs={{0,6},{2,4},{4,2},{6,0},{1,7},{3,5},{5,3},{7,1},{8,14},{10,12},{12... | collective-permute-start | bytes 245768 | tf_op jit(solution)/shard_map/ppermute | solution.py:19
  12.1 4.0 %collective-permute-start.5 = (f32[72,128]{1,0:T(8,128)S(1)}, f32[72,128]{1,0:T(8,128)S(1)}, u32[]{:S(2)}, u32[]{:S(2)}) collective-permute-start(f32[72,128]{1,0:T(8,128)S(1)} %get-tuple-element.23.after_ref.mine_ref), channel_id=1, source_target_pairs={{0,4},{2,6},{4,0},{6,2},{1,5},{3,7},{5,1},{7,3},{8,12},{10,14},{12... | collective-permute-start | bytes 110600 | tf_op jit(solution)/shard_map/ppermute | solution.py:19
  12.6 12.8 %collective-permute-start.6 = (bf16[8,64,128]{2,1,0:T(8,128)(2,1)S(1)}, bf16[8,64,128]{2,1,0:T(8,128)(2,1)S(1)}, u32[]{:S(2)}, u32[]{:S(2)}) collective-permute-start(bf16[8,64,128]{2,1,0:T(8,128)(2,1)S(1)} %get-tuple-element.27.pair_ref), channel_id=1, source_target_pairs={{0,16},{8,24},{16,0},{24,8},{1,17},{9,25},{17,1},{25,9},{2,18},{10... | collective-permute-start | bytes 393224 | tf_op jit(solution)/shard_map/ppermute | solution.py:19
  16.2 6.3 %collective-permute-start.7 = (bf16[64,128]{1,0:T(8,128)(2,1)S(1)}, bf16[64,128]{1,0:T(8,128)(2,1)S(1)}, u32[]{:S(2)}, u32[]{:S(2)}) collective-permute-start(bf16[64,128]{1,0:T(8,128)(2,1)S(1)} %get-tuple-element.28.low0_ref), channel_id=1, source_target_pairs={{0,8},{8,0},{16,24},{24,16},{1,9},{9,1},{17,25},{25,17},{2,10},{10... | collective-permute-start | bytes 49160 | tf_op jit(solution)/shard_map/ppermute | solution.py:19
  17.4 5.2 %collective-permute-start.8 = (bf16[64,128]{1,0:T(8,128)(2,1)S(1)}, bf16[64,128]{1,0:T(8,128)(2,1)S(1)}, u32[]{:S(2)}, u32[]{:S(2)}) collective-permute-start(bf16[64,128]{1,0:T(8,128)(2,1)S(1)} %get-tuple-element.28.low0_ref), channel_id=1, source_target_pairs={{0,16},{8,24},{16,0},{24,8},{1,17},{9,25},{17,1},{25,9},{2,18},{10... | collective-permute-start | bytes 49160 | tf_op jit(solution)/shard_map/ppermute | solution.py:19
  20.0 5.5 %collective-permute-start.9 = (bf16[64,128]{1,0:T(8,128)(2,1)S(1)}, bf16[64,128]{1,0:T(8,128)(2,1)S(1)}, u32[]{:S(2)}, u32[]{:S(2)}) collective-permute-start(bf16[64,128]{1,0:T(8,128)(2,1)S(1)} %get-tuple-element.28.low0_ref), channel_id=1, source_target_pairs={{0,24},{8,16},{16,8},{24,0},{1,25},{9,17},{17,9},{25,1},{2,26},{10... | collective-permute-start | bytes 49160 | tf_op jit(solution)/shard_map/ppermute | solution.py:19

commit v8 on v7

--- a/solution.py
+++ b/solution.py
@@ -13,6 +13,7 @@
 VMEM_BYTES = 40 << 20
 PRIOR_FLOPS = 1 << 30
 EDGE_FLOPS = 1 << 30
+ORDER_FLOPS = 1 << 32
 
 
 def swap(own, axis, partner):
@@ -161,7 +162,7 @@
 
 
 def edge(after_ref, got_ref, field_ref, marks_ref, *refs):
-    *far_ref, side_ref, wide_ref, near_ref = refs
+    *far_ref, side_ref, wide_ref, rows_ref = refs
     rows, cols, real = field_ref.shape
     one = got_ref[got_ref.shape[0] - rows * (SWEEPS + 1) :]
     before, after = sides_of(one, far_ref[0][...] if far_ref else one, "py")
@@ -174,17 +175,15 @@
     for x in range(rows):
         pick = slice(x * SWEEPS, (x + 1) * SWEEPS)
         side_ref[x] = jnp.concatenate([after[pick], before[pick]], axis=0)
-    lay_rows(near_ref, lax.axis_index("px") % 2 == 0, field_ref, side_ref, wide_ref)
-
-
-def lay_rows(ref, chosen, field_ref, side_ref, wide_ref):
-    rows, _, real = field_ref.shape
+    chosen = lax.axis_index("px") % 2 == 0
+    if lax.axis_size("px") > 2:
+        chosen = chosen == (lax.axis_index("freq") % 2 == 0)
     top = lax.broadcasted_iota(jnp.int32, (TILE, real), 0) == 0
-    step = ref.shape[0] // SWEEPS
+    step = rows_ref.shape[0] // SWEEPS
     for k in range(SWEEPS):
         last = rows - SWEEPS + k
         marks = jnp.where(chosen, wide_ref[last : last + 1], wide_ref[k : k + 1])
-        ref[k * step : (k + 1) * step] = jnp.concatenate(
+        rows_ref[k * step : (k + 1) * step] = jnp.concatenate(
             [
                 jnp.where(chosen, field_ref[last], field_ref[k]),
                 jnp.where(chosen, side_ref[last], side_ref[k]),
@@ -194,11 +193,7 @@
         ).astype(jnp.bfloat16)
 
 
-def far_edge(after_ref, field_ref, side_ref, wide_ref, out_ref):
-    lay_rows(out_ref, lax.axis_index("px") % 2 != 0, field_ref, side_ref, wide_ref)
-
-
-def weigh(mine_ref, got_ref, low_ref, weighted_ref):
+def weigh(mine_ref, got_ref, rows_ref, low_ref, both_ref, weighted_ref):
     comps, sensors, real = weighted_ref.shape
     points = comps * sensors
     total = mine_ref[...] + got_ref[...]
@@ -219,16 +214,19 @@
             low_ref[c * sensors + k * chunk : c * sensors + (k + 1) * chunk] = weighted.astype(
                 jnp.bfloat16
             )
+    both_ref[:points] = low_ref[...]
+    both_ref[points:] = rows_ref[...]
 
 
 def prior(
     field_ref,
     side_ref,
     wide_ref,
-    near_ref,
-    far_ref,
+    rows_ref,
+    both_ref,
     table_ref,
     weighted_ref,
+    after_ref,
     prior_ref,
     own_out,
     state_ref,
@@ -249,11 +247,13 @@
     out.start()
     rows, cols, _ = field_ref.shape
     wide = cols + 2 * SWEEPS
-    step = near_ref.shape[0] // SWEEPS
+    step = rows_ref.shape[0] // SWEEPS
+    mine = rows_ref[...].astype(jnp.float32)
+    other = both_ref[both_ref.shape[0] - rows_ref.shape[0] :].astype(jnp.float32)
+    even = lax.axis_index("freq") % 2 == 0
     before, after = sides_of(
-        near_ref[...].astype(jnp.float32), far_ref[...].astype(jnp.float32), "px"
-    )
-    marks = []
+        jnp.where(even, mine, other), jnp.where(even, other, mine), "px"
+    )
     for k in range(SWEEPS):
         state_ref[0, k] = before[k * step : k * step + wide]
         state_ref[0, SWEEPS + rows + k] = after[k * step : k * step + wide]
@@ -307,11 +307,14 @@
     out.wait()
 
 
-def finish(pair_ref, far_ref, low0_ref, low1_ref, low2_ref, low3_ref, prior_ref, out, held_ref, sems):
+def finish(pair_ref, far_ref, prior_ref, low0_ref, low1_ref, low3_ref, low2_ref, out, held_ref, sems):
     rows, cols, real = held_ref.shape
     beside = pair_ref.shape[0] // 2
     side = rows // beside
-    low = jnp.concatenate([low0_ref[...], low1_ref[...], low2_ref[...], low3_ref[...]], axis=0)
+    points = low0_ref.shape[0]
+    low = jnp.concatenate(
+        [low0_ref[...], low1_ref[:points], low2_ref[...], low3_ref[...]], axis=0
+    )
     copies = []
     for x in range(beside):
         kernel = jnp.concatenate(
@@ -367,32 +370,40 @@
     for bit in bits("py")[1:]:
         (total,) = call(add, summed)(total, swap(total, "py", lambda i: i ^ bit))
     step = cols + 2 * SWEEPS + TILE
-    side_rim, wide_marks, near_rows = call(
+    side_rim, wide_marks, rim_rows = call(
         edge,
         ((rows, 2 * SWEEPS, real), jnp.float32),
         ((rows, LANES), jnp.float32),
         ((SWEEPS * step, real), jnp.bfloat16),
         flops=EDGE_FLOPS,
     )(total, got, model_field, marks, *two)
-    near_rows = swap(near_rows, "px", near)
+    peers = lax.axis_size("px")
+    rim_rows = lax.ppermute(
+        rim_rows,
+        ("freq", "px"),
+        [
+            (f * peers + i, f * peers + (far("px")(i) if f % 2 and wide_px else near(i)))
+            for f in range(lax.axis_size("freq"))
+            for i in range(peers)
+        ],
+    )
     *steps, last = bits("px")
     for bit in steps[:-1]:
         (total,) = call(add, summed)(total, swap(total, "px", lambda i: i ^ bit))
     total, kernel_pair = call(
-        add_and_join, summed, ((2 * beside, points, side * cols), jnp.bfloat16)
+        add_and_join, summed, ((2 * beside, points, side * cols), jnp.bfloat16), flops=ORDER_FLOPS
     )(total, swap(total, "px", lambda i: i ^ steps[-1]), kernel_own, kernel_next)
     kernel_far = swap(kernel_pair, "freq", lambda i: i ^ 2)
-    (far_rows,) = call(far_edge, ((SWEEPS * step, real), jnp.bfloat16), flops=EDGE_FLOPS)(
-        total, model_field, side_rim, wide_marks
-    )
-    far_rows = swap(far_rows, "px", far("px")) if wide_px else near_rows
     assert lax.axis_size("freq") == 4
-    weighted_low, weighted = call(
+    weighted_low, weighted_both, weighted = call(
         weigh,
         ((points, real), jnp.bfloat16),
+        ((points + SWEEPS * step, real), jnp.bfloat16),
         ((comps, sensors, real), jnp.float32),
-    )(total, swap(total, "px", lambda i: i ^ last))
-    lows = [swap(weighted_low, "freq", lambda i: i ^ k) for k in (3, 2, 1)][::-1]
+    )(total, swap(total, "px", lambda i: i ^ last), rim_rows)
+    both_next = swap(weighted_both, "freq", near)
+    low_three = swap(weighted_low, "freq", lambda i: i ^ 3)
+    low_two = swap(weighted_low, "freq", lambda i: i ^ 2)
     wide = cols + 2 * SWEEPS
     prior_term, weighted_own = call(
         prior,
@@ -406,7 +417,7 @@
             pltpu.SemaphoreType.DMA(()),
         ),
         flops=PRIOR_FLOPS,
-    )(model_field, side_rim, wide_marks, near_rows, far_rows, table, weighted)
+    )(model_field, side_rim, wide_marks, rim_rows, both_next, table, weighted, kernel_far)
     (gradient,) = call(
         finish,
         (model_field.shape, jnp.float32),
@@ -415,7 +426,7 @@
             pltpu.VMEM(model_field.shape, jnp.float32),
             pltpu.SemaphoreType.DMA((rows,)),
         ),
-    )(kernel_pair, kernel_far, weighted_low, *lows, prior_term)
+    )(kernel_pair, kernel_far, prior_term, weighted_low, both_next, low_three, low_two)
     return weighted_own[None], gradient
 
 

time: 26.6 us -> 23.2 us (0.87)
  starting transfers between devices: 15.7 us -> 13.4 us
  waiting for transfers between devices: 5.64 us -> 4.54 us
    ppermute x10 -> x8, starting transfers between devices: 15.7 us -> 12.9 us  [swap(): lax.ppermute(own, axis, [(i, partner(i)) for i in range(lax.axis_size(axi...]
    ppermute x10 -> x8, waiting for transfers between devices: 5.64 us -> 4.54 us  [swap(): lax.ppermute(own, axis, [(i, partner(i)) for i in range(lax.axis_size(axi...]
    ppermute x0 -> x1, starting transfers between devices: none -> 0.56 us  [local(): lax.ppermute(rim_rows, ('freq', 'px'), [(f * peers + i, f * peers + (far(...]
    pallas_call x8 -> x7, Pallas kernels: 4.43 us -> 4.44 us  [run(): pl.pallas_call(fetched if fetch else body, out_shape=[jax.ShapeDtypeStruc...]
  transfers between devices with their start and end apart: 10 -> 9, of which waited for: 4 -> 5; matrix products, arithmetic and copies ran while one was open for 0% -> 0% of each run, Pallas kernels for 8% -> 9%
where the time goes in v8:
time: 23.2 us; the launch traced here: 23.1 us
  starting transfers between devices  13.4 us (58%)
  waiting for transfers between devices  4.54 us (20%)
  Pallas kernels  4.44 us (19%)
  between operations  0.67 us (3%)
    ppermute x8, starting transfers between devices, swap(): lax.ppermute(own, axis, [(i, partner(i)) for i in range(lax.axis_size(axi...  12.9 us
    ppermute x8, waiting for transfers between devices, swap(): lax.ppermute(own, axis, [(i, partner(i)) for i in range(lax.axis_size(axi...  4.54 us
    pallas_call x7, Pallas kernels, run(): pl.pallas_call(fetched if fetch else body, out_shape=[jax.ShapeDtypeStruc...  4.44 us
    ppermute x1, starting transfers between devices, local(): lax.ppermute(rim_rows, ('freq', 'px'), [(f * peers + i, f * peers + (far(...  0.56 us
  transfers between devices with their start and end apart: 9, of which 5 were waited for; matrix products, arithmetic and copies ran while one was open for 0% of the time, Pallas kernels for 9%

profile of v8, /device:TPU:0, one launch (start us, length us, event | category | flops | bytes accessed | tf_op | source)
XLA Modules:
  0.0 23.1 jit_solution(6797504605364818449)
XLA Ops:
  0.6 1.4 %shard_map.86 = (f32[112,128]{1,0:T(8,128)S(1)}, bf16[4,64,128]{2,1,0:T(8,128)(2,1)S(1)}, f32[8,64,128]{2,1,0:T(8,128)S(1)}, f32[8,128]{1,0:T(8,128)S(1)}, f32[5,16]{1,0:T(8,128)S(1)}) custom-call(f32[1,4]{1,0:T(1,128)} %refs_0_.1, f32[4,2,128]{2,1,0:T(2,128)} %bitcast.9, bf16[8,64,64]{2,1,0:T(8,128)(2,1)} %bitcast.8, f32[8,64,128]{2,1,0:T(8,128)} %refs_3_.1, ...), custom_call_target="tpu_custom_call" | custom-call | tf_op jit(solution)/shard_map/pallas_call | solution.py:59
  2.0 0.5 %collective-permute-start = (f32[112,128]{1,0:T(8,128)S(1)}, f32[112,128]{1,0:T(8,128)S(1)}, u32[]{:S(2)}, u32[]{:S(2)}) collective-permute-start(f32[112,128]{1,0:T(8,128)S(1)} %get-tuple-element.18.mine_ref), channel_id=1, source_target_pairs={{0,1},{1,0},{2,3},{3,2},{4,5},{5,4},{6,7},{7,6},{8,9},{9,8},{10,11... | collective-permute-start | bytes 172040 | tf_op jit(solution)/shard_map/ppermute | solution.py:20
  2.5 2.6 %collective-permute-start.3 = (bf16[4,64,128]{2,1,0:T(8,128)(2,1)S(1)}, bf16[4,64,128]{2,1,0:T(8,128)(2,1)S(1)}, u32[]{:S(2)}, u32[]{:S(2)}) collective-permute-start(bf16[4,64,128]{2,1,0:T(8,128)(2,1)S(1)} %get-tuple-element.23.one_ref), channel_id=1, source_target_pairs={{0,8},{8,0},{16,24},{24,16},{1,9},{9,1},{17,25},{25,17},{2,10},{10... | collective-permute-start | bytes 196616 | tf_op jit(solution)/shard_map/ppermute | solution.py:20
  5.2 0.0 collective-permute-done.got_ref
  5.2 1.6 %collective-permute-start.2 = (f32[72,128]{1,0:T(8,128)S(1)}, f32[72,128]{1,0:T(8,128)S(1)}, u32[]{:S(2)}, u32[]{:S(2)}) collective-permute-start(f32[72,128]{1,0:T(8,128)S(1)} %shard_map.87.after_ref.mine_ref), channel_id=1, source_target_pairs={{0,2},{2,0},{4,6},{6,4},{1,3},{3,1},{5,7},{7,5},{8,10},{10,8},{12,... | collective-permute-start | bytes 110600 | tf_op jit(solution)/shard_map/ppermute | solution.py:20
  6.7 0.1 shard_map.88
  6.8 0.6 %collective-permute-start.1 = (bf16[320,128]{1,0:T(8,128)(2,1)S(1)}, bf16[320,128]{1,0:T(8,128)(2,1)S(1)}, u32[]{:S(2)}, u32[]{:S(2)}) collective-permute-start(bf16[320,128]{1,0:T(8,128)(2,1)S(1)} %get-tuple-element.22), channel_id=1, source_target_pairs={{0,2},{2,0},{4,6},{6,4},{8,14},{10,12},{12,10},{14,8},{16,18},{18,... | collective-permute-start | bytes 245768 | tf_op jit(solution)/shard_map/ppermute | solution.py:381
  7.4 0.5 %collective-permute-done.3.two_ref = bf16[4,64,128]{2,1,0:T(8,128)(2,1)S(1)} collective-permute-done((bf16[4,64,128]{2,1,0:T(8,128)(2,1)S(1)}, bf16[4,64,128]{2,1,0:T(8,128)(2,1)S(1)}, u32[]{:S(2)}, u32[]{:S(2)}) %collective-permute-start.3) | collective-permute-done | bytes 65568 | tf_op jit(solution)/shard_map/ppermute | solution.py:20
  7.9 1.3 %collective-permute-done.2.got_ref = f32[72,128]{1,0:T(8,128)S(1)} collective-permute-done((f32[72,128]{1,0:T(8,128)S(1)}, f32[72,128]{1,0:T(8,128)S(1)}, u32[]{:S(2)}, u32[]{:S(2)}) %collective-permute-start.2) | collective-permute-done | bytes 36896 | tf_op jit(solution)/shard_map/ppermute | solution.py:20
  9.2 1.6 %collective-permute-start.4 = (f32[72,128]{1,0:T(8,128)S(1)}, f32[72,128]{1,0:T(8,128)S(1)}, u32[]{:S(2)}, u32[]{:S(2)}) collective-permute-start(f32[72,128]{1,0:T(8,128)S(1)} %get-tuple-element.24.mine_ref), channel_id=1, source_target_pairs={{0,4},{2,6},{4,0},{6,2},{1,5},{3,7},{5,1},{7,3},{8,12},{10,14},{12... | collective-permute-start | bytes 110600 | tf_op jit(solution)/shard_map/ppermute | solution.py:20
  10.8 2.6 %collective-permute-start.6 = (bf16[8,64,128]{2,1,0:T(8,128)(2,1)S(1)}, bf16[8,64,128]{2,1,0:T(8,128)(2,1)S(1)}, u32[]{:S(2)}, u32[]{:S(2)}) collective-permute-start(bf16[8,64,128]{2,1,0:T(8,128)(2,1)S(1)} %get-tuple-element.28.pair_ref), channel_id=1, source_target_pairs={{0,16},{8,24},{16,0},{24,8},{1,17},{9,25},{17,1},{25,9},{2,18},{10... | collective-permute-start | bytes 393224 | tf_op jit(solution)/shard_map/ppermute | solution.py:20
  13.4 0.0 collective-permute-done.4.got_ref
  13.4 0.0 collective-permute-done.1.rows_ref
  13.4 0.1 shard_map.90
  13.5 1.2 %collective-permute-start.5 = (bf16[384,128]{1,0:T(8,128)(2,1)S(1)}, bf16[384,128]{1,0:T(8,128)(2,1)S(1)}, u32[]{:S(2)}, u32[]{:S(2)}) collective-permute-start(bf16[384,128]{1,0:T(8,128)(2,1)S(1)} %get-tuple-element.25), channel_id=1, source_target_pairs={{0,8},{8,0},{16,24},{24,16},{1,9},{9,1},{17,25},{25,17},{2,10},{10... | collective-permute-start | bytes 294920 | tf_op jit(solution)/shard_map/ppermute | solution.py:20
  14.7 2.8 %collective-permute-start.7 = (bf16[64,128]{1,0:T(8,128)(2,1)S(1)}, bf16[64,128]{1,0:T(8,128)(2,1)S(1)}, u32[]{:S(2)}, u32[]{:S(2)}) collective-permute-start(bf16[64,128]{1,0:T(8,128)(2,1)S(1)} %get-tuple-element.31.low0_ref), channel_id=1, source_target_pairs={{0,24},{8,16},{16,8},{24,0},{1,25},{9,17},{17,9},{25,1},{2,26},{10... | collective-permute-start | bytes 49160 | tf_op jit(solution)/shard_map/ppermute | solution.py:20
  17.5 0.0 collective-permute-start.8
  17.5 1.7 %collective-permute-done.6.after_ref.far_ref = bf16[8,64,128]{2,1,0:T(8,128)(2,1)S(1)} collective-permute-done((bf16[8,64,128]{2,1,0:T(8,128)(2,1)S(1)}, bf16[8,64,128]{2,1,0:T(8,128)(2,1)S(1)}, u32[]{:S(2)}, u32[]{:S(2)}) %collective-permute-start.6) | collective-permute-done | bytes 131104 | tf_op jit(solution)/shard_map/ppermute | solution.py:20
  19.1 0.5 %collective-permute-done.5.both_ref.low1_ref = bf16[384,128]{1,0:T(8,128)(2,1)S(1)} collective-permute-done((bf16[384,128]{1,0:T(8,128)(2,1)S(1)}, bf16[384,128]{1,0:T(8,128)(2,1)S(1)}, u32[]{:S(2)}, u32[]{:S(2)}) %collective-permute-start.5) | collective-permute-done | bytes 98336 | tf_op jit(solution)/shard_map/ppermute | solution.py:20
  19.6 1.9 %shard_map.91 = (f32[8,64,128]{2,1,0:T(8,128)S(1)}, f32[4,2,128]{2,1,0:T(2,128)}) custom-call(f32[8,64,128]{2,1,0:T(8,128)S(1)} %get-tuple-element.17.field_ref, f32[8,8,128]{2,1,0:T(8,128)S(1)} %get-tuple-element.20.side_ref, f32[8,128]{1,0:T(8,128)S(1)} %get-tuple-element.21.wide_ref, bf16[320,128]{1,0:T(8,128)(2,1)S(1)} %collective-permute-done.1.rows_ref, ...), custom_call_target="tpu_custom_call" | custom-call | flops 1073741824 | tf_op jit(solution)/shard_map/pallas_call | solution.py:59
  21.5 0.0 collective-permute-done.7.low3_ref
  21.5 0.6 %collective-permute-done.8.low2_ref = bf16[64,128]{1,0:T(8,128)(2,1)S(1)} collective-permute-done((bf16[64,128]{1,0:T(8,128)(2,1)S(1)}, bf16[64,128]{1,0:T(8,128)(2,1)S(1)}, u32[]{:S(2)}, u32[]{:S(2)}) %collective-permute-start.8) | collective-permute-done | bytes 16416 | tf_op jit(solution)/shard_map/ppermute | solution.py:20
  22.1 1.0 %shard_map.92 = f32[8,64,128]{2,1,0:T(8,128)} custom-call(bf16[8,64,128]{2,1,0:T(8,128)(2,1)S(1)} %get-tuple-element.28.pair_ref, bf16[8,64,128]{2,1,0:T(8,128)(2,1)S(1)} %collective-permute-done.6.after_ref.far_ref, f32[8,64,128]{2,1,0:T(8,128)S(1)} %get-tuple-element.30.prior_ref, bf16[64,128]{1,0:T(8,128)(2,1)S(1)} %get-tuple-element.31.low0_ref, ...), custom_call_target="tpu_custom_call" | custom-call | tf_op jit(solution)/shard_map/pallas_call | solution.py:59
  (2 shorter events, 0.0 us)
Async XLA Ops:
  2.0 3.2 %collective-permute-start = (f32[112,128]{1,0:T(8,128)S(1)}, f32[112,128]{1,0:T(8,128)S(1)}, u32[]{:S(2)}, u32[]{:S(2)}) collective-permute-start(f32[112,128]{1,0:T(8,128)S(1)} %get-tuple-element.18.mine_ref), channel_id=1, source_target_pairs={{0,1},{1,0},{2,3},{3,2},{4,5},{5,4},{6,7},{7,6},{8,9},{9,8},{10,11... | collective-permute-start | bytes 172040 | tf_op jit(solution)/shard_map/ppermute | solution.py:20
  2.5 5.3 %collective-permute-start.3 = (bf16[4,64,128]{2,1,0:T(8,128)(2,1)S(1)}, bf16[4,64,128]{2,1,0:T(8,128)(2,1)S(1)}, u32[]{:S(2)}, u32[]{:S(2)}) collective-permute-start(bf16[4,64,128]{2,1,0:T(8,128)(2,1)S(1)} %get-tuple-element.23.one_ref), channel_id=1, source_target_pairs={{0,8},{8,0},{16,24},{24,16},{1,9},{9,1},{17,25},{25,17},{2,10},{10... | collective-permute-start | bytes 196616 | tf_op jit(solution)/shard_map/ppermute | solution.py:20
  5.2 4.0 %collective-permute-start.2 = (f32[72,128]{1,0:T(8,128)S(1)}, f32[72,128]{1,0:T(8,128)S(1)}, u32[]{:S(2)}, u32[]{:S(2)}) collective-permute-start(f32[72,128]{1,0:T(8,128)S(1)} %shard_map.87.after_ref.mine_ref), channel_id=1, source_target_pairs={{0,2},{2,0},{4,6},{6,4},{1,3},{3,1},{5,7},{7,5},{8,10},{10,8},{12,... | collective-permute-start | bytes 110600 | tf_op jit(solution)/shard_map/ppermute | solution.py:20
  6.8 6.6 %collective-permute-start.1 = (bf16[320,128]{1,0:T(8,128)(2,1)S(1)}, bf16[320,128]{1,0:T(8,128)(2,1)S(1)}, u32[]{:S(2)}, u32[]{:S(2)}) collective-permute-start(bf16[320,128]{1,0:T(8,128)(2,1)S(1)} %get-tuple-element.22), channel_id=1, source_target_pairs={{0,2},{2,0},{4,6},{6,4},{8,14},{10,12},{12,10},{14,8},{16,18},{18,... | collective-permute-start | bytes 245768 | tf_op jit(solution)/shard_map/ppermute | solution.py:381
  9.2 4.2 %collective-permute-start.4 = (f32[72,128]{1,0:T(8,128)S(1)}, f32[72,128]{1,0:T(8,128)S(1)}, u32[]{:S(2)}, u32[]{:S(2)}) collective-permute-start(f32[72,128]{1,0:T(8,128)S(1)} %get-tuple-element.24.mine_ref), channel_id=1, source_target_pairs={{0,4},{2,6},{4,0},{6,2},{1,5},{3,7},{5,1},{7,3},{8,12},{10,14},{12... | collective-permute-start | bytes 110600 | tf_op jit(solution)/shard_map/ppermute | solution.py:20
  10.8 8.3 %collective-permute-start.6 = (bf16[8,64,128]{2,1,0:T(8,128)(2,1)S(1)}, bf16[8,64,128]{2,1,0:T(8,128)(2,1)S(1)}, u32[]{:S(2)}, u32[]{:S(2)}) collective-permute-start(bf16[8,64,128]{2,1,0:T(8,128)(2,1)S(1)} %get-tuple-element.28.pair_ref), channel_id=1, source_target_pairs={{0,16},{8,24},{16,0},{24,8},{1,17},{9,25},{17,1},{25,9},{2,18},{10... | collective-permute-start | bytes 393224 | tf_op jit(solution)/shard_map/ppermute | solution.py:20
  13.5 6.1 %collective-permute-start.5 = (bf16[384,128]{1,0:T(8,128)(2,1)S(1)}, bf16[384,128]{1,0:T(8,128)(2,1)S(1)}, u32[]{:S(2)}, u32[]{:S(2)}) collective-permute-start(bf16[384,128]{1,0:T(8,128)(2,1)S(1)} %get-tuple-element.25), channel_id=1, source_target_pairs={{0,8},{8,0},{16,24},{24,16},{1,9},{9,1},{17,25},{25,17},{2,10},{10... | collective-permute-start | bytes 294920 | tf_op jit(solution)/shard_map/ppermute | solution.py:20
  14.7 6.9 %collective-permute-start.7 = (bf16[64,128]{1,0:T(8,128)(2,1)S(1)}, bf16[64,128]{1,0:T(8,128)(2,1)S(1)}, u32[]{:S(2)}, u32[]{:S(2)}) collective-permute-start(bf16[64,128]{1,0:T(8,128)(2,1)S(1)} %get-tuple-element.31.low0_ref), channel_id=1, source_target_pairs={{0,24},{8,16},{16,8},{24,0},{1,25},{9,17},{17,9},{25,1},{2,26},{10... | collective-permute-start | bytes 49160 | tf_op jit(solution)/shard_map/ppermute | solution.py:20
  17.5 4.6 %collective-permute-start.8 = (bf16[64,128]{1,0:T(8,128)(2,1)S(1)}, bf16[64,128]{1,0:T(8,128)(2,1)S(1)}, u32[]{:S(2)}, u32[]{:S(2)}) collective-permute-start(bf16[64,128]{1,0:T(8,128)(2,1)S(1)} %get-tuple-element.31.low0_ref), channel_id=1, source_target_pairs={{0,16},{8,24},{16,0},{24,8},{1,17},{9,25},{17,1},{25,9},{2,18},{10... | collective-permute-start | bytes 49160 | tf_op jit(solution)/shard_map/ppermute | solution.py:20

commit v9 on v8

--- a/solution.py
+++ b/solution.py
@@ -193,7 +193,7 @@
         ).astype(jnp.bfloat16)
 
 
-def weigh(mine_ref, got_ref, rows_ref, low_ref, both_ref, weighted_ref):
+def weigh(mine_ref, got_ref, low_ref, weighted_ref):
     comps, sensors, real = weighted_ref.shape
     points = comps * sensors
     total = mine_ref[...] + got_ref[...]
@@ -214,8 +214,6 @@
             low_ref[c * sensors + k * chunk : c * sensors + (k + 1) * chunk] = weighted.astype(
                 jnp.bfloat16
             )
-    both_ref[:points] = low_ref[...]
-    both_ref[points:] = rows_ref[...]
 
 
 def prior(
@@ -223,10 +221,9 @@
     side_ref,
     wide_ref,
     rows_ref,
-    both_ref,
+    other_ref,
     table_ref,
     weighted_ref,
-    after_ref,
     prior_ref,
     own_out,
     state_ref,
@@ -249,7 +246,7 @@
     wide = cols + 2 * SWEEPS
     step = rows_ref.shape[0] // SWEEPS
     mine = rows_ref[...].astype(jnp.float32)
-    other = both_ref[both_ref.shape[0] - rows_ref.shape[0] :].astype(jnp.float32)
+    other = other_ref[...].astype(jnp.float32)
     even = lax.axis_index("freq") % 2 == 0
     before, after = sides_of(
         jnp.where(even, mine, other), jnp.where(even, other, mine), "px"
@@ -307,14 +304,11 @@
     out.wait()
 
 
-def finish(pair_ref, far_ref, prior_ref, low0_ref, low1_ref, low3_ref, low2_ref, out, held_ref, sems):
+def finish(pair_ref, far_ref, prior_ref, low0_ref, low3_ref, low2_ref, low1_ref, out, held_ref, sems):
     rows, cols, real = held_ref.shape
     beside = pair_ref.shape[0] // 2
     side = rows // beside
-    points = low0_ref.shape[0]
-    low = jnp.concatenate(
-        [low0_ref[...], low1_ref[:points], low2_ref[...], low3_ref[...]], axis=0
-    )
+    low = jnp.concatenate([low0_ref[...], low1_ref[...], low2_ref[...], low3_ref[...]], axis=0)
     copies = []
     for x in range(beside):
         kernel = jnp.concatenate(
@@ -395,13 +389,14 @@
     )(total, swap(total, "px", lambda i: i ^ steps[-1]), kernel_own, kernel_next)
     kernel_far = swap(kernel_pair, "freq", lambda i: i ^ 2)
     assert lax.axis_size("freq") == 4
-    weighted_low, weighted_both, weighted = call(
+    weighted_low, weighted = call(
         weigh,
         ((points, real), jnp.bfloat16),
-        ((points + SWEEPS * step, real), jnp.bfloat16),
         ((comps, sensors, real), jnp.float32),
-    )(total, swap(total, "px", lambda i: i ^ last), rim_rows)
-    both_next = swap(weighted_both, "freq", near)
+        flops=ORDER_FLOPS,
+    )(total, swap(total, "px", lambda i: i ^ last))
+    other_rows = swap(rim_rows, "freq", near)
+    low_one = swap(weighted_low, "freq", near)
     low_three = swap(weighted_low, "freq", lambda i: i ^ 3)
     low_two = swap(weighted_low, "freq", lambda i: i ^ 2)
     wide = cols + 2 * SWEEPS
@@ -417,7 +412,7 @@
             pltpu.SemaphoreType.DMA(()),
         ),
         flops=PRIOR_FLOPS,
-    )(model_field, side_rim, wide_marks, rim_rows, both_next, table, weighted, kernel_far)
+    )(model_field, side_rim, wide_marks, rim_rows, other_rows, table, weighted)
     (gradient,) = call(
         finish,
         (model_field.shape, jnp.float32),
@@ -426,7 +421,7 @@
             pltpu.VMEM(model_field.shape, jnp.float32),
             pltpu.SemaphoreType.DMA((rows,)),
         ),
-    )(kernel_pair, kernel_far, prior_term, weighted_low, both_next, low_three, low_two)
+    )(kernel_pair, kernel_far, prior_term, weighted_low, low_three, low_two, low_one)
     return weighted_own[None], gradient
 
 

time: 23.2 us -> 22.3 us (0.961)
  waiting for transfers between devices: 4.54 us -> 2.03 us
  starting transfers between devices: 13.4 us -> 15 us
    ppermute x8 -> x9, waiting for transfers between devices: 4.54 us -> 2.03 us  [swap(): lax.ppermute(own, axis, [(i, partner(i)) for i in range(lax.axis_size(axi...]
    ppermute x8 -> x9, starting transfers between devices: 12.9 us -> 14.4 us  [swap(): lax.ppermute(own, axis, [(i, partner(i)) for i in range(lax.axis_size(axi...]
  transfers between devices with their start and end apart: 9 -> 10, of which waited for: 5 -> 3; matrix products, arithmetic and copies ran while one was open for 0% -> 0% of each run, Pallas kernels for 9% -> 10%
where the time goes in v9:
time: 22.3 us; the launch traced here: 22.1 us
  starting transfers between devices  15 us (67%)
  Pallas kernels  4.44 us (20%)
  waiting for transfers between devices  2.03 us (9%)
  between operations  0.68 us (3%)
    ppermute x9, starting transfers between devices, swap(): lax.ppermute(own, axis, [(i, partner(i)) for i in range(lax.axis_size(axi...  14.4 us
    pallas_call x7, Pallas kernels, run(): pl.pallas_call(fetched if fetch else body, out_shape=[jax.ShapeDtypeStruc...  4.44 us
    ppermute x9, waiting for transfers between devices, swap(): lax.ppermute(own, axis, [(i, partner(i)) for i in range(lax.axis_size(axi...  2.03 us
    ppermute x1, starting transfers between devices, local(): lax.ppermute(rim_rows, ('freq', 'px'), [(f * peers + i, f * peers + (far(...  0.56 us
  transfers between devices with their start and end apart: 10, of which 3 were waited for; matrix products, arithmetic and copies ran while one was open for 0% of the time, Pallas kernels for 10%

profile of v9, /device:TPU:0, one launch (start us, length us, event | category | flops | bytes accessed | tf_op | source)
XLA Modules:
  0.0 22.1 jit_solution(8520620513563907505)
XLA Ops:
  0.6 1.4 %shard_map.86 = (f32[112,128]{1,0:T(8,128)S(1)}, bf16[4,64,128]{2,1,0:T(8,128)(2,1)S(1)}, f32[8,64,128]{2,1,0:T(8,128)S(1)}, f32[8,128]{1,0:T(8,128)S(1)}, f32[5,16]{1,0:T(8,128)S(1)}) custom-call(f32[1,4]{1,0:T(1,128)} %refs_0_.1, f32[4,2,128]{2,1,0:T(2,128)} %bitcast.9, bf16[8,64,64]{2,1,0:T(8,128)(2,1)} %bitcast.8, f32[8,64,128]{2,1,0:T(8,128)} %refs_3_.1, ...), custom_call_target="tpu_custom_call" | custom-call | tf_op jit(solution)/shard_map/pallas_call | solution.py:59
  2.0 0.5 %collective-permute-start = (f32[112,128]{1,0:T(8,128)S(1)}, f32[112,128]{1,0:T(8,128)S(1)}, u32[]{:S(2)}, u32[]{:S(2)}) collective-permute-start(f32[112,128]{1,0:T(8,128)S(1)} %get-tuple-element.17.mine_ref), channel_id=1, source_target_pairs={{0,1},{1,0},{2,3},{3,2},{4,5},{5,4},{6,7},{7,6},{8,9},{9,8},{10,11... | collective-permute-start | bytes 172040 | tf_op jit(solution)/shard_map/ppermute | solution.py:20
  2.5 2.6 %collective-permute-start.4 = (bf16[4,64,128]{2,1,0:T(8,128)(2,1)S(1)}, bf16[4,64,128]{2,1,0:T(8,128)(2,1)S(1)}, u32[]{:S(2)}, u32[]{:S(2)}) collective-permute-start(bf16[4,64,128]{2,1,0:T(8,128)(2,1)S(1)} %get-tuple-element.23.one_ref), channel_id=1, source_target_pairs={{0,8},{8,0},{16,24},{24,16},{1,9},{9,1},{17,25},{25,17},{2,10},{10... | collective-permute-start | bytes 196616 | tf_op jit(solution)/shard_map/ppermute | solution.py:20
  5.2 0.0 collective-permute-done.got_ref
  5.2 1.6 %collective-permute-start.3 = (f32[72,128]{1,0:T(8,128)S(1)}, f32[72,128]{1,0:T(8,128)S(1)}, u32[]{:S(2)}, u32[]{:S(2)}) collective-permute-start(f32[72,128]{1,0:T(8,128)S(1)} %shard_map.87.after_ref.mine_ref), channel_id=1, source_target_pairs={{0,2},{2,0},{4,6},{6,4},{1,3},{3,1},{5,7},{7,5},{8,10},{10,8},{12,... | collective-permute-start | bytes 110600 | tf_op jit(solution)/shard_map/ppermute | solution.py:20
  6.7 0.1 shard_map.88
  6.8 0.6 %collective-permute-start.1 = (bf16[320,128]{1,0:T(8,128)(2,1)S(1)}, bf16[320,128]{1,0:T(8,128)(2,1)S(1)}, u32[]{:S(2)}, u32[]{:S(2)}) collective-permute-start(bf16[320,128]{1,0:T(8,128)(2,1)S(1)} %get-tuple-element.21), channel_id=1, source_target_pairs={{0,2},{2,0},{4,6},{6,4},{8,14},{10,12},{12,10},{14,8},{16,18},{18,... | collective-permute-start | bytes 245768 | tf_op jit(solution)/shard_map/ppermute | solution.py:375
  7.4 0.5 %collective-permute-done.4.two_ref = bf16[4,64,128]{2,1,0:T(8,128)(2,1)S(1)} collective-permute-done((bf16[4,64,128]{2,1,0:T(8,128)(2,1)S(1)}, bf16[4,64,128]{2,1,0:T(8,128)(2,1)S(1)}, u32[]{:S(2)}, u32[]{:S(2)}) %collective-permute-start.4) | collective-permute-done | bytes 65568 | tf_op jit(solution)/shard_map/ppermute | solution.py:20
  7.9 1.3 %collective-permute-done.3.got_ref = f32[72,128]{1,0:T(8,128)S(1)} collective-permute-done((f32[72,128]{1,0:T(8,128)S(1)}, f32[72,128]{1,0:T(8,128)S(1)}, u32[]{:S(2)}, u32[]{:S(2)}) %collective-permute-start.3) | collective-permute-done | bytes 36896 | tf_op jit(solution)/shard_map/ppermute | solution.py:20
  9.2 1.6 %collective-permute-start.5 = (f32[72,128]{1,0:T(8,128)S(1)}, f32[72,128]{1,0:T(8,128)S(1)}, u32[]{:S(2)}, u32[]{:S(2)}) collective-permute-start(f32[72,128]{1,0:T(8,128)S(1)} %get-tuple-element.24.mine_ref), channel_id=1, source_target_pairs={{0,4},{2,6},{4,0},{6,2},{1,5},{3,7},{5,1},{7,3},{8,12},{10,14},{12... | collective-permute-start | bytes 110600 | tf_op jit(solution)/shard_map/ppermute | solution.py:20
  10.8 2.6 %collective-permute-start.6 = (bf16[8,64,128]{2,1,0:T(8,128)(2,1)S(1)}, bf16[8,64,128]{2,1,0:T(8,128)(2,1)S(1)}, u32[]{:S(2)}, u32[]{:S(2)}) collective-permute-start(bf16[8,64,128]{2,1,0:T(8,128)(2,1)S(1)} %get-tuple-element.27.pair_ref), channel_id=1, source_target_pairs={{0,16},{8,24},{16,0},{24,8},{1,17},{9,25},{17,1},{25,9},{2,18},{10... | collective-permute-start | bytes 393224 | tf_op jit(solution)/shard_map/ppermute | solution.py:20
  13.4 0.0 collective-permute-done.1.rows_ref
  13.4 1.1 %collective-permute-start.2 = (bf16[320,128]{1,0:T(8,128)(2,1)S(1)}, bf16[320,128]{1,0:T(8,128)(2,1)S(1)}, u32[]{:S(2)}, u32[]{:S(2)}) collective-permute-start(bf16[320,128]{1,0:T(8,128)(2,1)S(1)} %collective-permute-done.1.rows_ref), channel_id=1, source_target_pairs={{0,8},{8,0},{16,24},{24,16},{1,9},{9,1},{17,25},{25,17},{2,10},{10... | collective-permute-start | bytes 245768 | tf_op jit(solution)/shard_map/ppermute | solution.py:20
  14.5 0.0 collective-permute-done.5.got_ref
  14.5 0.1 shard_map.90
  14.6 1.9 %collective-permute-start.7 = (bf16[64,128]{1,0:T(8,128)(2,1)S(1)}, bf16[64,128]{1,0:T(8,128)(2,1)S(1)}, u32[]{:S(2)}, u32[]{:S(2)}) collective-permute-start(bf16[64,128]{1,0:T(8,128)(2,1)S(1)} %get-tuple-element.29.low0_ref), channel_id=1, source_target_pairs={{0,24},{8,16},{16,8},{24,0},{1,25},{9,17},{17,9},{25,1},{2,26},{10... | collective-permute-start | bytes 49160 | tf_op jit(solution)/shard_map/ppermute | solution.py:20
  16.5 0.5 %collective-permute-start.8 = (bf16[64,128]{1,0:T(8,128)(2,1)S(1)}, bf16[64,128]{1,0:T(8,128)(2,1)S(1)}, u32[]{:S(2)}, u32[]{:S(2)}) collective-permute-start(bf16[64,128]{1,0:T(8,128)(2,1)S(1)} %get-tuple-element.29.low0_ref), channel_id=1, source_target_pairs={{0,16},{8,24},{16,0},{24,8},{1,17},{9,25},{17,1},{25,9},{2,18},{10... | collective-permute-start | bytes 49160 | tf_op jit(solution)/shard_map/ppermute | solution.py:20
  17.1 2.0 %collective-permute-start.9 = (bf16[64,128]{1,0:T(8,128)(2,1)S(1)}, bf16[64,128]{1,0:T(8,128)(2,1)S(1)}, u32[]{:S(2)}, u32[]{:S(2)}) collective-permute-start(bf16[64,128]{1,0:T(8,128)(2,1)S(1)} %get-tuple-element.29.low0_ref), channel_id=1, source_target_pairs={{0,8},{8,0},{16,24},{24,16},{1,9},{9,1},{17,25},{25,17},{2,10},{10... | collective-permute-start | bytes 49160 | tf_op jit(solution)/shard_map/ppermute | solution.py:20
  19.1 0.0 collective-permute-done.2.other_ref
  19.1 1.9 %shard_map.91 = (f32[8,64,128]{2,1,0:T(8,128)S(1)}, f32[4,2,128]{2,1,0:T(2,128)}) custom-call(f32[8,64,128]{2,1,0:T(8,128)S(1)} %get-tuple-element.16.field_ref, f32[8,8,128]{2,1,0:T(8,128)S(1)} %get-tuple-element.19.side_ref, f32[8,128]{1,0:T(8,128)S(1)} %get-tuple-element.20.wide_ref, bf16[320,128]{1,0:T(8,128)(2,1)S(1)} %collective-permute-done.1.rows_ref, ...), custom_call_target="tpu_custom_call" | custom-call | flops 1073741824 | tf_op jit(solution)/shard_map/pallas_call | solution.py:59
  21.0 0.0 collective-permute-done.7.low3_ref
  21.0 0.2 collective-permute-done.8.low2_ref
  21.2 0.0 collective-permute-done.9.low1_ref
  21.2 0.0 collective-permute-done.6.far_ref
  21.2 1.0 %shard_map.92 = f32[8,64,128]{2,1,0:T(8,128)} custom-call(bf16[8,64,128]{2,1,0:T(8,128)(2,1)S(1)} %get-tuple-element.27.pair_ref, bf16[8,64,128]{2,1,0:T(8,128)(2,1)S(1)} %collective-permute-done.6.far_ref, f32[8,64,128]{2,1,0:T(8,128)S(1)} %get-tuple-element.28.prior_ref, bf16[64,128]{1,0:T(8,128)(2,1)S(1)} %get-tuple-element.29.low0_ref, ...), custom_call_target="tpu_custom_call" | custom-call | tf_op jit(solution)/shard_map/pallas_call | solution.py:59
  (2 shorter events, 0.0 us)
Async XLA Ops:
  2.0 3.2 %collective-permute-start = (f32[112,128]{1,0:T(8,128)S(1)}, f32[112,128]{1,0:T(8,128)S(1)}, u32[]{:S(2)}, u32[]{:S(2)}) collective-permute-start(f32[112,128]{1,0:T(8,128)S(1)} %get-tuple-element.17.mine_ref), channel_id=1, source_target_pairs={{0,1},{1,0},{2,3},{3,2},{4,5},{5,4},{6,7},{7,6},{8,9},{9,8},{10,11... | collective-permute-start | bytes 172040 | tf_op jit(solution)/shard_map/ppermute | solution.py:20
  2.5 5.3 %collective-permute-start.4 = (bf16[4,64,128]{2,1,0:T(8,128)(2,1)S(1)}, bf16[4,64,128]{2,1,0:T(8,128)(2,1)S(1)}, u32[]{:S(2)}, u32[]{:S(2)}) collective-permute-start(bf16[4,64,128]{2,1,0:T(8,128)(2,1)S(1)} %get-tuple-element.23.one_ref), channel_id=1, source_target_pairs={{0,8},{8,0},{16,24},{24,16},{1,9},{9,1},{17,25},{25,17},{2,10},{10... | collective-permute-start | bytes 196616 | tf_op jit(solution)/shard_map/ppermute | solution.py:20
  5.2 4.0 %collective-permute-start.3 = (f32[72,128]{1,0:T(8,128)S(1)}, f32[72,128]{1,0:T(8,128)S(1)}, u32[]{:S(2)}, u32[]{:S(2)}) collective-permute-start(f32[72,128]{1,0:T(8,128)S(1)} %shard_map.87.after_ref.mine_ref), channel_id=1, source_target_pairs={{0,2},{2,0},{4,6},{6,4},{1,3},{3,1},{5,7},{7,5},{8,10},{10,8},{12,... | collective-permute-start | bytes 110600 | tf_op jit(solution)/shard_map/ppermute | solution.py:20
  6.8 6.6 %collective-permute-start.1 = (bf16[320,128]{1,0:T(8,128)(2,1)S(1)}, bf16[320,128]{1,0:T(8,128)(2,1)S(1)}, u32[]{:S(2)}, u32[]{:S(2)}) collective-permute-start(bf16[320,128]{1,0:T(8,128)(2,1)S(1)} %get-tuple-element.21), channel_id=1, source_target_pairs={{0,2},{2,0},{4,6},{6,4},{8,14},{10,12},{12,10},{14,8},{16,18},{18,... | collective-permute-start | bytes 245768 | tf_op jit(solution)/shard_map/ppermute | solution.py:375
  9.2 5.3 %collective-permute-start.5 = (f32[72,128]{1,0:T(8,128)S(1)}, f32[72,128]{1,0:T(8,128)S(1)}, u32[]{:S(2)}, u32[]{:S(2)}) collective-permute-start(f32[72,128]{1,0:T(8,128)S(1)} %get-tuple-element.24.mine_ref), channel_id=1, source_target_pairs={{0,4},{2,6},{4,0},{6,2},{1,5},{3,7},{5,1},{7,3},{8,12},{10,14},{12... | collective-permute-start | bytes 110600 | tf_op jit(solution)/shard_map/ppermute | solution.py:20
  10.8 10.4 %collective-permute-start.6 = (bf16[8,64,128]{2,1,0:T(8,128)(2,1)S(1)}, bf16[8,64,128]{2,1,0:T(8,128)(2,1)S(1)}, u32[]{:S(2)}, u32[]{:S(2)}) collective-permute-start(bf16[8,64,128]{2,1,0:T(8,128)(2,1)S(1)} %get-tuple-element.27.pair_ref), channel_id=1, source_target_pairs={{0,16},{8,24},{16,0},{24,8},{1,17},{9,25},{17,1},{25,9},{2,18},{10... | collective-permute-start | bytes 393224 | tf_op jit(solution)/shard_map/ppermute | solution.py:20
  13.4 5.7 %collective-permute-start.2 = (bf16[320,128]{1,0:T(8,128)(2,1)S(1)}, bf16[320,128]{1,0:T(8,128)(2,1)S(1)}, u32[]{:S(2)}, u32[]{:S(2)}) collective-permute-start(bf16[320,128]{1,0:T(8,128)(2,1)S(1)} %collective-permute-done.1.rows_ref), channel_id=1, source_target_pairs={{0,8},{8,0},{16,24},{24,16},{1,9},{9,1},{17,25},{25,17},{2,10},{10... | collective-permute-start | bytes 245768 | tf_op jit(solution)/shard_map/ppermute | solution.py:20
  14.6 6.4 %collective-permute-start.7 = (bf16[64,128]{1,0:T(8,128)(2,1)S(1)}, bf16[64,128]{1,0:T(8,128)(2,1)S(1)}, u32[]{:S(2)}, u32[]{:S(2)}) collective-permute-start(bf16[64,128]{1,0:T(8,128)(2,1)S(1)} %get-tuple-element.29.low0_ref), channel_id=1, source_target_pairs={{0,24},{8,16},{16,8},{24,0},{1,25},{9,17},{17,9},{25,1},{2,26},{10... | collective-permute-start | bytes 49160 | tf_op jit(solution)/shard_map/ppermute | solution.py:20
  16.5 4.6 %collective-permute-start.8 = (bf16[64,128]{1,0:T(8,128)(2,1)S(1)}, bf16[64,128]{1,0:T(8,128)(2,1)S(1)}, u32[]{:S(2)}, u32[]{:S(2)}) collective-permute-start(bf16[64,128]{1,0:T(8,128)(2,1)S(1)} %get-tuple-element.29.low0_ref), channel_id=1, source_target_pairs={{0,16},{8,24},{16,0},{24,8},{1,17},{9,25},{17,1},{25,9},{2,18},{10... | collective-permute-start | bytes 49160 | tf_op jit(solution)/shard_map/ppermute | solution.py:20
  17.1 4.1 %collective-permute-start.9 = (bf16[64,128]{1,0:T(8,128)(2,1)S(1)}, bf16[64,128]{1,0:T(8,128)(2,1)S(1)}, u32[]{:S(2)}, u32[]{:S(2)}) collective-permute-start(bf16[64,128]{1,0:T(8,128)(2,1)S(1)} %get-tuple-element.29.low0_ref), channel_id=1, source_target_pairs={{0,8},{8,0},{16,24},{24,16},{1,9},{9,1},{17,25},{25,17},{2,10},{10... | collective-permute-start | bytes 49160 | tf_op jit(solution)/shard_map/ppermute | solution.py:20

commit v10 on v9

--- a/solution.py
+++ b/solution.py
@@ -13,6 +13,7 @@
 VMEM_BYTES = 40 << 20
 PRIOR_FLOPS = 1 << 30
 EDGE_FLOPS = 1 << 30
+JOIN_FLOPS = 1 << 30
 ORDER_FLOPS = 1 << 32
 
 
@@ -161,8 +162,7 @@
     joined_ref[half:] = two_ref[...]
 
 
-def edge(after_ref, got_ref, field_ref, marks_ref, *refs):
-    *far_ref, side_ref, wide_ref, rows_ref = refs
+def lay(got_ref, field_ref, marks_ref, far_ref, side_ref, wide_ref, rows_ref, base):
     rows, cols, real = field_ref.shape
     one = got_ref[got_ref.shape[0] - rows * (SWEEPS + 1) :]
     before, after = sides_of(one, far_ref[0][...] if far_ref else one, "py")
@@ -179,11 +179,11 @@
     if lax.axis_size("px") > 2:
         chosen = chosen == (lax.axis_index("freq") % 2 == 0)
     top = lax.broadcasted_iota(jnp.int32, (TILE, real), 0) == 0
-    step = rows_ref.shape[0] // SWEEPS
+    step = (rows_ref.shape[0] - base) // SWEEPS
     for k in range(SWEEPS):
         last = rows - SWEEPS + k
         marks = jnp.where(chosen, wide_ref[last : last + 1], wide_ref[k : k + 1])
-        rows_ref[k * step : (k + 1) * step] = jnp.concatenate(
+        rows_ref[base + k * step : base + (k + 1) * step] = jnp.concatenate(
             [
                 jnp.where(chosen, field_ref[last], field_ref[k]),
                 jnp.where(chosen, side_ref[last], side_ref[k]),
@@ -193,10 +193,50 @@
         ).astype(jnp.bfloat16)
 
 
-def weigh(mine_ref, got_ref, low_ref, weighted_ref):
+def edge(after_ref, got_ref, field_ref, marks_ref, *refs):
+    *far_ref, side_ref, wide_ref, rows_ref = refs
+    lay(got_ref, field_ref, marks_ref, far_ref, side_ref, wide_ref, rows_ref, 0)
+
+
+def packed_rows(size):
+    return -(-size // 16) * 16
+
+
+def spread(mine_ref, got_ref, field_ref, marks_ref, *refs):
+    *far_ref, out_ref, side_ref, wide_ref, mixed_ref = refs
+    size, real = out_ref.shape
+    total = mine_ref[:size] + got_ref[:size]
+    out_ref[...] = total
+    part = packed_rows(size)
+    rest = total
+    if part > size:
+        rest = jnp.concatenate([total, jnp.zeros((part - size, real), jnp.float32)], axis=0)
+    for k in range(3):
+        low = rest.astype(jnp.bfloat16)
+        mixed_ref[k * part : (k + 1) * part] = low
+        rest = rest - low.astype(jnp.float32)
+    lay(got_ref, field_ref, marks_ref, far_ref, side_ref, wide_ref, mixed_ref, 3 * part)
+
+
+def join(one_ref, two_ref, after_ref, out_ref):
+    half = one_ref.shape[0]
+    out_ref[:half] = one_ref[...]
+    out_ref[half:] = two_ref[...]
+
+
+def weigh(*refs):
+    mine_ref, *got_refs, low_ref, weighted_ref = refs
     comps, sensors, real = weighted_ref.shape
     points = comps * sensors
-    total = mine_ref[...] + got_ref[...]
+    total = mine_ref[...]
+    size = total.shape[0]
+    for got_ref in got_refs:
+        if got_ref.dtype == jnp.bfloat16:
+            part = packed_rows(size)
+            three = [got_ref[k * part : (k + 1) * part].astype(jnp.float32) for k in range(3)]
+            total = total + (three[0] + three[1] + three[2])[:size]
+        else:
+            total = total + got_ref[...]
     chunk = min(sensors, real)
     eye = lax.broadcasted_iota(jnp.int32, (chunk, real), 0) == lax.broadcasted_iota(
         jnp.int32, (chunk, real), 1
@@ -244,8 +284,8 @@
     out.start()
     rows, cols, _ = field_ref.shape
     wide = cols + 2 * SWEEPS
-    step = rows_ref.shape[0] // SWEEPS
-    mine = rows_ref[...].astype(jnp.float32)
+    step = other_ref.shape[0] // SWEEPS
+    mine = rows_ref[rows_ref.shape[0] - other_ref.shape[0] :].astype(jnp.float32)
     other = other_ref[...].astype(jnp.float32)
     even = lax.axis_index("freq") % 2 == 0
     before, after = sides_of(
@@ -360,42 +400,63 @@
     kernel_next = swap(kernel_own, "freq", near)
     two = [swap(rim, "py", far("py")) for rim in far_rim]
     summed = ((points + TILE, real), jnp.float32)
-    (total,) = call(add, summed)(payload, got)
-    for bit in bits("py")[1:]:
-        (total,) = call(add, summed)(total, swap(total, "py", lambda i: i ^ bit))
     step = cols + 2 * SWEEPS + TILE
-    side_rim, wide_marks, rim_rows = call(
-        edge,
+    peers, freqs = lax.axis_size("px"), lax.axis_size("freq")
+    side_shapes = (
         ((rows, 2 * SWEEPS, real), jnp.float32),
         ((rows, LANES), jnp.float32),
-        ((SWEEPS * step, real), jnp.bfloat16),
-        flops=EDGE_FLOPS,
-    )(total, got, model_field, marks, *two)
-    peers = lax.axis_size("px")
-    rim_rows = lax.ppermute(
-        rim_rows,
-        ("freq", "px"),
-        [
-            (f * peers + i, f * peers + (far("px")(i) if f % 2 and wide_px else near(i)))
-            for f in range(lax.axis_size("freq"))
-            for i in range(peers)
-        ],
-    )
-    *steps, last = bits("px")
-    for bit in steps[:-1]:
-        (total,) = call(add, summed)(total, swap(total, "px", lambda i: i ^ bit))
-    total, kernel_pair = call(
-        add_and_join, summed, ((2 * beside, points, side * cols), jnp.bfloat16), flops=ORDER_FLOPS
-    )(total, swap(total, "px", lambda i: i ^ steps[-1]), kernel_own, kernel_next)
+    )
+    pair_shape = ((2 * beside, points, side * cols), jnp.bfloat16)
+
+    def by_parity(own, even_partner, odd_partner):
+        return lax.ppermute(
+            own,
+            ("freq", "px"),
+            [
+                (f * peers + i, f * peers + (odd_partner if f % 2 else even_partner)(i))
+                for f in range(freqs)
+                for i in range(peers)
+            ],
+        )
+
+    if peers == 4 and lax.axis_size("py") == 2:
+        part = packed_rows(points + TILE)
+        total, side_rim, wide_marks, mixed = call(
+            spread,
+            summed,
+            *side_shapes,
+            ((3 * part + SWEEPS * step, real), jnp.bfloat16),
+        )(payload, got, model_field, marks)
+        mixed = by_parity(mixed, near, far("px"))
+        cross = by_parity(total, far("px"), near)
+        skip = swap(total, "px", lambda i: i ^ 2)
+        (kernel_pair,) = call(join, pair_shape, flops=JOIN_FLOPS)(kernel_own, kernel_next, total)
+        sums = (total, cross, skip, mixed)
+        rim_rows, sent_rows = mixed, mixed[3 * part :]
+    else:
+        (total,) = call(add, summed)(payload, got)
+        for bit in bits("py")[1:]:
+            (total,) = call(add, summed)(total, swap(total, "py", lambda i: i ^ bit))
+        side_rim, wide_marks, rim_rows = call(
+            edge, *side_shapes, ((SWEEPS * step, real), jnp.bfloat16), flops=EDGE_FLOPS
+        )(total, got, model_field, marks, *two)
+        rim_rows = sent_rows = by_parity(rim_rows, near, far("px") if wide_px else near)
+        *steps, last = bits("px")
+        for bit in steps[:-1]:
+            (total,) = call(add, summed)(total, swap(total, "px", lambda i: i ^ bit))
+        total, kernel_pair = call(add_and_join, summed, pair_shape, flops=ORDER_FLOPS)(
+            total, swap(total, "px", lambda i: i ^ steps[-1]), kernel_own, kernel_next
+        )
+        sums = (total, swap(total, "px", lambda i: i ^ last))
     kernel_far = swap(kernel_pair, "freq", lambda i: i ^ 2)
-    assert lax.axis_size("freq") == 4
+    assert freqs == 4
     weighted_low, weighted = call(
         weigh,
         ((points, real), jnp.bfloat16),
         ((comps, sensors, real), jnp.float32),
         flops=ORDER_FLOPS,
-    )(total, swap(total, "px", lambda i: i ^ last))
-    other_rows = swap(rim_rows, "freq", near)
+    )(*sums)
+    other_rows = swap(sent_rows, "freq", near)
     low_one = swap(weighted_low, "freq", near)
     low_three = swap(weighted_low, "freq", lambda i: i ^ 3)
     low_two = swap(weighted_low, "freq", lambda i: i ^ 2)

time: 22.3 us -> 22 us (0.987)
  waiting for transfers between devices: 2.03 us -> 0.85 us
  starting transfers between devices: 15 us -> 15.9 us
    ppermute x1 -> x2, starting transfers between devices: 0.56 us -> 3.01 us  [by_parity(): lax.ppermute(own, ('freq', 'px'), [(f * peers + i, f * peers + (odd_partn...]
    ppermute x9 -> x8, starting transfers between devices: 14.4 us -> 12.9 us  [swap(): lax.ppermute(own, axis, [(i, partner(i)) for i in range(lax.axis_size(axi...]
    ppermute x9 -> x8, waiting for transfers between devices: 2.03 us -> 0.79 us  [swap(): lax.ppermute(own, axis, [(i, partner(i)) for i in range(lax.axis_size(axi...]
    pallas_call x7 -> x6, Pallas kernels: 4.44 us -> 4.45 us  [run(): pl.pallas_call(fetched if fetch else body, out_shape=[jax.ShapeDtypeStruc...]
  transfers between devices with their start and end apart: 10 -> 10, of which waited for: 3 -> 2; matrix products, arithmetic and copies ran while one was open for 0% -> 0% of each run, Pallas kernels for 10% -> 10%
where the time goes in v10:
time: 22 us; the launch traced here: 21.9 us
  starting transfers between devices  15.9 us (72%)
  Pallas kernels  4.45 us (20%)
  waiting for transfers between devices  0.85 us (4%)
  between operations  0.69 us (3%)
    ppermute x8, starting transfers between devices, swap(): lax.ppermute(own, axis, [(i, partner(i)) for i in range(lax.axis_size(axi...  12.9 us
    pallas_call x6, Pallas kernels, run(): pl.pallas_call(fetched if fetch else body, out_shape=[jax.ShapeDtypeStruc...  4.45 us
    ppermute x2, starting transfers between devices, by_parity(): lax.ppermute(own, ('freq', 'px'), [(f * peers + i, f * peers + (odd_partn...  3.01 us
    ppermute x8, waiting for transfers between devices, swap(): lax.ppermute(own, axis, [(i, partner(i)) for i in range(lax.axis_size(axi...  0.79 us
  transfers between devices with their start and end apart: 10, of which 2 were waited for; matrix products, arithmetic and copies ran while one was open for 0% of the time, Pallas kernels for 10%

profile of v10, /device:TPU:0, one launch (start us, length us, event | category | flops | bytes accessed | tf_op | source)
XLA Modules:
  0.0 21.9 jit_solution(11948995072248314343)
XLA Ops:
  0.6 1.4 %shard_map.86 = (f32[112,128]{1,0:T(8,128)S(1)}, bf16[4,64,128]{2,1,0:T(8,128)(2,1)S(1)}, f32[8,64,128]{2,1,0:T(8,128)S(1)}, f32[8,128]{1,0:T(8,128)S(1)}, f32[5,16]{1,0:T(8,128)S(1)}) custom-call(f32[1,4]{1,0:T(1,128)} %refs_0_.1, f32[4,2,128]{2,1,0:T(2,128)} %bitcast.9, bf16[8,64,64]{2,1,0:T(8,128)(2,1)} %bitcast.8, f32[8,64,128]{2,1,0:T(8,128)} %refs_3_.1, ...), custom_call_target="tpu_custom_call" | custom-call | tf_op jit(solution)/shard_map/pallas_call | solution.py:60
  2.0 0.5 %collective-permute-start = (f32[112,128]{1,0:T(8,128)S(1)}, f32[112,128]{1,0:T(8,128)S(1)}, u32[]{:S(2)}, u32[]{:S(2)}) collective-permute-start(f32[112,128]{1,0:T(8,128)S(1)} %get-tuple-element.16.mine_ref), channel_id=1, source_target_pairs={{0,1},{1,0},{2,3},{3,2},{4,5},{5,4},{6,7},{7,6},{8,9},{9,8},{10,11... | collective-permute-start | bytes 172040 | tf_op jit(solution)/shard_map/ppermute | solution.py:21
  2.5 2.6 %collective-permute-start.5 = (bf16[4,64,128]{2,1,0:T(8,128)(2,1)S(1)}, bf16[4,64,128]{2,1,0:T(8,128)(2,1)S(1)}, u32[]{:S(2)}, u32[]{:S(2)}) collective-permute-start(bf16[4,64,128]{2,1,0:T(8,128)(2,1)S(1)} %get-tuple-element.25.one_ref), channel_id=1, source_target_pairs={{0,8},{8,0},{16,24},{24,16},{1,9},{9,1},{17,25},{25,17},{2,10},{10... | collective-permute-start | bytes 196616 | tf_op jit(solution)/shard_map/ppermute | solution.py:21
  5.2 0.0 collective-permute-done.got_ref
  5.2 0.1 shard_map.87
  5.3 1.5 %collective-permute-start.1 = (bf16[560,128]{1,0:T(8,128)(2,1)S(1)}, bf16[560,128]{1,0:T(8,128)(2,1)S(1)}, u32[]{:S(2)}, u32[]{:S(2)}) collective-permute-start(bf16[560,128]{1,0:T(8,128)(2,1)S(1)} %get-tuple-element.20), channel_id=1, source_target_pairs={{0,2},{2,0},{4,6},{6,4},{8,14},{10,12},{12,10},{14,8},{16,18},{18,... | collective-permute-start | bytes 430088 | tf_op jit(solution)/shard_map/ppermute | solution.py:412
  6.8 1.5 %collective-permute-start.3 = (f32[72,128]{1,0:T(8,128)S(1)}, f32[72,128]{1,0:T(8,128)S(1)}, u32[]{:S(2)}, u32[]{:S(2)}) collective-permute-start(f32[72,128]{1,0:T(8,128)S(1)} %get-tuple-element.22.refs_0_.after_ref), channel_id=1, source_target_pairs={{0,6},{2,4},{4,2},{6,0},{8,10},{10,8},{12,14},{14,12},{16,22},{18,... | collective-permute-start | bytes 110600 | tf_op jit(solution)/shard_map/ppermute | solution.py:412
  8.3 0.5 %collective-permute-start.4 = (f32[72,128]{1,0:T(8,128)S(1)}, f32[72,128]{1,0:T(8,128)S(1)}, u32[]{:S(2)}, u32[]{:S(2)}) collective-permute-start(f32[72,128]{1,0:T(8,128)S(1)} %get-tuple-element.22.refs_0_.after_ref), channel_id=1, source_target_pairs={{0,4},{2,6},{4,0},{6,2},{1,5},{3,7},{5,1},{7,3},{8,12},{10,14},{12... | collective-permute-start | bytes 110600 | tf_op jit(solution)/shard_map/ppermute | solution.py:21
  8.8 0.0 collective-permute-done.5.two_ref
  8.8 2.7 %collective-permute-start.6 = (bf16[8,64,128]{2,1,0:T(8,128)(2,1)S(1)}, bf16[8,64,128]{2,1,0:T(8,128)(2,1)S(1)}, u32[]{:S(2)}, u32[]{:S(2)}) collective-permute-start(bf16[8,64,128]{2,1,0:T(8,128)(2,1)S(1)} %shard_map.90.pair_ref), channel_id=1, source_target_pairs={{0,16},{8,24},{16,0},{24,8},{1,17},{9,25},{17,1},{25,9},{2,18},{10... | collective-permute-start | bytes 393224 | tf_op jit(solution)/shard_map/ppermute | solution.py:21
  11.5 0.1 collective-permute-done.1.refs_3_.rows_ref
  11.5 2.1 %collective-permute-start.2 = (bf16[320,128]{1,0:T(8,128)(2,1)S(1)}, bf16[320,128]{1,0:T(8,128)(2,1)S(1)}, u32[]{:S(2)}, u32[]{:S(2)}) collective-permute-start(bf16[320,128]{1,0:T(8,128)(2,1)S(1)} %slice.4), channel_id=1, source_target_pairs={{0,8},{8,0},{16,24},{24,16},{1,9},{9,1},{17,25},{25,17},{2,10},{10... | collective-permute-start | bytes 245768 | tf_op jit(solution)/shard_map/ppermute | solution.py:21
  13.6 0.0 collective-permute-done.3.refs_1_
  13.6 0.0 collective-permute-done.4.refs_2_
  13.6 0.1 shard_map.88
  13.7 2.5 %collective-permute-start.7 = (bf16[64,128]{1,0:T(8,128)(2,1)S(1)}, bf16[64,128]{1,0:T(8,128)(2,1)S(1)}, u32[]{:S(2)}, u32[]{:S(2)}) collective-permute-start(bf16[64,128]{1,0:T(8,128)(2,1)S(1)} %get-tuple-element.27.low0_ref), channel_id=1, source_target_pairs={{0,24},{8,16},{16,8},{24,0},{1,25},{9,17},{17,9},{25,1},{2,26},{10... | collective-permute-start | bytes 49160 | tf_op jit(solution)/shard_map/ppermute | solution.py:21
  16.3 0.2 collective-permute-start.8
  16.5 1.7 %collective-permute-start.9 = (bf16[64,128]{1,0:T(8,128)(2,1)S(1)}, bf16[64,128]{1,0:T(8,128)(2,1)S(1)}, u32[]{:S(2)}, u32[]{:S(2)}) collective-permute-start(bf16[64,128]{1,0:T(8,128)(2,1)S(1)} %get-tuple-element.27.low0_ref), channel_id=1, source_target_pairs={{0,8},{8,0},{16,24},{24,16},{1,9},{9,1},{17,25},{25,17},{2,10},{10... | collective-permute-start | bytes 49160 | tf_op jit(solution)/shard_map/ppermute | solution.py:21
  18.2 0.0 collective-permute-done.2.other_ref
  18.2 1.9 %shard_map.89 = (f32[8,64,128]{2,1,0:T(8,128)S(1)}, f32[4,2,128]{2,1,0:T(2,128)}) custom-call(f32[8,64,128]{2,1,0:T(8,128)S(1)} %get-tuple-element.15.field_ref, f32[8,8,128]{2,1,0:T(8,128)S(1)} %get-tuple-element.18.side_ref, f32[8,128]{1,0:T(8,128)S(1)} %get-tuple-element.19.wide_ref, bf16[560,128]{1,0:T(8,128)(2,1)S(1)} %collective-permute-done.1.refs_3_.rows_ref, ...), custom_call_target="tpu_custom_call" | custom-call | flops 1073741824 | tf_op jit(solution)/shard_map/pallas_call | solution.py:60
  20.1 0.0 collective-permute-done.6.far_ref
  20.1 0.0 collective-permute-done.7.low3_ref
  20.1 0.8 %collective-permute-done.8.low2_ref = bf16[64,128]{1,0:T(8,128)(2,1)S(1)} collective-permute-done((bf16[64,128]{1,0:T(8,128)(2,1)S(1)}, bf16[64,128]{1,0:T(8,128)(2,1)S(1)}, u32[]{:S(2)}, u32[]{:S(2)}) %collective-permute-start.8) | collective-permute-done | bytes 16416 | tf_op jit(solution)/shard_map/ppermute | solution.py:21
  20.9 0.0 collective-permute-done.9.low1_ref
  20.9 1.0 %shard_map.91 = f32[8,64,128]{2,1,0:T(8,128)} custom-call(bf16[8,64,128]{2,1,0:T(8,128)(2,1)S(1)} %shard_map.90.pair_ref, bf16[8,64,128]{2,1,0:T(8,128)(2,1)S(1)} %collective-permute-done.6.far_ref, f32[8,64,128]{2,1,0:T(8,128)S(1)} %get-tuple-element.26.prior_ref, bf16[64,128]{1,0:T(8,128)(2,1)S(1)} %get-tuple-element.27.low0_ref, ...), custom_call_target="tpu_custom_call" | custom-call | tf_op jit(solution)/shard_map/pallas_call | solution.py:60
  (2 shorter events, 0.0 us)
Async XLA Ops:
  2.0 3.2 %collective-permute-start = (f32[112,128]{1,0:T(8,128)S(1)}, f32[112,128]{1,0:T(8,128)S(1)}, u32[]{:S(2)}, u32[]{:S(2)}) collective-permute-start(f32[112,128]{1,0:T(8,128)S(1)} %get-tuple-element.16.mine_ref), channel_id=1, source_target_pairs={{0,1},{1,0},{2,3},{3,2},{4,5},{5,4},{6,7},{7,6},{8,9},{9,8},{10,11... | collective-permute-start | bytes 172040 | tf_op jit(solution)/shard_map/ppermute | solution.py:21
  2.5 6.3 %collective-permute-start.5 = (bf16[4,64,128]{2,1,0:T(8,128)(2,1)S(1)}, bf16[4,64,128]{2,1,0:T(8,128)(2,1)S(1)}, u32[]{:S(2)}, u32[]{:S(2)}) collective-permute-start(bf16[4,64,128]{2,1,0:T(8,128)(2,1)S(1)} %get-tuple-element.25.one_ref), channel_id=1, source_target_pairs={{0,8},{8,0},{16,24},{24,16},{1,9},{9,1},{17,25},{25,17},{2,10},{10... | collective-permute-start | bytes 196616 | tf_op jit(solution)/shard_map/ppermute | solution.py:21
  5.3 6.3 %collective-permute-start.1 = (bf16[560,128]{1,0:T(8,128)(2,1)S(1)}, bf16[560,128]{1,0:T(8,128)(2,1)S(1)}, u32[]{:S(2)}, u32[]{:S(2)}) collective-permute-start(bf16[560,128]{1,0:T(8,128)(2,1)S(1)} %get-tuple-element.20), channel_id=1, source_target_pairs={{0,2},{2,0},{4,6},{6,4},{8,14},{10,12},{12,10},{14,8},{16,18},{18,... | collective-permute-start | bytes 430088 | tf_op jit(solution)/shard_map/ppermute | solution.py:412
  6.8 6.8 %collective-permute-start.3 = (f32[72,128]{1,0:T(8,128)S(1)}, f32[72,128]{1,0:T(8,128)S(1)}, u32[]{:S(2)}, u32[]{:S(2)}) collective-permute-start(f32[72,128]{1,0:T(8,128)S(1)} %get-tuple-element.22.refs_0_.after_ref), channel_id=1, source_target_pairs={{0,6},{2,4},{4,2},{6,0},{8,10},{10,8},{12,14},{14,12},{16,22},{18,... | collective-permute-start | bytes 110600 | tf_op jit(solution)/shard_map/ppermute | solution.py:412
  8.3 5.3 %collective-permute-start.4 = (f32[72,128]{1,0:T(8,128)S(1)}, f32[72,128]{1,0:T(8,128)S(1)}, u32[]{:S(2)}, u32[]{:S(2)}) collective-permute-start(f32[72,128]{1,0:T(8,128)S(1)} %get-tuple-element.22.refs_0_.after_ref), channel_id=1, source_target_pairs={{0,4},{2,6},{4,0},{6,2},{1,5},{3,7},{5,1},{7,3},{8,12},{10,14},{12... | collective-permute-start | bytes 110600 | tf_op jit(solution)/shard_map/ppermute | solution.py:21
  8.8 11.3 %collective-permute-start.6 = (bf16[8,64,128]{2,1,0:T(8,128)(2,1)S(1)}, bf16[8,64,128]{2,1,0:T(8,128)(2,1)S(1)}, u32[]{:S(2)}, u32[]{:S(2)}) collective-permute-start(bf16[8,64,128]{2,1,0:T(8,128)(2,1)S(1)} %shard_map.90.pair_ref), channel_id=1, source_target_pairs={{0,16},{8,24},{16,0},{24,8},{1,17},{9,25},{17,1},{25,9},{2,18},{10... | collective-permute-start | bytes 393224 | tf_op jit(solution)/shard_map/ppermute | solution.py:21
  11.5 6.7 %collective-permute-start.2 = (bf16[320,128]{1,0:T(8,128)(2,1)S(1)}, bf16[320,128]{1,0:T(8,128)(2,1)S(1)}, u32[]{:S(2)}, u32[]{:S(2)}) collective-permute-start(bf16[320,128]{1,0:T(8,128)(2,1)S(1)} %slice.4), channel_id=1, source_target_pairs={{0,8},{8,0},{16,24},{24,16},{1,9},{9,1},{17,25},{25,17},{2,10},{10... | collective-permute-start | bytes 245768 | tf_op jit(solution)/shard_map/ppermute | solution.py:21
  13.7 6.4 %collective-permute-start.7 = (bf16[64,128]{1,0:T(8,128)(2,1)S(1)}, bf16[64,128]{1,0:T(8,128)(2,1)S(1)}, u32[]{:S(2)}, u32[]{:S(2)}) collective-permute-start(bf16[64,128]{1,0:T(8,128)(2,1)S(1)} %get-tuple-element.27.low0_ref), channel_id=1, source_target_pairs={{0,24},{8,16},{16,8},{24,0},{1,25},{9,17},{17,9},{25,1},{2,26},{10... | collective-permute-start | bytes 49160 | tf_op jit(solution)/shard_map/ppermute | solution.py:21
  16.3 4.6 %collective-permute-start.8 = (bf16[64,128]{1,0:T(8,128)(2,1)S(1)}, bf16[64,128]{1,0:T(8,128)(2,1)S(1)}, u32[]{:S(2)}, u32[]{:S(2)}) collective-permute-start(bf16[64,128]{1,0:T(8,128)(2,1)S(1)} %get-tuple-element.27.low0_ref), channel_id=1, source_target_pairs={{0,16},{8,24},{16,0},{24,8},{1,17},{9,25},{17,1},{25,9},{2,18},{10... | collective-permute-start | bytes 49160 | tf_op jit(solution)/shard_map/ppermute | solution.py:21
  16.5 4.4 %collective-permute-start.9 = (bf16[64,128]{1,0:T(8,128)(2,1)S(1)}, bf16[64,128]{1,0:T(8,128)(2,1)S(1)}, u32[]{:S(2)}, u32[]{:S(2)}) collective-permute-start(bf16[64,128]{1,0:T(8,128)(2,1)S(1)} %get-tuple-element.27.low0_ref), channel_id=1, source_target_pairs={{0,8},{8,0},{16,24},{24,16},{1,9},{9,1},{17,25},{25,17},{2,10},{10... | collective-permute-start | bytes 49160 | tf_op jit(solution)/shard_map/ppermute | solution.py:21

commit v11 on v10

--- a/solution.py
+++ b/solution.py
@@ -14,6 +14,7 @@
 PRIOR_FLOPS = 1 << 30
 EDGE_FLOPS = 1 << 30
 JOIN_FLOPS = 1 << 30
+PARTS = 2
 ORDER_FLOPS = 1 << 32
 
 
@@ -96,13 +97,17 @@
     sensors = points // comps
     place = lax.axis_index("px") * lax.axis_size("py") + lax.axis_index("py")
     even = lax.axis_index("py") % 2 == 0
-    total = jnp.zeros((points, real), jnp.float32)
+    packed, field = [], []
     for x in range(beside):
         picks = range(x, rows, beside)
-        packed = jnp.concatenate([kernel_ref[k] for k in picks], axis=1)
-        packed_ref[x] = packed
-        field = jnp.concatenate([field_ref[k].astype(jnp.bfloat16) for k in picks], axis=0)
-        total = total + jnp.dot(packed, field, preferred_element_type=jnp.float32)
+        packed.append(jnp.concatenate([kernel_ref[k] for k in picks], axis=1))
+        packed_ref[x] = packed[-1]
+        field += [field_ref[k].astype(jnp.bfloat16) for k in picks]
+    total = jnp.dot(
+        jnp.concatenate(packed, axis=1),
+        jnp.concatenate(field, axis=0),
+        preferred_element_type=jnp.float32,
+    )
     spot = lax.broadcasted_iota(jnp.int32, (points, real), 0)
     for c in range(comps):
         for k in range(own):
@@ -178,19 +183,15 @@
     chosen = lax.axis_index("px") % 2 == 0
     if lax.axis_size("px") > 2:
         chosen = chosen == (lax.axis_index("freq") % 2 == 0)
-    top = lax.broadcasted_iota(jnp.int32, (TILE, real), 0) == 0
-    step = (rows_ref.shape[0] - base) // SWEEPS
+    spot = lax.broadcasted_iota(jnp.int32, (2 * TILE, real), 0)
+    blocks, tile = [], jnp.zeros((2 * TILE, real), jnp.float32)
     for k in range(SWEEPS):
         last = rows - SWEEPS + k
+        blocks.append(jnp.where(chosen, field_ref[last], field_ref[k]))
+        blocks.append(jnp.where(chosen, side_ref[last], side_ref[k]))
         marks = jnp.where(chosen, wide_ref[last : last + 1], wide_ref[k : k + 1])
-        rows_ref[base + k * step : base + (k + 1) * step] = jnp.concatenate(
-            [
-                jnp.where(chosen, field_ref[last], field_ref[k]),
-                jnp.where(chosen, side_ref[last], side_ref[k]),
-                jnp.where(top, marks, 0.0),
-            ],
-            axis=0,
-        ).astype(jnp.bfloat16)
+        tile = jnp.where(spot == k, marks, tile)
+    rows_ref[base:] = jnp.concatenate(blocks + [tile], axis=0).astype(jnp.bfloat16)
 
 
 def edge(after_ref, got_ref, field_ref, marks_ref, *refs):
@@ -211,11 +212,11 @@
     rest = total
     if part > size:
         rest = jnp.concatenate([total, jnp.zeros((part - size, real), jnp.float32)], axis=0)
-    for k in range(3):
+    for k in range(PARTS):
         low = rest.astype(jnp.bfloat16)
         mixed_ref[k * part : (k + 1) * part] = low
         rest = rest - low.astype(jnp.float32)
-    lay(got_ref, field_ref, marks_ref, far_ref, side_ref, wide_ref, mixed_ref, 3 * part)
+    lay(got_ref, field_ref, marks_ref, far_ref, side_ref, wide_ref, mixed_ref, PARTS * part)
 
 
 def join(one_ref, two_ref, after_ref, out_ref):
@@ -233,8 +234,8 @@
     for got_ref in got_refs:
         if got_ref.dtype == jnp.bfloat16:
             part = packed_rows(size)
-            three = [got_ref[k * part : (k + 1) * part].astype(jnp.float32) for k in range(3)]
-            total = total + (three[0] + three[1] + three[2])[:size]
+            parts = [got_ref[k * part : (k + 1) * part].astype(jnp.float32) for k in range(PARTS)]
+            total = total + sum(parts)[:size]
         else:
             total = total + got_ref[...]
     chunk = min(sensors, real)
@@ -284,7 +285,7 @@
     out.start()
     rows, cols, _ = field_ref.shape
     wide = cols + 2 * SWEEPS
-    step = other_ref.shape[0] // SWEEPS
+    tile = SWEEPS * wide
     mine = rows_ref[rows_ref.shape[0] - other_ref.shape[0] :].astype(jnp.float32)
     other = other_ref[...].astype(jnp.float32)
     even = lax.axis_index("freq") % 2 == 0
@@ -292,14 +293,14 @@
         jnp.where(even, mine, other), jnp.where(even, other, mine), "px"
     )
     for k in range(SWEEPS):
-        state_ref[0, k] = before[k * step : k * step + wide]
-        state_ref[0, SWEEPS + rows + k] = after[k * step : k * step + wide]
+        state_ref[0, k] = before[k * wide : (k + 1) * wide]
+        state_ref[0, SWEEPS + rows + k] = after[k * wide : (k + 1) * wide]
     for x in range(rows):
         state_ref[0, SWEEPS + x] = jnp.concatenate([field_ref[x], side_ref[x]], axis=0)
     marks = (
-        [before[k * step + wide : k * step + wide + 1] for k in range(SWEEPS)]
+        [before[tile + k : tile + k + 1] for k in range(SWEEPS)]
         + [wide_ref[x : x + 1] for x in range(rows)]
-        + [after[k * step + wide : k * step + wide + 1] for k in range(SWEEPS)]
+        + [after[tile + k : tile + k + 1] for k in range(SWEEPS)]
     )
     count, levels = table_ref.shape
     spread = (
@@ -375,7 +376,7 @@
     beside = rows // max(1, min(rows, LANES // cols))
     side = rows // beside
     assert sensors <= TILE * real and cols + 2 * SWEEPS <= LANES
-    assert rows >= SWEEPS and (cols + 2 * SWEEPS + TILE) % 16 == 0
+    assert rows >= SWEEPS and cols % TILE == 0
     rim_rows = rows * (SWEEPS + 1)
     wide_py, wide_px = lax.axis_size("py") > 2, lax.axis_size("px") > 2
     payload, kernel_own, model_field, marks, table, *far_rim = call(
@@ -400,7 +401,7 @@
     kernel_next = swap(kernel_own, "freq", near)
     two = [swap(rim, "py", far("py")) for rim in far_rim]
     summed = ((points + TILE, real), jnp.float32)
-    step = cols + 2 * SWEEPS + TILE
+    rim_size = SWEEPS * (cols + 2 * SWEEPS) + 2 * TILE
     peers, freqs = lax.axis_size("px"), lax.axis_size("freq")
     side_shapes = (
         ((rows, 2 * SWEEPS, real), jnp.float32),
@@ -425,20 +426,20 @@
             spread,
             summed,
             *side_shapes,
-            ((3 * part + SWEEPS * step, real), jnp.bfloat16),
+            ((PARTS * part + rim_size, real), jnp.bfloat16),
         )(payload, got, model_field, marks)
         mixed = by_parity(mixed, near, far("px"))
         cross = by_parity(total, far("px"), near)
         skip = swap(total, "px", lambda i: i ^ 2)
         (kernel_pair,) = call(join, pair_shape, flops=JOIN_FLOPS)(kernel_own, kernel_next, total)
         sums = (total, cross, skip, mixed)
-        rim_rows, sent_rows = mixed, mixed[3 * part :]
+        rim_rows, sent_rows = mixed, mixed[PARTS * part :]
     else:
         (total,) = call(add, summed)(payload, got)
         for bit in bits("py")[1:]:
             (total,) = call(add, summed)(total, swap(total, "py", lambda i: i ^ bit))
         side_rim, wide_marks, rim_rows = call(
-            edge, *side_shapes, ((SWEEPS * step, real), jnp.bfloat16), flops=EDGE_FLOPS
+            edge, *side_shapes, ((rim_size, real), jnp.bfloat16), flops=EDGE_FLOPS
         )(total, got, model_field, marks, *two)
         rim_rows = sent_rows = by_parity(rim_rows, near, far("px") if wide_px else near)
         *steps, last = bits("px")

time: 22 us -> 21.5 us (0.977)
  starting transfers between devices: 15.9 us -> 15.4 us
    ppermute x8, starting transfers between devices: 12.9 us -> 12.4 us  [swap(): lax.ppermute(own, axis, [(i, partner(i)) for i in range(lax.axis_size(axi...]
where the time goes in v11:
time: 21.5 us; the launch traced here: 21.3 us
  starting transfers between devices  15.4 us (72%)
  Pallas kernels  4.44 us (21%)
  waiting for transfers between devices  0.81 us (4%)
  between operations  0.68 us (3%)
    ppermute x8, starting transfers between devices, swap(): lax.ppermute(own, axis, [(i, partner(i)) for i in range(lax.axis_size(axi...  12.4 us
    pallas_call x6, Pallas kernels, run(): pl.pallas_call(fetched if fetch else body, out_shape=[jax.ShapeDtypeStruc...  4.44 us
    ppermute x2, starting transfers between devices, by_parity(): lax.ppermute(own, ('freq', 'px'), [(f * peers + i, f * peers + (odd_partn...  3.01 us
    ppermute x8, waiting for transfers between devices, swap(): lax.ppermute(own, axis, [(i, partner(i)) for i in range(lax.axis_size(axi...  0.81 us
  transfers between devices with their start and end apart: 10, of which 2 were waited for; matrix products, arithmetic and copies ran while one was open for 0% of the time, Pallas kernels for 10%

profile of v11, /device:TPU:0, one launch (start us, length us, event | category | flops | bytes accessed | tf_op | source)
XLA Modules:
  0.0 21.3 jit_solution(1417095695006136482)
XLA Ops:
  0.6 1.4 %shard_map.86 = (f32[112,128]{1,0:T(8,128)S(1)}, bf16[4,64,128]{2,1,0:T(8,128)(2,1)S(1)}, f32[8,64,128]{2,1,0:T(8,128)S(1)}, f32[8,128]{1,0:T(8,128)S(1)}, f32[5,16]{1,0:T(8,128)S(1)}) custom-call(f32[1,4]{1,0:T(1,128)} %refs_0_.1, f32[4,2,128]{2,1,0:T(2,128)} %bitcast.9, bf16[8,64,64]{2,1,0:T(8,128)(2,1)} %bitcast.8, f32[8,64,128]{2,1,0:T(8,128)} %refs_3_.1, ...), custom_call_target="tpu_custom_call" | custom-call | tf_op jit(solution)/shard_map/pallas_call | solution.py:61
  2.0 0.5 %collective-permute-start = (f32[112,128]{1,0:T(8,128)S(1)}, f32[112,128]{1,0:T(8,128)S(1)}, u32[]{:S(2)}, u32[]{:S(2)}) collective-permute-start(f32[112,128]{1,0:T(8,128)S(1)} %get-tuple-element.16.mine_ref), channel_id=1, source_target_pairs={{0,1},{1,0},{2,3},{3,2},{4,5},{5,4},{6,7},{7,6},{8,9},{9,8},{10,11... | collective-permute-start | bytes 172040 | tf_op jit(solution)/shard_map/ppermute | solution.py:22
  2.5 2.6 %collective-permute-start.5 = (bf16[4,64,128]{2,1,0:T(8,128)(2,1)S(1)}, bf16[4,64,128]{2,1,0:T(8,128)(2,1)S(1)}, u32[]{:S(2)}, u32[]{:S(2)}) collective-permute-start(bf16[4,64,128]{2,1,0:T(8,128)(2,1)S(1)} %get-tuple-element.25.one_ref), channel_id=1, source_target_pairs={{0,8},{8,0},{16,24},{24,16},{1,9},{9,1},{17,25},{25,17},{2,10},{10... | collective-permute-start | bytes 196616 | tf_op jit(solution)/shard_map/ppermute | solution.py:22
  5.2 0.0 collective-permute-done.got_ref
  5.2 0.1 shard_map.87
  5.3 1.5 %collective-permute-start.1 = (bf16[464,128]{1,0:T(8,128)(2,1)S(1)}, bf16[464,128]{1,0:T(8,128)(2,1)S(1)}, u32[]{:S(2)}, u32[]{:S(2)}) collective-permute-start(bf16[464,128]{1,0:T(8,128)(2,1)S(1)} %get-tuple-element.20), channel_id=1, source_target_pairs={{0,2},{2,0},{4,6},{6,4},{8,14},{10,12},{12,10},{14,8},{16,18},{18,... | collective-permute-start | bytes 356360 | tf_op jit(solution)/shard_map/ppermute | solution.py:413
  6.8 1.5 %collective-permute-start.3 = (f32[72,128]{1,0:T(8,128)S(1)}, f32[72,128]{1,0:T(8,128)S(1)}, u32[]{:S(2)}, u32[]{:S(2)}) collective-permute-start(f32[72,128]{1,0:T(8,128)S(1)} %get-tuple-element.22.refs_0_.after_ref), channel_id=1, source_target_pairs={{0,6},{2,4},{4,2},{6,0},{8,10},{10,8},{12,14},{14,12},{16,22},{18,... | collective-permute-start | bytes 110600 | tf_op jit(solution)/shard_map/ppermute | solution.py:413
  8.3 0.5 %collective-permute-start.4 = (f32[72,128]{1,0:T(8,128)S(1)}, f32[72,128]{1,0:T(8,128)S(1)}, u32[]{:S(2)}, u32[]{:S(2)}) collective-permute-start(f32[72,128]{1,0:T(8,128)S(1)} %get-tuple-element.22.refs_0_.after_ref), channel_id=1, source_target_pairs={{0,4},{2,6},{4,0},{6,2},{1,5},{3,7},{5,1},{7,3},{8,12},{10,14},{12... | collective-permute-start | bytes 110600 | tf_op jit(solution)/shard_map/ppermute | solution.py:22
  8.8 0.0 collective-permute-done.5.two_ref
  8.8 2.7 %collective-permute-start.6 = (bf16[8,64,128]{2,1,0:T(8,128)(2,1)S(1)}, bf16[8,64,128]{2,1,0:T(8,128)(2,1)S(1)}, u32[]{:S(2)}, u32[]{:S(2)}) collective-permute-start(bf16[8,64,128]{2,1,0:T(8,128)(2,1)S(1)} %shard_map.90.pair_ref), channel_id=1, source_target_pairs={{0,16},{8,24},{16,0},{24,8},{1,17},{9,25},{17,1},{25,9},{2,18},{10... | collective-permute-start | bytes 393224 | tf_op jit(solution)/shard_map/ppermute | solution.py:22
  11.4 0.0 collective-permute-done.1.refs_3_.rows_ref
  11.5 1.6 %collective-permute-start.2 = (bf16[304,128]{1,0:T(8,128)(2,1)S(1)}, bf16[304,128]{1,0:T(8,128)(2,1)S(1)}, u32[]{:S(2)}, u32[]{:S(2)}) collective-permute-start(bf16[304,128]{1,0:T(8,128)(2,1)S(1)} %slice.4), channel_id=1, source_target_pairs={{0,8},{8,0},{16,24},{24,16},{1,9},{9,1},{17,25},{25,17},{2,10},{10... | collective-permute-start | bytes 233480 | tf_op jit(solution)/shard_map/ppermute | solution.py:22
  13.0 0.0 collective-permute-done.3.refs_1_
  13.0 0.0 collective-permute-done.4.refs_2_
  13.0 0.1 shard_map.88
  13.2 2.5 %collective-permute-start.7 = (bf16[64,128]{1,0:T(8,128)(2,1)S(1)}, bf16[64,128]{1,0:T(8,128)(2,1)S(1)}, u32[]{:S(2)}, u32[]{:S(2)}) collective-permute-start(bf16[64,128]{1,0:T(8,128)(2,1)S(1)} %get-tuple-element.27.low0_ref), channel_id=1, source_target_pairs={{0,24},{8,16},{16,8},{24,0},{1,25},{9,17},{17,9},{25,1},{2,26},{10... | collective-permute-start | bytes 49160 | tf_op jit(solution)/shard_map/ppermute | solution.py:22
  15.7 0.2 collective-permute-start.8
  15.9 1.7 %collective-permute-start.9 = (bf16[64,128]{1,0:T(8,128)(2,1)S(1)}, bf16[64,128]{1,0:T(8,128)(2,1)S(1)}, u32[]{:S(2)}, u32[]{:S(2)}) collective-permute-start(bf16[64,128]{1,0:T(8,128)(2,1)S(1)} %get-tuple-element.27.low0_ref), channel_id=1, source_target_pairs={{0,8},{8,0},{16,24},{24,16},{1,9},{9,1},{17,25},{25,17},{2,10},{10... | collective-permute-start | bytes 49160 | tf_op jit(solution)/shard_map/ppermute | solution.py:22
  17.6 0.5 %collective-permute-done.2.other_ref = bf16[304,128]{1,0:T(8,128)(2,1)S(1)} collective-permute-done((bf16[304,128]{1,0:T(8,128)(2,1)S(1)}, bf16[304,128]{1,0:T(8,128)(2,1)S(1)}, u32[]{:S(2)}, u32[]{:S(2)}) %collective-permute-start.2) | collective-permute-done | bytes 77856 | tf_op jit(solution)/shard_map/ppermute | solution.py:22
  18.1 1.9 %shard_map.89 = (f32[8,64,128]{2,1,0:T(8,128)S(1)}, f32[4,2,128]{2,1,0:T(2,128)}) custom-call(f32[8,64,128]{2,1,0:T(8,128)S(1)} %get-tuple-element.15.field_ref, f32[8,8,128]{2,1,0:T(8,128)S(1)} %get-tuple-element.18.side_ref, f32[8,128]{1,0:T(8,128)S(1)} %get-tuple-element.19.wide_ref, bf16[464,128]{1,0:T(8,128)(2,1)S(1)} %collective-permute-done.1.refs_3_.rows_ref, ...), custom_call_target="tpu_custom_call" | custom-call | flops 1073741824 | tf_op jit(solution)/shard_map/pallas_call | solution.py:61
  20.0 0.0 collective-permute-done.7.low3_ref
  20.1 0.3 %collective-permute-done.8.low2_ref = bf16[64,128]{1,0:T(8,128)(2,1)S(1)} collective-permute-done((bf16[64,128]{1,0:T(8,128)(2,1)S(1)}, bf16[64,128]{1,0:T(8,128)(2,1)S(1)}, u32[]{:S(2)}, u32[]{:S(2)}) %collective-permute-start.8) | collective-permute-done | bytes 16416 | tf_op jit(solution)/shard_map/ppermute | solution.py:22
  20.3 0.0 collective-permute-done.9.low1_ref
  20.3 0.0 collective-permute-done.6.far_ref
  20.4 1.0 %shard_map.91 = f32[8,64,128]{2,1,0:T(8,128)} custom-call(bf16[8,64,128]{2,1,0:T(8,128)(2,1)S(1)} %shard_map.90.pair_ref, bf16[8,64,128]{2,1,0:T(8,128)(2,1)S(1)} %collective-permute-done.6.far_ref, f32[8,64,128]{2,1,0:T(8,128)S(1)} %get-tuple-element.26.prior_ref, bf16[64,128]{1,0:T(8,128)(2,1)S(1)} %get-tuple-element.27.low0_ref, ...), custom_call_target="tpu_custom_call" | custom-call | tf_op jit(solution)/shard_map/pallas_call | solution.py:61
  (2 shorter events, 0.0 us)
Async XLA Ops:
  2.0 3.2 %collective-permute-start = (f32[112,128]{1,0:T(8,128)S(1)}, f32[112,128]{1,0:T(8,128)S(1)}, u32[]{:S(2)}, u32[]{:S(2)}) collective-permute-start(f32[112,128]{1,0:T(8,128)S(1)} %get-tuple-element.16.mine_ref), channel_id=1, source_target_pairs={{0,1},{1,0},{2,3},{3,2},{4,5},{5,4},{6,7},{7,6},{8,9},{9,8},{10,11... | collective-permute-start | bytes 172040 | tf_op jit(solution)/shard_map/ppermute | solution.py:22
  2.5 6.3 %collective-permute-start.5 = (bf16[4,64,128]{2,1,0:T(8,128)(2,1)S(1)}, bf16[4,64,128]{2,1,0:T(8,128)(2,1)S(1)}, u32[]{:S(2)}, u32[]{:S(2)}) collective-permute-start(bf16[4,64,128]{2,1,0:T(8,128)(2,1)S(1)} %get-tuple-element.25.one_ref), channel_id=1, source_target_pairs={{0,8},{8,0},{16,24},{24,16},{1,9},{9,1},{17,25},{25,17},{2,10},{10... | collective-permute-start | bytes 196616 | tf_op jit(solution)/shard_map/ppermute | solution.py:22
  5.3 6.2 %collective-permute-start.1 = (bf16[464,128]{1,0:T(8,128)(2,1)S(1)}, bf16[464,128]{1,0:T(8,128)(2,1)S(1)}, u32[]{:S(2)}, u32[]{:S(2)}) collective-permute-start(bf16[464,128]{1,0:T(8,128)(2,1)S(1)} %get-tuple-element.20), channel_id=1, source_target_pairs={{0,2},{2,0},{4,6},{6,4},{8,14},{10,12},{12,10},{14,8},{16,18},{18,... | collective-permute-start | bytes 356360 | tf_op jit(solution)/shard_map/ppermute | solution.py:413
  6.8 6.3 %collective-permute-start.3 = (f32[72,128]{1,0:T(8,128)S(1)}, f32[72,128]{1,0:T(8,128)S(1)}, u32[]{:S(2)}, u32[]{:S(2)}) collective-permute-start(f32[72,128]{1,0:T(8,128)S(1)} %get-tuple-element.22.refs_0_.after_ref), channel_id=1, source_target_pairs={{0,6},{2,4},{4,2},{6,0},{8,10},{10,8},{12,14},{14,12},{16,22},{18,... | collective-permute-start | bytes 110600 | tf_op jit(solution)/shard_map/ppermute | solution.py:413
  8.3 4.8 %collective-permute-start.4 = (f32[72,128]{1,0:T(8,128)S(1)}, f32[72,128]{1,0:T(8,128)S(1)}, u32[]{:S(2)}, u32[]{:S(2)}) collective-permute-start(f32[72,128]{1,0:T(8,128)S(1)} %get-tuple-element.22.refs_0_.after_ref), channel_id=1, source_target_pairs={{0,4},{2,6},{4,0},{6,2},{1,5},{3,7},{5,1},{7,3},{8,12},{10,14},{12... | collective-permute-start | bytes 110600 | tf_op jit(solution)/shard_map/ppermute | solution.py:22
  8.8 11.6 %collective-permute-start.6 = (bf16[8,64,128]{2,1,0:T(8,128)(2,1)S(1)}, bf16[8,64,128]{2,1,0:T(8,128)(2,1)S(1)}, u32[]{:S(2)}, u32[]{:S(2)}) collective-permute-start(bf16[8,64,128]{2,1,0:T(8,128)(2,1)S(1)} %shard_map.90.pair_ref), channel_id=1, source_target_pairs={{0,16},{8,24},{16,0},{24,8},{1,17},{9,25},{17,1},{25,9},{2,18},{10... | collective-permute-start | bytes 393224 | tf_op jit(solution)/shard_map/ppermute | solution.py:22
  11.5 6.7 %collective-permute-start.2 = (bf16[304,128]{1,0:T(8,128)(2,1)S(1)}, bf16[304,128]{1,0:T(8,128)(2,1)S(1)}, u32[]{:S(2)}, u32[]{:S(2)}) collective-permute-start(bf16[304,128]{1,0:T(8,128)(2,1)S(1)} %slice.4), channel_id=1, source_target_pairs={{0,8},{8,0},{16,24},{24,16},{1,9},{9,1},{17,25},{25,17},{2,10},{10... | collective-permute-start | bytes 233480 | tf_op jit(solution)/shard_map/ppermute | solution.py:22
  13.2 6.9 %collective-permute-start.7 = (bf16[64,128]{1,0:T(8,128)(2,1)S(1)}, bf16[64,128]{1,0:T(8,128)(2,1)S(1)}, u32[]{:S(2)}, u32[]{:S(2)}) collective-permute-start(bf16[64,128]{1,0:T(8,128)(2,1)S(1)} %get-tuple-element.27.low0_ref), channel_id=1, source_target_pairs={{0,24},{8,16},{16,8},{24,0},{1,25},{9,17},{17,9},{25,1},{2,26},{10... | collective-permute-start | bytes 49160 | tf_op jit(solution)/shard_map/ppermute | solution.py:22
  15.7 4.6 %collective-permute-start.8 = (bf16[64,128]{1,0:T(8,128)(2,1)S(1)}, bf16[64,128]{1,0:T(8,128)(2,1)S(1)}, u32[]{:S(2)}, u32[]{:S(2)}) collective-permute-start(bf16[64,128]{1,0:T(8,128)(2,1)S(1)} %get-tuple-element.27.low0_ref), channel_id=1, source_target_pairs={{0,16},{8,24},{16,0},{24,8},{1,17},{9,25},{17,1},{25,9},{2,18},{10... | collective-permute-start | bytes 49160 | tf_op jit(solution)/shard_map/ppermute | solution.py:22
  15.9 4.5 %collective-permute-start.9 = (bf16[64,128]{1,0:T(8,128)(2,1)S(1)}, bf16[64,128]{1,0:T(8,128)(2,1)S(1)}, u32[]{:S(2)}, u32[]{:S(2)}) collective-permute-start(bf16[64,128]{1,0:T(8,128)(2,1)S(1)} %get-tuple-element.27.low0_ref), channel_id=1, source_target_pairs={{0,8},{8,0},{16,24},{24,16},{1,9},{9,1},{17,25},{25,17},{2,10},{10... | collective-permute-start | bytes 49160 | tf_op jit(solution)/shard_map/ppermute | solution.py:22

commit v12 on v11

--- a/solution.py
+++ b/solution.py
@@ -14,7 +14,6 @@
 PRIOR_FLOPS = 1 << 30
 EDGE_FLOPS = 1 << 30
 JOIN_FLOPS = 1 << 30
-PARTS = 2
 ORDER_FLOPS = 1 << 32
 
 
@@ -36,24 +35,22 @@
     return lambda i: (((i + 1) ^ 1) - 1) % lax.axis_size(axis)
 
 
-def call(body, *out_shapes, fetch=False, scratch=(), stored=(), flops=0):
+def call(body, *out_shapes, fetch=False, keep=(), scratch=(), stored=(), flops=0):
     def run(*operands):
-        count = len(operands)
+        count, kept = len(operands), dict(keep)
         if fetch:
             operands = [pltpu.with_memory_space_constraint(x, pltpu.HBM) for x in operands]
 
         def fetched(*refs):
-            outs, held, sems = (
-                refs[count : count + len(out_shapes)],
-                refs[count + len(out_shapes) : -1],
-                refs[-1],
-            )
+            outs = refs[count : count + len(out_shapes)]
+            room, sems = iter(refs[count + len(out_shapes) : -1]), refs[-1]
+            held = [outs[kept[k]] if k in kept else next(room) for k in range(count)]
             copies = [
                 pltpu.make_async_copy(src, dst, sems.at[k])
                 for k, (src, dst) in enumerate(zip(refs[:count], held))
             ]
-            for copy in copies:
-                copy.start()
+            for k in sorted(range(count), key=lambda k: -operands[k].size):
+                copies[k].start()
             for copy in copies:
                 copy.wait()
             body(*held, *outs)
@@ -67,7 +64,7 @@
                 for k in range(len(out_shapes))
             ],
             scratch_shapes=list(scratch)
-            + [pltpu.VMEM(x.shape, x.dtype) for x in operands] * fetch
+            + [pltpu.VMEM(x.shape, x.dtype) for k, x in enumerate(operands) if k not in kept] * fetch
             + [pltpu.SemaphoreType.DMA((count,))] * fetch,
             compiler_params=pltpu.CompilerParams(vmem_limit_bytes=VMEM_BYTES),
             cost_estimate=pl.CostEstimate(flops=flops, bytes_accessed=0, transcendentals=0),
@@ -86,7 +83,7 @@
     coupling_ref,
     pay_ref,
     packed_ref,
-    held_ref,
+    _,
     marks_ref,
     table_ref,
     *far_ref,
@@ -121,7 +118,6 @@
     for k in range(own):
         noise = noise + jnp.where(spot == place * own + k, noise_ref[0:1, k : k + 1], 0.0)
     pay_ref[points : points + TILE] = noise
-    held_ref[...] = field_ref[...]
     coupling = coupling_ref[...]
     table_ref[0:1] = kappa_ref[...] + jnp.sum(coupling, axis=0, keepdims=True)
     table_ref[1:] = coupling
@@ -199,24 +195,18 @@
     lay(got_ref, field_ref, marks_ref, far_ref, side_ref, wide_ref, rows_ref, 0)
 
 
-def packed_rows(size):
-    return -(-size // 16) * 16
-
-
 def spread(mine_ref, got_ref, field_ref, marks_ref, *refs):
     *far_ref, out_ref, side_ref, wide_ref, mixed_ref = refs
     size, real = out_ref.shape
     total = mine_ref[:size] + got_ref[:size]
     out_ref[...] = total
-    part = packed_rows(size)
-    rest = total
-    if part > size:
-        rest = jnp.concatenate([total, jnp.zeros((part - size, real), jnp.float32)], axis=0)
-    for k in range(PARTS):
-        low = rest.astype(jnp.bfloat16)
-        mixed_ref[k * part : (k + 1) * part] = low
-        rest = rest - low.astype(jnp.float32)
-    lay(got_ref, field_ref, marks_ref, far_ref, side_ref, wide_ref, mixed_ref, PARTS * part)
+    points = size - TILE
+    high = total.astype(jnp.bfloat16).astype(jnp.float32)
+    low = total - high
+    mixed_ref[: 2 * size] = jnp.concatenate(
+        [high[:points], low[:points], high[points:], low[points:]], axis=0
+    ).astype(jnp.bfloat16)
+    lay(got_ref, field_ref, marks_ref, far_ref, side_ref, wide_ref, mixed_ref, 2 * size)
 
 
 def join(one_ref, two_ref, after_ref, out_ref):
@@ -233,9 +223,10 @@
     size = total.shape[0]
     for got_ref in got_refs:
         if got_ref.dtype == jnp.bfloat16:
-            part = packed_rows(size)
-            parts = [got_ref[k * part : (k + 1) * part].astype(jnp.float32) for k in range(PARTS)]
-            total = total + sum(parts)[:size]
+            parts = got_ref[: 2 * size].astype(jnp.float32)
+            sums = parts[:points] + parts[points : 2 * points]
+            noises = parts[2 * points : 2 * points + TILE] + parts[2 * points + TILE :]
+            total = total + jnp.concatenate([sums, noises], axis=0)
         else:
             total = total + got_ref[...]
     chunk = min(sensors, real)
@@ -376,7 +367,7 @@
     beside = rows // max(1, min(rows, LANES // cols))
     side = rows // beside
     assert sensors <= TILE * real and cols + 2 * SWEEPS <= LANES
-    assert rows >= SWEEPS and cols % TILE == 0
+    assert rows >= SWEEPS and cols % TILE == 0 and points % 16 == 0
     rim_rows = rows * (SWEEPS + 1)
     wide_py, wide_px = lax.axis_size("py") > 2, lax.axis_size("px") > 2
     payload, kernel_own, model_field, marks, table, *far_rim = call(
@@ -388,6 +379,7 @@
         ((1 + coupling_table.shape[0], coupling_table.shape[1]), jnp.float32),
         *[((rim_rows, real), jnp.float32)] * wide_py,
         fetch=True,
+        keep=((3, 2),),
     )(
         noise_scale,
         observed[0],
@@ -421,19 +413,19 @@
         )
 
     if peers == 4 and lax.axis_size("py") == 2:
-        part = packed_rows(points + TILE)
+        part = 2 * (points + TILE)
         total, side_rim, wide_marks, mixed = call(
             spread,
             summed,
             *side_shapes,
-            ((PARTS * part + rim_size, real), jnp.bfloat16),
+            ((part + rim_size, real), jnp.bfloat16),
         )(payload, got, model_field, marks)
         mixed = by_parity(mixed, near, far("px"))
         cross = by_parity(total, far("px"), near)
         skip = swap(total, "px", lambda i: i ^ 2)
         (kernel_pair,) = call(join, pair_shape, flops=JOIN_FLOPS)(kernel_own, kernel_next, total)
         sums = (total, cross, skip, mixed)
-        rim_rows, sent_rows = mixed, mixed[PARTS * part :]
+        rim_rows, sent_rows = mixed, mixed[part:]
     else:
         (total,) = call(add, summed)(payload, got)
         for bit in bits("py")[1:]:

time: 21.5 us -> 21.3 us (level)
  no operation moved by 1% of the time
where the time goes in v12:
time: 21.3 us; the launch traced here: 21.2 us
  starting transfers between devices  15.3 us (72%)
  Pallas kernels  4.37 us (21%)
  waiting for transfers between devices  0.81 us (4%)
  between operations  0.68 us (3%)
    ppermute x8, starting transfers between devices, swap(): lax.ppermute(own, axis, [(i, partner(i)) for i in range(lax.axis_size(axi...  12.3 us
    pallas_call x6, Pallas kernels, run(): pl.pallas_call(fetched if fetch else body, out_shape=[jax.ShapeDtypeStruc...  4.37 us
    ppermute x2, starting transfers between devices, by_parity(): lax.ppermute(own, ('freq', 'px'), [(f * peers + i, f * peers + (odd_partn...  3.01 us
    ppermute x8, waiting for transfers between devices, swap(): lax.ppermute(own, axis, [(i, partner(i)) for i in range(lax.axis_size(axi...  0.8 us
  transfers between devices with their start and end apart: 10, of which 2 were waited for; matrix products, arithmetic and copies ran while one was open for 0% of the time, Pallas kernels for 10%

profile of v12, /device:TPU:0, one launch (start us, length us, event | category | flops | bytes accessed | tf_op | source)
XLA Modules:
  0.0 21.2 jit_solution(6997180340371824298)
XLA Ops:
  0.6 1.3 %shard_map.86 = (f32[112,128]{1,0:T(8,128)S(1)}, bf16[4,64,128]{2,1,0:T(8,128)(2,1)S(1)}, f32[8,64,128]{2,1,0:T(8,128)S(1)}, f32[8,128]{1,0:T(8,128)S(1)}, f32[5,16]{1,0:T(8,128)S(1)}) custom-call(f32[1,4]{1,0:T(1,128)} %refs_0_.1, f32[4,2,128]{2,1,0:T(2,128)} %bitcast.9, bf16[8,64,64]{2,1,0:T(8,128)(2,1)} %bitcast.8, f32[8,64,128]{2,1,0:T(8,128)} %refs_3_.1, ...), custom_call_target="tpu_custom_call" | custom-call | tf_op jit(solution)/shard_map/pallas_call | solution.py:58
  1.9 0.5 %collective-permute-start = (f32[112,128]{1,0:T(8,128)S(1)}, f32[112,128]{1,0:T(8,128)S(1)}, u32[]{:S(2)}, u32[]{:S(2)}) collective-permute-start(f32[112,128]{1,0:T(8,128)S(1)} %get-tuple-element.16.mine_ref), channel_id=1, source_target_pairs={{0,1},{1,0},{2,3},{3,2},{4,5},{5,4},{6,7},{7,6},{8,9},{9,8},{10,11... | collective-permute-start | bytes 172040 | tf_op jit(solution)/shard_map/ppermute | solution.py:21
  2.4 2.6 %collective-permute-start.5 = (bf16[4,64,128]{2,1,0:T(8,128)(2,1)S(1)}, bf16[4,64,128]{2,1,0:T(8,128)(2,1)S(1)}, u32[]{:S(2)}, u32[]{:S(2)}) collective-permute-start(bf16[4,64,128]{2,1,0:T(8,128)(2,1)S(1)} %get-tuple-element.25.one_ref), channel_id=1, source_target_pairs={{0,8},{8,0},{16,24},{24,16},{1,9},{9,1},{17,25},{25,17},{2,10},{10... | collective-permute-start | bytes 196616 | tf_op jit(solution)/shard_map/ppermute | solution.py:21
  5.1 0.0 collective-permute-done.got_ref
  5.1 0.1 shard_map.87
  5.2 1.5 %collective-permute-start.1 = (bf16[448,128]{1,0:T(8,128)(2,1)S(1)}, bf16[448,128]{1,0:T(8,128)(2,1)S(1)}, u32[]{:S(2)}, u32[]{:S(2)}) collective-permute-start(bf16[448,128]{1,0:T(8,128)(2,1)S(1)} %get-tuple-element.20), channel_id=1, source_target_pairs={{0,2},{2,0},{4,6},{6,4},{8,14},{10,12},{12,10},{14,8},{16,18},{18,... | collective-permute-start | bytes 344072 | tf_op jit(solution)/shard_map/ppermute | solution.py:405
  6.7 1.5 %collective-permute-start.3 = (f32[72,128]{1,0:T(8,128)S(1)}, f32[72,128]{1,0:T(8,128)S(1)}, u32[]{:S(2)}, u32[]{:S(2)}) collective-permute-start(f32[72,128]{1,0:T(8,128)S(1)} %get-tuple-element.22.refs_0_.after_ref), channel_id=1, source_target_pairs={{0,6},{2,4},{4,2},{6,0},{8,10},{10,8},{12,14},{14,12},{16,22},{18,... | collective-permute-start | bytes 110600 | tf_op jit(solution)/shard_map/ppermute | solution.py:405
  8.2 0.5 %collective-permute-start.4 = (f32[72,128]{1,0:T(8,128)S(1)}, f32[72,128]{1,0:T(8,128)S(1)}, u32[]{:S(2)}, u32[]{:S(2)}) collective-permute-start(f32[72,128]{1,0:T(8,128)S(1)} %get-tuple-element.22.refs_0_.after_ref), channel_id=1, source_target_pairs={{0,4},{2,6},{4,0},{6,2},{1,5},{3,7},{5,1},{7,3},{8,12},{10,14},{12... | collective-permute-start | bytes 110600 | tf_op jit(solution)/shard_map/ppermute | solution.py:21
  8.7 0.0 collective-permute-done.5.two_ref
  8.7 2.7 %collective-permute-start.6 = (bf16[8,64,128]{2,1,0:T(8,128)(2,1)S(1)}, bf16[8,64,128]{2,1,0:T(8,128)(2,1)S(1)}, u32[]{:S(2)}, u32[]{:S(2)}) collective-permute-start(bf16[8,64,128]{2,1,0:T(8,128)(2,1)S(1)} %shard_map.90.pair_ref), channel_id=1, source_target_pairs={{0,16},{8,24},{16,0},{24,8},{1,17},{9,25},{17,1},{25,9},{2,18},{10... | collective-permute-start | bytes 393224 | tf_op jit(solution)/shard_map/ppermute | solution.py:21
  11.4 0.0 collective-permute-done.1.refs_3_.rows_ref
  11.4 1.5 %collective-permute-start.2 = (bf16[304,128]{1,0:T(8,128)(2,1)S(1)}, bf16[304,128]{1,0:T(8,128)(2,1)S(1)}, u32[]{:S(2)}, u32[]{:S(2)}) collective-permute-start(bf16[304,128]{1,0:T(8,128)(2,1)S(1)} %slice.4), channel_id=1, source_target_pairs={{0,8},{8,0},{16,24},{24,16},{1,9},{9,1},{17,25},{25,17},{2,10},{10... | collective-permute-start | bytes 233480 | tf_op jit(solution)/shard_map/ppermute | solution.py:21
  12.9 0.0 collective-permute-done.3.refs_1_
  12.9 0.0 collective-permute-done.4.refs_2_
  12.9 0.1 shard_map.88
  13.0 2.5 %collective-permute-start.7 = (bf16[64,128]{1,0:T(8,128)(2,1)S(1)}, bf16[64,128]{1,0:T(8,128)(2,1)S(1)}, u32[]{:S(2)}, u32[]{:S(2)}) collective-permute-start(bf16[64,128]{1,0:T(8,128)(2,1)S(1)} %get-tuple-element.27.low0_ref), channel_id=1, source_target_pairs={{0,24},{8,16},{16,8},{24,0},{1,25},{9,17},{17,9},{25,1},{2,26},{10... | collective-permute-start | bytes 49160 | tf_op jit(solution)/shard_map/ppermute | solution.py:21
  15.5 0.2 collective-permute-start.8
  15.7 1.7 %collective-permute-start.9 = (bf16[64,128]{1,0:T(8,128)(2,1)S(1)}, bf16[64,128]{1,0:T(8,128)(2,1)S(1)}, u32[]{:S(2)}, u32[]{:S(2)}) collective-permute-start(bf16[64,128]{1,0:T(8,128)(2,1)S(1)} %get-tuple-element.27.low0_ref), channel_id=1, source_target_pairs={{0,8},{8,0},{16,24},{24,16},{1,9},{9,1},{17,25},{25,17},{2,10},{10... | collective-permute-start | bytes 49160 | tf_op jit(solution)/shard_map/ppermute | solution.py:21
  17.5 0.5 %collective-permute-done.2.other_ref = bf16[304,128]{1,0:T(8,128)(2,1)S(1)} collective-permute-done((bf16[304,128]{1,0:T(8,128)(2,1)S(1)}, bf16[304,128]{1,0:T(8,128)(2,1)S(1)}, u32[]{:S(2)}, u32[]{:S(2)}) %collective-permute-start.2) | collective-permute-done | bytes 77856 | tf_op jit(solution)/shard_map/ppermute | solution.py:21
  18.0 1.9 %shard_map.89 = (f32[8,64,128]{2,1,0:T(8,128)S(1)}, f32[4,2,128]{2,1,0:T(2,128)}) custom-call(f32[8,64,128]{2,1,0:T(8,128)S(1)} %get-tuple-element.15.field_ref, f32[8,8,128]{2,1,0:T(8,128)S(1)} %get-tuple-element.18.side_ref, f32[8,128]{1,0:T(8,128)S(1)} %get-tuple-element.19.wide_ref, bf16[448,128]{1,0:T(8,128)(2,1)S(1)} %collective-permute-done.1.refs_3_.rows_ref, ...), custom_call_target="tpu_custom_call" | custom-call | flops 1073741824 | tf_op jit(solution)/shard_map/pallas_call | solution.py:58
  19.9 0.0 collective-permute-done.7.low3_ref
  19.9 0.2 %collective-permute-done.8.low2_ref = bf16[64,128]{1,0:T(8,128)(2,1)S(1)} collective-permute-done((bf16[64,128]{1,0:T(8,128)(2,1)S(1)}, bf16[64,128]{1,0:T(8,128)(2,1)S(1)}, u32[]{:S(2)}, u32[]{:S(2)}) %collective-permute-start.8) | collective-permute-done | bytes 16416 | tf_op jit(solution)/shard_map/ppermute | solution.py:21
  20.2 0.0 collective-permute-done.9.low1_ref
  20.2 0.0 collective-permute-done.6.far_ref
  20.2 1.0 %shard_map.91 = f32[8,64,128]{2,1,0:T(8,128)} custom-call(bf16[8,64,128]{2,1,0:T(8,128)(2,1)S(1)} %shard_map.90.pair_ref, bf16[8,64,128]{2,1,0:T(8,128)(2,1)S(1)} %collective-permute-done.6.far_ref, f32[8,64,128]{2,1,0:T(8,128)S(1)} %get-tuple-element.26.prior_ref, bf16[64,128]{1,0:T(8,128)(2,1)S(1)} %get-tuple-element.27.low0_ref, ...), custom_call_target="tpu_custom_call" | custom-call | tf_op jit(solution)/shard_map/pallas_call | solution.py:58
  (2 shorter events, 0.0 us)
Async XLA Ops:
  1.9 3.2 %collective-permute-start = (f32[112,128]{1,0:T(8,128)S(1)}, f32[112,128]{1,0:T(8,128)S(1)}, u32[]{:S(2)}, u32[]{:S(2)}) collective-permute-start(f32[112,128]{1,0:T(8,128)S(1)} %get-tuple-element.16.mine_ref), channel_id=1, source_target_pairs={{0,1},{1,0},{2,3},{3,2},{4,5},{5,4},{6,7},{7,6},{8,9},{9,8},{10,11... | collective-permute-start | bytes 172040 | tf_op jit(solution)/shard_map/ppermute | solution.py:21
  2.4 6.3 %collective-permute-start.5 = (bf16[4,64,128]{2,1,0:T(8,128)(2,1)S(1)}, bf16[4,64,128]{2,1,0:T(8,128)(2,1)S(1)}, u32[]{:S(2)}, u32[]{:S(2)}) collective-permute-start(bf16[4,64,128]{2,1,0:T(8,128)(2,1)S(1)} %get-tuple-element.25.one_ref), channel_id=1, source_target_pairs={{0,8},{8,0},{16,24},{24,16},{1,9},{9,1},{17,25},{25,17},{2,10},{10... | collective-permute-start | bytes 196616 | tf_op jit(solution)/shard_map/ppermute | solution.py:21
  5.2 6.2 %collective-permute-start.1 = (bf16[448,128]{1,0:T(8,128)(2,1)S(1)}, bf16[448,128]{1,0:T(8,128)(2,1)S(1)}, u32[]{:S(2)}, u32[]{:S(2)}) collective-permute-start(bf16[448,128]{1,0:T(8,128)(2,1)S(1)} %get-tuple-element.20), channel_id=1, source_target_pairs={{0,2},{2,0},{4,6},{6,4},{8,14},{10,12},{12,10},{14,8},{16,18},{18,... | collective-permute-start | bytes 344072 | tf_op jit(solution)/shard_map/ppermute | solution.py:405
  6.7 6.2 %collective-permute-start.3 = (f32[72,128]{1,0:T(8,128)S(1)}, f32[72,128]{1,0:T(8,128)S(1)}, u32[]{:S(2)}, u32[]{:S(2)}) collective-permute-start(f32[72,128]{1,0:T(8,128)S(1)} %get-tuple-element.22.refs_0_.after_ref), channel_id=1, source_target_pairs={{0,6},{2,4},{4,2},{6,0},{8,10},{10,8},{12,14},{14,12},{16,22},{18,... | collective-permute-start | bytes 110600 | tf_op jit(solution)/shard_map/ppermute | solution.py:405
  8.2 4.7 %collective-permute-start.4 = (f32[72,128]{1,0:T(8,128)S(1)}, f32[72,128]{1,0:T(8,128)S(1)}, u32[]{:S(2)}, u32[]{:S(2)}) collective-permute-start(f32[72,128]{1,0:T(8,128)S(1)} %get-tuple-element.22.refs_0_.after_ref), channel_id=1, source_target_pairs={{0,4},{2,6},{4,0},{6,2},{1,5},{3,7},{5,1},{7,3},{8,12},{10,14},{12... | collective-permute-start | bytes 110600 | tf_op jit(solution)/shard_map/ppermute | solution.py:21
  8.7 11.5 %collective-permute-start.6 = (bf16[8,64,128]{2,1,0:T(8,128)(2,1)S(1)}, bf16[8,64,128]{2,1,0:T(8,128)(2,1)S(1)}, u32[]{:S(2)}, u32[]{:S(2)}) collective-permute-start(bf16[8,64,128]{2,1,0:T(8,128)(2,1)S(1)} %shard_map.90.pair_ref), channel_id=1, source_target_pairs={{0,16},{8,24},{16,0},{24,8},{1,17},{9,25},{17,1},{25,9},{2,18},{10... | collective-permute-start | bytes 393224 | tf_op jit(solution)/shard_map/ppermute | solution.py:21
  11.4 6.6 %collective-permute-start.2 = (bf16[304,128]{1,0:T(8,128)(2,1)S(1)}, bf16[304,128]{1,0:T(8,128)(2,1)S(1)}, u32[]{:S(2)}, u32[]{:S(2)}) collective-permute-start(bf16[304,128]{1,0:T(8,128)(2,1)S(1)} %slice.4), channel_id=1, source_target_pairs={{0,8},{8,0},{16,24},{24,16},{1,9},{9,1},{17,25},{25,17},{2,10},{10... | collective-permute-start | bytes 233480 | tf_op jit(solution)/shard_map/ppermute | solution.py:21
  13.0 6.9 %collective-permute-start.7 = (bf16[64,128]{1,0:T(8,128)(2,1)S(1)}, bf16[64,128]{1,0:T(8,128)(2,1)S(1)}, u32[]{:S(2)}, u32[]{:S(2)}) collective-permute-start(bf16[64,128]{1,0:T(8,128)(2,1)S(1)} %get-tuple-element.27.low0_ref), channel_id=1, source_target_pairs={{0,24},{8,16},{16,8},{24,0},{1,25},{9,17},{17,9},{25,1},{2,26},{10... | collective-permute-start | bytes 49160 | tf_op jit(solution)/shard_map/ppermute | solution.py:21
  15.5 4.6 %collective-permute-start.8 = (bf16[64,128]{1,0:T(8,128)(2,1)S(1)}, bf16[64,128]{1,0:T(8,128)(2,1)S(1)}, u32[]{:S(2)}, u32[]{:S(2)}) collective-permute-start(bf16[64,128]{1,0:T(8,128)(2,1)S(1)} %get-tuple-element.27.low0_ref), channel_id=1, source_target_pairs={{0,16},{8,24},{16,0},{24,8},{1,17},{9,25},{17,1},{25,9},{2,18},{10... | collective-permute-start | bytes 49160 | tf_op jit(solution)/shard_map/ppermute | solution.py:21
  15.7 4.5 %collective-permute-start.9 = (bf16[64,128]{1,0:T(8,128)(2,1)S(1)}, bf16[64,128]{1,0:T(8,128)(2,1)S(1)}, u32[]{:S(2)}, u32[]{:S(2)}) collective-permute-start(bf16[64,128]{1,0:T(8,128)(2,1)S(1)} %get-tuple-element.27.low0_ref), channel_id=1, source_target_pairs={{0,8},{8,0},{16,24},{24,16},{1,9},{9,1},{17,25},{25,17},{2,10},{10... | collective-permute-start | bytes 49160 | tf_op jit(solution)/shard_map/ppermute | solution.py:21

commit v13 on v12

--- a/solution.py
+++ b/solution.py
@@ -336,22 +336,36 @@
     out.wait()
 
 
-def finish(pair_ref, far_ref, prior_ref, low0_ref, low3_ref, low2_ref, low1_ref, out, held_ref, sems):
+def share(one, two, low):
+    return lax.dot_general(
+        jnp.concatenate([one, two], axis=0),
+        low,
+        (((0,), (0,)), ((), ())),
+        preferred_element_type=jnp.float32,
+    )
+
+
+def begin(pair_ref, far_ref, prior_ref, low0_ref, low3_ref, base_ref):
+    rows, cols, real = prior_ref.shape
+    beside = pair_ref.shape[0] // 2
+    low = jnp.concatenate([low0_ref[...], low3_ref[...]], axis=0)
+    for x in range(beside):
+        grad = share(pair_ref[x], far_ref[beside + x], low)
+        for k in range(rows // beside):
+            row = k * beside + x
+            base_ref[row] = grad[k * cols : (k + 1) * cols] + prior_ref[row]
+
+
+def finish(pair_ref, far_ref, base_ref, low2_ref, low1_ref, out, held_ref, sems):
     rows, cols, real = held_ref.shape
     beside = pair_ref.shape[0] // 2
-    side = rows // beside
-    low = jnp.concatenate([low0_ref[...], low1_ref[...], low2_ref[...], low3_ref[...]], axis=0)
+    low = jnp.concatenate([low1_ref[...], low2_ref[...]], axis=0)
     copies = []
     for x in range(beside):
-        kernel = jnp.concatenate(
-            [pair_ref[x], pair_ref[beside + x], far_ref[x], far_ref[beside + x]], axis=0
-        )
-        grad = lax.dot_general(
-            kernel, low, (((0,), (0,)), ((), ())), preferred_element_type=jnp.float32
-        )
-        for k in range(side):
+        grad = share(pair_ref[beside + x], far_ref[x], low)
+        for k in range(rows // beside):
             row = k * beside + x
-            held_ref[row] = grad[k * cols : (k + 1) * cols] + prior_ref[row]
+            held_ref[row] = grad[k * cols : (k + 1) * cols] + base_ref[row]
             copies.append(pltpu.make_async_copy(held_ref.at[row], out.at[row], sems.at[row]))
             copies[-1].start()
     for copy in copies:
@@ -467,6 +481,9 @@
         ),
         flops=PRIOR_FLOPS,
     )(model_field, side_rim, wide_marks, rim_rows, other_rows, table, weighted)
+    (base,) = call(begin, (model_field.shape, jnp.float32), flops=EDGE_FLOPS)(
+        kernel_pair, kernel_far, prior_term, weighted_low, low_three
+    )
     (gradient,) = call(
         finish,
         (model_field.shape, jnp.float32),
@@ -475,7 +492,7 @@
             pltpu.VMEM(model_field.shape, jnp.float32),
             pltpu.SemaphoreType.DMA((rows,)),
         ),
-    )(kernel_pair, kernel_far, prior_term, weighted_low, low_three, low_two, low_one)
+    )(kernel_pair, kernel_far, base, low_two, low_one)
     return weighted_own[None], gradient
 
 

time: 21.3 us -> 21.3 us (level)
  waiting for transfers between devices: 0.81 us -> 0.57 us
    ppermute x8, waiting for transfers between devices: 0.8 us -> 0.57 us  [swap(): lax.ppermute(own, axis, [(i, partner(i)) for i in range(lax.axis_size(axi...]
    pallas_call x6 -> x7, Pallas kernels: 4.37 us -> 4.57 us  [run(): pl.pallas_call(fetched if fetch else body, out_shape=[jax.ShapeDtypeStruc...]
  transfers between devices with their start and end apart: 10 -> 10, of which waited for: 2 -> 1; matrix products, arithmetic and copies ran while one was open for 0% -> 0% of each run, Pallas kernels for 10% -> 11%
where the time goes in v13:
time: 21.3 us; the launch traced here: 21.1 us
  starting transfers between devices  15.3 us (72%)
  Pallas kernels  4.57 us (21%)
  between operations  0.7 us (3%)
  waiting for transfers between devices  0.57 us (3%)
    ppermute x8, starting transfers between devices, swap(): lax.ppermute(own, axis, [(i, partner(i)) for i in range(lax.axis_size(axi...  12.3 us
    pallas_call x7, Pallas kernels, run(): pl.pallas_call(fetched if fetch else body, out_shape=[jax.ShapeDtypeStruc...  4.57 us
    ppermute x2, starting transfers between devices, by_parity(): lax.ppermute(own, ('freq', 'px'), [(f * peers + i, f * peers + (odd_partn...  3.01 us
    ppermute x8, waiting for transfers between devices, swap(): lax.ppermute(own, axis, [(i, partner(i)) for i in range(lax.axis_size(axi...  0.57 us
  transfers between devices with their start and end apart: 10, of which 1 were waited for; matrix products, arithmetic and copies ran while one was open for 0% of the time, Pallas kernels for 11%

profile of v13, /device:TPU:0, one launch (start us, length us, event | category | flops | bytes accessed | tf_op | source)
XLA Modules:
  0.0 21.1 jit_solution(7627001399258148415)
XLA Ops:
  0.6 1.3 %shard_map.86 = (f32[112,128]{1,0:T(8,128)S(1)}, bf16[4,64,128]{2,1,0:T(8,128)(2,1)S(1)}, f32[8,64,128]{2,1,0:T(8,128)S(1)}, f32[8,128]{1,0:T(8,128)S(1)}, f32[5,16]{1,0:T(8,128)S(1)}) custom-call(f32[1,4]{1,0:T(1,128)} %refs_0_.1, f32[4,2,128]{2,1,0:T(2,128)} %bitcast.9, bf16[8,64,64]{2,1,0:T(8,128)(2,1)} %bitcast.8, f32[8,64,128]{2,1,0:T(8,128)} %refs_3_.1, ...), custom_call_target="tpu_custom_call" | custom-call | tf_op jit(solution)/shard_map/pallas_call | solution.py:58
  1.9 0.5 %collective-permute-start = (f32[112,128]{1,0:T(8,128)S(1)}, f32[112,128]{1,0:T(8,128)S(1)}, u32[]{:S(2)}, u32[]{:S(2)}) collective-permute-start(f32[112,128]{1,0:T(8,128)S(1)} %get-tuple-element.16.mine_ref), channel_id=1, source_target_pairs={{0,1},{1,0},{2,3},{3,2},{4,5},{5,4},{6,7},{7,6},{8,9},{9,8},{10,11... | collective-permute-start | bytes 172040 | tf_op jit(solution)/shard_map/ppermute | solution.py:21
  2.4 2.6 %collective-permute-start.5 = (bf16[4,64,128]{2,1,0:T(8,128)(2,1)S(1)}, bf16[4,64,128]{2,1,0:T(8,128)(2,1)S(1)}, u32[]{:S(2)}, u32[]{:S(2)}) collective-permute-start(bf16[4,64,128]{2,1,0:T(8,128)(2,1)S(1)} %get-tuple-element.25.one_ref), channel_id=1, source_target_pairs={{0,8},{8,0},{16,24},{24,16},{1,9},{9,1},{17,25},{25,17},{2,10},{10... | collective-permute-start | bytes 196616 | tf_op jit(solution)/shard_map/ppermute | solution.py:21
  5.1 0.0 collective-permute-done.got_ref
  5.1 0.1 shard_map.87
  5.2 1.5 %collective-permute-start.1 = (bf16[448,128]{1,0:T(8,128)(2,1)S(1)}, bf16[448,128]{1,0:T(8,128)(2,1)S(1)}, u32[]{:S(2)}, u32[]{:S(2)}) collective-permute-start(bf16[448,128]{1,0:T(8,128)(2,1)S(1)} %get-tuple-element.20), channel_id=1, source_target_pairs={{0,2},{2,0},{4,6},{6,4},{8,14},{10,12},{12,10},{14,8},{16,18},{18,... | collective-permute-start | bytes 344072 | tf_op jit(solution)/shard_map/ppermute | solution.py:419
  6.7 1.5 %collective-permute-start.3 = (f32[72,128]{1,0:T(8,128)S(1)}, f32[72,128]{1,0:T(8,128)S(1)}, u32[]{:S(2)}, u32[]{:S(2)}) collective-permute-start(f32[72,128]{1,0:T(8,128)S(1)} %get-tuple-element.22.refs_0_.after_ref), channel_id=1, source_target_pairs={{0,6},{2,4},{4,2},{6,0},{8,10},{10,8},{12,14},{14,12},{16,22},{18,... | collective-permute-start | bytes 110600 | tf_op jit(solution)/shard_map/ppermute | solution.py:419
  8.2 0.5 %collective-permute-start.4 = (f32[72,128]{1,0:T(8,128)S(1)}, f32[72,128]{1,0:T(8,128)S(1)}, u32[]{:S(2)}, u32[]{:S(2)}) collective-permute-start(f32[72,128]{1,0:T(8,128)S(1)} %get-tuple-element.22.refs_0_.after_ref), channel_id=1, source_target_pairs={{0,4},{2,6},{4,0},{6,2},{1,5},{3,7},{5,1},{7,3},{8,12},{10,14},{12... | collective-permute-start | bytes 110600 | tf_op jit(solution)/shard_map/ppermute | solution.py:21
  8.7 0.0 collective-permute-done.5.two_ref
  8.7 2.7 %collective-permute-start.6 = (bf16[8,64,128]{2,1,0:T(8,128)(2,1)S(1)}, bf16[8,64,128]{2,1,0:T(8,128)(2,1)S(1)}, u32[]{:S(2)}, u32[]{:S(2)}) collective-permute-start(bf16[8,64,128]{2,1,0:T(8,128)(2,1)S(1)} %shard_map.90.pair_ref), channel_id=1, source_target_pairs={{0,16},{8,24},{16,0},{24,8},{1,17},{9,25},{17,1},{25,9},{2,18},{10... | collective-permute-start | bytes 393224 | tf_op jit(solution)/shard_map/ppermute | solution.py:21
  11.4 0.0 collective-permute-done.1.refs_3_.rows_ref
  11.4 1.5 %collective-permute-start.2 = (bf16[304,128]{1,0:T(8,128)(2,1)S(1)}, bf16[304,128]{1,0:T(8,128)(2,1)S(1)}, u32[]{:S(2)}, u32[]{:S(2)}) collective-permute-start(bf16[304,128]{1,0:T(8,128)(2,1)S(1)} %slice.4), channel_id=1, source_target_pairs={{0,8},{8,0},{16,24},{24,16},{1,9},{9,1},{17,25},{25,17},{2,10},{10... | collective-permute-start | bytes 233480 | tf_op jit(solution)/shard_map/ppermute | solution.py:21
  12.9 0.0 collective-permute-done.3.refs_1_
  12.9 0.0 collective-permute-done.4.refs_2_
  12.9 0.1 shard_map.88
  13.0 2.5 %collective-permute-start.7 = (bf16[64,128]{1,0:T(8,128)(2,1)S(1)}, bf16[64,128]{1,0:T(8,128)(2,1)S(1)}, u32[]{:S(2)}, u32[]{:S(2)}) collective-permute-start(bf16[64,128]{1,0:T(8,128)(2,1)S(1)} %get-tuple-element.27.low0_ref), channel_id=1, source_target_pairs={{0,24},{8,16},{16,8},{24,0},{1,25},{9,17},{17,9},{25,1},{2,26},{10... | collective-permute-start | bytes 49160 | tf_op jit(solution)/shard_map/ppermute | solution.py:21
  15.5 0.2 collective-permute-start.8
  15.7 1.7 %collective-permute-start.9 = (bf16[64,128]{1,0:T(8,128)(2,1)S(1)}, bf16[64,128]{1,0:T(8,128)(2,1)S(1)}, u32[]{:S(2)}, u32[]{:S(2)}) collective-permute-start(bf16[64,128]{1,0:T(8,128)(2,1)S(1)} %get-tuple-element.27.low0_ref), channel_id=1, source_target_pairs={{0,8},{8,0},{16,24},{24,16},{1,9},{9,1},{17,25},{25,17},{2,10},{10... | collective-permute-start | bytes 49160 | tf_op jit(solution)/shard_map/ppermute | solution.py:21
  17.5 0.5 %collective-permute-done.2.other_ref = bf16[304,128]{1,0:T(8,128)(2,1)S(1)} collective-permute-done((bf16[304,128]{1,0:T(8,128)(2,1)S(1)}, bf16[304,128]{1,0:T(8,128)(2,1)S(1)}, u32[]{:S(2)}, u32[]{:S(2)}) %collective-permute-start.2) | collective-permute-done | bytes 77856 | tf_op jit(solution)/shard_map/ppermute | solution.py:21
  18.0 1.9 %shard_map.89 = (f32[8,64,128]{2,1,0:T(8,128)S(1)}, f32[4,2,128]{2,1,0:T(2,128)}) custom-call(f32[8,64,128]{2,1,0:T(8,128)S(1)} %get-tuple-element.15.field_ref, f32[8,8,128]{2,1,0:T(8,128)S(1)} %get-tuple-element.18.side_ref, f32[8,128]{1,0:T(8,128)S(1)} %get-tuple-element.19.wide_ref, bf16[448,128]{1,0:T(8,128)(2,1)S(1)} %collective-permute-done.1.refs_3_.rows_ref, ...), custom_call_target="tpu_custom_call" | custom-call | flops 1073741824 | tf_op jit(solution)/shard_map/pallas_call | solution.py:58
  19.9 0.0 collective-permute-done.7.low3_ref
  19.9 0.0 collective-permute-done.6.far_ref
  19.9 0.2 %shard_map.91.base_ref = f32[8,64,128]{2,1,0:T(8,128)S(1)} custom-call(bf16[8,64,128]{2,1,0:T(8,128)(2,1)S(1)} %shard_map.90.pair_ref, bf16[8,64,128]{2,1,0:T(8,128)(2,1)S(1)} %collective-permute-done.6.far_ref, f32[8,64,128]{2,1,0:T(8,128)S(1)} %get-tuple-element.26.prior_ref, bf16[64,128]{1,0:T(8,128)(2,1)S(1)} %get-tuple-element.27.low0_ref, ...), custom_call_target="tpu_custom_call" | custom-call | flops 1073741824 | tf_op jit(solution)/shard_map/pallas_call | solution.py:58
  20.2 0.0 collective-permute-done.8.low2_ref
  20.2 0.0 collective-permute-done.9.low1_ref
  20.2 0.9 %shard_map.92 = f32[8,64,128]{2,1,0:T(8,128)} custom-call(bf16[8,64,128]{2,1,0:T(8,128)(2,1)S(1)} %shard_map.90.pair_ref, bf16[8,64,128]{2,1,0:T(8,128)(2,1)S(1)} %collective-permute-done.6.far_ref, f32[8,64,128]{2,1,0:T(8,128)S(1)} %shard_map.91.base_ref, bf16[64,128]{1,0:T(8,128)(2,1)S(1)} %collective-permute-done.8.low2_ref, ...), custom_call_target="tpu_custom_call" | custom-call | tf_op jit(solution)/shard_map/pallas_call | solution.py:58
  (2 shorter events, 0.0 us)
Async XLA Ops:
  1.9 3.2 %collective-permute-start = (f32[112,128]{1,0:T(8,128)S(1)}, f32[112,128]{1,0:T(8,128)S(1)}, u32[]{:S(2)}, u32[]{:S(2)}) collective-permute-start(f32[112,128]{1,0:T(8,128)S(1)} %get-tuple-element.16.mine_ref), channel_id=1, source_target_pairs={{0,1},{1,0},{2,3},{3,2},{4,5},{5,4},{6,7},{7,6},{8,9},{9,8},{10,11... | collective-permute-start | bytes 172040 | tf_op jit(solution)/shard_map/ppermute | solution.py:21
  2.4 6.3 %collective-permute-start.5 = (bf16[4,64,128]{2,1,0:T(8,128)(2,1)S(1)}, bf16[4,64,128]{2,1,0:T(8,128)(2,1)S(1)}, u32[]{:S(2)}, u32[]{:S(2)}) collective-permute-start(bf16[4,64,128]{2,1,0:T(8,128)(2,1)S(1)} %get-tuple-element.25.one_ref), channel_id=1, source_target_pairs={{0,8},{8,0},{16,24},{24,16},{1,9},{9,1},{17,25},{25,17},{2,10},{10... | collective-permute-start | bytes 196616 | tf_op jit(solution)/shard_map/ppermute | solution.py:21
  5.2 6.2 %collective-permute-start.1 = (bf16[448,128]{1,0:T(8,128)(2,1)S(1)}, bf16[448,128]{1,0:T(8,128)(2,1)S(1)}, u32[]{:S(2)}, u32[]{:S(2)}) collective-permute-start(bf16[448,128]{1,0:T(8,128)(2,1)S(1)} %get-tuple-element.20), channel_id=1, source_target_pairs={{0,2},{2,0},{4,6},{6,4},{8,14},{10,12},{12,10},{14,8},{16,18},{18,... | collective-permute-start | bytes 344072 | tf_op jit(solution)/shard_map/ppermute | solution.py:419
  6.7 6.2 %collective-permute-start.3 = (f32[72,128]{1,0:T(8,128)S(1)}, f32[72,128]{1,0:T(8,128)S(1)}, u32[]{:S(2)}, u32[]{:S(2)}) collective-permute-start(f32[72,128]{1,0:T(8,128)S(1)} %get-tuple-element.22.refs_0_.after_ref), channel_id=1, source_target_pairs={{0,6},{2,4},{4,2},{6,0},{8,10},{10,8},{12,14},{14,12},{16,22},{18,... | collective-permute-start | bytes 110600 | tf_op jit(solution)/shard_map/ppermute | solution.py:419
  8.2 4.7 %collective-permute-start.4 = (f32[72,128]{1,0:T(8,128)S(1)}, f32[72,128]{1,0:T(8,128)S(1)}, u32[]{:S(2)}, u32[]{:S(2)}) collective-permute-start(f32[72,128]{1,0:T(8,128)S(1)} %get-tuple-element.22.refs_0_.after_ref), channel_id=1, source_target_pairs={{0,4},{2,6},{4,0},{6,2},{1,5},{3,7},{5,1},{7,3},{8,12},{10,14},{12... | collective-permute-start | bytes 110600 | tf_op jit(solution)/shard_map/ppermute | solution.py:21
  8.7 11.2 %collective-permute-start.6 = (bf16[8,64,128]{2,1,0:T(8,128)(2,1)S(1)}, bf16[8,64,128]{2,1,0:T(8,128)(2,1)S(1)}, u32[]{:S(2)}, u32[]{:S(2)}) collective-permute-start(bf16[8,64,128]{2,1,0:T(8,128)(2,1)S(1)} %shard_map.90.pair_ref), channel_id=1, source_target_pairs={{0,16},{8,24},{16,0},{24,8},{1,17},{9,25},{17,1},{25,9},{2,18},{10... | collective-permute-start | bytes 393224 | tf_op jit(solution)/shard_map/ppermute | solution.py:21
  11.4 6.6 %collective-permute-start.2 = (bf16[304,128]{1,0:T(8,128)(2,1)S(1)}, bf16[304,128]{1,0:T(8,128)(2,1)S(1)}, u32[]{:S(2)}, u32[]{:S(2)}) collective-permute-start(bf16[304,128]{1,0:T(8,128)(2,1)S(1)} %slice.4), channel_id=1, source_target_pairs={{0,8},{8,0},{16,24},{24,16},{1,9},{9,1},{17,25},{25,17},{2,10},{10... | collective-permute-start | bytes 233480 | tf_op jit(solution)/shard_map/ppermute | solution.py:21
  13.0 6.9 %collective-permute-start.7 = (bf16[64,128]{1,0:T(8,128)(2,1)S(1)}, bf16[64,128]{1,0:T(8,128)(2,1)S(1)}, u32[]{:S(2)}, u32[]{:S(2)}) collective-permute-start(bf16[64,128]{1,0:T(8,128)(2,1)S(1)} %get-tuple-element.27.low0_ref), channel_id=1, source_target_pairs={{0,24},{8,16},{16,8},{24,0},{1,25},{9,17},{17,9},{25,1},{2,26},{10... | collective-permute-start | bytes 49160 | tf_op jit(solution)/shard_map/ppermute | solution.py:21
  15.5 4.6 %collective-permute-start.8 = (bf16[64,128]{1,0:T(8,128)(2,1)S(1)}, bf16[64,128]{1,0:T(8,128)(2,1)S(1)}, u32[]{:S(2)}, u32[]{:S(2)}) collective-permute-start(bf16[64,128]{1,0:T(8,128)(2,1)S(1)} %get-tuple-element.27.low0_ref), channel_id=1, source_target_pairs={{0,16},{8,24},{16,0},{24,8},{1,17},{9,25},{17,1},{25,9},{2,18},{10... | collective-permute-start | bytes 49160 | tf_op jit(solution)/shard_map/ppermute | solution.py:21
  15.7 4.5 %collective-permute-start.9 = (bf16[64,128]{1,0:T(8,128)(2,1)S(1)}, bf16[64,128]{1,0:T(8,128)(2,1)S(1)}, u32[]{:S(2)}, u32[]{:S(2)}) collective-permute-start(bf16[64,128]{1,0:T(8,128)(2,1)S(1)} %get-tuple-element.27.low0_ref), channel_id=1, source_target_pairs={{0,8},{8,0},{16,24},{24,16},{1,9},{9,1},{17,25},{25,17},{2,10},{10... | collective-permute-start | bytes 49160 | tf_op jit(solution)/shard_map/ppermute | solution.py:21

commit v14 on v13

--- a/solution.py
+++ b/solution.py
@@ -248,21 +248,20 @@
             )
 
 
-def prior(
-    field_ref,
-    side_ref,
-    wide_ref,
-    rows_ref,
-    other_ref,
-    table_ref,
-    weighted_ref,
-    prior_ref,
-    own_out,
-    state_ref,
-    coef_ref,
-    own_ref,
-    sem,
-):
+def coefficients(marks, table_ref, count, wide):
+    levels, real = table_ref.shape[0] // 3, marks.shape[1]
+    level = lax.broadcasted_iota(jnp.int32, (levels, real), 0).astype(jnp.float32) + 1.0
+    onehot = (level == marks).astype(jnp.float32).astype(jnp.bfloat16)
+    coef = lax.dot_general(
+        jnp.concatenate([onehot] * 3, axis=0)[:, :wide],
+        table_ref[...],
+        (((0,), (0,)), ((), ())),
+        preferred_element_type=jnp.float32,
+    )
+    return [coef[:, c * real : (c + 1) * real] for c in range(count)]
+
+
+def ready(wide_ref, table_ref, weighted_ref, coef_ref, parts_ref, own_out, own_ref, sem):
     own, comps, real = own_ref.shape
     sensors = weighted_ref.shape[1]
     place = lax.axis_index("px") * lax.axis_size("py") + lax.axis_index("py")
@@ -274,25 +273,6 @@
             )
     out = pltpu.make_async_copy(own_ref, own_out, sem)
     out.start()
-    rows, cols, _ = field_ref.shape
-    wide = cols + 2 * SWEEPS
-    tile = SWEEPS * wide
-    mine = rows_ref[rows_ref.shape[0] - other_ref.shape[0] :].astype(jnp.float32)
-    other = other_ref[...].astype(jnp.float32)
-    even = lax.axis_index("freq") % 2 == 0
-    before, after = sides_of(
-        jnp.where(even, mine, other), jnp.where(even, other, mine), "px"
-    )
-    for k in range(SWEEPS):
-        state_ref[0, k] = before[k * wide : (k + 1) * wide]
-        state_ref[0, SWEEPS + rows + k] = after[k * wide : (k + 1) * wide]
-    for x in range(rows):
-        state_ref[0, SWEEPS + x] = jnp.concatenate([field_ref[x], side_ref[x]], axis=0)
-    marks = (
-        [before[tile + k : tile + k + 1] for k in range(SWEEPS)]
-        + [wide_ref[x : x + 1] for x in range(rows)]
-        + [after[tile + k : tile + k + 1] for k in range(SWEEPS)]
-    )
     count, levels = table_ref.shape
     spread = (
         lax.broadcasted_iota(jnp.int32, (count, count * real), 1) // real
@@ -311,29 +291,66 @@
     middle = rest.astype(jnp.bfloat16)
     low = (rest - middle.astype(jnp.float32)).astype(jnp.bfloat16)
     table = jnp.concatenate([high, middle, low], axis=0)
-    level = lax.broadcasted_iota(jnp.int32, (levels, real), 0).astype(jnp.float32) + 1.0
-    for x in range(1, 2 * SWEEPS + rows - 1):
-        onehot = (level == marks[x]).astype(jnp.float32).astype(jnp.bfloat16)
-        onehot = jnp.concatenate([onehot] * 3, axis=0)[:, :wide]
-        coef = lax.dot_general(onehot, table, turn, preferred_element_type=jnp.float32)
-        for c in range(count):
-            coef_ref[x, c] = coef[:, c * real : (c + 1) * real]
+    parts_ref[...] = table
+    for x in range(coef_ref.shape[0]):
+        for c, coef in enumerate(
+            coefficients(wide_ref[x : x + 1], parts_ref, count, coef_ref.shape[2])
+        ):
+            coef_ref[x, c] = coef
+    out.wait()
+
+
+def prior(
+    field_ref,
+    side_ref,
+    rows_ref,
+    other_ref,
+    own_coef_ref,
+    parts_ref,
+    prior_ref,
+    state_ref,
+    coef_ref,
+):
+    rows, cols, _ = field_ref.shape
+    wide = cols + 2 * SWEEPS
+    tile = SWEEPS * wide
+    mine = rows_ref[rows_ref.shape[0] - other_ref.shape[0] :].astype(jnp.float32)
+    other = other_ref[...].astype(jnp.float32)
+    even = lax.axis_index("freq") % 2 == 0
+    before, after = sides_of(
+        jnp.where(even, mine, other), jnp.where(even, other, mine), "px"
+    )
+    for k in range(SWEEPS):
+        state_ref[0, k] = before[k * wide : (k + 1) * wide]
+        state_ref[0, SWEEPS + rows + k] = after[k * wide : (k + 1) * wide]
+    for x in range(rows):
+        state_ref[0, SWEEPS + x] = jnp.concatenate([field_ref[x], side_ref[x]], axis=0)
+    marks = {k: before[tile + k : tile + k + 1] for k in range(1, SWEEPS)}
+    marks |= {SWEEPS + rows + k: after[tile + k : tile + k + 1] for k in range(SWEEPS - 1)}
+    count = own_coef_ref.shape[1]
+    for x in marks:
+        for c, coef in enumerate(coefficients(marks[x], parts_ref, count, wide)):
+            coef_ref[x, c] = coef
+
+    def coef_of(x, c):
+        own = SWEEPS <= x < SWEEPS + rows
+        return own_coef_ref[x - SWEEPS, c] if own else coef_ref[x, c]
+
     for sweep in range(SWEEPS):
         now, later = sweep % 2, (sweep + 1) % 2
         for x in range(sweep + 1, 2 * SWEEPS + rows - sweep - 1):
             center = state_ref[now, x]
             beside = (
-                coef_ref[x, 1] * state_ref[now, x - 1]
-                + coef_ref[x, 2] * state_ref[now, x + 1]
-                + coef_ref[x, 3] * pltpu.roll(center, 1, 0)
-                + coef_ref[x, 4] * pltpu.roll(center, wide - 1, 0)
+                coef_of(x, 1) * state_ref[now, x - 1]
+                + coef_of(x, 2) * state_ref[now, x + 1]
+                + coef_of(x, 3) * pltpu.roll(center, 1, 0)
+                + coef_of(x, 4) * pltpu.roll(center, wide - 1, 0)
             )
-            new = coef_ref[x, 0] * center - beside
+            new = coef_of(x, 0) * center - beside
             if sweep < SWEEPS - 1:
                 state_ref[later, x] = new
             else:
                 prior_ref[x - SWEEPS] = PRIOR_WEIGHT * new[:cols]
-    out.wait()
 
 
 def share(one, two, low):
@@ -468,19 +485,24 @@
     low_three = swap(weighted_low, "freq", lambda i: i ^ 3)
     low_two = swap(weighted_low, "freq", lambda i: i ^ 2)
     wide = cols + 2 * SWEEPS
-    prior_term, weighted_own = call(
+    count, levels = table.shape
+    own_coef, table_parts, weighted_own = call(
+        ready,
+        ((rows, count, wide, real), jnp.float32),
+        ((3 * levels, count * real), jnp.bfloat16),
+        ((own, comps, real), jnp.float32),
+        stored=(2,),
+        scratch=(pltpu.VMEM((own, comps, real), jnp.float32), pltpu.SemaphoreType.DMA(())),
+    )(wide_marks, table, weighted)
+    (prior_term,) = call(
         prior,
         (model_field.shape, jnp.float32),
-        ((own, comps, real), jnp.float32),
-        stored=(1,),
         scratch=(
             pltpu.VMEM((2, rows + 2 * SWEEPS, wide, real), jnp.float32),
-            pltpu.VMEM((rows + 2 * SWEEPS, table.shape[0], wide, real), jnp.float32),
-            pltpu.VMEM((own, comps, real), jnp.float32),
-            pltpu.SemaphoreType.DMA(()),
+            pltpu.VMEM((rows + 2 * SWEEPS, count, wide, real), jnp.float32),
         ),
         flops=PRIOR_FLOPS,
-    )(model_field, side_rim, wide_marks, rim_rows, other_rows, table, weighted)
+    )(model_field, side_rim, rim_rows, other_rows, own_coef, table_parts)
     (base,) = call(begin, (model_field.shape, jnp.float32), flops=EDGE_FLOPS)(
         kernel_pair, kernel_far, prior_term, weighted_low, low_three
     )

time: 21.3 us -> 21.3 us (level)
  waiting for transfers between devices: 0.57 us -> 0.24 us
  Pallas kernels: 4.57 us -> 4.89 us
    ppermute x8, waiting for transfers between devices: 0.57 us -> 0.24 us  [swap(): lax.ppermute(own, axis, [(i, partner(i)) for i in range(lax.axis_size(axi...]
    pallas_call x7 -> x8, Pallas kernels: 4.57 us -> 4.89 us  [run(): pl.pallas_call(fetched if fetch else body, out_shape=[jax.ShapeDtypeStruc...]
  transfers between devices with their start and end apart: 10 -> 10, of which waited for: 1 -> 1; matrix products, arithmetic and copies ran while one was open for 0% -> 0% of each run, Pallas kernels for 11% -> 13%
where the time goes in v14:
time: 21.3 us; the launch traced here: 21.1 us
  starting transfers between devices  15.3 us (72%)
  Pallas kernels  4.89 us (23%)
  between operations  0.71 us (3%)
  waiting for transfers between devices  0.24 us (1%)
    ppermute x8, starting transfers between devices, swap(): lax.ppermute(own, axis, [(i, partner(i)) for i in range(lax.axis_size(axi...  12.3 us
    pallas_call x8, Pallas kernels, run(): pl.pallas_call(fetched if fetch else body, out_shape=[jax.ShapeDtypeStruc...  4.89 us
    ppermute x2, starting transfers between devices, by_parity(): lax.ppermute(own, ('freq', 'px'), [(f * peers + i, f * peers + (odd_partn...  3.01 us
  transfers between devices with their start and end apart: 10, of which 1 were waited for; matrix products, arithmetic and copies ran while one was open for 0% of the time, Pallas kernels for 13%

profile of v14, /device:TPU:0, one launch (start us, length us, event | category | flops | bytes accessed | tf_op | source)
XLA Modules:
  0.0 21.1 jit_solution(3849701811770847914)
XLA Ops:
  0.6 1.3 %shard_map.86 = (f32[112,128]{1,0:T(8,128)S(1)}, bf16[4,64,128]{2,1,0:T(8,128)(2,1)S(1)}, f32[8,64,128]{2,1,0:T(8,128)S(1)}, f32[8,128]{1,0:T(8,128)S(1)}, f32[5,16]{1,0:T(8,128)S(1)}) custom-call(f32[1,4]{1,0:T(1,128)} %refs_0_.1, f32[4,2,128]{2,1,0:T(2,128)} %bitcast.9, bf16[8,64,64]{2,1,0:T(8,128)(2,1)} %bitcast.8, f32[8,64,128]{2,1,0:T(8,128)} %refs_3_.1, ...), custom_call_target="tpu_custom_call" | custom-call | tf_op jit(solution)/shard_map/pallas_call | solution.py:58
  1.9 0.5 %collective-permute-start = (f32[112,128]{1,0:T(8,128)S(1)}, f32[112,128]{1,0:T(8,128)S(1)}, u32[]{:S(2)}, u32[]{:S(2)}) collective-permute-start(f32[112,128]{1,0:T(8,128)S(1)} %get-tuple-element.16.mine_ref), channel_id=1, source_target_pairs={{0,1},{1,0},{2,3},{3,2},{4,5},{5,4},{6,7},{7,6},{8,9},{9,8},{10,11... | collective-permute-start | bytes 172040 | tf_op jit(solution)/shard_map/ppermute | solution.py:21
  2.4 2.6 %collective-permute-start.4 = (bf16[4,64,128]{2,1,0:T(8,128)(2,1)S(1)}, bf16[4,64,128]{2,1,0:T(8,128)(2,1)S(1)}, u32[]{:S(2)}, u32[]{:S(2)}) collective-permute-start(bf16[4,64,128]{2,1,0:T(8,128)(2,1)S(1)} %get-tuple-element.25.one_ref), channel_id=1, source_target_pairs={{0,8},{8,0},{16,24},{24,16},{1,9},{9,1},{17,25},{25,17},{2,10},{10... | collective-permute-start | bytes 196616 | tf_op jit(solution)/shard_map/ppermute | solution.py:21
  5.1 0.0 collective-permute-done.got_ref
  5.1 0.1 shard_map.87
  5.2 1.5 %collective-permute-start.3 = (bf16[448,128]{1,0:T(8,128)(2,1)S(1)}, bf16[448,128]{1,0:T(8,128)(2,1)S(1)}, u32[]{:S(2)}, u32[]{:S(2)}) collective-permute-start(bf16[448,128]{1,0:T(8,128)(2,1)S(1)} %get-tuple-element.22), channel_id=1, source_target_pairs={{0,2},{2,0},{4,6},{6,4},{8,14},{10,12},{12,10},{14,8},{16,18},{18,... | collective-permute-start | bytes 344072 | tf_op jit(solution)/shard_map/ppermute | solution.py:436
  6.7 1.5 %collective-permute-start.1 = (f32[72,128]{1,0:T(8,128)S(1)}, f32[72,128]{1,0:T(8,128)S(1)}, u32[]{:S(2)}, u32[]{:S(2)}) collective-permute-start(f32[72,128]{1,0:T(8,128)S(1)} %get-tuple-element.21.refs_0_.after_ref), channel_id=1, source_target_pairs={{0,6},{2,4},{4,2},{6,0},{8,10},{10,8},{12,14},{14,12},{16,22},{18,... | collective-permute-start | bytes 110600 | tf_op jit(solution)/shard_map/ppermute | solution.py:436
  8.2 0.5 %collective-permute-start.2 = (f32[72,128]{1,0:T(8,128)S(1)}, f32[72,128]{1,0:T(8,128)S(1)}, u32[]{:S(2)}, u32[]{:S(2)}) collective-permute-start(f32[72,128]{1,0:T(8,128)S(1)} %get-tuple-element.21.refs_0_.after_ref), channel_id=1, source_target_pairs={{0,4},{2,6},{4,0},{6,2},{1,5},{3,7},{5,1},{7,3},{8,12},{10,14},{12... | collective-permute-start | bytes 110600 | tf_op jit(solution)/shard_map/ppermute | solution.py:21
  8.7 0.0 collective-permute-done.4.two_ref
  8.7 2.7 %collective-permute-start.5 = (bf16[8,64,128]{2,1,0:T(8,128)(2,1)S(1)}, bf16[8,64,128]{2,1,0:T(8,128)(2,1)S(1)}, u32[]{:S(2)}, u32[]{:S(2)}) collective-permute-start(bf16[8,64,128]{2,1,0:T(8,128)(2,1)S(1)} %shard_map.90.pair_ref), channel_id=1, source_target_pairs={{0,16},{8,24},{16,0},{24,8},{1,17},{9,25},{17,1},{25,9},{2,18},{10... | collective-permute-start | bytes 393224 | tf_op jit(solution)/shard_map/ppermute | solution.py:21
  11.4 0.0 collective-permute-done.3.refs_3_.rows_ref
  11.4 1.5 %collective-permute-start.6 = (bf16[304,128]{1,0:T(8,128)(2,1)S(1)}, bf16[304,128]{1,0:T(8,128)(2,1)S(1)}, u32[]{:S(2)}, u32[]{:S(2)}) collective-permute-start(bf16[304,128]{1,0:T(8,128)(2,1)S(1)} %slice.4), channel_id=1, source_target_pairs={{0,8},{8,0},{16,24},{24,16},{1,9},{9,1},{17,25},{25,17},{2,10},{10... | collective-permute-start | bytes 233480 | tf_op jit(solution)/shard_map/ppermute | solution.py:21
  12.9 0.0 collective-permute-done.1.refs_1_
  12.9 0.0 collective-permute-done.2.refs_2_
  12.9 0.1 shard_map.88
  13.0 2.5 %collective-permute-start.7 = (bf16[64,128]{1,0:T(8,128)(2,1)S(1)}, bf16[64,128]{1,0:T(8,128)(2,1)S(1)}, u32[]{:S(2)}, u32[]{:S(2)}) collective-permute-start(bf16[64,128]{1,0:T(8,128)(2,1)S(1)} %get-tuple-element.29.low0_ref), channel_id=1, source_target_pairs={{0,24},{8,16},{16,8},{24,0},{1,25},{9,17},{17,9},{25,1},{2,26},{10... | collective-permute-start | bytes 49160 | tf_op jit(solution)/shard_map/ppermute | solution.py:21
  15.5 0.2 collective-permute-start.8
  15.7 1.7 %collective-permute-start.9 = (bf16[64,128]{1,0:T(8,128)(2,1)S(1)}, bf16[64,128]{1,0:T(8,128)(2,1)S(1)}, u32[]{:S(2)}, u32[]{:S(2)}) collective-permute-start(bf16[64,128]{1,0:T(8,128)(2,1)S(1)} %get-tuple-element.29.low0_ref), channel_id=1, source_target_pairs={{0,8},{8,0},{16,24},{24,16},{1,9},{9,1},{17,25},{25,17},{2,10},{10... | collective-permute-start | bytes 49160 | tf_op jit(solution)/shard_map/ppermute | solution.py:21
  17.5 1.2 %shard_map.89 = (f32[8,5,72,128]{3,2,1,0:T(8,128)S(1)}, bf16[48,640]{1,0:T(8,128)(2,1)S(1)}, f32[4,2,128]{2,1,0:T(2,128)}) custom-call(f32[8,128]{1,0:T(8,128)S(1)} %get-tuple-element.19.wide_ref, f32[5,16]{1,0:T(8,128)S(1)} %get-tuple-element.20.table_ref, f32[2,32,128]{2,1,0:T(8,128)S(1)} %get-tuple-element.23.weighted_ref), custom_call_target="tpu_custom_call" | custom-call | tf_op jit(solution)/shard_map/pallas_call | solution.py:58
  18.6 0.0 collective-permute-done.6.other_ref
  18.6 1.1 %shard_map.91.prior_ref = f32[8,64,128]{2,1,0:T(8,128)S(1)} custom-call(f32[8,64,128]{2,1,0:T(8,128)S(1)} %get-tuple-element.17.field_ref, f32[8,8,128]{2,1,0:T(8,128)S(1)} %get-tuple-element.26.side_ref, bf16[448,128]{1,0:T(8,128)(2,1)S(1)} %collective-permute-done.3.refs_3_.rows_ref, bf16[304,128]{1,0:T(8,128)(2,1)S(1)} %collective-permute-done.6.other_ref, ...), custom_call_target="tpu_custom_call" | custom-call | flops 1073741824 | tf_op jit(solution)/shard_map/pallas_call | solution.py:58
  19.7 0.0 collective-permute-done.7.low3_ref
  19.7 0.0 collective-permute-done.5.far_ref
  19.7 0.2 %shard_map.92.base_ref = f32[8,64,128]{2,1,0:T(8,128)S(1)} custom-call(bf16[8,64,128]{2,1,0:T(8,128)(2,1)S(1)} %shard_map.90.pair_ref, bf16[8,64,128]{2,1,0:T(8,128)(2,1)S(1)} %collective-permute-done.5.far_ref, f32[8,64,128]{2,1,0:T(8,128)S(1)} %shard_map.91.prior_ref, bf16[64,128]{1,0:T(8,128)(2,1)S(1)} %get-tuple-element.29.low0_ref, ...), custom_call_target="tpu_custom_call" | custom-call | flops 1073741824 | tf_op jit(solution)/shard_map/pallas_call | solution.py:58
  20.0 0.2 %collective-permute-done.8.low2_ref = bf16[64,128]{1,0:T(8,128)(2,1)S(1)} collective-permute-done((bf16[64,128]{1,0:T(8,128)(2,1)S(1)}, bf16[64,128]{1,0:T(8,128)(2,1)S(1)}, u32[]{:S(2)}, u32[]{:S(2)}) %collective-permute-start.8) | collective-permute-done | bytes 16416 | tf_op jit(solution)/shard_map/ppermute | solution.py:21
  20.2 0.0 collective-permute-done.9.low1_ref
  20.2 0.9 %shard_map.93 = f32[8,64,128]{2,1,0:T(8,128)} custom-call(bf16[8,64,128]{2,1,0:T(8,128)(2,1)S(1)} %shard_map.90.pair_ref, bf16[8,64,128]{2,1,0:T(8,128)(2,1)S(1)} %collective-permute-done.5.far_ref, f32[8,64,128]{2,1,0:T(8,128)S(1)} %shard_map.92.base_ref, bf16[64,128]{1,0:T(8,128)(2,1)S(1)} %collective-permute-done.8.low2_ref, ...), custom_call_target="tpu_custom_call" | custom-call | tf_op jit(solution)/shard_map/pallas_call | solution.py:58
  (2 shorter events, 0.0 us)
Async XLA Ops:
  1.9 3.2 %collective-permute-start = (f32[112,128]{1,0:T(8,128)S(1)}, f32[112,128]{1,0:T(8,128)S(1)}, u32[]{:S(2)}, u32[]{:S(2)}) collective-permute-start(f32[112,128]{1,0:T(8,128)S(1)} %get-tuple-element.16.mine_ref), channel_id=1, source_target_pairs={{0,1},{1,0},{2,3},{3,2},{4,5},{5,4},{6,7},{7,6},{8,9},{9,8},{10,11... | collective-permute-start | bytes 172040 | tf_op jit(solution)/shard_map/ppermute | solution.py:21
  2.4 6.3 %collective-permute-start.4 = (bf16[4,64,128]{2,1,0:T(8,128)(2,1)S(1)}, bf16[4,64,128]{2,1,0:T(8,128)(2,1)S(1)}, u32[]{:S(2)}, u32[]{:S(2)}) collective-permute-start(bf16[4,64,128]{2,1,0:T(8,128)(2,1)S(1)} %get-tuple-element.25.one_ref), channel_id=1, source_target_pairs={{0,8},{8,0},{16,24},{24,16},{1,9},{9,1},{17,25},{25,17},{2,10},{10... | collective-permute-start | bytes 196616 | tf_op jit(solution)/shard_map/ppermute | solution.py:21
  5.2 6.2 %collective-permute-start.3 = (bf16[448,128]{1,0:T(8,128)(2,1)S(1)}, bf16[448,128]{1,0:T(8,128)(2,1)S(1)}, u32[]{:S(2)}, u32[]{:S(2)}) collective-permute-start(bf16[448,128]{1,0:T(8,128)(2,1)S(1)} %get-tuple-element.22), channel_id=1, source_target_pairs={{0,2},{2,0},{4,6},{6,4},{8,14},{10,12},{12,10},{14,8},{16,18},{18,... | collective-permute-start | bytes 344072 | tf_op jit(solution)/shard_map/ppermute | solution.py:436
  6.7 6.2 %collective-permute-start.1 = (f32[72,128]{1,0:T(8,128)S(1)}, f32[72,128]{1,0:T(8,128)S(1)}, u32[]{:S(2)}, u32[]{:S(2)}) collective-permute-start(f32[72,128]{1,0:T(8,128)S(1)} %get-tuple-element.21.refs_0_.after_ref), channel_id=1, source_target_pairs={{0,6},{2,4},{4,2},{6,0},{8,10},{10,8},{12,14},{14,12},{16,22},{18,... | collective-permute-start | bytes 110600 | tf_op jit(solution)/shard_map/ppermute | solution.py:436
  8.2 4.7 %collective-permute-start.2 = (f32[72,128]{1,0:T(8,128)S(1)}, f32[72,128]{1,0:T(8,128)S(1)}, u32[]{:S(2)}, u32[]{:S(2)}) collective-permute-start(f32[72,128]{1,0:T(8,128)S(1)} %get-tuple-element.21.refs_0_.after_ref), channel_id=1, source_target_pairs={{0,4},{2,6},{4,0},{6,2},{1,5},{3,7},{5,1},{7,3},{8,12},{10,14},{12... | collective-permute-start | bytes 110600 | tf_op jit(solution)/shard_map/ppermute | solution.py:21
  8.7 11.0 %collective-permute-start.5 = (bf16[8,64,128]{2,1,0:T(8,128)(2,1)S(1)}, bf16[8,64,128]{2,1,0:T(8,128)(2,1)S(1)}, u32[]{:S(2)}, u32[]{:S(2)}) collective-permute-start(bf16[8,64,128]{2,1,0:T(8,128)(2,1)S(1)} %shard_map.90.pair_ref), channel_id=1, source_target_pairs={{0,16},{8,24},{16,0},{24,8},{1,17},{9,25},{17,1},{25,9},{2,18},{10... | collective-permute-start | bytes 393224 | tf_op jit(solution)/shard_map/ppermute | solution.py:21
  11.4 7.2 %collective-permute-start.6 = (bf16[304,128]{1,0:T(8,128)(2,1)S(1)}, bf16[304,128]{1,0:T(8,128)(2,1)S(1)}, u32[]{:S(2)}, u32[]{:S(2)}) collective-permute-start(bf16[304,128]{1,0:T(8,128)(2,1)S(1)} %slice.4), channel_id=1, source_target_pairs={{0,8},{8,0},{16,24},{24,16},{1,9},{9,1},{17,25},{25,17},{2,10},{10... | collective-permute-start | bytes 233480 | tf_op jit(solution)/shard_map/ppermute | solution.py:21
  13.0 6.7 %collective-permute-start.7 = (bf16[64,128]{1,0:T(8,128)(2,1)S(1)}, bf16[64,128]{1,0:T(8,128)(2,1)S(1)}, u32[]{:S(2)}, u32[]{:S(2)}) collective-permute-start(bf16[64,128]{1,0:T(8,128)(2,1)S(1)} %get-tuple-element.29.low0_ref), channel_id=1, source_target_pairs={{0,24},{8,16},{16,8},{24,0},{1,25},{9,17},{17,9},{25,1},{2,26},{10... | collective-permute-start | bytes 49160 | tf_op jit(solution)/shard_map/ppermute | solution.py:21
  15.5 4.6 %collective-permute-start.8 = (bf16[64,128]{1,0:T(8,128)(2,1)S(1)}, bf16[64,128]{1,0:T(8,128)(2,1)S(1)}, u32[]{:S(2)}, u32[]{:S(2)}) collective-permute-start(bf16[64,128]{1,0:T(8,128)(2,1)S(1)} %get-tuple-element.29.low0_ref), channel_id=1, source_target_pairs={{0,16},{8,24},{16,0},{24,8},{1,17},{9,25},{17,1},{25,9},{2,18},{10... | collective-permute-start | bytes 49160 | tf_op jit(solution)/shard_map/ppermute | solution.py:21
  15.7 4.5 %collective-permute-start.9 = (bf16[64,128]{1,0:T(8,128)(2,1)S(1)}, bf16[64,128]{1,0:T(8,128)(2,1)S(1)}, u32[]{:S(2)}, u32[]{:S(2)}) collective-permute-start(bf16[64,128]{1,0:T(8,128)(2,1)S(1)} %get-tuple-element.29.low0_ref), channel_id=1, source_target_pairs={{0,8},{8,0},{16,24},{24,16},{1,9},{9,1},{17,25},{25,17},{2,10},{10... | collective-permute-start | bytes 49160 | tf_op jit(solution)/shard_map/ppermute | solution.py:21

commit v15 on v14

--- a/solution.py
+++ b/solution.py
@@ -373,20 +373,14 @@
             base_ref[row] = grad[k * cols : (k + 1) * cols] + prior_ref[row]
 
 
-def finish(pair_ref, far_ref, base_ref, low2_ref, low1_ref, out, held_ref, sems):
-    rows, cols, real = held_ref.shape
+def finish(pair_ref, far_ref, low2_ref, low1_ref, rest_ref):
+    rows, cols, real = rest_ref.shape
     beside = pair_ref.shape[0] // 2
     low = jnp.concatenate([low1_ref[...], low2_ref[...]], axis=0)
-    copies = []
     for x in range(beside):
         grad = share(pair_ref[beside + x], far_ref[x], low)
         for k in range(rows // beside):
-            row = k * beside + x
-            held_ref[row] = grad[k * cols : (k + 1) * cols] + base_ref[row]
-            copies.append(pltpu.make_async_copy(held_ref.at[row], out.at[row], sems.at[row]))
-            copies[-1].start()
-    for copy in copies:
-        copy.wait()
+            rest_ref[k * beside + x] = grad[k * cols : (k + 1) * cols]
 
 
 def local(observed, noise_scale, forward_kernel, model_field, classes, kappa_table, coupling_table):
@@ -506,16 +500,10 @@
     (base,) = call(begin, (model_field.shape, jnp.float32), flops=EDGE_FLOPS)(
         kernel_pair, kernel_far, prior_term, weighted_low, low_three
     )
-    (gradient,) = call(
-        finish,
-        (model_field.shape, jnp.float32),
-        stored=(0,),
-        scratch=(
-            pltpu.VMEM(model_field.shape, jnp.float32),
-            pltpu.SemaphoreType.DMA((rows,)),
-        ),
-    )(kernel_pair, kernel_far, base, low_two, low_one)
-    return weighted_own[None], gradient
+    (rest,) = call(finish, (model_field.shape, jnp.float32))(
+        kernel_pair, kernel_far, low_two, low_one
+    )
+    return weighted_own[None], base + rest
 
 
 def solution(mesh):

time: 21.3 us -> 22.7 us (1.066)
  waiting for transfers between devices: 0.24 us -> 1.69 us
  other arithmetic: 0 us -> 0.74 us
  Pallas kernels: 4.89 us -> 4.16 us
    ppermute x8, waiting for transfers between devices: 0.24 us -> 1.69 us  [swap(): lax.ppermute(own, axis, [(i, partner(i)) for i in range(lax.axis_size(axi...]
    add x0 -> x1, other arithmetic: none -> 0.74 us  [local(): return (weighted_own[None], base + rest)]
    pallas_call x8, Pallas kernels: 4.89 us -> 4.16 us  [run(): pl.pallas_call(fetched if fetch else body, out_shape=[jax.ShapeDtypeStruc...]
  transfers between devices with their start and end apart: 10 -> 10, of which waited for: 1 -> 2; matrix products, arithmetic and copies ran while one was open for 0% -> 0% of each run, Pallas kernels for 13% -> 12%
where the time goes in v15:
time: 22.7 us; the launch traced here: 22.6 us
  starting transfers between devices  15.3 us (67%)
  Pallas kernels  4.16 us (18%)
  waiting for transfers between devices  1.69 us (7%)
  other arithmetic  0.74 us (3%)
  between operations  0.71 us (3%)
    ppermute x8, starting transfers between devices, swap(): lax.ppermute(own, axis, [(i, partner(i)) for i in range(lax.axis_size(axi...  12.3 us
    pallas_call x8, Pallas kernels, run(): pl.pallas_call(fetched if fetch else body, out_shape=[jax.ShapeDtypeStruc...  4.16 us
    ppermute x2, starting transfers between devices, by_parity(): lax.ppermute(own, ('freq', 'px'), [(f * peers + i, f * peers + (odd_partn...  3.01 us
    ppermute x8, waiting for transfers between devices, swap(): lax.ppermute(own, axis, [(i, partner(i)) for i in range(lax.axis_size(axi...  1.69 us
    add x1, other arithmetic, local(): return (weighted_own[None], base + rest)  0.74 us
  transfers between devices with their start and end apart: 10, of which 2 were waited for; matrix products, arithmetic and copies ran while one was open for 0% of the time, Pallas kernels for 12%

profile of v15, /device:TPU:0, one launch (start us, length us, event | category | flops | bytes accessed | tf_op | source)
XLA Modules:
  0.0 22.6 jit_solution(3198007125516235392)
XLA Ops:
  0.6 1.3 %shard_map.86 = (f32[112,128]{1,0:T(8,128)S(1)}, bf16[4,64,128]{2,1,0:T(8,128)(2,1)S(1)}, f32[8,64,128]{2,1,0:T(8,128)S(1)}, f32[8,128]{1,0:T(8,128)S(1)}, f32[5,16]{1,0:T(8,128)S(1)}) custom-call(f32[1,4]{1,0:T(1,128)} %refs_0_.1, f32[4,2,128]{2,1,0:T(2,128)} %bitcast.9, bf16[8,64,64]{2,1,0:T(8,128)(2,1)} %bitcast.8, f32[8,64,128]{2,1,0:T(8,128)} %refs_3_.1, ...), custom_call_target="tpu_custom_call" | custom-call | tf_op jit(solution)/shard_map/pallas_call | solution.py:58
  1.9 0.5 %collective-permute-start = (f32[112,128]{1,0:T(8,128)S(1)}, f32[112,128]{1,0:T(8,128)S(1)}, u32[]{:S(2)}, u32[]{:S(2)}) collective-permute-start(f32[112,128]{1,0:T(8,128)S(1)} %get-tuple-element.16.mine_ref), channel_id=1, source_target_pairs={{0,1},{1,0},{2,3},{3,2},{4,5},{5,4},{6,7},{7,6},{8,9},{9,8},{10,11... | collective-permute-start | bytes 172040 | tf_op jit(solution)/shard_map/ppermute | solution.py:21
  2.4 2.6 %collective-permute-start.4 = (bf16[4,64,128]{2,1,0:T(8,128)(2,1)S(1)}, bf16[4,64,128]{2,1,0:T(8,128)(2,1)S(1)}, u32[]{:S(2)}, u32[]{:S(2)}) collective-permute-start(bf16[4,64,128]{2,1,0:T(8,128)(2,1)S(1)} %get-tuple-element.25.one_ref), channel_id=1, source_target_pairs={{0,8},{8,0},{16,24},{24,16},{1,9},{9,1},{17,25},{25,17},{2,10},{10... | collective-permute-start | bytes 196616 | tf_op jit(solution)/shard_map/ppermute | solution.py:21
  5.1 0.0 collective-permute-done.got_ref
  5.1 0.1 shard_map.87
  5.2 1.5 %collective-permute-start.3 = (bf16[448,128]{1,0:T(8,128)(2,1)S(1)}, bf16[448,128]{1,0:T(8,128)(2,1)S(1)}, u32[]{:S(2)}, u32[]{:S(2)}) collective-permute-start(bf16[448,128]{1,0:T(8,128)(2,1)S(1)} %get-tuple-element.22), channel_id=1, source_target_pairs={{0,2},{2,0},{4,6},{6,4},{8,14},{10,12},{12,10},{14,8},{16,18},{18,... | collective-permute-start | bytes 344072 | tf_op jit(solution)/shard_map/ppermute | solution.py:430
  6.7 1.5 %collective-permute-start.1 = (f32[72,128]{1,0:T(8,128)S(1)}, f32[72,128]{1,0:T(8,128)S(1)}, u32[]{:S(2)}, u32[]{:S(2)}) collective-permute-start(f32[72,128]{1,0:T(8,128)S(1)} %get-tuple-element.21.refs_0_.after_ref), channel_id=1, source_target_pairs={{0,6},{2,4},{4,2},{6,0},{8,10},{10,8},{12,14},{14,12},{16,22},{18,... | collective-permute-start | bytes 110600 | tf_op jit(solution)/shard_map/ppermute | solution.py:430
  8.2 0.5 %collective-permute-start.2 = (f32[72,128]{1,0:T(8,128)S(1)}, f32[72,128]{1,0:T(8,128)S(1)}, u32[]{:S(2)}, u32[]{:S(2)}) collective-permute-start(f32[72,128]{1,0:T(8,128)S(1)} %get-tuple-element.21.refs_0_.after_ref), channel_id=1, source_target_pairs={{0,4},{2,6},{4,0},{6,2},{1,5},{3,7},{5,1},{7,3},{8,12},{10,14},{12... | collective-permute-start | bytes 110600 | tf_op jit(solution)/shard_map/ppermute | solution.py:21
  8.7 0.0 collective-permute-done.4.two_ref
  8.7 2.7 %collective-permute-start.5 = (bf16[8,64,128]{2,1,0:T(8,128)(2,1)S(1)}, bf16[8,64,128]{2,1,0:T(8,128)(2,1)S(1)}, u32[]{:S(2)}, u32[]{:S(2)}) collective-permute-start(bf16[8,64,128]{2,1,0:T(8,128)(2,1)S(1)} %shard_map.90.pair_ref), channel_id=1, source_target_pairs={{0,16},{8,24},{16,0},{24,8},{1,17},{9,25},{17,1},{25,9},{2,18},{10... | collective-permute-start | bytes 393224 | tf_op jit(solution)/shard_map/ppermute | solution.py:21
  11.4 0.0 collective-permute-done.3.refs_3_.rows_ref
  11.4 1.5 %collective-permute-start.6 = (bf16[304,128]{1,0:T(8,128)(2,1)S(1)}, bf16[304,128]{1,0:T(8,128)(2,1)S(1)}, u32[]{:S(2)}, u32[]{:S(2)}) collective-permute-start(bf16[304,128]{1,0:T(8,128)(2,1)S(1)} %slice.4), channel_id=1, source_target_pairs={{0,8},{8,0},{16,24},{24,16},{1,9},{9,1},{17,25},{25,17},{2,10},{10... | collective-permute-start | bytes 233480 | tf_op jit(solution)/shard_map/ppermute | solution.py:21
  12.9 0.0 collective-permute-done.1.refs_1_
  12.9 0.0 collective-permute-done.2.refs_2_
  12.9 0.1 shard_map.88
  13.0 2.7 %collective-permute-start.8 = (bf16[64,128]{1,0:T(8,128)(2,1)S(1)}, bf16[64,128]{1,0:T(8,128)(2,1)S(1)}, u32[]{:S(2)}, u32[]{:S(2)}) collective-permute-start(bf16[64,128]{1,0:T(8,128)(2,1)S(1)} %get-tuple-element.29.low0_ref), channel_id=1, source_target_pairs={{0,16},{8,24},{16,0},{24,8},{1,17},{9,25},{17,1},{25,9},{2,18},{10... | collective-permute-start | bytes 49160 | tf_op jit(solution)/shard_map/ppermute | solution.py:21
  15.7 0.4 %collective-permute-start.9 = (bf16[64,128]{1,0:T(8,128)(2,1)S(1)}, bf16[64,128]{1,0:T(8,128)(2,1)S(1)}, u32[]{:S(2)}, u32[]{:S(2)}) collective-permute-start(bf16[64,128]{1,0:T(8,128)(2,1)S(1)} %get-tuple-element.29.low0_ref), channel_id=1, source_target_pairs={{0,8},{8,0},{16,24},{24,16},{1,9},{9,1},{17,25},{25,17},{2,10},{10... | collective-permute-start | bytes 49160 | tf_op jit(solution)/shard_map/ppermute | solution.py:21
  16.1 1.4 %collective-permute-start.7 = (bf16[64,128]{1,0:T(8,128)(2,1)S(1)}, bf16[64,128]{1,0:T(8,128)(2,1)S(1)}, u32[]{:S(2)}, u32[]{:S(2)}) collective-permute-start(bf16[64,128]{1,0:T(8,128)(2,1)S(1)} %get-tuple-element.29.low0_ref), channel_id=1, source_target_pairs={{0,24},{8,16},{16,8},{24,0},{1,25},{9,17},{17,9},{25,1},{2,26},{10... | collective-permute-start | bytes 49160 | tf_op jit(solution)/shard_map/ppermute | solution.py:21
  17.5 1.2 %shard_map.89 = (f32[8,5,72,128]{3,2,1,0:T(8,128)S(1)}, bf16[48,640]{1,0:T(8,128)(2,1)S(1)}, f32[4,2,128]{2,1,0:T(2,128)}) custom-call(f32[8,128]{1,0:T(8,128)S(1)} %get-tuple-element.19.wide_ref, f32[5,16]{1,0:T(8,128)S(1)} %get-tuple-element.20.table_ref, f32[2,32,128]{2,1,0:T(8,128)S(1)} %get-tuple-element.23.weighted_ref), custom_call_target="tpu_custom_call" | custom-call | tf_op jit(solution)/shard_map/pallas_call | solution.py:58
  18.6 0.0 collective-permute-done.8.low2_ref
  18.6 0.9 %collective-permute-done.9.low1_ref = bf16[64,128]{1,0:T(8,128)(2,1)S(1)} collective-permute-done((bf16[64,128]{1,0:T(8,128)(2,1)S(1)}, bf16[64,128]{1,0:T(8,128)(2,1)S(1)}, u32[]{:S(2)}, u32[]{:S(2)}) %collective-permute-start.9) | collective-permute-done | bytes 16416 | tf_op jit(solution)/shard_map/ppermute | solution.py:21
  19.6 0.0 collective-permute-done.5.far_ref
  19.6 0.2 shard_map.93
  19.8 0.0 collective-permute-done.6.other_ref
  19.8 1.1 %shard_map.91.prior_ref = f32[8,64,128]{2,1,0:T(8,128)S(1)} custom-call(f32[8,64,128]{2,1,0:T(8,128)S(1)} %get-tuple-element.17.field_ref, f32[8,8,128]{2,1,0:T(8,128)S(1)} %get-tuple-element.26.side_ref, bf16[448,128]{1,0:T(8,128)(2,1)S(1)} %collective-permute-done.3.refs_3_.rows_ref, bf16[304,128]{1,0:T(8,128)(2,1)S(1)} %collective-permute-done.6.other_ref, ...), custom_call_target="tpu_custom_call" | custom-call | flops 1073741824 | tf_op jit(solution)/shard_map/pallas_call | solution.py:58
  20.9 0.7 %collective-permute-done.7.low3_ref = bf16[64,128]{1,0:T(8,128)(2,1)S(1)} collective-permute-done((bf16[64,128]{1,0:T(8,128)(2,1)S(1)}, bf16[64,128]{1,0:T(8,128)(2,1)S(1)}, u32[]{:S(2)}, u32[]{:S(2)}) %collective-permute-start.7) | collective-permute-done | bytes 16416 | tf_op jit(solution)/shard_map/ppermute | solution.py:21
  21.6 0.2 shard_map.92
  21.9 0.7 %add.3 = f32[8,64,128]{2,1,0:T(8,128)} add(f32[8,64,128]{2,1,0:T(8,128)S(1)} %shard_map.92, f32[8,64,128]{2,1,0:T(8,128)S(1)} %shard_map.93) | non-fusion elementwise | flops 65536 | bytes 786432 | tf_op jit(solution)/shard_map/add | solution.py:506
  (2 shorter events, 0.0 us)
Async XLA Ops:
  1.9 3.2 %collective-permute-start = (f32[112,128]{1,0:T(8,128)S(1)}, f32[112,128]{1,0:T(8,128)S(1)}, u32[]{:S(2)}, u32[]{:S(2)}) collective-permute-start(f32[112,128]{1,0:T(8,128)S(1)} %get-tuple-element.16.mine_ref), channel_id=1, source_target_pairs={{0,1},{1,0},{2,3},{3,2},{4,5},{5,4},{6,7},{7,6},{8,9},{9,8},{10,11... | collective-permute-start | bytes 172040 | tf_op jit(solution)/shard_map/ppermute | solution.py:21
  2.4 6.3 %collective-permute-start.4 = (bf16[4,64,128]{2,1,0:T(8,128)(2,1)S(1)}, bf16[4,64,128]{2,1,0:T(8,128)(2,1)S(1)}, u32[]{:S(2)}, u32[]{:S(2)}) collective-permute-start(bf16[4,64,128]{2,1,0:T(8,128)(2,1)S(1)} %get-tuple-element.25.one_ref), channel_id=1, source_target_pairs={{0,8},{8,0},{16,24},{24,16},{1,9},{9,1},{17,25},{25,17},{2,10},{10... | collective-permute-start | bytes 196616 | tf_op jit(solution)/shard_map/ppermute | solution.py:21
  5.2 6.2 %collective-permute-start.3 = (bf16[448,128]{1,0:T(8,128)(2,1)S(1)}, bf16[448,128]{1,0:T(8,128)(2,1)S(1)}, u32[]{:S(2)}, u32[]{:S(2)}) collective-permute-start(bf16[448,128]{1,0:T(8,128)(2,1)S(1)} %get-tuple-element.22), channel_id=1, source_target_pairs={{0,2},{2,0},{4,6},{6,4},{8,14},{10,12},{12,10},{14,8},{16,18},{18,... | collective-permute-start | bytes 344072 | tf_op jit(solution)/shard_map/ppermute | solution.py:430
  6.7 6.2 %collective-permute-start.1 = (f32[72,128]{1,0:T(8,128)S(1)}, f32[72,128]{1,0:T(8,128)S(1)}, u32[]{:S(2)}, u32[]{:S(2)}) collective-permute-start(f32[72,128]{1,0:T(8,128)S(1)} %get-tuple-element.21.refs_0_.after_ref), channel_id=1, source_target_pairs={{0,6},{2,4},{4,2},{6,0},{8,10},{10,8},{12,14},{14,12},{16,22},{18,... | collective-permute-start | bytes 110600 | tf_op jit(solution)/shard_map/ppermute | solution.py:430
  8.2 4.7 %collective-permute-start.2 = (f32[72,128]{1,0:T(8,128)S(1)}, f32[72,128]{1,0:T(8,128)S(1)}, u32[]{:S(2)}, u32[]{:S(2)}) collective-permute-start(f32[72,128]{1,0:T(8,128)S(1)} %get-tuple-element.21.refs_0_.after_ref), channel_id=1, source_target_pairs={{0,4},{2,6},{4,0},{6,2},{1,5},{3,7},{5,1},{7,3},{8,12},{10,14},{12... | collective-permute-start | bytes 110600 | tf_op jit(solution)/shard_map/ppermute | solution.py:21
  8.7 10.9 %collective-permute-start.5 = (bf16[8,64,128]{2,1,0:T(8,128)(2,1)S(1)}, bf16[8,64,128]{2,1,0:T(8,128)(2,1)S(1)}, u32[]{:S(2)}, u32[]{:S(2)}) collective-permute-start(bf16[8,64,128]{2,1,0:T(8,128)(2,1)S(1)} %shard_map.90.pair_ref), channel_id=1, source_target_pairs={{0,16},{8,24},{16,0},{24,8},{1,17},{9,25},{17,1},{25,9},{2,18},{10... | collective-permute-start | bytes 393224 | tf_op jit(solution)/shard_map/ppermute | solution.py:21
  11.4 8.4 %collective-permute-start.6 = (bf16[304,128]{1,0:T(8,128)(2,1)S(1)}, bf16[304,128]{1,0:T(8,128)(2,1)S(1)}, u32[]{:S(2)}, u32[]{:S(2)}) collective-permute-start(bf16[304,128]{1,0:T(8,128)(2,1)S(1)} %slice.4), channel_id=1, source_target_pairs={{0,8},{8,0},{16,24},{24,16},{1,9},{9,1},{17,25},{25,17},{2,10},{10... | collective-permute-start | bytes 233480 | tf_op jit(solution)/shard_map/ppermute | solution.py:21
  13.0 5.6 %collective-permute-start.8 = (bf16[64,128]{1,0:T(8,128)(2,1)S(1)}, bf16[64,128]{1,0:T(8,128)(2,1)S(1)}, u32[]{:S(2)}, u32[]{:S(2)}) collective-permute-start(bf16[64,128]{1,0:T(8,128)(2,1)S(1)} %get-tuple-element.29.low0_ref), channel_id=1, source_target_pairs={{0,16},{8,24},{16,0},{24,8},{1,17},{9,25},{17,1},{25,9},{2,18},{10... | collective-permute-start | bytes 49160 | tf_op jit(solution)/shard_map/ppermute | solution.py:21
  15.7 3.9 %collective-permute-start.9 = (bf16[64,128]{1,0:T(8,128)(2,1)S(1)}, bf16[64,128]{1,0:T(8,128)(2,1)S(1)}, u32[]{:S(2)}, u32[]{:S(2)}) collective-permute-start(bf16[64,128]{1,0:T(8,128)(2,1)S(1)} %get-tuple-element.29.low0_ref), channel_id=1, source_target_pairs={{0,8},{8,0},{16,24},{24,16},{1,9},{9,1},{17,25},{25,17},{2,10},{10... | collective-permute-start | bytes 49160 | tf_op jit(solution)/shard_map/ppermute | solution.py:21
  16.1 5.5 %collective-permute-start.7 = (bf16[64,128]{1,0:T(8,128)(2,1)S(1)}, bf16[64,128]{1,0:T(8,128)(2,1)S(1)}, u32[]{:S(2)}, u32[]{:S(2)}) collective-permute-start(bf16[64,128]{1,0:T(8,128)(2,1)S(1)} %get-tuple-element.29.low0_ref), channel_id=1, source_target_pairs={{0,24},{8,16},{16,8},{24,0},{1,25},{9,17},{17,9},{25,1},{2,26},{10... | collective-permute-start | bytes 49160 | tf_op jit(solution)/shard_map/ppermute | solution.py:21
